TPU v7x, 512 devices: a whole 4x8x8 slice. The times are simulated.
512 devices in a mesh: grp: 32 (over z_lo, y), rep: 16 (over z_hi, x, core).
Axes of the slice: x: 4, y: 8, z: 8 (z_hi: 2, z_lo: 4; z = z_hi * 4 + z_lo), core: 2. Of those that a mesh axis runs over, the one named last changes fastest.
Arguments:
- embeddings: bfloat16 [98304, 1024], P(('grp', 'rep'))
- labels: int32 [98304], P(('grp', 'rep')), may hold values from 0 to 31, as said below
- order: int32 [98304], P(('grp', 'rep')), may hold values from 0 to 98303, each once
Outputs:
- best: float32 [98304], P(('grp', 'rep'))
Inputs may be any that keep to these rules, and one draw needn't show every extreme that they name: `labels`: the indices of grp form consecutive runs of 1 to 4 indices (cluster groups); all members on the devices of one run have one cluster number, and no other run has it; the first run has 4 indices. `order`: each value appears once.
All inputs are finite; a program needn't handle non-finite values.
Results may differ from a plain program's by a relative error of at most 0.00051.
Values may be sent and summed in bfloat16 or wider, within the bound.
No kernel may reach another device: no remote copies, remote signals or barrier semaphores. Data moves between devices by JAX's collectives and lax.ppermute only.
A program may use at most 64 MiB of HBM per device.

v0:
```python
import jax
import jax.numpy as jnp
from jax import lax
from jax.sharding import PartitionSpec as P

GMAX = 4


def from_behind(value, axis, steps):
    count = lax.axis_size(axis)
    leading, last = (max(0, -steps), min(count, count - steps))
    return lax.ppermute(value, axis, [(source, source + steps) for source in range(leading, last)])


def normalize(embeddings):
    values = embeddings.astype(jnp.float32)
    return (values * lax.rsqrt(jnp.sum(values * values, axis=1, keepdims=True) + 1e-06)).astype(
        jnp.bfloat16
    )


def similarity(left, right):
    return lax.dot_general(
        left, right, (((1,), (1,)), ((), ())), preferred_element_type=jnp.float32
    )


def row_maxima(left, left_label, left_order, right, right_label, right_order):
    sims = similarity(left, right)
    same = left_label[:, None] == right_label[None, :]
    return jnp.max(
        jnp.where(same & (right_order[None, :] < left_order[:, None]), sims, -1.0), axis=1
    )


def both_maxima(left, left_label, left_order, right, right_label, right_order):
    sims = similarity(left, right)
    same = left_label[:, None] == right_label[None, :]
    rows = jnp.max(
        jnp.where(same & (right_order[None, :] < left_order[:, None]), sims, -1.0), axis=1
    )
    cols = jnp.max(
        jnp.where(same & (left_order[:, None] < right_order[None, :]), sims, -1.0), axis=0
    )
    return (rows, cols)


def per_device(embeddings, labels, order):
    unit = normalize(embeddings)
    block = unit.shape[0]
    grp_count = lax.axis_size("grp")
    rep_index = lax.axis_index("rep")
    grp_index = lax.axis_index("grp")
    panel_unit, panel_label, panel_order = (
        lax.all_gather(unit, "rep", axis=0, tiled=True),
        lax.all_gather(labels, "rep", axis=0, tiled=True),
        lax.all_gather(order, "rep", axis=0, tiled=True),
    )
    width = panel_unit.shape[0]
    column = jnp.full((width,), -1.0, jnp.float32)
    row_best = row_maxima(unit, labels, order, panel_unit, panel_label, panel_order)
    for step in range(1, GMAX):
        near = from_behind((unit, labels, order), "grp", step)
        active = grp_index >= step
        rows, cols = both_maxima(near[0], near[1], near[2], panel_unit, panel_label, panel_order)
        column = jnp.maximum(column, jnp.where(active, cols, -1.0))
        rows = jnp.where(active, rows, -1.0)
        returned = from_behind(rows, "grp", -step)
        row_best = jnp.maximum(row_best, jnp.where(grp_index + step < grp_count, returned, -1.0))
    column = lax.pmax(column, "rep")
    mine = lax.dynamic_slice_in_dim(column, rep_index * block, block, 0)
    return jnp.maximum(row_best, mine)


def solution(mesh):
    in_specs = (P(("grp", "rep"), None), P(("grp", "rep")), P(("grp", "rep")))
    out_specs = P(("grp", "rep"))
    return jax.shard_map(
        per_device, mesh=mesh, in_specs=in_specs, out_specs=out_specs, check_vma=False
    )
```

profile of v0, /device:TPU:64, one launch (start us, length us, event | category | flops | bytes accessed | tf_op | source)
XLA Modules:
  0.0 284.4 jit_solution(18216079744256748278)
XLA Ops:
  6.5 0.0 all-gather.2.cloned.1.call-start
  6.5 1.2 fusion.1
  7.7 1.9 fusion.2
  9.6 0.0 all-gather.2.cloned.1.call-update
  9.6 4.5 %collective-permute-start.6 = (bf16[192,1024]{1,0:T(8,128)(2,1)}, bf16[192,1024]{1,0:T(8,128)(2,1)S(1)}, u32[]{:S(2)}, u32[]{:S(2)}) collective-permute-start(bf16[192,1024]{1,0:T(8,128)(2,1)} %fusion.2), channel_id=1, source_target_pairs={{0,32},{16,48},{32,64},{48,80},{64,96},{80,112},{96,128},{112,144}... | collective-permute-start | bytes 1179656 | tf_op jit(solution)/shard_map/ppermute | solution.py:12
  14.1 3.5 %collective-permute-start = (s32[192]{0:T(256)}, s32[192]{0:T(256)S(1)}, u32[]{:S(2)}, u32[]{:S(2)}) collective-permute-start(s32[192]{0:T(256)} %param.4), channel_id=1, source_target_pairs={{0,16},{16,32},{32,48},{48,64},{64,80},{80,96},{96,112},{112,128},... | collective-permute-start | bytes 2312 | tf_op jit(solution)/shard_map/ppermute | solution.py:12
  17.6 4.9 %collective-permute-start.8 = (s32[192]{0:T(256)}, s32[192]{0:T(256)S(1)}, u32[]{:S(2)}, u32[]{:S(2)}) collective-permute-start(s32[192]{0:T(256)} %param.4), channel_id=1, source_target_pairs={{0,48},{16,64},{32,80},{48,96},{64,112},{80,128},{96,144},{112,160... | collective-permute-start | bytes 2312 | tf_op jit(solution)/shard_map/ppermute | solution.py:12
  22.6 3.6 %collective-permute-start.4 = (s32[192]{0:T(256)}, s32[192]{0:T(256)S(1)}, u32[]{:S(2)}, u32[]{:S(2)}) collective-permute-start(s32[192]{0:T(256)} %param.4), channel_id=1, source_target_pairs={{0,32},{16,48},{32,64},{48,80},{64,96},{80,112},{96,128},{112,144}... | collective-permute-start | bytes 2312 | tf_op jit(solution)/shard_map/ppermute | solution.py:12
  26.2 3.5 %collective-permute-start.1 = (s32[192]{0:T(256)}, s32[192]{0:T(256)S(1)}, u32[]{:S(2)}, u32[]{:S(2)}) collective-permute-start(s32[192]{0:T(256)} %param.5), channel_id=1, source_target_pairs={{0,16},{16,32},{32,48},{48,64},{64,80},{80,96},{96,112},{112,128},... | collective-permute-start | bytes 2312 | tf_op jit(solution)/shard_map/ppermute | solution.py:12
  29.7 1.3 dynamic-slice
  31.6 0.9 dynamic-update-slice.1
  32.5 0.9 dynamic-update-slice
  33.4 96.6 %all-reduce.2 = (s32[3072]{0:T(1024)S(1)}, s32[3072]{0:T(1024)S(1)}) all-reduce(s32[3072]{0:T(1024)S(1)} %dynamic-update-slice.1, s32[3072]{0:T(1024)S(1)} %dynamic-update-slice), channel_id=1, replica_groups=mesh['grp'=32,'rep'=16] {'rep'}, use_global_device_ids=true, to_apply=%add.1 | all-reduce | flops 6144 | bytes 49152
  130.0 0.0 copy-start.2
  130.0 0.0 copy-start.1
  130.0 0.0 collective-permute-done.6
  130.0 5.7 %collective-permute-start.10 = (bf16[192,1024]{1,0:T(8,128)(2,1)}, bf16[192,1024]{1,0:T(8,128)(2,1)S(1)}, u32[]{:S(2)}, u32[]{:S(2)}) collective-permute-start(bf16[192,1024]{1,0:T(8,128)(2,1)} %fusion.2), channel_id=1, source_target_pairs={{0,48},{16,64},{32,80},{48,96},{64,112},{80,128},{96,144},{112,160... | collective-permute-start | bytes 1179656 | tf_op jit(solution)/shard_map/ppermute | solution.py:12
  135.7 0.0 all-gather.2.cloned.1.call-done
  135.7 0.0 copy-start
  135.7 5.1 %fusion.3 = f32[192,3072]{1,0:T(8,128)S(1)} fusion(bf16[192,1024]{1,0:T(8,128)(2,1)S(1)} %collective-permute-done.6, bf16[3072,1024]{1,0:T(8,128)(2,1)} %all-gather.2.cloned.1.call-done), kind=kOutput, calls=%fused_computation.24 | convolution fusion | flops 1207959552 | bytes 9043968 | tf_op jit(solution)/shard_map/dot_general | solution.py:23
  140.9 0.0 collective-permute-done
  140.9 0.0 copy-done.2
  140.9 2.8 collective-permute-start.9
  143.8 0.0 collective-permute-done.8
  143.8 4.0 %collective-permute-start.5 = (s32[192]{0:T(256)S(1)}, s32[192]{0:T(256)S(1)}, u32[]{:S(2)}, u32[]{:S(2)}) collective-permute-start(s32[192]{0:T(256)S(1)} %copy-done.2), channel_id=1, source_target_pairs={{0,32},{16,48},{32,64},{48,80},{64,96},{80,112},{96,128},{112,144}... | collective-permute-start | bytes 2312 | tf_op jit(solution)/shard_map/ppermute | solution.py:12
  147.8 9.9 %collective-permute-done.10 = bf16[192,1024]{1,0:T(8,128)(2,1)S(1)} collective-permute-done((bf16[192,1024]{1,0:T(8,128)(2,1)}, bf16[192,1024]{1,0:T(8,128)(2,1)S(1)}, u32[]{:S(2)}, u32[]{:S(2)}) %collective-permute-start.10) | collective-permute-done | bytes 393248 | tf_op jit(solution)/shard_map/ppermute | solution.py:12
  157.6 0.0 copy-done.1
  157.6 3.8 %collective-permute-start.2 = (bf16[192,1024]{1,0:T(8,128)(2,1)S(1)}, bf16[192,1024]{1,0:T(8,128)(2,1)S(1)}, u32[]{:S(2)}, u32[]{:S(2)}) collective-permute-start(bf16[192,1024]{1,0:T(8,128)(2,1)S(1)} %copy-done.1), channel_id=1, source_target_pairs={{0,16},{16,32},{32,48},{48,64},{64,80},{80,96},{96,112},{112,128},... | collective-permute-start | bytes 1179656 | tf_op jit(solution)/shard_map/ppermute | solution.py:12
  161.4 0.0 copy-done
  161.4 2.2 fusion.4
  163.7 0.0 collective-permute-done.4
  163.7 0.0 collective-permute-done.1
  163.7 0.0 collective-permute-done.9
  163.7 0.0 collective-permute-done.5
  163.7 6.6 %collective-permute-done.2 = bf16[192,1024]{1,0:T(8,128)(2,1)S(1)} collective-permute-done((bf16[192,1024]{1,0:T(8,128)(2,1)S(1)}, bf16[192,1024]{1,0:T(8,128)(2,1)S(1)}, u32[]{:S(2)}, u32[]{:S(2)}) %collective-permute-start.2) | collective-permute-done | bytes 393248 | tf_op jit(solution)/shard_map/ppermute | solution.py:12
  170.3 0.0 copy-start.3
  170.3 5.1 %select_reduce_fusion.5 = (f32[192]{0:T(256)S(1)}, f32[3072]{0:T(1024)S(1)}, f32[3072]{0:T(1024)S(1)}, f32[192]{0:T(256)S(1)}, f32[3072]{0:T(1024)S(1)}, /*index=5*/f32[192]{0:T(256)S(1)}) fusion(s32[3072]{0:T(1024)S(1)} %get-tuple-element.15, s32[3072]{0:T(1024)S(1)} %get-tuple-element.16, s32[192]{0:T(256)S(1)} %collective-permute-done, ...), kind=kOutput, calls=%fused_computation.12 | convolution fusion | flops 1223874816 | bytes 11471616 | tf_op jit(solution)/shard_map/dot_general | solution.py:23
  175.4 8.0 %collective-permute-start.11 = (f32[192]{0:T(256)S(1)}, f32[192]{0:T(256)S(1)}, u32[]{:S(2)}, u32[]{:S(2)}) collective-permute-start(f32[192]{0:T(256)S(1)} %broadcast_select_fusion), channel_id=1, source_target_pairs={{48,0},{64,16},{80,32},{96,48},{112,64},{128,80},{144,96},{160,112... | collective-permute-start | bytes 2312 | tf_op jit(solution)/shard_map/ppermute | solution.py:12
  183.4 3.8 %collective-permute-start.7 = (f32[192]{0:T(256)S(1)}, f32[192]{0:T(256)S(1)}, u32[]{:S(2)}, u32[]{:S(2)}) collective-permute-start(f32[192]{0:T(256)S(1)} %broadcast_select_fusion.1), channel_id=1, source_target_pairs={{32,0},{48,16},{64,32},{80,48},{96,64},{112,80},{128,96},{144,112}... | collective-permute-start | bytes 2312 | tf_op jit(solution)/shard_map/ppermute | solution.py:12
  187.3 2.9 %collective-permute-start.3 = (f32[192]{0:T(256)S(1)}, f32[192]{0:T(256)S(1)}, u32[]{:S(2)}, u32[]{:S(2)}) collective-permute-start(f32[192]{0:T(256)S(1)} %broadcast_select_fusion.2), channel_id=1, source_target_pairs={{16,0},{32,16},{48,32},{64,48},{80,64},{96,80},{112,96},{128,112},... | collective-permute-start | bytes 2312 | tf_op jit(solution)/shard_map/ppermute | solution.py:12
  190.3 0.0 copy-done.3
  190.3 2.4 fusion
  192.7 84.2 %pmax.7 = f32[3072]{0:T(1024)S(1)} all-reduce(f32[3072]{0:T(1024)S(1)} %select_maximum_fusion), channel_id=1, replica_groups=mesh['grp'=32,'rep'=16] {'rep'}, use_global_device_ids=true, to_apply=%region_8.9 | all-reduce | flops 3072 | bytes 24576 | tf_op jit(solution)/shard_map/pmax | solution.py:70
  276.9 0.0 collective-permute-done.11
  276.9 0.0 collective-permute-done.7
  276.9 0.0 collective-permute-done.3
  276.9 0.6 dynamic-slice_maximum_fusion
  (7 shorter events, 0.0 us)
Async XLA Ops:
  6.5 129.2 %all-gather.2.cloned.1.call-start = ((), (), s32[]{:S(2)}) async-start(), calls=%async_computation | async-start | bytes 6684672 | tf_op jit(solution)/shard_map/all_gather | solution.py:55
  9.6 120.4 %collective-permute-start.6 = (bf16[192,1024]{1,0:T(8,128)(2,1)}, bf16[192,1024]{1,0:T(8,128)(2,1)S(1)}, u32[]{:S(2)}, u32[]{:S(2)}) collective-permute-start(bf16[192,1024]{1,0:T(8,128)(2,1)} %fusion.2), channel_id=1, source_target_pairs={{0,32},{16,48},{32,64},{48,80},{64,96},{80,112},{96,128},{112,144}... | collective-permute-start | bytes 1179656 | tf_op jit(solution)/shard_map/ppermute | solution.py:12
  14.1 126.8 %collective-permute-start = (s32[192]{0:T(256)}, s32[192]{0:T(256)S(1)}, u32[]{:S(2)}, u32[]{:S(2)}) collective-permute-start(s32[192]{0:T(256)} %param.4), channel_id=1, source_target_pairs={{0,16},{16,32},{32,48},{48,64},{64,80},{80,96},{96,112},{112,128},... | collective-permute-start | bytes 2312 | tf_op jit(solution)/shard_map/ppermute | solution.py:12
  17.6 126.1 %collective-permute-start.8 = (s32[192]{0:T(256)}, s32[192]{0:T(256)S(1)}, u32[]{:S(2)}, u32[]{:S(2)}) collective-permute-start(s32[192]{0:T(256)} %param.4), channel_id=1, source_target_pairs={{0,48},{16,64},{32,80},{48,96},{64,112},{80,128},{96,144},{112,160... | collective-permute-start | bytes 2312 | tf_op jit(solution)/shard_map/ppermute | solution.py:12
  22.6 141.1 %collective-permute-start.4 = (s32[192]{0:T(256)}, s32[192]{0:T(256)S(1)}, u32[]{:S(2)}, u32[]{:S(2)}) collective-permute-start(s32[192]{0:T(256)} %param.4), channel_id=1, source_target_pairs={{0,32},{16,48},{32,64},{48,80},{64,96},{80,112},{96,128},{112,144}... | collective-permute-start | bytes 2312 | tf_op jit(solution)/shard_map/ppermute | solution.py:12
  26.2 137.5 %collective-permute-start.1 = (s32[192]{0:T(256)}, s32[192]{0:T(256)S(1)}, u32[]{:S(2)}, u32[]{:S(2)}) collective-permute-start(s32[192]{0:T(256)} %param.5), channel_id=1, source_target_pairs={{0,16},{16,32},{32,48},{48,64},{64,80},{80,96},{96,112},{112,128},... | collective-permute-start | bytes 2312 | tf_op jit(solution)/shard_map/ppermute | solution.py:12
  130.0 10.9 %copy-start.2 = (s32[192]{0:T(256)S(1)}, s32[192]{0:T(256)}, u32[]{:S(2)}) copy-start(s32[192]{0:T(256)} %param.5) | copy-start | bytes 2308
  130.0 27.6 %copy-start.1 = (bf16[192,1024]{1,0:T(8,128)(2,1)S(1)}, bf16[192,1024]{1,0:T(8,128)(2,1)}, u32[]{:S(2)}) copy-start(bf16[192,1024]{1,0:T(8,128)(2,1)} %fusion.2) | copy-start | bytes 1179652
  130.0 27.6 %collective-permute-start.10 = (bf16[192,1024]{1,0:T(8,128)(2,1)}, bf16[192,1024]{1,0:T(8,128)(2,1)S(1)}, u32[]{:S(2)}, u32[]{:S(2)}) collective-permute-start(bf16[192,1024]{1,0:T(8,128)(2,1)} %fusion.2), channel_id=1, source_target_pairs={{0,48},{16,64},{32,80},{48,96},{64,112},{80,128},{96,144},{112,160... | collective-permute-start | bytes 1179656 | tf_op jit(solution)/shard_map/ppermute | solution.py:12
  135.7 25.7 %copy-start = (bf16[3072,1024]{1,0:T(8,128)(2,1)S(1)}, bf16[3072,1024]{1,0:T(8,128)(2,1)}, u32[]{:S(2)}) copy-start(bf16[3072,1024]{1,0:T(8,128)(2,1)} %all-gather.2.cloned.1.call-done) | copy-start | bytes 18874372
  140.9 22.8 %collective-permute-start.9 = (s32[192]{0:T(256)S(1)}, s32[192]{0:T(256)S(1)}, u32[]{:S(2)}, u32[]{:S(2)}) collective-permute-start(s32[192]{0:T(256)S(1)} %copy-done.2), channel_id=1, source_target_pairs={{0,48},{16,64},{32,80},{48,96},{64,112},{80,128},{96,144},{112,160... | collective-permute-start | bytes 2312 | tf_op jit(solution)/shard_map/ppermute | solution.py:12
  143.8 19.9 %collective-permute-start.5 = (s32[192]{0:T(256)S(1)}, s32[192]{0:T(256)S(1)}, u32[]{:S(2)}, u32[]{:S(2)}) collective-permute-start(s32[192]{0:T(256)S(1)} %copy-done.2), channel_id=1, source_target_pairs={{0,32},{16,48},{32,64},{48,80},{64,96},{80,112},{96,128},{112,144}... | collective-permute-start | bytes 2312 | tf_op jit(solution)/shard_map/ppermute | solution.py:12
  157.6 12.6 %collective-permute-start.2 = (bf16[192,1024]{1,0:T(8,128)(2,1)S(1)}, bf16[192,1024]{1,0:T(8,128)(2,1)S(1)}, u32[]{:S(2)}, u32[]{:S(2)}) collective-permute-start(bf16[192,1024]{1,0:T(8,128)(2,1)S(1)} %copy-done.1), channel_id=1, source_target_pairs={{0,16},{16,32},{32,48},{48,64},{64,80},{80,96},{96,112},{112,128},... | collective-permute-start | bytes 1179656 | tf_op jit(solution)/shard_map/ppermute | solution.py:12
  170.3 20.0 %copy-start.3 = (s32[192]{0:T(256)S(1)}, s32[192]{0:T(256)}, u32[]{:S(2)}) copy-start(s32[192]{0:T(256)} %param.4) | copy-start | bytes 2308
  175.4 101.5 %collective-permute-start.11 = (f32[192]{0:T(256)S(1)}, f32[192]{0:T(256)S(1)}, u32[]{:S(2)}, u32[]{:S(2)}) collective-permute-start(f32[192]{0:T(256)S(1)} %broadcast_select_fusion), channel_id=1, source_target_pairs={{48,0},{64,16},{80,32},{96,48},{112,64},{128,80},{144,96},{160,112... | collective-permute-start | bytes 2312 | tf_op jit(solution)/shard_map/ppermute | solution.py:12
  183.4 93.4 %collective-permute-start.7 = (f32[192]{0:T(256)S(1)}, f32[192]{0:T(256)S(1)}, u32[]{:S(2)}, u32[]{:S(2)}) collective-permute-start(f32[192]{0:T(256)S(1)} %broadcast_select_fusion.1), channel_id=1, source_target_pairs={{32,0},{48,16},{64,32},{80,48},{96,64},{112,80},{128,96},{144,112}... | collective-permute-start | bytes 2312 | tf_op jit(solution)/shard_map/ppermute | solution.py:12
  187.3 89.6 %collective-permute-start.3 = (f32[192]{0:T(256)S(1)}, f32[192]{0:T(256)S(1)}, u32[]{:S(2)}, u32[]{:S(2)}) collective-permute-start(f32[192]{0:T(256)S(1)} %broadcast_select_fusion.2), channel_id=1, source_target_pairs={{16,0},{32,16},{48,32},{64,48},{80,64},{96,80},{112,96},{128,112},... | collective-permute-start | bytes 2312 | tf_op jit(solution)/shard_map/ppermute | solution.py:12
Sparse Core Ops, SparseCore 0:
  10.7 102.2 all-gather.1
where the time goes:
time: 285 us; the launch traced here: 284 us
  blocking collectives  181 us (64%)
  starting transfers between devices  51.1 us (18%)
  waiting for transfers between devices  16.5 us (6%)
  matrix products  14.9 us (5%)
  between operations  14.3 us (5%)
  other arithmetic  3.74 us (1%)
  local copies, waits for them, and re-layouts  3.06 us (1%)
    unnamed x1, blocking collectives  96.6 us
    pmax x1, blocking collectives, per_device(): column = lax.pmax(column, 'rep')  84.2 us
    ppermute x12, starting transfers between devices, from_behind(): lax.ppermute(value, axis, [(source, source + steps) for source in range(l...  51 us
    ppermute x12, waiting for transfers between devices, from_behind(): lax.ppermute(value, axis, [(source, source + steps) for source in range(l...  16.5 us
    dot_general x4, matrix products, similarity(): lax.dot_general(left, right, (((1,), (1,)), ((), ())), preferred_element_...  14.9 us
  transfers between devices with their start and end apart: 13, of which 2 were waited for; matrix products, arithmetic and copies ran while one was open for 5% of the time, Pallas kernels for 0%

commit v1 on v0

v1 whole, which is shorter than its diff:
```python
import functools

import jax
import jax.numpy as jnp
from jax import lax
from jax.experimental import pallas as pl
from jax.experimental.pallas import tpu as pltpu
from jax.sharding import Mesh, PartitionSpec as P

ROWS = 192
EXTRA = 16
PACK = ROWS + EXTRA
D = 1024
NEAR = 4
XC = 8
TILE = 256
FAR = 1.0e9


def pack_kernel(emb_ref, lab_ref, ord_ref, out_ref):
    values = emb_ref[...].astype(jnp.float32)
    scale = lax.rsqrt(jnp.sum(values * values, axis=1, keepdims=True) + 1e-06)
    out_ref[0:ROWS, :] = (values * scale).astype(jnp.bfloat16)
    rank = jnp.broadcast_to(ord_ref[...], (EXTRA, ROWS))
    label = jnp.broadcast_to(lab_ref[...], (EXTRA, ROWS))
    line = lax.broadcasted_iota(jnp.int32, (EXTRA, ROWS), 0)
    digits = jnp.where(
        line == 0,
        rank >> 12,
        jnp.where(line == 1, (rank >> 6) & 63, jnp.where(line == 2, rank & 63, label + 1)),
    )
    digits = jnp.where(line < 4, digits, 0).astype(jnp.float32)
    digits = jnp.concatenate([digits, jnp.zeros((EXTRA, D - ROWS), jnp.float32)], axis=1)
    out_ref[ROWS:PACK, :] = digits.astype(jnp.bfloat16)


def pack(embeddings, labels, order):
    return pl.pallas_call(
        pack_kernel,
        out_shape=jax.ShapeDtypeStruct((PACK, D), jnp.bfloat16),
        name="normalize_pack",
        cost_estimate=pl.CostEstimate(flops=4 * ROWS * D, bytes_accessed=4 * ROWS * D, transcendentals=ROWS),
    )(embeddings, labels.reshape(1, ROWS), order.reshape(1, ROWS))


def ranks(extra):
    digits = extra.astype(jnp.float32)
    return digits[0:1, :ROWS] * 4096.0 + digits[1:2, :ROWS] * 64.0 + digits[2:3, :ROWS]


def half_kernel(
    own_ref, a_ref, b_ref, c_ref, panel_ref, prior_ref, cols_ref, rows_ref,
    left, left_extra, right, right_extra, rank_col, row_best, near_sem, panel_sem,
):
    copies = []
    for s, ref in enumerate((own_ref, a_ref, b_ref, c_ref)):
        copies.append(pltpu.make_async_copy(ref.at[ROWS:PACK], left_extra.at[s], near_sem.at[2 * s]))
        copies.append(pltpu.make_async_copy(ref.at[0:ROWS], left.at[s * ROWS:(s + 1) * ROWS], near_sem.at[2 * s + 1]))
    for k in range(XC):
        copies.append(pltpu.make_async_copy(panel_ref.at[k, ROWS:PACK], right_extra.at[k], panel_sem.at[2 * k]))
        copies.append(
            pltpu.make_async_copy(panel_ref.at[k, 0:ROWS], right.at[k * ROWS:(k + 1) * ROWS], panel_sem.at[2 * k + 1])
        )
    for copy in copies:
        copy.start()
    for copy in copies:
        copy.wait()
    own_label = left_extra[0].astype(jnp.float32)[3:4, :ROWS]
    same = [left_extra[s].astype(jnp.float32)[3:4, :ROWS] == own_label for s in range(NEAR)]
    near_rank = jnp.concatenate(
        [jnp.where(same[s], ranks(left_extra[s]), FAR) for s in range(NEAR)], axis=1
    )
    rank_col[...] = jnp.transpose(jnp.broadcast_to(near_rank, (128, NEAR * ROWS)), (1, 0))
    panel_rank = jnp.concatenate([ranks(right_extra[k]) for k in range(XC)], axis=1)
    row_best[...] = jnp.full(row_best.shape, -1.0, jnp.float32)
    cols = []
    for t in range(XC * ROWS // TILE):
        sims = lax.dot_general(
            left[...], right[t * TILE:(t + 1) * TILE, :], (((1,), (1,)), ((), ())),
            preferred_element_type=jnp.float32,
        )
        for h in range(TILE // 128):
            part = sims[:, h * 128:(h + 1) * 128]
            rank_row = panel_rank[:, t * TILE + h * 128:t * TILE + (h + 1) * 128]
            here = part[:ROWS]
            best = jnp.max(jnp.where(rank_col[:ROWS] < rank_row, here, -1.0), axis=0, keepdims=True)
            there = part[ROWS:]
            earlier = rank_row < rank_col[ROWS:]
            best = jnp.maximum(best, jnp.max(jnp.where(earlier, -1.0, there), axis=0, keepdims=True))
            row_best[...] = jnp.maximum(row_best[...], jnp.where(earlier, there, -1.0))
            cols.append(best)
    best = jnp.concatenate(cols, axis=1)
    for k in range(XC):
        cols_ref[k:k + 1, :] = best[:, k * ROWS:(k + 1) * ROWS]
    rows = jnp.max(jnp.transpose(row_best[...], (1, 0)), axis=0, keepdims=True)
    for s in range(1, NEAR):
        line = jnp.where(same[s], rows[:, (s - 1) * ROWS:s * ROWS], -1.0)
        rows_ref[s - 1] = jnp.maximum(line, prior_ref[s - 1])


def half(own, near, panel, prior):
    anywhere = pl.BlockSpec(memory_space=pl.ANY)
    inside = pl.BlockSpec(memory_space=pltpu.VMEM)
    return pl.pallas_call(
        half_kernel,
        out_shape=(
            jax.ShapeDtypeStruct((XC, ROWS), jnp.float32),
            jax.ShapeDtypeStruct((NEAR - 1, 1, ROWS), jnp.float32),
        ),
        in_specs=[anywhere] * 5 + [inside],
        out_specs=(inside, inside),
        scratch_shapes=[
            pltpu.VMEM((NEAR * ROWS, D), jnp.bfloat16),
            pltpu.VMEM((NEAR, EXTRA, D), jnp.bfloat16),
            pltpu.VMEM((XC * ROWS, D), jnp.bfloat16),
            pltpu.VMEM((XC, EXTRA, D), jnp.bfloat16),
            pltpu.VMEM((NEAR * ROWS, 128), jnp.float32),
            pltpu.VMEM(((NEAR - 1) * ROWS, 128), jnp.float32),
            pltpu.SemaphoreType.DMA((2 * NEAR,)),
            pltpu.SemaphoreType.DMA((2 * XC,)),
        ],
        compiler_params=pltpu.CompilerParams(vmem_limit_bytes=40 * 1024 * 1024),
        name="half_maxima",
        cost_estimate=pl.CostEstimate(
            flops=2 * NEAR * XC * ROWS * ROWS * D, bytes_accessed=2 * (NEAR + XC) * PACK * D, transcendentals=0
        ),
    )(own, *near, panel, prior)


def shift(value, steps, count):
    pairs = [(i, i + steps) for i in range(count) if 0 <= i + steps < count]
    return lax.ppermute(value, "grp", pairs)


def per_device(embeddings, labels, order):
    count = lax.axis_size("grp")
    grp = lax.axis_index("grp")
    zh = lax.axis_index("zh")
    block = pack(embeddings, labels, order)
    flipped = lax.ppermute(block, "zh", [(0, 1), (1, 0)])
    panel = lax.all_gather(block, "xc", axis=0, tiled=False)
    moves = (3 * -1, 1, 2)
    near = [shift(block, steps, count) for steps in moves]
    other = lax.all_gather(flipped, "xc", axis=0, tiled=False)
    prior = jnp.full((NEAR - 1, 1, ROWS), -1.0, jnp.float32)
    cols_own, prior = half(block, near, panel, prior)
    cols_other, rows = half(block, near, other, prior)
    cols = jnp.where(
        zh == 0,
        jnp.concatenate([cols_own, cols_other], axis=0),
        jnp.concatenate([cols_other, cols_own], axis=0),
    )
    best = jnp.max(lax.all_to_all(cols, ("zh", "xc"), 0, 0, tiled=True), axis=0)
    for i, steps in enumerate(moves):
        back = shift(rows[i], -steps, count).reshape(ROWS)
        source = grp + steps
        best = jnp.maximum(best, jnp.where((source >= 0) & (source < count), back, -1.0))
    return best


def solution(mesh):
    fine = Mesh(mesh.devices.reshape(mesh.shape["grp"], 2, XC), ("grp", "zh", "xc"))
    spec = P(("grp", "zh", "xc"))
    return jax.shard_map(
        per_device,
        mesh=fine,
        in_specs=(P(("grp", "zh", "xc"), None), spec, spec),
        out_specs=spec,
        check_vma=False,
    )
```

time: 285 us -> 129 us (0.45)
  the two profiles are of different devices: /device:TPU:64 before, /device:TPU:186 now
where the time goes in v1:
time: 129 us; the launch traced here: 128 us
  waiting for transfers between devices  50.5 us (39%)
  starting transfers between devices  43.6 us (34%)
  Pallas kernels  13.6 us (11%)
  between operations  13.6 us (11%)
  local copies, waits for them, and re-layouts  6.38 us (5%)
    ppermute x6, waiting for transfers between devices, shift(): return lax.ppermute(value, 'grp', pairs)  31.2 us
    ppermute x6, starting transfers between devices, shift(): return lax.ppermute(value, 'grp', pairs)  25.9 us
    ppermute x1, waiting for transfers between devices, per_device(): flipped = lax.ppermute(block, 'zh', [(0, 1), (1, 0)])  19.2 us
    pallas_call x2, Pallas kernels, half(): pl.pallas_call(half_kernel, out_shape=(jax.ShapeDtypeStruct((XC, ROWS), j...  11.7 us
    ppermute x1, starting transfers between devices, per_device(): flipped = lax.ppermute(block, 'zh', [(0, 1), (1, 0)])  9.12 us
    all_to_all x1, starting transfers between devices, per_device(): best = jnp.max(lax.all_to_all(cols, ('zh', 'xc'), 0, 0, tiled=True), axis=0)  8.56 us
    unnamed x10, local copies, waits for them, and re-layouts  5.76 us
  transfers between devices with their start and end apart: 10, of which 4 were waited for; matrix products, arithmetic and copies ran while one was open for 1% of the time, Pallas kernels for 5%

profile of v1, /device:TPU:186, one launch (start us, length us, event | category | flops | bytes accessed | tf_op | source)
XLA Modules:
  0.0 128.3 jit_solution(8962269699704105365)
XLA Ops:
  6.5 0.0 all-gather.5.cloned.1.call-start
  6.5 1.9 %normalize_pack.1.own_ref = bf16[208,1024]{1,0:T(8,128)(2,1)} custom-call(bf16[192,1024]{1,0:T(8,128)(2,1)} %emb_ref.1, s32[1,192]{1,0:T(1,128)} %bitcast.22, s32[1,192]{1,0:T(1,128)} %bitcast.23), custom_call_target="tpu_custom_call" | custom-call | flops 786432 | bytes 786432 | tf_op jit(solution)/shard_map/normalize_pack/pallas_call | solution.py:38
  8.5 0.0 all-gather.5.cloned.1.call-update
  8.5 0.0 all-gather.7.cloned.1.call-start
  8.6 9.1 %collective-permute-start.3 = (bf16[208,1024]{1,0:T(8,128)(2,1)}, bf16[208,1024]{1,0:T(8,128)(2,1)S(1)}, u32[]{:S(2)}, u32[]{:S(2)}) collective-permute-start(bf16[208,1024]{1,0:T(8,128)(2,1)} %normalize_pack.1.own_ref), channel_id=1, source_target_pairs={{0,8},{8,0},{1,9},{9,1},{2,10},{10,2},{3,11},{11,3},{4,12},{12,4},... | collective-permute-start | bytes 1277960 | tf_op jit(solution)/shard_map/ppermute | solution.py:140
  17.7 19.2 %collective-permute-done.3 = bf16[208,1024]{1,0:T(8,128)(2,1)S(1)} collective-permute-done((bf16[208,1024]{1,0:T(8,128)(2,1)}, bf16[208,1024]{1,0:T(8,128)(2,1)S(1)}, u32[]{:S(2)}, u32[]{:S(2)}) %collective-permute-start.3) | collective-permute-done | bytes 426016 | tf_op jit(solution)/shard_map/ppermute | solution.py:140
  36.9 0.0 copy-start.4
  36.9 0.8 copy-done.4
  37.7 0.0 all-gather.7.cloned.1.call-update
  37.7 4.8 %collective-permute-start = (bf16[208,1024]{1,0:T(8,128)(2,1)}, bf16[208,1024]{1,0:T(8,128)(2,1)S(1)}, u32[]{:S(2)}, u32[]{:S(2)}) collective-permute-start(bf16[208,1024]{1,0:T(8,128)(2,1)} %normalize_pack.1.own_ref), channel_id=1, source_target_pairs={{48,0},{64,16},{80,32},{96,48},{112,64},{128,80},{144,96},{160,112... | collective-permute-start | bytes 1277960 | tf_op jit(solution)/shard_map/ppermute | solution.py:132
  42.5 4.7 %collective-permute-start.1 = (bf16[208,1024]{1,0:T(8,128)(2,1)}, bf16[208,1024]{1,0:T(8,128)(2,1)S(1)}, u32[]{:S(2)}, u32[]{:S(2)}) collective-permute-start(bf16[208,1024]{1,0:T(8,128)(2,1)} %normalize_pack.1.own_ref), channel_id=1, source_target_pairs={{0,16},{16,32},{32,48},{48,64},{64,80},{80,96},{96,112},{112,128},... | collective-permute-start | bytes 1277960 | tf_op jit(solution)/shard_map/ppermute | solution.py:132
  47.2 2.7 %collective-permute-start.2 = (bf16[208,1024]{1,0:T(8,128)(2,1)}, bf16[208,1024]{1,0:T(8,128)(2,1)S(1)}, u32[]{:S(2)}, u32[]{:S(2)}) collective-permute-start(bf16[208,1024]{1,0:T(8,128)(2,1)} %normalize_pack.1.own_ref), channel_id=1, source_target_pairs={{0,32},{16,48},{32,64},{48,80},{64,96},{80,112},{96,128},{112,144}... | collective-permute-start | bytes 1277960 | tf_op jit(solution)/shard_map/ppermute | solution.py:132
  49.9 19.1 %collective-permute-done.a_ref = bf16[208,1024]{1,0:T(8,128)(2,1)S(1)} collective-permute-done((bf16[208,1024]{1,0:T(8,128)(2,1)}, bf16[208,1024]{1,0:T(8,128)(2,1)S(1)}, u32[]{:S(2)}, u32[]{:S(2)}) %collective-permute-start) | collective-permute-done | bytes 426016 | tf_op jit(solution)/shard_map/ppermute | solution.py:132
  69.0 0.0 collective-permute-done.1.b_ref
  69.0 5.6 %collective-permute-done.2.c_ref = bf16[208,1024]{1,0:T(8,128)(2,1)S(1)} collective-permute-done((bf16[208,1024]{1,0:T(8,128)(2,1)}, bf16[208,1024]{1,0:T(8,128)(2,1)S(1)}, u32[]{:S(2)}, u32[]{:S(2)}) %collective-permute-start.2) | collective-permute-done | bytes 426016 | tf_op jit(solution)/shard_map/ppermute | solution.py:132
  74.7 0.0 all-gather.5.cloned.1.call-done
  74.7 0.0 copy-start
  74.7 1.0 copy-done
  75.7 0.0 copy-start.2
  75.7 2.0 %copy-done.2 = bf16[1664,1024]{1,0:T(8,128)(2,1)S(1)} copy-done((bf16[1664,1024]{1,0:T(8,128)(2,1)S(1)}, bf16[1664,1024]{1,0:T(8,128)(2,1)}, u32[]{:S(2)}) %copy-start.2) | copy-done | bytes 3407896
  77.7 0.0 copy-start.1
  77.7 5.9 %half_maxima.2 = (f32[8,192]{1,0:T(8,128)S(1)}, f32[3,1,192]{2,1,0:T(1,128)S(1)}) custom-call(bf16[208,1024]{1,0:T(8,128)(2,1)S(1)} %copy-done, bf16[208,1024]{1,0:T(8,128)(2,1)S(1)} %collective-permute-done.a_ref, bf16[208,1024]{1,0:T(8,128)(2,1)S(1)} %collective-permute-done.1.b_ref, bf16[208,1024]{1,0:T(8,128)(2,1)S(1)} %collective-permute-done.2.c_ref, ...), custom_call_target="tpu_custom_call" | custom-call | flops 2415919104 | bytes 5111808 | tf_op jit(solution)/shard_map/half_maxima/pallas_call | solution.py:104
  83.6 0.0 all-gather.7.cloned.1.call-done
  83.6 0.0 copy-done.1
  83.6 0.0 copy-start.3
  83.6 2.0 %copy-done.3 = bf16[1664,1024]{1,0:T(8,128)(2,1)S(1)} copy-done((bf16[1664,1024]{1,0:T(8,128)(2,1)S(1)}, bf16[1664,1024]{1,0:T(8,128)(2,1)}, u32[]{:S(2)}) %copy-start.3) | copy-done | bytes 3407896
  85.6 5.8 %half_maxima.3 = (f32[8,192]{1,0:T(8,128)S(1)}, f32[3,1,192]{2,1,0:T(1,128)S(1)}) custom-call(bf16[208,1024]{1,0:T(8,128)(2,1)S(1)} %copy-done.1, bf16[208,1024]{1,0:T(8,128)(2,1)S(1)} %collective-permute-done.a_ref, bf16[208,1024]{1,0:T(8,128)(2,1)S(1)} %collective-permute-done.1.b_ref, bf16[208,1024]{1,0:T(8,128)(2,1)S(1)} %collective-permute-done.2.c_ref, ...), custom_call_target="tpu_custom_call" | custom-call | flops 2415919104 | bytes 5111808 | tf_op jit(solution)/shard_map/half_maxima/pallas_call | solution.py:104
  91.4 3.1 %collective-permute-start.4 = (f32[1,192]{1,0:T(1,128)S(1)}, f32[1,192]{1,0:T(1,128)S(1)}, u32[]{:S(2)}, u32[]{:S(2)}) collective-permute-start(f32[1,192]{1,0:T(1,128)S(1)} %get-tuple-element.13), channel_id=1, source_target_pairs={{0,48},{16,64},{32,80},{48,96},{64,112},{80,128},{96,144},{112,160... | collective-permute-start | bytes 2312 | tf_op jit(solution)/shard_map/ppermute | solution.py:132
  94.5 0.6 copy.4
  95.1 8.6 %all-to-all-start = ((f32[16,1,192]{2,1,0:T(1,128)}), f32[16,1,192]{2,1,0:T(1,128)S(1)}, u32[]{:S(2)}, u32[]{:S(2)}) async-start(f32[16,1,192]{2,1,0:T(1,128)} %copy.4), calls=%async_computation | async-start | bytes 32768 | tf_op jit(solution)/shard_map/all_to_all | solution.py:153
  103.7 8.7 %collective-permute-start.5 = (f32[1,192]{1,0:T(1,128)S(1)}, f32[1,192]{1,0:T(1,128)S(1)}, u32[]{:S(2)}, u32[]{:S(2)}) collective-permute-start(f32[1,192]{1,0:T(1,128)S(1)} %get-tuple-element.15), channel_id=1, source_target_pairs={{16,0},{32,16},{48,32},{64,48},{80,64},{96,80},{112,96},{128,112},... | collective-permute-start | bytes 2312 | tf_op jit(solution)/shard_map/ppermute | solution.py:132
  112.4 1.9 %collective-permute-start.6 = (f32[1,192]{1,0:T(1,128)S(1)}, f32[1,192]{1,0:T(1,128)S(1)}, u32[]{:S(2)}, u32[]{:S(2)}) collective-permute-start(f32[1,192]{1,0:T(1,128)S(1)} %get-tuple-element.14), channel_id=1, source_target_pairs={{32,0},{48,16},{64,32},{80,48},{96,64},{112,80},{128,96},{144,112}... | collective-permute-start | bytes 2312 | tf_op jit(solution)/shard_map/ppermute | solution.py:132
  114.3 0.0 collective-permute-done.4
  114.4 0.0 collective-permute-done.5
  114.4 6.5 %collective-permute-done.6 = f32[1,192]{1,0:T(1,128)S(1)} collective-permute-done((f32[1,192]{1,0:T(1,128)S(1)}, f32[1,192]{1,0:T(1,128)S(1)}, u32[]{:S(2)}, u32[]{:S(2)}) %collective-permute-start.6) | collective-permute-done | bytes 800 | tf_op jit(solution)/shard_map/ppermute | solution.py:132
  120.9 0.0 all-to-all-done
  120.9 0.6 maximum_maximum_fusion
  (7 shorter events, 0.1 us)
Async XLA Ops:
  6.5 68.1 %all-gather.5.cloned.1.call-start = ((), (), s32[]{:S(2)}) async-start(), calls=%async_computation.1 | async-start | bytes 3833856 | tf_op jit(solution)/shard_map/all_gather | solution.py:141
  8.5 75.1 %all-gather.7.cloned.1.call-start = ((), (), s32[]{:S(2)}) async-start(), calls=%async_computation.2 | async-start | bytes 3833856 | tf_op jit(solution)/shard_map/all_gather | solution.py:144
  8.6 28.3 %collective-permute-start.3 = (bf16[208,1024]{1,0:T(8,128)(2,1)}, bf16[208,1024]{1,0:T(8,128)(2,1)S(1)}, u32[]{:S(2)}, u32[]{:S(2)}) collective-permute-start(bf16[208,1024]{1,0:T(8,128)(2,1)} %normalize_pack.1.own_ref), channel_id=1, source_target_pairs={{0,8},{8,0},{1,9},{9,1},{2,10},{10,2},{3,11},{11,3},{4,12},{12,4},... | collective-permute-start | bytes 1277960 | tf_op jit(solution)/shard_map/ppermute | solution.py:140
  36.9 0.8 copy-start.4
  37.7 31.3 %collective-permute-start = (bf16[208,1024]{1,0:T(8,128)(2,1)}, bf16[208,1024]{1,0:T(8,128)(2,1)S(1)}, u32[]{:S(2)}, u32[]{:S(2)}) collective-permute-start(bf16[208,1024]{1,0:T(8,128)(2,1)} %normalize_pack.1.own_ref), channel_id=1, source_target_pairs={{48,0},{64,16},{80,32},{96,48},{112,64},{128,80},{144,96},{160,112... | collective-permute-start | bytes 1277960 | tf_op jit(solution)/shard_map/ppermute | solution.py:132
  42.5 26.5 %collective-permute-start.1 = (bf16[208,1024]{1,0:T(8,128)(2,1)}, bf16[208,1024]{1,0:T(8,128)(2,1)S(1)}, u32[]{:S(2)}, u32[]{:S(2)}) collective-permute-start(bf16[208,1024]{1,0:T(8,128)(2,1)} %normalize_pack.1.own_ref), channel_id=1, source_target_pairs={{0,16},{16,32},{32,48},{48,64},{64,80},{80,96},{96,112},{112,128},... | collective-permute-start | bytes 1277960 | tf_op jit(solution)/shard_map/ppermute | solution.py:132
  47.2 27.4 %collective-permute-start.2 = (bf16[208,1024]{1,0:T(8,128)(2,1)}, bf16[208,1024]{1,0:T(8,128)(2,1)S(1)}, u32[]{:S(2)}, u32[]{:S(2)}) collective-permute-start(bf16[208,1024]{1,0:T(8,128)(2,1)} %normalize_pack.1.own_ref), channel_id=1, source_target_pairs={{0,32},{16,48},{32,64},{48,80},{64,96},{80,112},{96,128},{112,144}... | collective-permute-start | bytes 1277960 | tf_op jit(solution)/shard_map/ppermute | solution.py:132
  74.7 1.0 copy-start
  75.7 2.0 %copy-start.2 = (bf16[1664,1024]{1,0:T(8,128)(2,1)S(1)}, bf16[1664,1024]{1,0:T(8,128)(2,1)}, u32[]{:S(2)}) copy-start(bf16[1664,1024]{1,0:T(8,128)(2,1)} %all-gather.5.cloned.1.call-done) | copy-start | bytes 10223620
  77.7 5.9 %copy-start.1 = (bf16[208,1024]{1,0:T(8,128)(2,1)S(1)}, bf16[208,1024]{1,0:T(8,128)(2,1)}, u32[]{:S(2)}) copy-start(bf16[208,1024]{1,0:T(8,128)(2,1)} %normalize_pack.1.own_ref) | copy-start | bytes 1277956
  83.6 2.0 %copy-start.3 = (bf16[1664,1024]{1,0:T(8,128)(2,1)S(1)}, bf16[1664,1024]{1,0:T(8,128)(2,1)}, u32[]{:S(2)}) copy-start(bf16[1664,1024]{1,0:T(8,128)(2,1)} %all-gather.7.cloned.1.call-done) | copy-start | bytes 10223620
  91.4 22.9 %collective-permute-start.4 = (f32[1,192]{1,0:T(1,128)S(1)}, f32[1,192]{1,0:T(1,128)S(1)}, u32[]{:S(2)}, u32[]{:S(2)}) collective-permute-start(f32[1,192]{1,0:T(1,128)S(1)} %get-tuple-element.13), channel_id=1, source_target_pairs={{0,48},{16,64},{32,80},{48,96},{64,112},{80,128},{96,144},{112,160... | collective-permute-start | bytes 2312 | tf_op jit(solution)/shard_map/ppermute | solution.py:132
  95.1 25.8 %all-to-all-start = ((f32[16,1,192]{2,1,0:T(1,128)}), f32[16,1,192]{2,1,0:T(1,128)S(1)}, u32[]{:S(2)}, u32[]{:S(2)}) async-start(f32[16,1,192]{2,1,0:T(1,128)} %copy.4), calls=%async_computation | async-start | bytes 32768 | tf_op jit(solution)/shard_map/all_to_all | solution.py:153
  103.7 10.7 %collective-permute-start.5 = (f32[1,192]{1,0:T(1,128)S(1)}, f32[1,192]{1,0:T(1,128)S(1)}, u32[]{:S(2)}, u32[]{:S(2)}) collective-permute-start(f32[1,192]{1,0:T(1,128)S(1)} %get-tuple-element.15), channel_id=1, source_target_pairs={{16,0},{32,16},{48,32},{64,48},{80,64},{96,80},{112,96},{128,112},... | collective-permute-start | bytes 2312 | tf_op jit(solution)/shard_map/ppermute | solution.py:132
  112.4 8.5 %collective-permute-start.6 = (f32[1,192]{1,0:T(1,128)S(1)}, f32[1,192]{1,0:T(1,128)S(1)}, u32[]{:S(2)}, u32[]{:S(2)}) collective-permute-start(f32[1,192]{1,0:T(1,128)S(1)} %get-tuple-element.14), channel_id=1, source_target_pairs={{32,0},{48,16},{64,32},{80,48},{96,64},{112,80},{128,96},{144,112}... | collective-permute-start | bytes 2312 | tf_op jit(solution)/shard_map/ppermute | solution.py:132
Sparse Core Ops, SparseCore 0:
  9.5 35.6 all-gather.4
  47.3 34.1 all-gather.6

commit v2 on v1

v2 whole, which is shorter than its diff:
```python
import jax
import jax.numpy as jnp
from jax import lax
from jax.experimental import pallas as pl
from jax.experimental.pallas import tpu as pltpu
from jax.sharding import Mesh, PartitionSpec as P

ROWS = 192
EXTRA = 16
PACK = ROWS + EXTRA
D = 1024
X = 4
MOVES = (-3, 1, 2)
NEAR = 1 + len(MOVES)
LEFT = 2 * NEAR * ROWS
TILE = 256
FAR = 1.0e9


def pack_kernel(emb_ref, lab_ref, ord_ref, out_ref):
    values = emb_ref[...].astype(jnp.float32)
    scale = lax.rsqrt(jnp.sum(values * values, axis=1, keepdims=True) + 1e-06)
    out_ref[0:ROWS, :] = (values * scale).astype(jnp.bfloat16)
    rank = jnp.broadcast_to(ord_ref[...], (EXTRA, ROWS))
    label = jnp.broadcast_to(lab_ref[...], (EXTRA, ROWS))
    line = lax.broadcasted_iota(jnp.int32, (EXTRA, ROWS), 0)
    digits = jnp.where(
        line == 0,
        rank >> 12,
        jnp.where(line == 1, (rank >> 6) & 63, jnp.where(line == 2, rank & 63, label + 1)),
    )
    digits = jnp.where(line < 4, digits, 0).astype(jnp.float32)
    digits = jnp.concatenate([digits, jnp.zeros((EXTRA, D - ROWS), jnp.float32)], axis=1)
    out_ref[ROWS:PACK, :] = digits.astype(jnp.bfloat16)


def pack(embeddings, labels, order):
    return pl.pallas_call(
        pack_kernel,
        out_shape=jax.ShapeDtypeStruct((PACK, D), jnp.bfloat16),
        name="normalize_pack",
        cost_estimate=pl.CostEstimate(flops=4 * ROWS * D, bytes_accessed=4 * ROWS * D, transcendentals=ROWS),
    )(embeddings, labels.reshape(1, ROWS), order.reshape(1, ROWS))


def ranks(extra):
    return extra[0:1] * 4096.0 + extra[1:2] * 64.0 + extra[2:3]


def extra_of(ref):
    return ref[ROWS:PACK, 0:256].astype(jnp.float32)[:, :ROWS]


def half_kernel(place_ref, *refs):
    near = refs[:2 * NEAR]
    panel = refs[2 * NEAR:2 * NEAR + X]
    prior_ref, cols_ref, rows_ref, left, right, rank_col, row_best = refs[2 * NEAR + X:]
    for s in range(2 * NEAR):
        left[s * ROWS:(s + 1) * ROWS, :] = near[s][0:ROWS, :]
    for k in range(X):
        right[k * ROWS:(k + 1) * ROWS, :] = panel[k][0:ROWS, :]
    extras = [extra_of(ref) for ref in near]
    same = [extra[3:4] == extras[0][3:4] for extra in extras]
    near_rank = jnp.concatenate(
        [jnp.where(same[s], ranks(extras[s]), FAR) for s in range(2 * NEAR)], axis=1
    )
    rank_col[...] = jnp.transpose(jnp.broadcast_to(near_rank, (128, LEFT)), (1, 0))
    panel_rank = jnp.concatenate([ranks(extra_of(ref)) for ref in panel], axis=1)
    row_best[...] = jnp.full(row_best.shape, -1.0, jnp.float32)
    cols = []
    split = 2 * ROWS
    for t in range(X * ROWS // TILE):
        sims = lax.dot_general(
            left[...], right[t * TILE:(t + 1) * TILE, :], (((1,), (1,)), ((), ())),
            preferred_element_type=jnp.float32,
        )
        for h in range(TILE // 128):
            part = sims[:, h * 128:(h + 1) * 128]
            rank_row = panel_rank[:, t * TILE + h * 128:t * TILE + (h + 1) * 128]
            here = part[:split]
            best = jnp.max(jnp.where(rank_col[:split] < rank_row, here, -1.0), axis=0, keepdims=True)
            there = part[split:]
            earlier = rank_row < rank_col[split:]
            best = jnp.maximum(best, jnp.max(jnp.where(earlier, -1.0, there), axis=0, keepdims=True))
            row_best[...] = jnp.maximum(row_best[...], jnp.where(earlier, there, -1.0))
            cols.append(best)
    best = jnp.concatenate(cols, axis=1)
    for k in range(X):
        cols_ref[place_ref[k]] = best[:, k * ROWS:(k + 1) * ROWS]
    rows = jnp.max(jnp.transpose(row_best[...], (1, 0)), axis=0, keepdims=True)
    for s in range(2, 2 * NEAR):
        line = jnp.where(same[s], rows[:, (s - 2) * ROWS:(s - 1) * ROWS], -1.0)
        rows_ref[s - 2] = jnp.maximum(line, prior_ref[s - 2])


def half(place, near, panel, prior):
    inside = pl.BlockSpec(memory_space=pltpu.VMEM)
    return pl.pallas_call(
        half_kernel,
        out_shape=(
            jax.ShapeDtypeStruct((X, 1, ROWS), jnp.float32),
            jax.ShapeDtypeStruct((2 * (NEAR - 1), 1, ROWS), jnp.float32),
        ),
        in_specs=[pl.BlockSpec(memory_space=pltpu.SMEM)] + [inside] * (2 * NEAR + X + 1),
        out_specs=(inside, inside),
        scratch_shapes=[
            pltpu.VMEM((LEFT, D), jnp.bfloat16),
            pltpu.VMEM((X * ROWS, D), jnp.bfloat16),
            pltpu.VMEM((LEFT, 128), jnp.float32),
            pltpu.VMEM((LEFT - 2 * ROWS, 128), jnp.float32),
        ],
        compiler_params=pltpu.CompilerParams(vmem_limit_bytes=40 * 1024 * 1024),
        name="half_maxima",
        cost_estimate=pl.CostEstimate(
            flops=2 * LEFT * X * ROWS * D, bytes_accessed=2 * (2 * NEAR + X) * PACK * D, transcendentals=0
        ),
    )(place, *near, *panel, prior)


def shift(value, steps, count):
    pairs = [(i, i + steps) for i in range(count) if 0 <= i + steps < count]
    return lax.ppermute(value, "grp", pairs)


def swap(value, axis):
    return lax.ppermute(value, axis, [(0, 1), (1, 0)])


def spread(block, core):
    ahead = lax.ppermute(block, "x", [(i, (i + 1) % X) for i in range(X)])
    behind = lax.ppermute(block, "x", [(i, (i + X - 1) % X) for i in range(X)])
    pairs = [(2 * i, 2 * ((i + 1) % X)) for i in range(X)]
    pairs += [(2 * i + 1, 2 * ((i + X - 1) % X) + 1) for i in range(X)]
    across = lax.ppermute(jnp.where(core == 0, ahead, behind), ("x", "core"), pairs)
    return [block, ahead, behind, across]


def per_device(embeddings, labels, order):
    count = lax.axis_size("grp")
    grp, zh, x, core = (lax.axis_index(axis) for axis in ("grp", "zh", "x", "core"))
    block = pack(embeddings, labels, order)
    flipped = swap(block, "zh")
    near = [block] + [shift(block, steps, count) for steps in MOVES]
    panel = spread(block, core)
    other = spread(flipped, core)
    both = []
    for value in near:
        both += [value, swap(value, "core")]
    place = jnp.stack([x, (x + X - 1) % X, (x + 1) % X, (x + 2) % X]).astype(jnp.int32)
    prior = jnp.full((2 * (NEAR - 1), 1, ROWS), -1.0, jnp.float32)
    cols_own, prior = half(place, both, panel, prior)
    cols_other, rows = half(place, both, other, prior)
    cols = jnp.where(
        zh == 0,
        jnp.concatenate([cols_own, cols_other], axis=0),
        jnp.concatenate([cols_other, cols_own], axis=0),
    )
    best = jnp.max(lax.all_to_all(cols, ("zh", "x"), 0, 0, tiled=True), axis=0)
    mine = jnp.maximum(rows[0::2], swap(rows[1::2], "core"))
    for i, steps in enumerate(MOVES):
        back = shift(mine[i], -steps, count)
        source = grp + steps
        best = jnp.maximum(best, jnp.where((source >= 0) & (source < count), back, -1.0))
    return best.reshape(ROWS)


def solution(mesh):
    axes = ("grp", "zh", "x", "core")
    fine = Mesh(mesh.devices.reshape(mesh.shape["grp"], 2, X, 2), axes)
    return jax.shard_map(
        per_device,
        mesh=fine,
        in_specs=(P(axes, None), P(axes), P(axes)),
        out_specs=P(axes),
        check_vma=False,
    )
```

time: 129 us -> 119 us (0.922)
  the two profiles are of different devices: /device:TPU:186 before, /device:TPU:114 now
where the time goes in v2:
time: 119 us; the launch traced here: 118 us
  starting transfers between devices  78.8 us (66%)
  waiting for transfers between devices  23.6 us (20%)
  Pallas kernels  11 us (9%)
  other arithmetic  2.91 us (2%)
  local copies, waits for them, and re-layouts  1.78 us (1%)
    ppermute x6, starting transfers between devices, shift(): return lax.ppermute(value, 'grp', pairs)  34.4 us
    ppermute x6, starting transfers between devices, swap(): return lax.ppermute(value, axis, [(0, 1), (1, 0)])  20.6 us
    ppermute x6, waiting for transfers between devices, shift(): return lax.ppermute(value, 'grp', pairs)  10.8 us
    ppermute x6, waiting for transfers between devices, swap(): return lax.ppermute(value, axis, [(0, 1), (1, 0)])  10.8 us
    pallas_call x2, Pallas kernels, half(): pl.pallas_call(half_kernel, out_shape=(jax.ShapeDtypeStruct((X, 1, ROWS),...  9.05 us
    ppermute x2, starting transfers between devices, spread(): ahead = lax.ppermute(block, 'x', [(i, (i + 1) % X) for i in range(X)])  6.17 us
    ppermute x2, starting transfers between devices, spread(): lax.ppermute(jnp.where(core == 0, ahead, behind), ('x', 'core'), pairs)  6.16 us
    all_to_all x1, starting transfers between devices, per_device(): best = jnp.max(lax.all_to_all(cols, ('zh', 'x'), 0, 0, tiled=True), axis=0)  5.98 us
  transfers between devices with their start and end apart: 19, of which 4 were waited for; matrix products, arithmetic and copies ran while one was open for 2% of the time, Pallas kernels for 4%

profile of v2, /device:TPU:114, one launch (start us, length us, event | category | flops | bytes accessed | tf_op | source)
XLA Modules:
  0.0 118.4 jit_solution(14287883839417900953)
XLA Ops:
  0.0 1.9 %normalize_pack.1.refs_0_.refs_8_ = bf16[208,1024]{1,0:T(8,128)(2,1)} custom-call(bf16[192,1024]{1,0:T(8,128)(2,1)} %emb_ref.1, s32[1,192]{1,0:T(1,128)} %bitcast.15, s32[1,192]{1,0:T(1,128)} %bitcast.16), custom_call_target="tpu_custom_call" | custom-call | flops 786432 | bytes 786432 | tf_op jit(solution)/shard_map/normalize_pack/pallas_call | solution.py:38
  1.9 3.4 %collective-permute-start.7 = (bf16[208,1024]{1,0:T(8,128)(2,1)}, bf16[208,1024]{1,0:T(8,128)(2,1)S(1)}, u32[]{:S(2)}, u32[]{:S(2)}) collective-permute-start(bf16[208,1024]{1,0:T(8,128)(2,1)} %normalize_pack.1.refs_0_.refs_8_), channel_id=1, source_target_pairs={{0,2},{2,4},{4,6},{6,0},{1,3},{3,5},{5,7},{7,1},{8,10},{10,12},{12... | collective-permute-start | bytes 1277960 | tf_op jit(solution)/shard_map/ppermute | solution.py:130
  5.3 10.0 %collective-permute-start.10 = (bf16[208,1024]{1,0:T(8,128)(2,1)}, bf16[208,1024]{1,0:T(8,128)(2,1)S(1)}, u32[]{:S(2)}, u32[]{:S(2)}) collective-permute-start(bf16[208,1024]{1,0:T(8,128)(2,1)} %normalize_pack.1.refs_0_.refs_8_), channel_id=1, source_target_pairs={{0,8},{8,0},{1,9},{9,1},{2,10},{10,2},{3,11},{11,3},{4,12},{12,4},... | collective-permute-start | bytes 1277960 | tf_op jit(solution)/shard_map/ppermute | solution.py:126
  15.4 2.4 %collective-permute-start.8 = (bf16[208,1024]{1,0:T(8,128)(2,1)}, bf16[208,1024]{1,0:T(8,128)(2,1)S(1)}, u32[]{:S(2)}, u32[]{:S(2)}) collective-permute-start(bf16[208,1024]{1,0:T(8,128)(2,1)} %normalize_pack.1.refs_0_.refs_8_), channel_id=1, source_target_pairs={{0,6},{2,0},{4,2},{6,4},{1,7},{3,1},{5,3},{7,5},{8,14},{10,8},{12,... | collective-permute-start | bytes 1277960 | tf_op jit(solution)/shard_map/ppermute | solution.py:131
  17.8 3.9 %collective-permute-start.1 = (bf16[208,1024]{1,0:T(8,128)(2,1)}, bf16[208,1024]{1,0:T(8,128)(2,1)S(1)}, u32[]{:S(2)}, u32[]{:S(2)}) collective-permute-start(bf16[208,1024]{1,0:T(8,128)(2,1)} %normalize_pack.1.refs_0_.refs_8_), channel_id=1, source_target_pairs={{48,0},{64,16},{80,32},{96,48},{112,64},{128,80},{144,96},{160,112... | collective-permute-start | bytes 1277960 | tf_op jit(solution)/shard_map/ppermute | solution.py:122
  21.7 3.5 %collective-permute-start.3 = (bf16[208,1024]{1,0:T(8,128)(2,1)}, bf16[208,1024]{1,0:T(8,128)(2,1)S(1)}, u32[]{:S(2)}, u32[]{:S(2)}) collective-permute-start(bf16[208,1024]{1,0:T(8,128)(2,1)} %normalize_pack.1.refs_0_.refs_8_), channel_id=1, source_target_pairs={{0,16},{16,32},{32,48},{48,64},{64,80},{80,96},{96,112},{112,128},... | collective-permute-start | bytes 1277960 | tf_op jit(solution)/shard_map/ppermute | solution.py:122
  25.2 0.0 collective-permute-done.7.refs_9_
  25.2 4.8 %collective-permute-start.5 = (bf16[208,1024]{1,0:T(8,128)(2,1)}, bf16[208,1024]{1,0:T(8,128)(2,1)}, u32[]{:S(2)}, u32[]{:S(2)}) collective-permute-start(bf16[208,1024]{1,0:T(8,128)(2,1)} %normalize_pack.1.refs_0_.refs_8_), channel_id=1, source_target_pairs={{0,32},{16,48},{32,64},{48,80},{64,96},{80,112},{96,128},{112,144}... | collective-permute-start | bytes 1277960 | tf_op jit(solution)/shard_map/ppermute | solution.py:122
  30.1 10.7 %collective-permute-done.10.refs_8_ = bf16[208,1024]{1,0:T(8,128)(2,1)S(1)} collective-permute-done((bf16[208,1024]{1,0:T(8,128)(2,1)}, bf16[208,1024]{1,0:T(8,128)(2,1)S(1)}, u32[]{:S(2)}, u32[]{:S(2)}) %collective-permute-start.10) | collective-permute-done | bytes 426016 | tf_op jit(solution)/shard_map/ppermute | solution.py:126
  40.8 2.8 %collective-permute-start.11 = (bf16[208,1024]{1,0:T(8,128)(2,1)S(1)}, bf16[208,1024]{1,0:T(8,128)(2,1)S(1)}, u32[]{:S(2)}, u32[]{:S(2)}) collective-permute-start(bf16[208,1024]{1,0:T(8,128)(2,1)S(1)} %collective-permute-done.10.refs_8_), channel_id=1, source_target_pairs={{0,2},{2,4},{4,6},{6,0},{1,3},{3,5},{5,7},{7,1},{8,10},{10,12},{12... | collective-permute-start | bytes 1277960 | tf_op jit(solution)/shard_map/ppermute | solution.py:130
  43.6 0.0 collective-permute-done.8.refs_10_
  43.6 3.0 %collective-permute-start.12 = (bf16[208,1024]{1,0:T(8,128)(2,1)S(1)}, bf16[208,1024]{1,0:T(8,128)(2,1)S(1)}, u32[]{:S(2)}, u32[]{:S(2)}) collective-permute-start(bf16[208,1024]{1,0:T(8,128)(2,1)S(1)} %collective-permute-done.10.refs_8_), channel_id=1, source_target_pairs={{0,6},{2,0},{4,2},{6,4},{1,7},{3,1},{5,3},{7,5},{8,14},{10,8},{12,... | collective-permute-start | bytes 1277960 | tf_op jit(solution)/shard_map/ppermute | solution.py:131
  46.7 4.4 %collective-permute-done.1.refs_2_ = bf16[208,1024]{1,0:T(8,128)(2,1)S(1)} collective-permute-done((bf16[208,1024]{1,0:T(8,128)(2,1)}, bf16[208,1024]{1,0:T(8,128)(2,1)S(1)}, u32[]{:S(2)}, u32[]{:S(2)}) %collective-permute-start.1) | collective-permute-done | bytes 426016 | tf_op jit(solution)/shard_map/ppermute | solution.py:122
  51.0 1.9 %collective-permute-start = (bf16[208,1024]{1,0:T(8,128)(2,1)}, bf16[208,1024]{1,0:T(8,128)(2,1)S(1)}, u32[]{:S(2)}, u32[]{:S(2)}) collective-permute-start(bf16[208,1024]{1,0:T(8,128)(2,1)} %normalize_pack.1.refs_0_.refs_8_), channel_id=1, source_target_pairs={{0,1},{1,0},{2,3},{3,2},{4,5},{5,4},{6,7},{7,6},{8,9},{9,8},{10,11... | collective-permute-start | bytes 1277960 | tf_op jit(solution)/shard_map/ppermute | solution.py:126
  52.9 0.8 broadcast_select_fusion.1
  53.8 0.0 collective-permute-done.3.refs_4_
  53.8 3.5 %collective-permute-start.9 = (bf16[208,1024]{1,0:T(8,128)(2,1)}, bf16[208,1024]{1,0:T(8,128)(2,1)}, u32[]{:S(2)}, u32[]{:S(2)}) collective-permute-start(bf16[208,1024]{1,0:T(8,128)(2,1)} %broadcast_select_fusion.1), channel_id=1, source_target_pairs={{0,2},{2,4},{4,6},{6,0},{1,7},{3,1},{5,3},{7,5},{8,10},{10,12},{12... | collective-permute-start | bytes 1277960 | tf_op jit(solution)/shard_map/ppermute | solution.py:134
  57.3 0.0 collective-permute-done.5.refs_6_
  57.3 2.4 %collective-permute-start.2 = (bf16[208,1024]{1,0:T(8,128)(2,1)S(1)}, bf16[208,1024]{1,0:T(8,128)(2,1)}, u32[]{:S(2)}, u32[]{:S(2)}) collective-permute-start(bf16[208,1024]{1,0:T(8,128)(2,1)S(1)} %collective-permute-done.1.refs_2_), channel_id=1, source_target_pairs={{0,1},{1,0},{2,3},{3,2},{4,5},{5,4},{6,7},{7,6},{8,9},{9,8},{10,11... | collective-permute-start | bytes 1277960 | tf_op jit(solution)/shard_map/ppermute | solution.py:126
  59.7 0.0 collective-permute-done.11.refs_9_
  59.7 1.9 %collective-permute-start.4 = (bf16[208,1024]{1,0:T(8,128)(2,1)S(1)}, bf16[208,1024]{1,0:T(8,128)(2,1)}, u32[]{:S(2)}, u32[]{:S(2)}) collective-permute-start(bf16[208,1024]{1,0:T(8,128)(2,1)S(1)} %collective-permute-done.3.refs_4_), channel_id=1, source_target_pairs={{0,1},{1,0},{2,3},{3,2},{4,5},{5,4},{6,7},{7,6},{8,9},{9,8},{10,11... | collective-permute-start | bytes 1277960 | tf_op jit(solution)/shard_map/ppermute | solution.py:126
  61.7 0.0 collective-permute-done.12.refs_10_
  61.7 2.4 %collective-permute-start.6 = (bf16[208,1024]{1,0:T(8,128)(2,1)}, bf16[208,1024]{1,0:T(8,128)(2,1)}, u32[]{:S(2)}, u32[]{:S(2)}) collective-permute-start(bf16[208,1024]{1,0:T(8,128)(2,1)} %collective-permute-done.5.refs_6_), channel_id=1, source_target_pairs={{0,1},{1,0},{2,3},{3,2},{4,5},{5,4},{6,7},{7,6},{8,9},{9,8},{10,11... | collective-permute-start | bytes 1277960 | tf_op jit(solution)/shard_map/ppermute | solution.py:126
  64.1 0.8 broadcast_select_fusion
  64.9 0.0 collective-permute-done.refs_1_
  64.9 0.8 copy-done.1
  65.6 2.6 %collective-permute-start.13 = (bf16[208,1024]{1,0:T(8,128)(2,1)}, bf16[208,1024]{1,0:T(8,128)(2,1)}, u32[]{:S(2)}, u32[]{:S(2)}) collective-permute-start(bf16[208,1024]{1,0:T(8,128)(2,1)} %broadcast_select_fusion), channel_id=1, source_target_pairs={{0,2},{2,4},{4,6},{6,0},{1,7},{3,1},{5,3},{7,5},{8,10},{10,12},{12... | collective-permute-start | bytes 1277960 | tf_op jit(solution)/shard_map/ppermute | solution.py:134
  68.3 0.1 pad_add_fusion.place_ref
  68.4 0.0 collective-permute-done.9.refs_11_
  68.4 0.0 collective-permute-done.2.refs_3_
  68.4 0.0 collective-permute-done.4.refs_5_
  68.4 0.0 collective-permute-done.6.refs_7_
  68.4 1.0 copy-done.2
  69.4 4.5 %half_maxima.2 = (f32[4,1,192]{2,1,0:T(1,128)S(1)}, f32[6,1,192]{2,1,0:T(1,128)S(1)}) custom-call(s32[4]{0:T(128)S(1)} %pad_add_fusion.place_ref, bf16[208,1024]{1,0:T(8,128)(2,1)S(1)} %copy-done, bf16[208,1024]{1,0:T(8,128)(2,1)S(1)} %copy-done.2, bf16[208,1024]{1,0:T(8,128)(2,1)S(1)} %collective-permute-done.1.refs_2_, ...), custom_call_target="tpu_custom_call" | custom-call | flops 2415919104 | bytes 5111808 | tf_op jit(solution)/shard_map/half_maxima/pallas_call | solution.py:98
  74.0 2.0 %collective-permute-done.13.refs_11_ = bf16[208,1024]{1,0:T(8,128)(2,1)} collective-permute-done((bf16[208,1024]{1,0:T(8,128)(2,1)}, bf16[208,1024]{1,0:T(8,128)(2,1)}, u32[]{:S(2)}, u32[]{:S(2)}) %collective-permute-start.13) | collective-permute-done | bytes 426016 | tf_op jit(solution)/shard_map/ppermute | solution.py:134
  76.0 4.5 %half_maxima.3 = (f32[4,1,192]{2,1,0:T(1,128)S(1)}, f32[6,1,192]{2,1,0:T(1,128)S(1)}) custom-call(s32[4]{0:T(128)S(1)} %pad_add_fusion.place_ref, bf16[208,1024]{1,0:T(8,128)(2,1)S(1)} %copy-done, bf16[208,1024]{1,0:T(8,128)(2,1)S(1)} %copy-done.2, bf16[208,1024]{1,0:T(8,128)(2,1)S(1)} %collective-permute-done.1.refs_2_, ...), custom_call_target="tpu_custom_call" | custom-call | flops 2415919104 | bytes 5111808 | tf_op jit(solution)/shard_map/half_maxima/pallas_call | solution.py:98
  80.5 1.9 %collective-permute-start.14 = (f32[3,1,192]{2,1,0:T(1,128)S(1)}, f32[3,1,192]{2,1,0:T(1,128)S(1)}, u32[]{:S(2)}, u32[]{:S(2)}) collective-permute-start(f32[3,1,192]{2,1,0:T(1,128)S(1)} %slice.16), channel_id=1, source_target_pairs={{0,1},{1,0},{2,3},{3,2},{4,5},{5,4},{6,7},{7,6},{8,9},{9,8},{10,11... | collective-permute-start | bytes 6920 | tf_op jit(solution)/shard_map/ppermute | solution.py:126
  82.4 0.6 broadcast_select_fusion.2
  83.0 6.0 %all-to-all-start = ((f32[8,1,192]{2,1,0:T(1,128)}), f32[8,1,192]{2,1,0:T(1,128)S(1)}, u32[]{:S(2)}, u32[]{:S(2)}) async-start(f32[8,1,192]{2,1,0:T(1,128)} %broadcast_select_fusion.2), calls=%async_computation | async-start | bytes 16384 | tf_op jit(solution)/shard_map/all_to_all | solution.py:158
  89.0 0.0 collective-permute-done.14
  89.0 8.0 %collective-permute-start.15 = (f32[1,192]{1,0:T(1,128)S(1)}, f32[1,192]{1,0:T(1,128)S(1)}, u32[]{:S(2)}, u32[]{:S(2)}) collective-permute-start(f32[1,192]{1,0:T(1,128)S(1)} %get-tuple-element.15), channel_id=1, source_target_pairs={{0,48},{16,64},{32,80},{48,96},{64,112},{80,128},{96,144},{112,160... | collective-permute-start | bytes 2312 | tf_op jit(solution)/shard_map/ppermute | solution.py:122
  97.1 12.3 %collective-permute-start.16 = (f32[1,192]{1,0:T(1,128)S(1)}, f32[1,192]{1,0:T(1,128)S(1)}, u32[]{:S(2)}, u32[]{:S(2)}) collective-permute-start(f32[1,192]{1,0:T(1,128)S(1)} %get-tuple-element.14), channel_id=1, source_target_pairs={{16,0},{32,16},{48,32},{64,48},{80,64},{96,80},{112,96},{128,112},... | collective-permute-start | bytes 2312 | tf_op jit(solution)/shard_map/ppermute | solution.py:122
  109.3 1.9 %collective-permute-start.17 = (f32[1,192]{1,0:T(1,128)S(1)}, f32[1,192]{1,0:T(1,128)S(1)}, u32[]{:S(2)}, u32[]{:S(2)}) collective-permute-start(f32[1,192]{1,0:T(1,128)S(1)} %get-tuple-element.13), channel_id=1, source_target_pairs={{32,0},{48,16},{64,32},{80,48},{96,64},{112,80},{128,96},{144,112}... | collective-permute-start | bytes 2312 | tf_op jit(solution)/shard_map/ppermute | solution.py:122
  111.3 0.0 all-to-all-done
  111.3 0.0 collective-permute-done.15
  111.3 0.0 collective-permute-done.16
  111.4 6.5 %collective-permute-done.17 = f32[1,192]{1,0:T(1,128)S(1)} collective-permute-done((f32[1,192]{1,0:T(1,128)S(1)}, f32[1,192]{1,0:T(1,128)S(1)}, u32[]{:S(2)}, u32[]{:S(2)}) %collective-permute-start.17) | collective-permute-done | bytes 800 | tf_op jit(solution)/shard_map/ppermute | solution.py:122
  117.8 0.6 fusion.2
  (9 shorter events, 0.1 us)
Async XLA Ops:
  1.9 23.3 %collective-permute-start.7 = (bf16[208,1024]{1,0:T(8,128)(2,1)}, bf16[208,1024]{1,0:T(8,128)(2,1)S(1)}, u32[]{:S(2)}, u32[]{:S(2)}) collective-permute-start(bf16[208,1024]{1,0:T(8,128)(2,1)} %normalize_pack.1.refs_0_.refs_8_), channel_id=1, source_target_pairs={{0,2},{2,4},{4,6},{6,0},{1,3},{3,5},{5,7},{7,1},{8,10},{10,12},{12... | collective-permute-start | bytes 1277960 | tf_op jit(solution)/shard_map/ppermute | solution.py:130
  5.3 35.5 %collective-permute-start.10 = (bf16[208,1024]{1,0:T(8,128)(2,1)}, bf16[208,1024]{1,0:T(8,128)(2,1)S(1)}, u32[]{:S(2)}, u32[]{:S(2)}) collective-permute-start(bf16[208,1024]{1,0:T(8,128)(2,1)} %normalize_pack.1.refs_0_.refs_8_), channel_id=1, source_target_pairs={{0,8},{8,0},{1,9},{9,1},{2,10},{10,2},{3,11},{11,3},{4,12},{12,4},... | collective-permute-start | bytes 1277960 | tf_op jit(solution)/shard_map/ppermute | solution.py:126
  15.4 28.2 %collective-permute-start.8 = (bf16[208,1024]{1,0:T(8,128)(2,1)}, bf16[208,1024]{1,0:T(8,128)(2,1)S(1)}, u32[]{:S(2)}, u32[]{:S(2)}) collective-permute-start(bf16[208,1024]{1,0:T(8,128)(2,1)} %normalize_pack.1.refs_0_.refs_8_), channel_id=1, source_target_pairs={{0,6},{2,0},{4,2},{6,4},{1,7},{3,1},{5,3},{7,5},{8,14},{10,8},{12,... | collective-permute-start | bytes 1277960 | tf_op jit(solution)/shard_map/ppermute | solution.py:131
  17.8 33.2 %collective-permute-start.1 = (bf16[208,1024]{1,0:T(8,128)(2,1)}, bf16[208,1024]{1,0:T(8,128)(2,1)S(1)}, u32[]{:S(2)}, u32[]{:S(2)}) collective-permute-start(bf16[208,1024]{1,0:T(8,128)(2,1)} %normalize_pack.1.refs_0_.refs_8_), channel_id=1, source_target_pairs={{48,0},{64,16},{80,32},{96,48},{112,64},{128,80},{144,96},{160,112... | collective-permute-start | bytes 1277960 | tf_op jit(solution)/shard_map/ppermute | solution.py:122
  21.7 32.0 %collective-permute-start.3 = (bf16[208,1024]{1,0:T(8,128)(2,1)}, bf16[208,1024]{1,0:T(8,128)(2,1)S(1)}, u32[]{:S(2)}, u32[]{:S(2)}) collective-permute-start(bf16[208,1024]{1,0:T(8,128)(2,1)} %normalize_pack.1.refs_0_.refs_8_), channel_id=1, source_target_pairs={{0,16},{16,32},{32,48},{48,64},{64,80},{80,96},{96,112},{112,128},... | collective-permute-start | bytes 1277960 | tf_op jit(solution)/shard_map/ppermute | solution.py:122
  25.2 32.0 %collective-permute-start.5 = (bf16[208,1024]{1,0:T(8,128)(2,1)}, bf16[208,1024]{1,0:T(8,128)(2,1)}, u32[]{:S(2)}, u32[]{:S(2)}) collective-permute-start(bf16[208,1024]{1,0:T(8,128)(2,1)} %normalize_pack.1.refs_0_.refs_8_), channel_id=1, source_target_pairs={{0,32},{16,48},{32,64},{48,80},{64,96},{80,112},{96,128},{112,144}... | collective-permute-start | bytes 1277960 | tf_op jit(solution)/shard_map/ppermute | solution.py:122
  40.8 18.9 %collective-permute-start.11 = (bf16[208,1024]{1,0:T(8,128)(2,1)S(1)}, bf16[208,1024]{1,0:T(8,128)(2,1)S(1)}, u32[]{:S(2)}, u32[]{:S(2)}) collective-permute-start(bf16[208,1024]{1,0:T(8,128)(2,1)S(1)} %collective-permute-done.10.refs_8_), channel_id=1, source_target_pairs={{0,2},{2,4},{4,6},{6,0},{1,3},{3,5},{5,7},{7,1},{8,10},{10,12},{12... | collective-permute-start | bytes 1277960 | tf_op jit(solution)/shard_map/ppermute | solution.py:130
  43.6 18.0 %collective-permute-start.12 = (bf16[208,1024]{1,0:T(8,128)(2,1)S(1)}, bf16[208,1024]{1,0:T(8,128)(2,1)S(1)}, u32[]{:S(2)}, u32[]{:S(2)}) collective-permute-start(bf16[208,1024]{1,0:T(8,128)(2,1)S(1)} %collective-permute-done.10.refs_8_), channel_id=1, source_target_pairs={{0,6},{2,0},{4,2},{6,4},{1,7},{3,1},{5,3},{7,5},{8,14},{10,8},{12,... | collective-permute-start | bytes 1277960 | tf_op jit(solution)/shard_map/ppermute | solution.py:131
  51.0 13.8 %collective-permute-start = (bf16[208,1024]{1,0:T(8,128)(2,1)}, bf16[208,1024]{1,0:T(8,128)(2,1)S(1)}, u32[]{:S(2)}, u32[]{:S(2)}) collective-permute-start(bf16[208,1024]{1,0:T(8,128)(2,1)} %normalize_pack.1.refs_0_.refs_8_), channel_id=1, source_target_pairs={{0,1},{1,0},{2,3},{3,2},{4,5},{5,4},{6,7},{7,6},{8,9},{9,8},{10,11... | collective-permute-start | bytes 1277960 | tf_op jit(solution)/shard_map/ppermute | solution.py:126
  53.8 14.7 %copy-start = (bf16[208,1024]{1,0:T(8,128)(2,1)S(1)}, bf16[208,1024]{1,0:T(8,128)(2,1)}, u32[]{:S(2)}) copy-start(bf16[208,1024]{1,0:T(8,128)(2,1)} %normalize_pack.1.refs_0_.refs_8_) | copy-start | bytes 1277956
  53.8 14.6 %collective-permute-start.9 = (bf16[208,1024]{1,0:T(8,128)(2,1)}, bf16[208,1024]{1,0:T(8,128)(2,1)}, u32[]{:S(2)}, u32[]{:S(2)}) collective-permute-start(bf16[208,1024]{1,0:T(8,128)(2,1)} %broadcast_select_fusion.1), channel_id=1, source_target_pairs={{0,2},{2,4},{4,6},{6,0},{1,7},{3,1},{5,3},{7,5},{8,10},{10,12},{12... | collective-permute-start | bytes 1277960 | tf_op jit(solution)/shard_map/ppermute | solution.py:134
  57.3 11.1 %collective-permute-start.2 = (bf16[208,1024]{1,0:T(8,128)(2,1)S(1)}, bf16[208,1024]{1,0:T(8,128)(2,1)}, u32[]{:S(2)}, u32[]{:S(2)}) collective-permute-start(bf16[208,1024]{1,0:T(8,128)(2,1)S(1)} %collective-permute-done.1.refs_2_), channel_id=1, source_target_pairs={{0,1},{1,0},{2,3},{3,2},{4,5},{5,4},{6,7},{7,6},{8,9},{9,8},{10,11... | collective-permute-start | bytes 1277960 | tf_op jit(solution)/shard_map/ppermute | solution.py:126
  59.7 8.7 %collective-permute-start.4 = (bf16[208,1024]{1,0:T(8,128)(2,1)S(1)}, bf16[208,1024]{1,0:T(8,128)(2,1)}, u32[]{:S(2)}, u32[]{:S(2)}) collective-permute-start(bf16[208,1024]{1,0:T(8,128)(2,1)S(1)} %collective-permute-done.3.refs_4_), channel_id=1, source_target_pairs={{0,1},{1,0},{2,3},{3,2},{4,5},{5,4},{6,7},{7,6},{8,9},{9,8},{10,11... | collective-permute-start | bytes 1277960 | tf_op jit(solution)/shard_map/ppermute | solution.py:126
  61.7 6.7 %collective-permute-start.6 = (bf16[208,1024]{1,0:T(8,128)(2,1)}, bf16[208,1024]{1,0:T(8,128)(2,1)}, u32[]{:S(2)}, u32[]{:S(2)}) collective-permute-start(bf16[208,1024]{1,0:T(8,128)(2,1)} %collective-permute-done.5.refs_6_), channel_id=1, source_target_pairs={{0,1},{1,0},{2,3},{3,2},{4,5},{5,4},{6,7},{7,6},{8,9},{9,8},{10,11... | collective-permute-start | bytes 1277960 | tf_op jit(solution)/shard_map/ppermute | solution.py:126
  64.9 0.8 copy-start.1
  65.6 10.3 %collective-permute-start.13 = (bf16[208,1024]{1,0:T(8,128)(2,1)}, bf16[208,1024]{1,0:T(8,128)(2,1)}, u32[]{:S(2)}, u32[]{:S(2)}) collective-permute-start(bf16[208,1024]{1,0:T(8,128)(2,1)} %broadcast_select_fusion), channel_id=1, source_target_pairs={{0,2},{2,4},{4,6},{6,0},{1,7},{3,1},{5,3},{7,5},{8,10},{10,12},{12... | collective-permute-start | bytes 1277960 | tf_op jit(solution)/shard_map/ppermute | solution.py:134
  68.4 1.0 copy-start.2
  80.5 8.5 %collective-permute-start.14 = (f32[3,1,192]{2,1,0:T(1,128)S(1)}, f32[3,1,192]{2,1,0:T(1,128)S(1)}, u32[]{:S(2)}, u32[]{:S(2)}) collective-permute-start(f32[3,1,192]{2,1,0:T(1,128)S(1)} %slice.16), channel_id=1, source_target_pairs={{0,1},{1,0},{2,3},{3,2},{4,5},{5,4},{6,7},{7,6},{8,9},{9,8},{10,11... | collective-permute-start | bytes 6920 | tf_op jit(solution)/shard_map/ppermute | solution.py:126
  83.0 28.3 %all-to-all-start = ((f32[8,1,192]{2,1,0:T(1,128)}), f32[8,1,192]{2,1,0:T(1,128)S(1)}, u32[]{:S(2)}, u32[]{:S(2)}) async-start(f32[8,1,192]{2,1,0:T(1,128)} %broadcast_select_fusion.2), calls=%async_computation | async-start | bytes 16384 | tf_op jit(solution)/shard_map/all_to_all | solution.py:158
  89.0 22.3 %collective-permute-start.15 = (f32[1,192]{1,0:T(1,128)S(1)}, f32[1,192]{1,0:T(1,128)S(1)}, u32[]{:S(2)}, u32[]{:S(2)}) collective-permute-start(f32[1,192]{1,0:T(1,128)S(1)} %get-tuple-element.15), channel_id=1, source_target_pairs={{0,48},{16,64},{32,80},{48,96},{64,112},{80,128},{96,144},{112,160... | collective-permute-start | bytes 2312 | tf_op jit(solution)/shard_map/ppermute | solution.py:122
  97.1 14.3 %collective-permute-start.16 = (f32[1,192]{1,0:T(1,128)S(1)}, f32[1,192]{1,0:T(1,128)S(1)}, u32[]{:S(2)}, u32[]{:S(2)}) collective-permute-start(f32[1,192]{1,0:T(1,128)S(1)} %get-tuple-element.14), channel_id=1, source_target_pairs={{16,0},{32,16},{48,32},{64,48},{80,64},{96,80},{112,96},{128,112},... | collective-permute-start | bytes 2312 | tf_op jit(solution)/shard_map/ppermute | solution.py:122
  109.3 8.5 %collective-permute-start.17 = (f32[1,192]{1,0:T(1,128)S(1)}, f32[1,192]{1,0:T(1,128)S(1)}, u32[]{:S(2)}, u32[]{:S(2)}) collective-permute-start(f32[1,192]{1,0:T(1,128)S(1)} %get-tuple-element.13), channel_id=1, source_target_pairs={{32,0},{48,16},{64,32},{80,48},{96,64},{112,80},{128,96},{144,112}... | collective-permute-start | bytes 2312 | tf_op jit(solution)/shard_map/ppermute | solution.py:122

commit v3 on v2

--- a/solution.py
+++ b/solution.py
@@ -51,10 +51,24 @@
     return ref[ROWS:PACK, 0:256].astype(jnp.float32)[:, :ROWS]
 
 
-def half_kernel(place_ref, *refs):
+def repeat_kernel(block_ref, out_ref):
+    for k in range(X):
+        out_ref[k] = block_ref[...]
+
+
+def repeat(block):
+    return pl.pallas_call(
+        repeat_kernel,
+        out_shape=jax.ShapeDtypeStruct((X, PACK, D), jnp.bfloat16),
+        name="repeat",
+        cost_estimate=pl.CostEstimate(flops=0, bytes_accessed=2 * (X + 1) * PACK * D, transcendentals=0),
+    )(block)
+
+
+def half_kernel(*refs):
     near = refs[:2 * NEAR]
-    panel = refs[2 * NEAR:2 * NEAR + X]
-    prior_ref, cols_ref, rows_ref, left, right, rank_col, row_best = refs[2 * NEAR + X:]
+    panel_ref, prior_ref, cols_ref, rows_ref, left, right, rank_col, row_best = refs[2 * NEAR:]
+    panel = [panel_ref.at[k] for k in range(X)]
     for s in range(2 * NEAR):
         left[s * ROWS:(s + 1) * ROWS, :] = near[s][0:ROWS, :]
     for k in range(X):
@@ -86,14 +100,14 @@
             cols.append(best)
     best = jnp.concatenate(cols, axis=1)
     for k in range(X):
-        cols_ref[place_ref[k]] = best[:, k * ROWS:(k + 1) * ROWS]
+        cols_ref[k] = best[:, k * ROWS:(k + 1) * ROWS]
     rows = jnp.max(jnp.transpose(row_best[...], (1, 0)), axis=0, keepdims=True)
     for s in range(2, 2 * NEAR):
         line = jnp.where(same[s], rows[:, (s - 2) * ROWS:(s - 1) * ROWS], -1.0)
         rows_ref[s - 2] = jnp.maximum(line, prior_ref[s - 2])
 
 
-def half(place, near, panel, prior):
+def half(near, panel, prior):
     inside = pl.BlockSpec(memory_space=pltpu.VMEM)
     return pl.pallas_call(
         half_kernel,
@@ -101,7 +115,7 @@
             jax.ShapeDtypeStruct((X, 1, ROWS), jnp.float32),
             jax.ShapeDtypeStruct((2 * (NEAR - 1), 1, ROWS), jnp.float32),
         ),
-        in_specs=[pl.BlockSpec(memory_space=pltpu.SMEM)] + [inside] * (2 * NEAR + X + 1),
+        in_specs=[inside] * (2 * NEAR + 2),
         out_specs=(inside, inside),
         scratch_shapes=[
             pltpu.VMEM((LEFT, D), jnp.bfloat16),
@@ -114,7 +128,7 @@
         cost_estimate=pl.CostEstimate(
             flops=2 * LEFT * X * ROWS * D, bytes_accessed=2 * (2 * NEAR + X) * PACK * D, transcendentals=0
         ),
-    )(place, *near, *panel, prior)
+    )(*near, panel, prior)
 
 
 def shift(value, steps, count):
@@ -126,30 +140,24 @@
     return lax.ppermute(value, axis, [(0, 1), (1, 0)])
 
 
-def spread(block, core):
-    ahead = lax.ppermute(block, "x", [(i, (i + 1) % X) for i in range(X)])
-    behind = lax.ppermute(block, "x", [(i, (i + X - 1) % X) for i in range(X)])
-    pairs = [(2 * i, 2 * ((i + 1) % X)) for i in range(X)]
-    pairs += [(2 * i + 1, 2 * ((i + X - 1) % X) + 1) for i in range(X)]
-    across = lax.ppermute(jnp.where(core == 0, ahead, behind), ("x", "core"), pairs)
-    return [block, ahead, behind, across]
+def spread(block):
+    return lax.all_to_all(repeat(block), "x", 0, 0, tiled=True)
 
 
 def per_device(embeddings, labels, order):
     count = lax.axis_size("grp")
-    grp, zh, x, core = (lax.axis_index(axis) for axis in ("grp", "zh", "x", "core"))
+    grp, zh = lax.axis_index("grp"), lax.axis_index("zh")
     block = pack(embeddings, labels, order)
     flipped = swap(block, "zh")
     near = [block] + [shift(block, steps, count) for steps in MOVES]
-    panel = spread(block, core)
-    other = spread(flipped, core)
+    panel = spread(block)
+    other = spread(flipped)
     both = []
     for value in near:
         both += [value, swap(value, "core")]
-    place = jnp.stack([x, (x + X - 1) % X, (x + 1) % X, (x + 2) % X]).astype(jnp.int32)
     prior = jnp.full((2 * (NEAR - 1), 1, ROWS), -1.0, jnp.float32)
-    cols_own, prior = half(place, both, panel, prior)
-    cols_other, rows = half(place, both, other, prior)
+    cols_own, prior = half(both, panel, prior)
+    cols_other, rows = half(both, other, prior)
     cols = jnp.where(
         zh == 0,
         jnp.concatenate([cols_own, cols_other], axis=0),

time: 119 us -> 129 us (1.084)
  the two profiles are of different devices: /device:TPU:114 before, /device:TPU:194 now
where the time goes in v3:
time: 129 us; the launch traced here: 128 us
  starting transfers between devices  66.7 us (52%)
  waiting for transfers between devices  43.6 us (34%)
  Pallas kernels  16 us (12%)
    ppermute x6, starting transfers between devices, shift(): return lax.ppermute(value, 'grp', pairs)  28.8 us
    ppermute x6, waiting for transfers between devices, shift(): return lax.ppermute(value, 'grp', pairs)  28.4 us
    ppermute x6, starting transfers between devices, swap(): return lax.ppermute(value, axis, [(0, 1), (1, 0)])  18.4 us
    ppermute x6, waiting for transfers between devices, swap(): return lax.ppermute(value, axis, [(0, 1), (1, 0)])  15.2 us
    all_to_all x2, starting transfers between devices, spread(): return lax.all_to_all(repeat(block), 'x', 0, 0, tiled=True)  9.75 us
    all_to_all x1, starting transfers between devices, per_device(): best = jnp.max(lax.all_to_all(cols, ('zh', 'x'), 0, 0, tiled=True), axis=0)  9.72 us
    pallas_call x2, Pallas kernels, half(): pl.pallas_call(half_kernel, out_shape=(jax.ShapeDtypeStruct((X, 1, ROWS),...  9.39 us
    pallas_call x2, Pallas kernels, repeat(): pl.pallas_call(repeat_kernel, out_shape=jax.ShapeDtypeStruct((X, PACK, D)...  4.63 us
  transfers between devices with their start and end apart: 15, of which 5 were waited for; matrix products, arithmetic and copies ran while one was open for 1% of the time, Pallas kernels for 5%

profile of v3, /device:TPU:194, one launch (start us, length us, event | category | flops | bytes accessed | tf_op | source)
XLA Modules:
  0.0 128.4 jit_solution(9805668152850190875)
XLA Ops:
  0.0 1.9 %normalize_pack.1.block_ref.refs_0_ = bf16[208,1024]{1,0:T(8,128)(2,1)} custom-call(bf16[192,1024]{1,0:T(8,128)(2,1)} %emb_ref.1, s32[1,192]{1,0:T(1,128)} %bitcast.11, s32[1,192]{1,0:T(1,128)} %bitcast.12), custom_call_target="tpu_custom_call" | custom-call | flops 786432 | bytes 786432 | tf_op jit(solution)/shard_map/normalize_pack/pallas_call | solution.py:38
  1.9 2.3 %repeat.2 = bf16[4,208,1024]{2,1,0:T(8,128)(2,1)} custom-call(bf16[208,1024]{1,0:T(8,128)(2,1)} %normalize_pack.1.block_ref.refs_0_), custom_call_target="tpu_custom_call" | custom-call | bytes 2129920 | tf_op jit(solution)/shard_map/repeat/pallas_call | solution.py:60
  4.2 0.0 copy-start
  4.2 5.0 %all-to-all-start = ((bf16[4,208,1024]{2,1,0:T(8,128)(2,1)}), bf16[4,208,1024]{2,1,0:T(8,128)(2,1)S(1)}, u32[]{:S(2)}, u32[]{:S(2)}) async-start(bf16[4,208,1024]{2,1,0:T(8,128)(2,1)} %repeat.2), calls=%async_computation | async-start | bytes 3407872 | tf_op jit(solution)/shard_map/all_to_all | solution.py:144
  9.2 0.0 copy-done
  9.2 8.2 %collective-permute-start.7 = (bf16[208,1024]{1,0:T(8,128)(2,1)S(1)}, bf16[208,1024]{1,0:T(8,128)(2,1)S(1)}, u32[]{:S(2)}, u32[]{:S(2)}) collective-permute-start(bf16[208,1024]{1,0:T(8,128)(2,1)S(1)} %copy-done), channel_id=1, source_target_pairs={{0,8},{8,0},{1,9},{9,1},{2,10},{10,2},{3,11},{11,3},{4,12},{12,4},... | collective-permute-start | bytes 1277960 | tf_op jit(solution)/shard_map/ppermute | solution.py:140
  17.4 13.4 %collective-permute-done.7.block_ref = bf16[208,1024]{1,0:T(8,128)(2,1)S(1)} collective-permute-done((bf16[208,1024]{1,0:T(8,128)(2,1)S(1)}, bf16[208,1024]{1,0:T(8,128)(2,1)S(1)}, u32[]{:S(2)}, u32[]{:S(2)}) %collective-permute-start.7) | collective-permute-done | bytes 426016 | tf_op jit(solution)/shard_map/ppermute | solution.py:140
  30.8 0.0 copy-start.1
  30.8 0.8 copy-done.1
  31.6 2.3 %repeat.3 = bf16[4,208,1024]{2,1,0:T(8,128)(2,1)} custom-call(bf16[208,1024]{1,0:T(8,128)(2,1)} %copy-done.1), custom_call_target="tpu_custom_call" | custom-call | bytes 2129920 | tf_op jit(solution)/shard_map/repeat/pallas_call | solution.py:60
  33.9 0.0 all-to-all-done.refs_8_
  33.9 4.8 %all-to-all-start.1 = ((bf16[4,208,1024]{2,1,0:T(8,128)(2,1)}), bf16[4,208,1024]{2,1,0:T(8,128)(2,1)}, u32[]{:S(2)}, u32[]{:S(2)}) async-start(bf16[4,208,1024]{2,1,0:T(8,128)(2,1)} %repeat.3), calls=%async_computation.1 | async-start | bytes 3407872 | tf_op jit(solution)/shard_map/all_to_all | solution.py:144
  38.7 12.0 %collective-permute-start.1 = (bf16[208,1024]{1,0:T(8,128)(2,1)S(1)}, bf16[208,1024]{1,0:T(8,128)(2,1)S(1)}, u32[]{:S(2)}, u32[]{:S(2)}) collective-permute-start(bf16[208,1024]{1,0:T(8,128)(2,1)S(1)} %copy-done), channel_id=1, source_target_pairs={{48,0},{64,16},{80,32},{96,48},{112,64},{128,80},{144,96},{160,112... | collective-permute-start | bytes 1277960 | tf_op jit(solution)/shard_map/ppermute | solution.py:136
  50.7 2.6 %collective-permute-start.3 = (bf16[208,1024]{1,0:T(8,128)(2,1)S(1)}, bf16[208,1024]{1,0:T(8,128)(2,1)S(1)}, u32[]{:S(2)}, u32[]{:S(2)}) collective-permute-start(bf16[208,1024]{1,0:T(8,128)(2,1)S(1)} %copy-done), channel_id=1, source_target_pairs={{0,16},{16,32},{32,48},{48,64},{64,80},{80,96},{96,112},{112,128},... | collective-permute-start | bytes 1277960 | tf_op jit(solution)/shard_map/ppermute | solution.py:136
  53.3 2.0 %collective-permute-start.5 = (bf16[208,1024]{1,0:T(8,128)(2,1)S(1)}, bf16[208,1024]{1,0:T(8,128)(2,1)S(1)}, u32[]{:S(2)}, u32[]{:S(2)}) collective-permute-start(bf16[208,1024]{1,0:T(8,128)(2,1)S(1)} %copy-done), channel_id=1, source_target_pairs={{0,32},{16,48},{32,64},{48,80},{64,96},{80,112},{96,128},{112,144}... | collective-permute-start | bytes 1277960 | tf_op jit(solution)/shard_map/ppermute | solution.py:136
  55.3 1.9 %collective-permute-start = (bf16[208,1024]{1,0:T(8,128)(2,1)S(1)}, bf16[208,1024]{1,0:T(8,128)(2,1)}, u32[]{:S(2)}, u32[]{:S(2)}) collective-permute-start(bf16[208,1024]{1,0:T(8,128)(2,1)S(1)} %copy-done), channel_id=1, source_target_pairs={{0,1},{1,0},{2,3},{3,2},{4,5},{5,4},{6,7},{7,6},{8,9},{9,8},{10,11... | collective-permute-start | bytes 1277960 | tf_op jit(solution)/shard_map/ppermute | solution.py:140
  57.3 20.4 %collective-permute-done.1.refs_2_ = bf16[208,1024]{1,0:T(8,128)(2,1)S(1)} collective-permute-done((bf16[208,1024]{1,0:T(8,128)(2,1)S(1)}, bf16[208,1024]{1,0:T(8,128)(2,1)S(1)}, u32[]{:S(2)}, u32[]{:S(2)}) %collective-permute-start.1) | collective-permute-done | bytes 426016 | tf_op jit(solution)/shard_map/ppermute | solution.py:136
  77.7 1.9 %collective-permute-start.2 = (bf16[208,1024]{1,0:T(8,128)(2,1)S(1)}, bf16[208,1024]{1,0:T(8,128)(2,1)}, u32[]{:S(2)}, u32[]{:S(2)}) collective-permute-start(bf16[208,1024]{1,0:T(8,128)(2,1)S(1)} %collective-permute-done.1.refs_2_), channel_id=1, source_target_pairs={{0,1},{1,0},{2,3},{3,2},{4,5},{5,4},{6,7},{7,6},{8,9},{9,8},{10,11... | collective-permute-start | bytes 1277960 | tf_op jit(solution)/shard_map/ppermute | solution.py:140
  79.6 0.0 collective-permute-done.3.refs_4_
  79.6 2.4 %collective-permute-start.4 = (bf16[208,1024]{1,0:T(8,128)(2,1)S(1)}, bf16[208,1024]{1,0:T(8,128)(2,1)}, u32[]{:S(2)}, u32[]{:S(2)}) collective-permute-start(bf16[208,1024]{1,0:T(8,128)(2,1)S(1)} %collective-permute-done.3.refs_4_), channel_id=1, source_target_pairs={{0,1},{1,0},{2,3},{3,2},{4,5},{5,4},{6,7},{7,6},{8,9},{9,8},{10,11... | collective-permute-start | bytes 1277960 | tf_op jit(solution)/shard_map/ppermute | solution.py:140
  82.0 0.6 collective-permute-done.5.refs_6_
  82.6 1.9 %collective-permute-start.6 = (bf16[208,1024]{1,0:T(8,128)(2,1)S(1)}, bf16[208,1024]{1,0:T(8,128)(2,1)}, u32[]{:S(2)}, u32[]{:S(2)}) collective-permute-start(bf16[208,1024]{1,0:T(8,128)(2,1)S(1)} %collective-permute-done.5.refs_6_), channel_id=1, source_target_pairs={{0,1},{1,0},{2,3},{3,2},{4,5},{5,4},{6,7},{7,6},{8,9},{9,8},{10,11... | collective-permute-start | bytes 1277960 | tf_op jit(solution)/shard_map/ppermute | solution.py:140
  84.5 0.0 collective-permute-done.refs_1_
  84.5 0.0 collective-permute-done.2.refs_3_
  84.6 0.0 collective-permute-done.4.refs_5_
  84.6 1.8 %collective-permute-done.6.refs_7_ = bf16[208,1024]{1,0:T(8,128)(2,1)} collective-permute-done((bf16[208,1024]{1,0:T(8,128)(2,1)S(1)}, bf16[208,1024]{1,0:T(8,128)(2,1)}, u32[]{:S(2)}, u32[]{:S(2)}) %collective-permute-start.6) | collective-permute-done | bytes 426016 | tf_op jit(solution)/shard_map/ppermute | solution.py:140
  86.4 4.4 %half_maxima.2 = (f32[4,1,192]{2,1,0:T(1,128)S(1)}, f32[6,1,192]{2,1,0:T(1,128)S(1)}) custom-call(bf16[208,1024]{1,0:T(8,128)(2,1)S(1)} %copy-done, bf16[208,1024]{1,0:T(8,128)(2,1)} %collective-permute-done.refs_1_, bf16[208,1024]{1,0:T(8,128)(2,1)S(1)} %collective-permute-done.1.refs_2_, bf16[208,1024]{1,0:T(8,128)(2,1)} %collective-permute-done.2.refs_3_, ...), custom_call_target="tpu_custom_call" | custom-call | flops 2415919104 | bytes 5111808 | tf_op jit(solution)/shard_map/half_maxima/pallas_call | solution.py:112
  90.8 0.0 all-to-all-done.1.refs_8_
  90.8 5.0 %half_maxima.3 = (f32[4,1,192]{2,1,0:T(1,128)S(1)}, f32[6,1,192]{2,1,0:T(1,128)S(1)}) custom-call(bf16[208,1024]{1,0:T(8,128)(2,1)S(1)} %copy-done, bf16[208,1024]{1,0:T(8,128)(2,1)} %collective-permute-done.refs_1_, bf16[208,1024]{1,0:T(8,128)(2,1)S(1)} %collective-permute-done.1.refs_2_, bf16[208,1024]{1,0:T(8,128)(2,1)} %collective-permute-done.2.refs_3_, ...), custom_call_target="tpu_custom_call" | custom-call | flops 2415919104 | bytes 5111808 | tf_op jit(solution)/shard_map/half_maxima/pallas_call | solution.py:112
  95.8 2.0 %collective-permute-start.8 = (f32[3,1,192]{2,1,0:T(1,128)S(1)}, f32[3,1,192]{2,1,0:T(1,128)S(1)}, u32[]{:S(2)}, u32[]{:S(2)}) collective-permute-start(f32[3,1,192]{2,1,0:T(1,128)S(1)} %slice.16), channel_id=1, source_target_pairs={{0,1},{1,0},{2,3},{3,2},{4,5},{5,4},{6,7},{7,6},{8,9},{9,8},{10,11... | collective-permute-start | bytes 6920 | tf_op jit(solution)/shard_map/ppermute | solution.py:140
  97.9 0.6 broadcast_select_fusion
  98.5 9.7 %all-to-all-start.2 = ((f32[8,1,192]{2,1,0:T(1,128)}), f32[8,1,192]{2,1,0:T(1,128)S(1)}, u32[]{:S(2)}, u32[]{:S(2)}) async-start(f32[8,1,192]{2,1,0:T(1,128)} %broadcast_select_fusion), calls=%async_computation.2 | async-start | bytes 16384 | tf_op jit(solution)/shard_map/all_to_all | solution.py:166
  108.2 0.0 collective-permute-done.8
  108.2 2.8 %collective-permute-start.10 = (f32[1,192]{1,0:T(1,128)S(1)}, f32[1,192]{1,0:T(1,128)S(1)}, u32[]{:S(2)}, u32[]{:S(2)}) collective-permute-start(f32[1,192]{1,0:T(1,128)S(1)} %get-tuple-element.14), channel_id=1, source_target_pairs={{16,0},{32,16},{48,32},{64,48},{80,64},{96,80},{112,96},{128,112},... | collective-permute-start | bytes 2312 | tf_op jit(solution)/shard_map/ppermute | solution.py:136
  111.0 7.5 %collective-permute-start.11 = (f32[1,192]{1,0:T(1,128)S(1)}, f32[1,192]{1,0:T(1,128)S(1)}, u32[]{:S(2)}, u32[]{:S(2)}) collective-permute-start(f32[1,192]{1,0:T(1,128)S(1)} %get-tuple-element.13), channel_id=1, source_target_pairs={{32,0},{48,16},{64,32},{80,48},{96,64},{112,80},{128,96},{144,112}... | collective-permute-start | bytes 2312 | tf_op jit(solution)/shard_map/ppermute | solution.py:136
  118.5 1.9 %collective-permute-start.9 = (f32[1,192]{1,0:T(1,128)S(1)}, f32[1,192]{1,0:T(1,128)S(1)}, u32[]{:S(2)}, u32[]{:S(2)}) collective-permute-start(f32[1,192]{1,0:T(1,128)S(1)} %get-tuple-element.15), channel_id=1, source_target_pairs={{0,48},{16,64},{32,80},{48,96},{64,112},{80,128},{96,144},{112,160... | collective-permute-start | bytes 2312 | tf_op jit(solution)/shard_map/ppermute | solution.py:136
  120.4 0.0 all-to-all-done.2
  120.5 0.0 collective-permute-done.10
  120.5 0.0 collective-permute-done.11
  120.5 7.4 %collective-permute-done.9 = f32[1,192]{1,0:T(1,128)S(1)} collective-permute-done((f32[1,192]{1,0:T(1,128)S(1)}, f32[1,192]{1,0:T(1,128)S(1)}, u32[]{:S(2)}, u32[]{:S(2)}) %collective-permute-start.9) | collective-permute-done | bytes 800 | tf_op jit(solution)/shard_map/ppermute | solution.py:136
  127.8 0.6 fusion.2
  (5 shorter events, 0.0 us)
Async XLA Ops:
  4.2 5.0 %copy-start = (bf16[208,1024]{1,0:T(8,128)(2,1)S(1)}, bf16[208,1024]{1,0:T(8,128)(2,1)}, u32[]{:S(2)}) copy-start(bf16[208,1024]{1,0:T(8,128)(2,1)} %normalize_pack.1.block_ref.refs_0_) | copy-start | bytes 1277956
  4.2 29.6 %all-to-all-start = ((bf16[4,208,1024]{2,1,0:T(8,128)(2,1)}), bf16[4,208,1024]{2,1,0:T(8,128)(2,1)S(1)}, u32[]{:S(2)}, u32[]{:S(2)}) async-start(bf16[4,208,1024]{2,1,0:T(8,128)(2,1)} %repeat.2), calls=%async_computation | async-start | bytes 3407872 | tf_op jit(solution)/shard_map/all_to_all | solution.py:144
  9.2 21.6 %collective-permute-start.7 = (bf16[208,1024]{1,0:T(8,128)(2,1)S(1)}, bf16[208,1024]{1,0:T(8,128)(2,1)S(1)}, u32[]{:S(2)}, u32[]{:S(2)}) collective-permute-start(bf16[208,1024]{1,0:T(8,128)(2,1)S(1)} %copy-done), channel_id=1, source_target_pairs={{0,8},{8,0},{1,9},{9,1},{2,10},{10,2},{3,11},{11,3},{4,12},{12,4},... | collective-permute-start | bytes 1277960 | tf_op jit(solution)/shard_map/ppermute | solution.py:140
  30.8 0.8 copy-start.1
  33.9 56.9 %all-to-all-start.1 = ((bf16[4,208,1024]{2,1,0:T(8,128)(2,1)}), bf16[4,208,1024]{2,1,0:T(8,128)(2,1)}, u32[]{:S(2)}, u32[]{:S(2)}) async-start(bf16[4,208,1024]{2,1,0:T(8,128)(2,1)} %repeat.3), calls=%async_computation.1 | async-start | bytes 3407872 | tf_op jit(solution)/shard_map/all_to_all | solution.py:144
  38.7 39.0 %collective-permute-start.1 = (bf16[208,1024]{1,0:T(8,128)(2,1)S(1)}, bf16[208,1024]{1,0:T(8,128)(2,1)S(1)}, u32[]{:S(2)}, u32[]{:S(2)}) collective-permute-start(bf16[208,1024]{1,0:T(8,128)(2,1)S(1)} %copy-done), channel_id=1, source_target_pairs={{48,0},{64,16},{80,32},{96,48},{112,64},{128,80},{144,96},{160,112... | collective-permute-start | bytes 1277960 | tf_op jit(solution)/shard_map/ppermute | solution.py:136
  50.7 28.9 %collective-permute-start.3 = (bf16[208,1024]{1,0:T(8,128)(2,1)S(1)}, bf16[208,1024]{1,0:T(8,128)(2,1)S(1)}, u32[]{:S(2)}, u32[]{:S(2)}) collective-permute-start(bf16[208,1024]{1,0:T(8,128)(2,1)S(1)} %copy-done), channel_id=1, source_target_pairs={{0,16},{16,32},{32,48},{48,64},{64,80},{80,96},{96,112},{112,128},... | collective-permute-start | bytes 1277960 | tf_op jit(solution)/shard_map/ppermute | solution.py:136
  53.3 29.3 %collective-permute-start.5 = (bf16[208,1024]{1,0:T(8,128)(2,1)S(1)}, bf16[208,1024]{1,0:T(8,128)(2,1)S(1)}, u32[]{:S(2)}, u32[]{:S(2)}) collective-permute-start(bf16[208,1024]{1,0:T(8,128)(2,1)S(1)} %copy-done), channel_id=1, source_target_pairs={{0,32},{16,48},{32,64},{48,80},{64,96},{80,112},{96,128},{112,144}... | collective-permute-start | bytes 1277960 | tf_op jit(solution)/shard_map/ppermute | solution.py:136
  55.3 29.2 %collective-permute-start = (bf16[208,1024]{1,0:T(8,128)(2,1)S(1)}, bf16[208,1024]{1,0:T(8,128)(2,1)}, u32[]{:S(2)}, u32[]{:S(2)}) collective-permute-start(bf16[208,1024]{1,0:T(8,128)(2,1)S(1)} %copy-done), channel_id=1, source_target_pairs={{0,1},{1,0},{2,3},{3,2},{4,5},{5,4},{6,7},{7,6},{8,9},{9,8},{10,11... | collective-permute-start | bytes 1277960 | tf_op jit(solution)/shard_map/ppermute | solution.py:140
  77.7 6.8 %collective-permute-start.2 = (bf16[208,1024]{1,0:T(8,128)(2,1)S(1)}, bf16[208,1024]{1,0:T(8,128)(2,1)}, u32[]{:S(2)}, u32[]{:S(2)}) collective-permute-start(bf16[208,1024]{1,0:T(8,128)(2,1)S(1)} %collective-permute-done.1.refs_2_), channel_id=1, source_target_pairs={{0,1},{1,0},{2,3},{3,2},{4,5},{5,4},{6,7},{7,6},{8,9},{9,8},{10,11... | collective-permute-start | bytes 1277960 | tf_op jit(solution)/shard_map/ppermute | solution.py:140
  79.6 4.9 %collective-permute-start.4 = (bf16[208,1024]{1,0:T(8,128)(2,1)S(1)}, bf16[208,1024]{1,0:T(8,128)(2,1)}, u32[]{:S(2)}, u32[]{:S(2)}) collective-permute-start(bf16[208,1024]{1,0:T(8,128)(2,1)S(1)} %collective-permute-done.3.refs_4_), channel_id=1, source_target_pairs={{0,1},{1,0},{2,3},{3,2},{4,5},{5,4},{6,7},{7,6},{8,9},{9,8},{10,11... | collective-permute-start | bytes 1277960 | tf_op jit(solution)/shard_map/ppermute | solution.py:140
  82.6 3.8 %collective-permute-start.6 = (bf16[208,1024]{1,0:T(8,128)(2,1)S(1)}, bf16[208,1024]{1,0:T(8,128)(2,1)}, u32[]{:S(2)}, u32[]{:S(2)}) collective-permute-start(bf16[208,1024]{1,0:T(8,128)(2,1)S(1)} %collective-permute-done.5.refs_6_), channel_id=1, source_target_pairs={{0,1},{1,0},{2,3},{3,2},{4,5},{5,4},{6,7},{7,6},{8,9},{9,8},{10,11... | collective-permute-start | bytes 1277960 | tf_op jit(solution)/shard_map/ppermute | solution.py:140
  95.8 12.4 %collective-permute-start.8 = (f32[3,1,192]{2,1,0:T(1,128)S(1)}, f32[3,1,192]{2,1,0:T(1,128)S(1)}, u32[]{:S(2)}, u32[]{:S(2)}) collective-permute-start(f32[3,1,192]{2,1,0:T(1,128)S(1)} %slice.16), channel_id=1, source_target_pairs={{0,1},{1,0},{2,3},{3,2},{4,5},{5,4},{6,7},{7,6},{8,9},{9,8},{10,11... | collective-permute-start | bytes 6920 | tf_op jit(solution)/shard_map/ppermute | solution.py:140
  98.5 21.9 %all-to-all-start.2 = ((f32[8,1,192]{2,1,0:T(1,128)}), f32[8,1,192]{2,1,0:T(1,128)S(1)}, u32[]{:S(2)}, u32[]{:S(2)}) async-start(f32[8,1,192]{2,1,0:T(1,128)} %broadcast_select_fusion), calls=%async_computation.2 | async-start | bytes 16384 | tf_op jit(solution)/shard_map/all_to_all | solution.py:166
  108.2 12.2 %collective-permute-start.10 = (f32[1,192]{1,0:T(1,128)S(1)}, f32[1,192]{1,0:T(1,128)S(1)}, u32[]{:S(2)}, u32[]{:S(2)}) collective-permute-start(f32[1,192]{1,0:T(1,128)S(1)} %get-tuple-element.14), channel_id=1, source_target_pairs={{16,0},{32,16},{48,32},{64,48},{80,64},{96,80},{112,96},{128,112},... | collective-permute-start | bytes 2312 | tf_op jit(solution)/shard_map/ppermute | solution.py:136
  111.0 9.5 %collective-permute-start.11 = (f32[1,192]{1,0:T(1,128)S(1)}, f32[1,192]{1,0:T(1,128)S(1)}, u32[]{:S(2)}, u32[]{:S(2)}) collective-permute-start(f32[1,192]{1,0:T(1,128)S(1)} %get-tuple-element.13), channel_id=1, source_target_pairs={{32,0},{48,16},{64,32},{80,48},{96,64},{112,80},{128,96},{144,112}... | collective-permute-start | bytes 2312 | tf_op jit(solution)/shard_map/ppermute | solution.py:136
  118.5 9.4 %collective-permute-start.9 = (f32[1,192]{1,0:T(1,128)S(1)}, f32[1,192]{1,0:T(1,128)S(1)}, u32[]{:S(2)}, u32[]{:S(2)}) collective-permute-start(f32[1,192]{1,0:T(1,128)S(1)} %get-tuple-element.15), channel_id=1, source_target_pairs={{0,48},{16,64},{32,80},{48,96},{64,112},{80,128},{96,144},{112,160... | collective-permute-start | bytes 2312 | tf_op jit(solution)/shard_map/ppermute | solution.py:136

commit v4 on v2

v4 whole, which is shorter than its diff:
```python
import jax
import jax.numpy as jnp
from jax import lax
from jax.experimental import pallas as pl
from jax.experimental.pallas import tpu as pltpu
from jax.sharding import Mesh, PartitionSpec as P

ROWS = 192
EXTRA = 16
PACK = ROWS + EXTRA
D = 1024
X = 4
MOVES = (1, -3, 2)
NEAR = 1 + len(MOVES)
LEFT = 2 * NEAR * ROWS
TILE = 256
FAR = 1.0e9


def pack_kernel(emb_ref, lab_ref, ord_ref, out_ref):
    values = emb_ref[...].astype(jnp.float32)
    scale = lax.rsqrt(jnp.sum(values * values, axis=1, keepdims=True) + 1e-06)
    out_ref[0:ROWS, :] = (values * scale).astype(jnp.bfloat16)
    rank = jnp.broadcast_to(ord_ref[...], (EXTRA, ROWS))
    label = jnp.broadcast_to(lab_ref[...], (EXTRA, ROWS))
    line = lax.broadcasted_iota(jnp.int32, (EXTRA, ROWS), 0)
    digits = jnp.where(
        line == 0,
        rank >> 12,
        jnp.where(line == 1, (rank >> 6) & 63, jnp.where(line == 2, rank & 63, label + 1)),
    )
    digits = jnp.where(line < 4, digits, 0).astype(jnp.float32)
    digits = jnp.concatenate([digits, jnp.zeros((EXTRA, D - ROWS), jnp.float32)], axis=1)
    out_ref[ROWS:PACK, :] = digits.astype(jnp.bfloat16)


def pack(embeddings, labels, order):
    return pl.pallas_call(
        pack_kernel,
        out_shape=jax.ShapeDtypeStruct((PACK, D), jnp.bfloat16),
        compiler_params=pltpu.CompilerParams(vmem_limit_bytes=8 * 1024 * 1024),
        name="normalize_pack",
        cost_estimate=pl.CostEstimate(flops=4 * ROWS * D, bytes_accessed=4 * ROWS * D, transcendentals=ROWS),
    )(embeddings, labels.reshape(1, ROWS), order.reshape(1, ROWS))


def ranks(extra):
    return extra[0:1] * 4096.0 + extra[1:2] * 64.0 + extra[2:3]


def pair_kernel(core_ref, block_ref, sib_ref, out_ref):
    core = core_ref[0]
    out_ref[core] = block_ref[...]
    out_ref[1 - core] = sib_ref[...]


def pair(core, block, sib):
    inside = pl.BlockSpec(memory_space=pltpu.VMEM)
    return pl.pallas_call(
        pair_kernel,
        out_shape=jax.ShapeDtypeStruct((2, PACK, D), jnp.bfloat16),
        in_specs=[pl.BlockSpec(memory_space=pltpu.SMEM), inside, inside],
        out_specs=inside,
        compiler_params=pltpu.CompilerParams(vmem_limit_bytes=8 * 1024 * 1024),
        name="pair",
        cost_estimate=pl.CostEstimate(flops=0, bytes_accessed=8 * PACK * D, transcendentals=0),
    )(jnp.reshape(core, (1,)).astype(jnp.int32), block, sib)


def fetch(sources, rows_ref, extra_ref, sems):
    copies = []
    for k, ref in enumerate(sources):
        copies.append(pltpu.make_async_copy(ref.at[ROWS:PACK], extra_ref.at[k], sems.at[2 * k]))
        copies.append(
            pltpu.make_async_copy(ref.at[0:ROWS], rows_ref.at[k * ROWS:(k + 1) * ROWS], sems.at[2 * k + 1])
        )
    for copy in copies:
        copy.start()
    for copy in copies:
        copy.wait()


def extra_of(extra):
    return extra[:, 0:256].astype(jnp.float32)[:, :ROWS]


def prep_kernel(block_ref, sib_ref, first_ref, second_ref, two_ref, two_sib_ref, left_ref, rank_ref, valid_ref, extra_ref, sems):
    near = [block_ref, sib_ref, first_ref.at[0], first_ref.at[1], second_ref.at[0], second_ref.at[1], two_ref, two_sib_ref]
    fetch(near, left_ref, extra_ref, sems)
    extras = [extra_of(extra_ref[s]) for s in range(2 * NEAR)]
    same = [extra[3:4] == extras[0][3:4] for extra in extras]
    near_rank = jnp.concatenate([jnp.where(same[s], ranks(extras[s]), FAR) for s in range(2 * NEAR)], axis=1)
    rank_ref[...] = jnp.transpose(jnp.broadcast_to(near_rank, (128, LEFT)), (1, 0))
    for s in range(2, 2 * NEAR):
        valid_ref[s - 2] = same[s].astype(jnp.float32)


def prep(near):
    inside = pl.BlockSpec(memory_space=pltpu.VMEM)
    return pl.pallas_call(
        prep_kernel,
        out_shape=(
            jax.ShapeDtypeStruct((LEFT, D), jnp.bfloat16),
            jax.ShapeDtypeStruct((LEFT, 128), jnp.float32),
            jax.ShapeDtypeStruct((LEFT // ROWS - 2, 1, ROWS), jnp.float32),
        ),
        in_specs=[pl.BlockSpec(memory_space=pl.ANY)] * len(near),
        out_specs=(inside, inside, inside),
        scratch_shapes=[
            pltpu.VMEM((2 * NEAR, EXTRA, D), jnp.bfloat16),
            pltpu.SemaphoreType.DMA((4 * NEAR,)),
        ],
        compiler_params=pltpu.CompilerParams(vmem_limit_bytes=8 * 1024 * 1024),
        name="near_prep",
        cost_estimate=pl.CostEstimate(flops=0, bytes_accessed=4 * LEFT * D, transcendentals=0),
    )(*near)


def maxima_kernel(blocks, at, first, last, place_ref, left_ref, rank_ref, valid_ref, *refs):
    panel = refs[:blocks]
    *refs, right, extra_ref, sems = refs[blocks:]
    if first:
        cols_ref, *rows_ref = refs
    else:
        prior_cols_ref, prior_ref, cols_ref, *rows_ref = refs
        cols_ref[...] = prior_cols_ref[...]
    width = blocks * ROWS
    fetch(panel, right, extra_ref, sems)
    panel_rank = jnp.concatenate([ranks(extra_of(extra_ref[k])) for k in range(blocks)], axis=1)
    split = 2 * ROWS
    cols = []
    rows = None
    for start in range(0, width, TILE):
        tile = min(TILE, width - start)
        sims = lax.dot_general(
            left_ref[...], right[start:start + tile, :], (((1,), (1,)), ((), ())),
            preferred_element_type=jnp.float32,
        )
        for lane in range(0, tile, 128):
            lanes = min(128, tile - lane)
            part = sims[:, lane:lane + lanes]
            rank_row = panel_rank[:, start + lane:start + lane + lanes]
            rank_col = rank_ref[:, :lanes]
            here = part[:split]
            best = jnp.max(jnp.where(rank_col[:split] < rank_row, here, -1.0), axis=0, keepdims=True)
            there = part[split:]
            earlier = rank_row < rank_col[split:]
            best = jnp.maximum(best, jnp.max(jnp.where(earlier, -1.0, there), axis=0, keepdims=True))
            cols.append(best)
            found = jnp.where(earlier, there, -1.0)
            if lanes < 128:
                found = jnp.concatenate([found, jnp.full((LEFT - split, 128 - lanes), -1.0, jnp.float32)], axis=1)
            rows = found if rows is None else jnp.maximum(rows, found)
    best = jnp.concatenate(cols, axis=1)
    for k in range(blocks):
        cols_ref[place_ref[at + k]] = best[:, k * ROWS:(k + 1) * ROWS]
    if not first:
        rows = jnp.maximum(rows, prior_ref[...])
    if not last:
        rows_ref[0][...] = rows
    else:
        line = jnp.max(jnp.transpose(rows, (1, 0)), axis=0, keepdims=True)
        kept = [
            jnp.where(valid_ref[s] > 0.5, line[:, s * ROWS:(s + 1) * ROWS], -1.0) for s in range(LEFT // ROWS - 2)
        ]
        even = place_ref[2 * X] == 0
        rows_ref[0][0] = jnp.where(even, kept[0], kept[3])
        rows_ref[1][0] = jnp.where(even, kept[1], kept[2])
        rows_ref[0][1] = jnp.where(even, kept[2], kept[1])
        rows_ref[1][1] = jnp.where(even, kept[3], kept[0])
        rows_ref[0][2] = kept[4]
        rows_ref[1][2] = kept[5]


def maxima(place, laid, panel, at, prior, last):
    inside = pl.BlockSpec(memory_space=pltpu.VMEM)
    blocks = len(panel)
    operands = (*laid, *panel, *prior)
    lines = jax.ShapeDtypeStruct((NEAR - 1, 1, ROWS), jnp.float32)
    held = jax.ShapeDtypeStruct((LEFT - 2 * ROWS, 128), jnp.float32)
    rows = (lines, lines) if last else (held,)
    return pl.pallas_call(
        lambda *refs: maxima_kernel(blocks, at, not prior, last, *refs),
        out_shape=(jax.ShapeDtypeStruct((2 * X, 1, ROWS), jnp.float32), *rows),
        in_specs=(
            [pl.BlockSpec(memory_space=pltpu.SMEM)] + [inside] * len(laid)
            + [pl.BlockSpec(memory_space=pl.ANY)] * blocks + [inside] * len(prior)
        ),
        out_specs=(inside,) * (1 + len(rows)),
        scratch_shapes=[
            pltpu.VMEM((blocks * ROWS, D), jnp.bfloat16),
            pltpu.VMEM((blocks, EXTRA, D), jnp.bfloat16),
            pltpu.SemaphoreType.DMA((2 * blocks,)),
        ],
        compiler_params=pltpu.CompilerParams(vmem_limit_bytes=16 * 1024 * 1024),
        name="panel_maxima",
        cost_estimate=pl.CostEstimate(
            flops=2 * LEFT * blocks * ROWS * D, bytes_accessed=2 * (2 * NEAR + blocks) * PACK * D, transcendentals=0
        ),
    )(place, *operands)


def shift(value, steps, count):
    pairs = [(i, i + steps) for i in range(count) if 0 <= i + steps < count]
    return lax.ppermute(value, "grp", pairs)


def swap(value, axis):
    return lax.ppermute(value, axis, [(0, 1), (1, 0)])


def forward(value):
    pairs = [(2 * i, 2 * ((i + 1) % X)) for i in range(X)]
    pairs += [(2 * i + 1, 2 * ((i + X - 1) % X) + 1) for i in range(X)]
    return lax.ppermute(value, ("x", "core"), pairs)


def shift_both(value, even, odd, count):
    pairs = [(2 * i, 2 * (i + even)) for i in range(count) if 0 <= i + even < count]
    pairs += [(2 * i + 1, 2 * (i + odd) + 1) for i in range(count) if 0 <= i + odd < count]
    return lax.ppermute(value, ("grp", "core"), pairs)


def per_device(embeddings, labels, order):
    count = lax.axis_size("grp")
    grp, zh, x, core = (lax.axis_index(axis) for axis in ("grp", "zh", "x", "core"))
    block = pack(embeddings, labels, order)
    sib = swap(block, "core")
    panel = [block, forward(block)]
    both = pair(core, block, sib)
    ready, both = lax.optimization_barrier((block, both))
    first = shift_both(both, MOVES[0], MOVES[1], count)
    flipped = swap(ready, "zh")
    two = shift(ready, MOVES[2], count)
    panel.append(forward(panel[-1]))
    first, flipped, two, panel[-1] = lax.optimization_barrier((first, flipped, two, panel[-1]))
    panel.append(forward(panel[-1]))
    other = [flipped]
    for _ in range(X - 1):
        other.append(forward(other[-1]))
    laid = prep((block, sib, first, swap(first, "core"), two, swap(two, "core")))
    turn = jnp.where(core == 0, 1, X - 1)
    place = [(zh + h) % 2 * X + (x + (X - k) * turn) % X for h in range(2) for k in range(X)]
    place = jnp.stack([*place, core]).astype(jnp.int32)
    cols, rows = maxima(place, laid, panel, 0, (), False)
    cols, rows = maxima(place, laid, other[:3], X, (cols, rows), False)
    cols, rows, rows_sib = maxima(place, laid, other[3:], X + 3, (cols, rows), True)
    best = jnp.max(lax.all_to_all(cols, ("zh", "x"), 0, 0, tiled=True), axis=0)
    mine = jnp.maximum(rows, swap(rows_sib, "core"))
    for i, steps in enumerate(MOVES):
        back = shift(mine[i], -steps, count)
        source = grp + steps
        best = jnp.maximum(best, jnp.where((source >= 0) & (source < count), back, -1.0))
    return best.reshape(ROWS)


def solution(mesh):
    axes = ("grp", "zh", "x", "core")
    fine = Mesh(mesh.devices.reshape(mesh.shape["grp"], 2, X, 2), axes)
    return jax.shard_map(
        per_device,
        mesh=fine,
        in_specs=(P(axes, None), P(axes), P(axes)),
        out_specs=P(axes),
        check_vma=False,
    )
```

time: 119 us -> 122 us (1.025)
  starting transfers between devices: 78.8 us -> 65.3 us
  waiting for transfers between devices: 23.6 us -> 34.2 us
  Pallas kernels: 11 us -> 15.9 us
  local copies, waits for them, and re-layouts: 1.78 us -> 4.73 us
  other arithmetic: 2.91 us -> 0.6 us
    ppermute x6 -> x4, starting transfers between devices: 34.4 us -> 17.8 us  [shift(): return lax.ppermute(value, 'grp', pairs)]
    ppermute x6 -> x5, waiting for transfers between devices: 10.8 us -> 21.3 us  [swap(): return lax.ppermute(value, axis, [(0, 1), (1, 0)])]
    pallas_call x2 -> x5, Pallas kernels: 9.05 us -> 15.8 us  [the longest x3 13.4 us: maxima(): pl.pallas_call(lambda *refs: maxima_kernel(blocks, at, not prior, last, *...]
    ppermute x6 -> x7, waiting for transfers between devices: 2 us -> 6.4 us  [the longest x6 6.39 us: forward(): return lax.ppermute(value, ('x', 'core'), pairs)]
    ppermute x6 -> x4, waiting for transfers between devices: 10.8 us -> 6.47 us  [shift(): return lax.ppermute(value, 'grp', pairs)]
    ppermute x6 -> x7, starting transfers between devices: 17.8 us -> 21.3 us  [the longest x6 18.7 us: forward(): return lax.ppermute(value, ('x', 'core'), pairs)]
    ppermute x6 -> x5, starting transfers between devices: 20.6 us -> 17.7 us  [swap(): return lax.ppermute(value, axis, [(0, 1), (1, 0)])]
    unnamed x6 -> x18, local copies, waits for them, and re-layouts: 1.76 us -> 4.64 us
  transfers between devices with their start and end apart: 19 -> 17, of which waited for: 4 -> 5; matrix products, arithmetic and copies ran while one was open for 2% -> 0% of each run, Pallas kernels for 4% -> 10%
where the time goes in v4:
time: 122 us; the launch traced here: 121 us
  starting transfers between devices  65.3 us (54%)
  waiting for transfers between devices  34.2 us (28%)
  Pallas kernels  15.9 us (13%)
  local copies, waits for them, and re-layouts  4.73 us (4%)
    ppermute x5, waiting for transfers between devices, swap(): return lax.ppermute(value, axis, [(0, 1), (1, 0)])  21.3 us
    ppermute x6, starting transfers between devices, forward(): return lax.ppermute(value, ('x', 'core'), pairs)  18.7 us
    ppermute x4, starting transfers between devices, shift(): return lax.ppermute(value, 'grp', pairs)  17.8 us
    ppermute x5, starting transfers between devices, swap(): return lax.ppermute(value, axis, [(0, 1), (1, 0)])  17.7 us
    pallas_call x3, Pallas kernels, maxima(): pl.pallas_call(lambda *refs: maxima_kernel(blocks, at, not prior, last, *...  13.4 us
    all_to_all x1, starting transfers between devices, per_device(): best = jnp.max(lax.all_to_all(cols, ('zh', 'x'), 0, 0, tiled=True), axis=0)  8.53 us
    ppermute x4, waiting for transfers between devices, shift(): return lax.ppermute(value, 'grp', pairs)  6.47 us
    ppermute x6, waiting for transfers between devices, forward(): return lax.ppermute(value, ('x', 'core'), pairs)  6.39 us
  transfers between devices with their start and end apart: 17, of which 5 were waited for; matrix products, arithmetic and copies ran while one was open for 0% of the time, Pallas kernels for 10%

profile of v4, /device:TPU:114, one launch (start us, length us, event | category | flops | bytes accessed | tf_op | source)
XLA Modules:
  0.0 121.1 jit_solution(9910239664186618916)
XLA Ops:
  0.0 1.0 copy-done
  1.0 0.7 copy-done.1
  1.7 0.7 copy-done.2
  2.4 0.2 normalize_pack.1.block_ref.refs_4_
  2.5 1.9 %collective-permute-start = (bf16[208,1024]{1,0:T(8,128)(2,1)S(1)}, bf16[208,1024]{1,0:T(8,128)(2,1)S(1)}, u32[]{:S(2)}, u32[]{:S(2)}) collective-permute-start(bf16[208,1024]{1,0:T(8,128)(2,1)S(1)} %normalize_pack.1.block_ref.refs_4_), channel_id=1, source_target_pairs={{0,1},{1,0},{2,3},{3,2},{4,5},{5,4},{6,7},{7,6},{8,9},{9,8},{10,11... | collective-permute-start | bytes 1277960 | tf_op jit(solution)/shard_map/ppermute | solution.py:209
  4.5 3.4 %collective-permute-start.4 = (bf16[208,1024]{1,0:T(8,128)(2,1)S(1)}, bf16[208,1024]{1,0:T(8,128)(2,1)S(1)}, u32[]{:S(2)}, u32[]{:S(2)}) collective-permute-start(bf16[208,1024]{1,0:T(8,128)(2,1)S(1)} %normalize_pack.1.block_ref.refs_4_), channel_id=1, source_target_pairs={{0,2},{2,4},{4,6},{6,0},{1,7},{3,1},{5,3},{7,5},{8,10},{10,12},{12... | collective-permute-start | bytes 1277960 | tf_op jit(solution)/shard_map/ppermute | solution.py:215
  7.9 0.0 collective-permute-done.sib_ref
  7.9 0.1 pair.1
  7.9 2.6 %collective-permute-start.1 = (bf16[2,208,1024]{2,1,0:T(8,128)(2,1)S(1)}, bf16[2,208,1024]{2,1,0:T(8,128)(2,1)S(1)}, u32[]{:S(2)}, u32[]{:S(2)}) collective-permute-start(bf16[2,208,1024]{2,1,0:T(8,128)(2,1)S(1)} %pair.1), channel_id=1, source_target_pairs={{0,16},{16,32},{32,48},{48,64},{64,80},{80,96},{96,112},{112,128},... | collective-permute-start | bytes 2555912 | tf_op jit(solution)/shard_map/ppermute | solution.py:221
  10.5 10.0 %collective-permute-start.2 = (bf16[208,1024]{1,0:T(8,128)(2,1)S(1)}, bf16[208,1024]{1,0:T(8,128)(2,1)S(1)}, u32[]{:S(2)}, u32[]{:S(2)}) collective-permute-start(bf16[208,1024]{1,0:T(8,128)(2,1)S(1)} %normalize_pack.1.block_ref.refs_4_), channel_id=1, source_target_pairs={{0,8},{8,0},{1,9},{9,1},{2,10},{10,2},{3,11},{11,3},{4,12},{12,4},... | collective-permute-start | bytes 1277960 | tf_op jit(solution)/shard_map/ppermute | solution.py:209
  20.6 3.6 %collective-permute-start.3 = (bf16[208,1024]{1,0:T(8,128)(2,1)S(1)}, bf16[208,1024]{1,0:T(8,128)(2,1)S(1)}, u32[]{:S(2)}, u32[]{:S(2)}) collective-permute-start(bf16[208,1024]{1,0:T(8,128)(2,1)S(1)} %normalize_pack.1.block_ref.refs_4_), channel_id=1, source_target_pairs={{0,32},{16,48},{32,64},{48,80},{64,96},{80,112},{96,128},{112,144}... | collective-permute-start | bytes 1277960 | tf_op jit(solution)/shard_map/ppermute | solution.py:205
  24.2 0.0 collective-permute-done.4.refs_5_
  24.2 3.1 %collective-permute-start.5 = (bf16[208,1024]{1,0:T(8,128)(2,1)S(1)}, bf16[208,1024]{1,0:T(8,128)(2,1)}, u32[]{:S(2)}, u32[]{:S(2)}) collective-permute-start(bf16[208,1024]{1,0:T(8,128)(2,1)S(1)} %collective-permute-done.4.refs_5_), channel_id=1, source_target_pairs={{0,2},{2,4},{4,6},{6,0},{1,7},{3,1},{5,3},{7,5},{8,10},{10,12},{12... | collective-permute-start | bytes 1277960 | tf_op jit(solution)/shard_map/ppermute | solution.py:215
  27.3 0.8 copy-done.3
  28.1 21.3 %collective-permute-done.2.refs_4_ = bf16[208,1024]{1,0:T(8,128)(2,1)S(1)} collective-permute-done((bf16[208,1024]{1,0:T(8,128)(2,1)S(1)}, bf16[208,1024]{1,0:T(8,128)(2,1)S(1)}, u32[]{:S(2)}, u32[]{:S(2)}) %collective-permute-start.2) | collective-permute-done | bytes 426016 | tf_op jit(solution)/shard_map/ppermute | solution.py:209
  49.4 0.0 collective-permute-done.3.two_ref
  49.4 0.0 collective-permute-done.5.refs_6_
  49.4 0.0 collective-permute-done.1.first_ref
  49.4 3.4 %collective-permute-start.8 = (bf16[208,1024]{1,0:T(8,128)(2,1)S(1)}, bf16[208,1024]{1,0:T(8,128)(2,1)S(1)}, u32[]{:S(2)}, u32[]{:S(2)}) collective-permute-start(bf16[208,1024]{1,0:T(8,128)(2,1)S(1)} %collective-permute-done.2.refs_4_), channel_id=1, source_target_pairs={{0,2},{2,4},{4,6},{6,0},{1,7},{3,1},{5,3},{7,5},{8,10},{10,12},{12... | collective-permute-start | bytes 1277960 | tf_op jit(solution)/shard_map/ppermute | solution.py:215
  52.8 0.8 copy-done.5
  53.6 1.9 %collective-permute-start.6 = (bf16[2,208,1024]{2,1,0:T(8,128)(2,1)S(1)}, bf16[2,208,1024]{2,1,0:T(8,128)(2,1)S(1)}, u32[]{:S(2)}, u32[]{:S(2)}) collective-permute-start(bf16[2,208,1024]{2,1,0:T(8,128)(2,1)S(1)} %collective-permute-done.1.first_ref), channel_id=1, source_target_pairs={{0,1},{1,0},{2,3},{3,2},{4,5},{5,4},{6,7},{7,6},{8,9},{9,8},{10,11... | collective-permute-start | bytes 2555912 | tf_op jit(solution)/shard_map/ppermute | solution.py:209
  55.5 3.9 %collective-permute-done.8.refs_5_ = bf16[208,1024]{1,0:T(8,128)(2,1)S(1)} collective-permute-done((bf16[208,1024]{1,0:T(8,128)(2,1)S(1)}, bf16[208,1024]{1,0:T(8,128)(2,1)S(1)}, u32[]{:S(2)}, u32[]{:S(2)}) %collective-permute-start.8) | collective-permute-done | bytes 426016 | tf_op jit(solution)/shard_map/ppermute | solution.py:215
  59.4 3.4 %collective-permute-start.9 = (bf16[208,1024]{1,0:T(8,128)(2,1)S(1)}, bf16[208,1024]{1,0:T(8,128)(2,1)}, u32[]{:S(2)}, u32[]{:S(2)}) collective-permute-start(bf16[208,1024]{1,0:T(8,128)(2,1)S(1)} %collective-permute-done.8.refs_5_), channel_id=1, source_target_pairs={{0,2},{2,4},{4,6},{6,0},{1,7},{3,1},{5,3},{7,5},{8,10},{10,12},{12... | collective-permute-start | bytes 1277960 | tf_op jit(solution)/shard_map/ppermute | solution.py:215
  62.8 0.7 copy-done.7
  63.6 1.9 %collective-permute-start.7 = (bf16[208,1024]{1,0:T(8,128)(2,1)S(1)}, bf16[208,1024]{1,0:T(8,128)(2,1)S(1)}, u32[]{:S(2)}, u32[]{:S(2)}) collective-permute-start(bf16[208,1024]{1,0:T(8,128)(2,1)S(1)} %collective-permute-done.3.two_ref), channel_id=1, source_target_pairs={{0,1},{1,0},{2,3},{3,2},{4,5},{5,4},{6,7},{7,6},{8,9},{9,8},{10,11... | collective-permute-start | bytes 1277960 | tf_op jit(solution)/shard_map/ppermute | solution.py:209
  65.5 1.9 %collective-permute-start.11 = (bf16[208,1024]{1,0:T(8,128)(2,1)}, bf16[208,1024]{1,0:T(8,128)(2,1)}, u32[]{:S(2)}, u32[]{:S(2)}) collective-permute-start(bf16[208,1024]{1,0:T(8,128)(2,1)} %collective-permute-done.5.refs_6_), channel_id=1, source_target_pairs={{0,2},{2,4},{4,6},{6,0},{1,7},{3,1},{5,3},{7,5},{8,10},{10,12},{12... | collective-permute-start | bytes 1277960 | tf_op jit(solution)/shard_map/ppermute | solution.py:215
  67.4 2.1 %collective-permute-done.9.refs_6_ = bf16[208,1024]{1,0:T(8,128)(2,1)} collective-permute-done((bf16[208,1024]{1,0:T(8,128)(2,1)S(1)}, bf16[208,1024]{1,0:T(8,128)(2,1)}, u32[]{:S(2)}, u32[]{:S(2)}) %collective-permute-start.9) | collective-permute-done | bytes 426016 | tf_op jit(solution)/shard_map/ppermute | solution.py:215
  69.5 3.4 %collective-permute-start.10 = (bf16[208,1024]{1,0:T(8,128)(2,1)}, bf16[208,1024]{1,0:T(8,128)(2,1)}, u32[]{:S(2)}, u32[]{:S(2)}) collective-permute-start(bf16[208,1024]{1,0:T(8,128)(2,1)} %collective-permute-done.9.refs_6_), channel_id=1, source_target_pairs={{0,2},{2,4},{4,6},{6,0},{1,7},{3,1},{5,3},{7,5},{8,10},{10,12},{12... | collective-permute-start | bytes 1277960 | tf_op jit(solution)/shard_map/ppermute | solution.py:215
  73.0 0.1 stack.39.refs_0_
  73.1 0.0 collective-permute-done.7.two_sib_ref
  73.1 0.0 collective-permute-done.6.second_ref
  73.1 2.3 %near_prep.1 = (bf16[1536,1024]{1,0:T(8,128)(2,1)S(1)}, f32[1536,128]{1,0:T(8,128)S(1)}, f32[6,1,192]{2,1,0:T(1,128)S(1)}) custom-call(bf16[208,1024]{1,0:T(8,128)(2,1)S(1)} %normalize_pack.1.block_ref.refs_4_, bf16[208,1024]{1,0:T(8,128)(2,1)S(1)} %collective-permute-done.sib_ref, bf16[2,208,1024]{2,1,0:T(8,128)(2,1)S(1)} %collective-permute-done.1.first_ref, ...), custom_call_target="tpu_custom_call" | custom-call | bytes 6291456 | tf_op jit(solution)/shard_map/near_prep/pallas_call | solution.py:100
  75.4 0.4 collective-permute-done.11.refs_7_
  75.8 5.2 %panel_maxima.3 = (f32[8,1,192]{2,1,0:T(1,128)S(1)}, f32[1152,128]{1,0:T(8,128)S(1)}) custom-call(s32[9]{0:T(128)S(1)} %stack.39.refs_0_, bf16[1536,1024]{1,0:T(8,128)(2,1)S(1)} %get-tuple-element.25.refs_1_, f32[1536,128]{1,0:T(8,128)S(1)} %get-tuple-element.26.refs_2_, f32[6,1,192]{2,1,0:T(1,128)S(1)} %get-tuple-element.27.refs_3_, ...), custom_call_target="tpu_custom_call" | custom-call | flops 2415919104 | bytes 5111808 | tf_op jit(solution)/shard_map/panel_maxima/pallas_call | solution.py:182
  81.0 5.0 %panel_maxima.4 = (f32[8,1,192]{2,1,0:T(1,128)S(1)}, f32[1152,128]{1,0:T(8,128)S(1)}) custom-call(s32[9]{0:T(128)S(1)} %stack.39.refs_0_, bf16[1536,1024]{1,0:T(8,128)(2,1)S(1)} %get-tuple-element.25.refs_1_, f32[1536,128]{1,0:T(8,128)S(1)} %get-tuple-element.26.refs_2_, f32[6,1,192]{2,1,0:T(1,128)S(1)} %get-tuple-element.27.refs_3_, ...), custom_call_target="tpu_custom_call" | custom-call | flops 1811939328 | bytes 4685824 | tf_op jit(solution)/shard_map/panel_maxima/pallas_call | solution.py:182
  86.0 0.0 collective-permute-done.10.refs_4_
  86.0 3.2 %panel_maxima.5 = (f32[8,1,192]{2,1,0:T(1,128)}, f32[3,1,192]{2,1,0:T(1,128)S(1)}, f32[3,1,192]{2,1,0:T(1,128)S(1)}) custom-call(s32[9]{0:T(128)S(1)} %stack.39.refs_0_, bf16[1536,1024]{1,0:T(8,128)(2,1)S(1)} %get-tuple-element.25.refs_1_, f32[1536,128]{1,0:T(8,128)S(1)} %get-tuple-element.26.refs_2_, f32[6,1,192]{2,1,0:T(1,128)S(1)} %get-tuple-element.27.refs_3_, ...), custom_call_target="tpu_custom_call" | custom-call | flops 603979776 | bytes 3833856 | tf_op jit(solution)/shard_map/panel_maxima/pallas_call | solution.py:182
  89.3 1.9 %collective-permute-start.12 = (f32[3,1,192]{2,1,0:T(1,128)S(1)}, f32[3,1,192]{2,1,0:T(1,128)S(1)}, u32[]{:S(2)}, u32[]{:S(2)}) collective-permute-start(f32[3,1,192]{2,1,0:T(1,128)S(1)} %get-tuple-element.36), channel_id=1, source_target_pairs={{0,1},{1,0},{2,3},{3,2},{4,5},{5,4},{6,7},{7,6},{8,9},{9,8},{10,11... | collective-permute-start | bytes 6920 | tf_op jit(solution)/shard_map/ppermute | solution.py:209
  91.2 8.5 %all-to-all-start = ((f32[8,1,192]{2,1,0:T(1,128)}), f32[8,1,192]{2,1,0:T(1,128)S(1)}, u32[]{:S(2)}, u32[]{:S(2)}) async-start(f32[8,1,192]{2,1,0:T(1,128)} %get-tuple-element.34), calls=%async_computation | async-start | bytes 16384 | tf_op jit(solution)/shard_map/all_to_all | solution.py:248
  99.7 0.0 collective-permute-done.12
  99.8 2.7 %collective-permute-start.13 = (f32[1,192]{1,0:T(1,128)S(1)}, f32[1,192]{1,0:T(1,128)S(1)}, u32[]{:S(2)}, u32[]{:S(2)}) collective-permute-start(f32[1,192]{1,0:T(1,128)S(1)} %get-tuple-element.39), channel_id=1, source_target_pairs={{16,0},{32,16},{48,32},{64,48},{80,64},{96,80},{112,96},{128,112},... | collective-permute-start | bytes 2312 | tf_op jit(solution)/shard_map/ppermute | solution.py:205
  102.5 9.6 %collective-permute-start.14 = (f32[1,192]{1,0:T(1,128)S(1)}, f32[1,192]{1,0:T(1,128)S(1)}, u32[]{:S(2)}, u32[]{:S(2)}) collective-permute-start(f32[1,192]{1,0:T(1,128)S(1)} %get-tuple-element.38), channel_id=1, source_target_pairs={{0,48},{16,64},{32,80},{48,96},{64,112},{80,128},{96,144},{112,160... | collective-permute-start | bytes 2312 | tf_op jit(solution)/shard_map/ppermute | solution.py:205
  112.1 1.9 %collective-permute-start.15 = (f32[1,192]{1,0:T(1,128)S(1)}, f32[1,192]{1,0:T(1,128)S(1)}, u32[]{:S(2)}, u32[]{:S(2)}) collective-permute-start(f32[1,192]{1,0:T(1,128)S(1)} %get-tuple-element.37), channel_id=1, source_target_pairs={{32,0},{48,16},{64,32},{80,48},{96,64},{112,80},{128,96},{144,112}... | collective-permute-start | bytes 2312 | tf_op jit(solution)/shard_map/ppermute | solution.py:205
  114.0 0.0 all-to-all-done
  114.1 0.0 collective-permute-done.13
  114.1 0.0 collective-permute-done.14
  114.1 6.5 %collective-permute-done.15 = f32[1,192]{1,0:T(1,128)S(1)} collective-permute-done((f32[1,192]{1,0:T(1,128)S(1)}, f32[1,192]{1,0:T(1,128)S(1)}, u32[]{:S(2)}, u32[]{:S(2)}) %collective-permute-start.15) | collective-permute-done | bytes 800 | tf_op jit(solution)/shard_map/ppermute | solution.py:205
  120.6 0.6 fusion.2
  (15 shorter events, 0.1 us)
Async XLA Ops:
  0.0 1.0 copy-start
  1.0 0.7 copy-start.1
  1.7 0.7 copy-start.2
  2.5 5.3 %collective-permute-start = (bf16[208,1024]{1,0:T(8,128)(2,1)S(1)}, bf16[208,1024]{1,0:T(8,128)(2,1)S(1)}, u32[]{:S(2)}, u32[]{:S(2)}) collective-permute-start(bf16[208,1024]{1,0:T(8,128)(2,1)S(1)} %normalize_pack.1.block_ref.refs_4_), channel_id=1, source_target_pairs={{0,1},{1,0},{2,3},{3,2},{4,5},{5,4},{6,7},{7,6},{8,9},{9,8},{10,11... | collective-permute-start | bytes 1277960 | tf_op jit(solution)/shard_map/ppermute | solution.py:209
  4.5 19.7 %collective-permute-start.4 = (bf16[208,1024]{1,0:T(8,128)(2,1)S(1)}, bf16[208,1024]{1,0:T(8,128)(2,1)S(1)}, u32[]{:S(2)}, u32[]{:S(2)}) collective-permute-start(bf16[208,1024]{1,0:T(8,128)(2,1)S(1)} %normalize_pack.1.block_ref.refs_4_), channel_id=1, source_target_pairs={{0,2},{2,4},{4,6},{6,0},{1,7},{3,1},{5,3},{7,5},{8,10},{10,12},{12... | collective-permute-start | bytes 1277960 | tf_op jit(solution)/shard_map/ppermute | solution.py:215
  7.9 41.4 %collective-permute-start.1 = (bf16[2,208,1024]{2,1,0:T(8,128)(2,1)S(1)}, bf16[2,208,1024]{2,1,0:T(8,128)(2,1)S(1)}, u32[]{:S(2)}, u32[]{:S(2)}) collective-permute-start(bf16[2,208,1024]{2,1,0:T(8,128)(2,1)S(1)} %pair.1), channel_id=1, source_target_pairs={{0,16},{16,32},{32,48},{48,64},{64,80},{80,96},{96,112},{112,128},... | collective-permute-start | bytes 2555912 | tf_op jit(solution)/shard_map/ppermute | solution.py:221
  10.5 38.8 %collective-permute-start.2 = (bf16[208,1024]{1,0:T(8,128)(2,1)S(1)}, bf16[208,1024]{1,0:T(8,128)(2,1)S(1)}, u32[]{:S(2)}, u32[]{:S(2)}) collective-permute-start(bf16[208,1024]{1,0:T(8,128)(2,1)S(1)} %normalize_pack.1.block_ref.refs_4_), channel_id=1, source_target_pairs={{0,8},{8,0},{1,9},{9,1},{2,10},{10,2},{3,11},{11,3},{4,12},{12,4},... | collective-permute-start | bytes 1277960 | tf_op jit(solution)/shard_map/ppermute | solution.py:209
  20.6 28.8 %collective-permute-start.3 = (bf16[208,1024]{1,0:T(8,128)(2,1)S(1)}, bf16[208,1024]{1,0:T(8,128)(2,1)S(1)}, u32[]{:S(2)}, u32[]{:S(2)}) collective-permute-start(bf16[208,1024]{1,0:T(8,128)(2,1)S(1)} %normalize_pack.1.block_ref.refs_4_), channel_id=1, source_target_pairs={{0,32},{16,48},{32,64},{48,80},{64,96},{80,112},{96,128},{112,144}... | collective-permute-start | bytes 1277960 | tf_op jit(solution)/shard_map/ppermute | solution.py:205
  24.2 25.2 %collective-permute-start.5 = (bf16[208,1024]{1,0:T(8,128)(2,1)S(1)}, bf16[208,1024]{1,0:T(8,128)(2,1)}, u32[]{:S(2)}, u32[]{:S(2)}) collective-permute-start(bf16[208,1024]{1,0:T(8,128)(2,1)S(1)} %collective-permute-done.4.refs_5_), channel_id=1, source_target_pairs={{0,2},{2,4},{4,6},{6,0},{1,7},{3,1},{5,3},{7,5},{8,10},{10,12},{12... | collective-permute-start | bytes 1277960 | tf_op jit(solution)/shard_map/ppermute | solution.py:215
  27.3 0.8 copy-start.3
  49.4 10.0 %collective-permute-start.8 = (bf16[208,1024]{1,0:T(8,128)(2,1)S(1)}, bf16[208,1024]{1,0:T(8,128)(2,1)S(1)}, u32[]{:S(2)}, u32[]{:S(2)}) collective-permute-start(bf16[208,1024]{1,0:T(8,128)(2,1)S(1)} %collective-permute-done.2.refs_4_), channel_id=1, source_target_pairs={{0,2},{2,4},{4,6},{6,0},{1,7},{3,1},{5,3},{7,5},{8,10},{10,12},{12... | collective-permute-start | bytes 1277960 | tf_op jit(solution)/shard_map/ppermute | solution.py:215
  52.8 0.8 copy-start.5
  53.6 19.5 %collective-permute-start.6 = (bf16[2,208,1024]{2,1,0:T(8,128)(2,1)S(1)}, bf16[2,208,1024]{2,1,0:T(8,128)(2,1)S(1)}, u32[]{:S(2)}, u32[]{:S(2)}) collective-permute-start(bf16[2,208,1024]{2,1,0:T(8,128)(2,1)S(1)} %collective-permute-done.1.first_ref), channel_id=1, source_target_pairs={{0,1},{1,0},{2,3},{3,2},{4,5},{5,4},{6,7},{7,6},{8,9},{9,8},{10,11... | collective-permute-start | bytes 2555912 | tf_op jit(solution)/shard_map/ppermute | solution.py:209
  59.4 10.1 %collective-permute-start.9 = (bf16[208,1024]{1,0:T(8,128)(2,1)S(1)}, bf16[208,1024]{1,0:T(8,128)(2,1)}, u32[]{:S(2)}, u32[]{:S(2)}) collective-permute-start(bf16[208,1024]{1,0:T(8,128)(2,1)S(1)} %collective-permute-done.8.refs_5_), channel_id=1, source_target_pairs={{0,2},{2,4},{4,6},{6,0},{1,7},{3,1},{5,3},{7,5},{8,10},{10,12},{12... | collective-permute-start | bytes 1277960 | tf_op jit(solution)/shard_map/ppermute | solution.py:215
  62.8 0.8 copy-start.7
  63.6 9.5 %collective-permute-start.7 = (bf16[208,1024]{1,0:T(8,128)(2,1)S(1)}, bf16[208,1024]{1,0:T(8,128)(2,1)S(1)}, u32[]{:S(2)}, u32[]{:S(2)}) collective-permute-start(bf16[208,1024]{1,0:T(8,128)(2,1)S(1)} %collective-permute-done.3.two_ref), channel_id=1, source_target_pairs={{0,1},{1,0},{2,3},{3,2},{4,5},{5,4},{6,7},{7,6},{8,9},{9,8},{10,11... | collective-permute-start | bytes 1277960 | tf_op jit(solution)/shard_map/ppermute | solution.py:209
  65.5 10.3 %collective-permute-start.11 = (bf16[208,1024]{1,0:T(8,128)(2,1)}, bf16[208,1024]{1,0:T(8,128)(2,1)}, u32[]{:S(2)}, u32[]{:S(2)}) collective-permute-start(bf16[208,1024]{1,0:T(8,128)(2,1)} %collective-permute-done.5.refs_6_), channel_id=1, source_target_pairs={{0,2},{2,4},{4,6},{6,0},{1,7},{3,1},{5,3},{7,5},{8,10},{10,12},{12... | collective-permute-start | bytes 1277960 | tf_op jit(solution)/shard_map/ppermute | solution.py:215
  69.5 16.5 %collective-permute-start.10 = (bf16[208,1024]{1,0:T(8,128)(2,1)}, bf16[208,1024]{1,0:T(8,128)(2,1)}, u32[]{:S(2)}, u32[]{:S(2)}) collective-permute-start(bf16[208,1024]{1,0:T(8,128)(2,1)} %collective-permute-done.9.refs_6_), channel_id=1, source_target_pairs={{0,2},{2,4},{4,6},{6,0},{1,7},{3,1},{5,3},{7,5},{8,10},{10,12},{12... | collective-permute-start | bytes 1277960 | tf_op jit(solution)/shard_map/ppermute | solution.py:215
  73.1 2.7 %copy-start.4 = (bf16[208,1024]{1,0:T(8,128)(2,1)S(1)}, bf16[208,1024]{1,0:T(8,128)(2,1)}, u32[]{:S(2)}) copy-start(bf16[208,1024]{1,0:T(8,128)(2,1)} %copy-done.3) | copy-start | bytes 1277956
  75.8 5.2 %copy-start.6 = (bf16[208,1024]{1,0:T(8,128)(2,1)S(1)}, bf16[208,1024]{1,0:T(8,128)(2,1)}, u32[]{:S(2)}) copy-start(bf16[208,1024]{1,0:T(8,128)(2,1)} %copy-done.5) | copy-start | bytes 1277956
  75.8 5.2 %copy-start.8 = (bf16[208,1024]{1,0:T(8,128)(2,1)S(1)}, bf16[208,1024]{1,0:T(8,128)(2,1)}, u32[]{:S(2)}) copy-start(bf16[208,1024]{1,0:T(8,128)(2,1)} %copy-done.7) | copy-start | bytes 1277956
  89.3 10.5 %collective-permute-start.12 = (f32[3,1,192]{2,1,0:T(1,128)S(1)}, f32[3,1,192]{2,1,0:T(1,128)S(1)}, u32[]{:S(2)}, u32[]{:S(2)}) collective-permute-start(f32[3,1,192]{2,1,0:T(1,128)S(1)} %get-tuple-element.36), channel_id=1, source_target_pairs={{0,1},{1,0},{2,3},{3,2},{4,5},{5,4},{6,7},{7,6},{8,9},{9,8},{10,11... | collective-permute-start | bytes 6920 | tf_op jit(solution)/shard_map/ppermute | solution.py:209
  91.2 22.8 %all-to-all-start = ((f32[8,1,192]{2,1,0:T(1,128)}), f32[8,1,192]{2,1,0:T(1,128)S(1)}, u32[]{:S(2)}, u32[]{:S(2)}) async-start(f32[8,1,192]{2,1,0:T(1,128)} %get-tuple-element.34), calls=%async_computation | async-start | bytes 16384 | tf_op jit(solution)/shard_map/all_to_all | solution.py:248
  99.8 14.3 %collective-permute-start.13 = (f32[1,192]{1,0:T(1,128)S(1)}, f32[1,192]{1,0:T(1,128)S(1)}, u32[]{:S(2)}, u32[]{:S(2)}) collective-permute-start(f32[1,192]{1,0:T(1,128)S(1)} %get-tuple-element.39), channel_id=1, source_target_pairs={{16,0},{32,16},{48,32},{64,48},{80,64},{96,80},{112,96},{128,112},... | collective-permute-start | bytes 2312 | tf_op jit(solution)/shard_map/ppermute | solution.py:205
  102.5 11.6 %collective-permute-start.14 = (f32[1,192]{1,0:T(1,128)S(1)}, f32[1,192]{1,0:T(1,128)S(1)}, u32[]{:S(2)}, u32[]{:S(2)}) collective-permute-start(f32[1,192]{1,0:T(1,128)S(1)} %get-tuple-element.38), channel_id=1, source_target_pairs={{0,48},{16,64},{32,80},{48,96},{64,112},{80,128},{96,144},{112,160... | collective-permute-start | bytes 2312 | tf_op jit(solution)/shard_map/ppermute | solution.py:205
  112.1 8.5 %collective-permute-start.15 = (f32[1,192]{1,0:T(1,128)S(1)}, f32[1,192]{1,0:T(1,128)S(1)}, u32[]{:S(2)}, u32[]{:S(2)}) collective-permute-start(f32[1,192]{1,0:T(1,128)S(1)} %get-tuple-element.37), channel_id=1, source_target_pairs={{32,0},{48,16},{64,32},{80,48},{96,64},{112,80},{128,96},{144,112}... | collective-permute-start | bytes 2312 | tf_op jit(solution)/shard_map/ppermute | solution.py:205

commit v5 on v4

--- a/solution.py
+++ b/solution.py
@@ -10,14 +10,24 @@
 PACK = ROWS + EXTRA
 D = 1024
 X = 4
+Z_LO = 4
 MOVES = (1, -3, 2)
 NEAR = 1 + len(MOVES)
 LEFT = 2 * NEAR * ROWS
 TILE = 256
 FAR = 1.0e9
-
-
-def pack_kernel(emb_ref, lab_ref, ord_ref, out_ref):
+SLOTS = (0, 7, 1, 2, 3, 4, 5, 6)
+
+
+def pack_kernel(emb_any, lab_any, ord_any, out_ref, emb_ref, lab_ref, ord_ref, sems):
+    copies = [
+        pltpu.make_async_copy(source, target, sems.at[k])
+        for k, (source, target) in enumerate(((emb_any, emb_ref), (lab_any, lab_ref), (ord_any, ord_ref)))
+    ]
+    for copy in copies:
+        copy.start()
+    for copy in copies:
+        copy.wait()
     values = emb_ref[...].astype(jnp.float32)
     scale = lax.rsqrt(jnp.sum(values * values, axis=1, keepdims=True) + 1e-06)
     out_ref[0:ROWS, :] = (values * scale).astype(jnp.bfloat16)
@@ -35,13 +45,34 @@
 
 
 def pack(embeddings, labels, order):
+    anywhere = pl.BlockSpec(memory_space=pl.ANY)
     return pl.pallas_call(
         pack_kernel,
         out_shape=jax.ShapeDtypeStruct((PACK, D), jnp.bfloat16),
-        compiler_params=pltpu.CompilerParams(vmem_limit_bytes=8 * 1024 * 1024),
+        in_specs=[anywhere] * 3,
+        out_specs=pl.BlockSpec(memory_space=pltpu.VMEM),
+        scratch_shapes=[
+            pltpu.VMEM((ROWS, D), jnp.bfloat16),
+            pltpu.VMEM((1, ROWS), jnp.int32),
+            pltpu.VMEM((1, ROWS), jnp.int32),
+            pltpu.SemaphoreType.DMA((3,)),
+        ],
         name="normalize_pack",
         cost_estimate=pl.CostEstimate(flops=4 * ROWS * D, bytes_accessed=4 * ROWS * D, transcendentals=ROWS),
     )(embeddings, labels.reshape(1, ROWS), order.reshape(1, ROWS))
+
+
+def weigh(value, cost):
+    anywhere = pl.BlockSpec(memory_space=pl.ANY)
+    return pl.pallas_call(
+        lambda value_ref, out_ref: None,
+        out_shape=jax.ShapeDtypeStruct(value.shape, value.dtype),
+        in_specs=[anywhere],
+        out_specs=anywhere,
+        input_output_aliases={0: 0},
+        name="weigh",
+        cost_estimate=pl.CostEstimate(flops=cost, bytes_accessed=0, transcendentals=0),
+    )(value)
 
 
 def ranks(extra):
@@ -67,27 +98,33 @@
     )(jnp.reshape(core, (1,)).astype(jnp.int32), block, sib)
 
 
-def fetch(sources, rows_ref, extra_ref, sems):
-    copies = []
-    for k, ref in enumerate(sources):
-        copies.append(pltpu.make_async_copy(ref.at[ROWS:PACK], extra_ref.at[k], sems.at[2 * k]))
-        copies.append(
-            pltpu.make_async_copy(ref.at[0:ROWS], rows_ref.at[k * ROWS:(k + 1) * ROWS], sems.at[2 * k + 1])
-        )
-    for copy in copies:
-        copy.start()
-    for copy in copies:
-        copy.wait()
-
-
-def extra_of(extra):
-    return extra[:, 0:256].astype(jnp.float32)[:, :ROWS]
-
-
-def prep_kernel(block_ref, sib_ref, first_ref, second_ref, two_ref, two_sib_ref, left_ref, rank_ref, valid_ref, extra_ref, sems):
-    near = [block_ref, sib_ref, first_ref.at[0], first_ref.at[1], second_ref.at[0], second_ref.at[1], two_ref, two_sib_ref]
-    fetch(near, left_ref, extra_ref, sems)
-    extras = [extra_of(extra_ref[s]) for s in range(2 * NEAR)]
+def extra_of(ref):
+    return ref[ROWS:PACK, 0:256].astype(jnp.float32)[:, :ROWS]
+
+
+def gate_kernel(*refs):
+    refs[-1][...] = refs[0][...]
+
+
+def gate(value, *others):
+    inside = pl.BlockSpec(memory_space=pltpu.VMEM)
+    return pl.pallas_call(
+        gate_kernel,
+        out_shape=jax.ShapeDtypeStruct(value.shape, value.dtype),
+        in_specs=[inside] + [pl.BlockSpec(memory_space=pl.ANY)] * len(others),
+        out_specs=inside,
+        compiler_params=pltpu.CompilerParams(vmem_limit_bytes=8 * 1024 * 1024),
+        name="gate",
+        cost_estimate=pl.CostEstimate(flops=0, bytes_accessed=4 * PACK * D, transcendentals=0),
+    )(value, *others)
+
+
+def prep_kernel(*refs):
+    *given, left_ref, rank_ref, valid_ref = refs
+    near = [given[k] for k in SLOTS]
+    for s in range(2 * NEAR):
+        left_ref[s * ROWS:(s + 1) * ROWS, :] = near[s][0:ROWS, :]
+    extras = [extra_of(ref) for ref in near]
     same = [extra[3:4] == extras[0][3:4] for extra in extras]
     near_rank = jnp.concatenate([jnp.where(same[s], ranks(extras[s]), FAR) for s in range(2 * NEAR)], axis=1)
     rank_ref[...] = jnp.transpose(jnp.broadcast_to(near_rank, (128, LEFT)), (1, 0))
@@ -104,12 +141,8 @@
             jax.ShapeDtypeStruct((LEFT, 128), jnp.float32),
             jax.ShapeDtypeStruct((LEFT // ROWS - 2, 1, ROWS), jnp.float32),
         ),
-        in_specs=[pl.BlockSpec(memory_space=pl.ANY)] * len(near),
+        in_specs=[inside] * len(near),
         out_specs=(inside, inside, inside),
-        scratch_shapes=[
-            pltpu.VMEM((2 * NEAR, EXTRA, D), jnp.bfloat16),
-            pltpu.SemaphoreType.DMA((4 * NEAR,)),
-        ],
         compiler_params=pltpu.CompilerParams(vmem_limit_bytes=8 * 1024 * 1024),
         name="near_prep",
         cost_estimate=pl.CostEstimate(flops=0, bytes_accessed=4 * LEFT * D, transcendentals=0),
@@ -118,15 +151,16 @@
 
 def maxima_kernel(blocks, at, first, last, place_ref, left_ref, rank_ref, valid_ref, *refs):
     panel = refs[:blocks]
-    *refs, right, extra_ref, sems = refs[blocks:]
+    *refs, right = refs[blocks:]
     if first:
         cols_ref, *rows_ref = refs
     else:
         prior_cols_ref, prior_ref, cols_ref, *rows_ref = refs
         cols_ref[...] = prior_cols_ref[...]
     width = blocks * ROWS
-    fetch(panel, right, extra_ref, sems)
-    panel_rank = jnp.concatenate([ranks(extra_of(extra_ref[k])) for k in range(blocks)], axis=1)
+    for k in range(blocks):
+        right[k * ROWS:(k + 1) * ROWS, :] = panel[k][0:ROWS, :]
+    panel_rank = jnp.concatenate([ranks(extra_of(ref)) for ref in panel], axis=1)
     split = 2 * ROWS
     cols = []
     rows = None
@@ -163,13 +197,9 @@
         kept = [
             jnp.where(valid_ref[s] > 0.5, line[:, s * ROWS:(s + 1) * ROWS], -1.0) for s in range(LEFT // ROWS - 2)
         ]
-        even = place_ref[2 * X] == 0
-        rows_ref[0][0] = jnp.where(even, kept[0], kept[3])
-        rows_ref[1][0] = jnp.where(even, kept[1], kept[2])
-        rows_ref[0][1] = jnp.where(even, kept[2], kept[1])
-        rows_ref[1][1] = jnp.where(even, kept[3], kept[0])
-        rows_ref[0][2] = kept[4]
-        rows_ref[1][2] = kept[5]
+        for s in range(NEAR - 1):
+            rows_ref[0][s] = kept[2 * s]
+            rows_ref[1][s] = kept[2 * s + 1]
 
 
 def maxima(place, laid, panel, at, prior, last):
@@ -182,16 +212,9 @@
     return pl.pallas_call(
         lambda *refs: maxima_kernel(blocks, at, not prior, last, *refs),
         out_shape=(jax.ShapeDtypeStruct((2 * X, 1, ROWS), jnp.float32), *rows),
-        in_specs=(
-            [pl.BlockSpec(memory_space=pltpu.SMEM)] + [inside] * len(laid)
-            + [pl.BlockSpec(memory_space=pl.ANY)] * blocks + [inside] * len(prior)
-        ),
+        in_specs=[pl.BlockSpec(memory_space=pltpu.SMEM)] + [inside] * len(operands),
         out_specs=(inside,) * (1 + len(rows)),
-        scratch_shapes=[
-            pltpu.VMEM((blocks * ROWS, D), jnp.bfloat16),
-            pltpu.VMEM((blocks, EXTRA, D), jnp.bfloat16),
-            pltpu.SemaphoreType.DMA((2 * blocks,)),
-        ],
+        scratch_shapes=[pltpu.VMEM((blocks * ROWS, D), jnp.bfloat16)],
         compiler_params=pltpu.CompilerParams(vmem_limit_bytes=16 * 1024 * 1024),
         name="panel_maxima",
         cost_estimate=pl.CostEstimate(
@@ -209,9 +232,21 @@
     return lax.ppermute(value, axis, [(0, 1), (1, 0)])
 
 
-def forward(value):
-    pairs = [(2 * i, 2 * ((i + 1) % X)) for i in range(X)]
-    pairs += [(2 * i + 1, 2 * ((i + X - 1) % X) + 1) for i in range(X)]
+def half_flip(value, count):
+    pairs = []
+    for g in range(count):
+        low, y = divmod(g, count // Z_LO)
+        for h in range(2):
+            for c in range(2):
+                z = (h * Z_LO + low + (2 if c == 0 else 2 * Z_LO - 2)) % (2 * Z_LO)
+                target = z % Z_LO * (count // Z_LO) + y
+                pairs.append(((g * 2 + h) * 2 + c, (target * 2 + z // Z_LO) * 2 + c))
+    return lax.ppermute(value, ("grp", "zh", "core"), pairs)
+
+
+def turn_x(value, even):
+    pairs = [(2 * i, 2 * ((i + even) % X)) for i in range(X)]
+    pairs += [(2 * i + 1, 2 * ((i + X - even) % X) + 1) for i in range(X)]
     return lax.ppermute(value, ("x", "core"), pairs)
 
 
@@ -225,23 +260,23 @@
     count = lax.axis_size("grp")
     grp, zh, x, core = (lax.axis_index(axis) for axis in ("grp", "zh", "x", "core"))
     block = pack(embeddings, labels, order)
+    flipped = half_flip(half_flip(block, count), count)
+    one = shift(block, MOVES[0], count)
+    far = shift(shift(block, -1, count), MOVES[1] + 1, count)
+    two = shift(one, MOVES[2] - MOVES[0], count)
     sib = swap(block, "core")
-    panel = [block, forward(block)]
-    both = pair(core, block, sib)
-    ready, both = lax.optimization_barrier((block, both))
-    first = shift_both(both, MOVES[0], MOVES[1], count)
-    flipped = swap(ready, "zh")
-    two = shift(ready, MOVES[2], count)
-    panel.append(forward(panel[-1]))
-    first, flipped, two, panel[-1] = lax.optimization_barrier((first, flipped, two, panel[-1]))
-    panel.append(forward(panel[-1]))
-    other = [flipped]
-    for _ in range(X - 1):
-        other.append(forward(other[-1]))
-    laid = prep((block, sib, first, swap(first, "core"), two, swap(two, "core")))
+    ahead, behind = turn_x(block, 1), turn_x(block, -1)
+    across = turn_x(ahead, 1)
+    one_sib, far_sib, two_sib = (swap(value, "core") for value in (one, far, two))
+    flipped = gate(flipped, across, one_sib, sib, behind)
+    flip_ahead, flip_behind = turn_x(flipped, 1), turn_x(flipped, -1)
+    flip_across = turn_x(flip_ahead, 1)
+    panel = [block, ahead, behind, across]
+    other = [flipped, flip_ahead, flip_behind, flip_across]
+    laid = prep((block, one, one_sib, far, far_sib, two, two_sib, sib))
     turn = jnp.where(core == 0, 1, X - 1)
-    place = [(zh + h) % 2 * X + (x + (X - k) * turn) % X for h in range(2) for k in range(X)]
-    place = jnp.stack([*place, core]).astype(jnp.int32)
+    place = [(zh + h) % 2 * X + (x + (X - k) * turn) % X for h in range(2) for k in (0, 1, X - 1, 2)]
+    place = jnp.stack(place).astype(jnp.int32)
     cols, rows = maxima(place, laid, panel, 0, (), False)
     cols, rows = maxima(place, laid, other[:3], X, (cols, rows), False)
     cols, rows, rows_sib = maxima(place, laid, other[3:], X + 3, (cols, rows), True)

time: 122 us -> 114 us (0.934)
  the two profiles are of different devices: /device:TPU:114 before, /device:TPU:10 now
where the time goes in v5:
time: 114 us; the launch traced here: 113 us
  starting transfers between devices  71.3 us (63%)
  waiting for transfers between devices  24.7 us (22%)
  Pallas kernels  13.9 us (12%)
  local copies, waits for them, and re-layouts  1.88 us (2%)
    ppermute x7, starting transfers between devices, shift(): return lax.ppermute(value, 'grp', pairs)  22.3 us
    ppermute x6, starting transfers between devices, turn_x(): return lax.ppermute(value, ('x', 'core'), pairs)  19.5 us
    ppermute x7, waiting for transfers between devices, shift(): return lax.ppermute(value, 'grp', pairs)  16.1 us
    ppermute x5, starting transfers between devices, swap(): return lax.ppermute(value, axis, [(0, 1), (1, 0)])  12.3 us
    pallas_call x3, Pallas kernels, maxima(): pl.pallas_call(lambda *refs: maxima_kernel(blocks, at, not prior, last, *...  10.1 us
    ppermute x2, starting transfers between devices, half_flip(): return lax.ppermute(value, ('grp', 'zh', 'core'), pairs)  10 us
    ppermute x2, waiting for transfers between devices, half_flip(): return lax.ppermute(value, ('grp', 'zh', 'core'), pairs)  8.53 us
    all_to_all x1, starting transfers between devices, per_device(): best = jnp.max(lax.all_to_all(cols, ('zh', 'x'), 0, 0, tiled=True), axis=0)  7.22 us
  transfers between devices with their start and end apart: 21, of which 3 were waited for; matrix products, arithmetic and copies ran while one was open for 0% of the time, Pallas kernels for 8%

profile of v5, /device:TPU:10, one launch (start us, length us, event | category | flops | bytes accessed | tf_op | source)
XLA Modules:
  0.0 112.9 jit_solution(6823360641766771655)
XLA Ops:
  0.0 2.0 %normalize_pack.1.refs_0_.refs_4_ = bf16[208,1024]{1,0:T(8,128)(2,1)} custom-call(bf16[192,1024]{1,0:T(8,128)(2,1)} %emb_any.1, s32[1,192]{1,0:T(1,128)} %bitcast.19, s32[1,192]{1,0:T(1,128)} %bitcast.20), custom_call_target="tpu_custom_call" | custom-call | flops 786432 | bytes 786432 | tf_op jit(solution)/shard_map/normalize_pack/pallas_call | solution.py:49
  2.0 3.6 %collective-permute-start = (bf16[208,1024]{1,0:T(8,128)(2,1)}, bf16[208,1024]{1,0:T(8,128)(2,1)S(1)}, u32[]{:S(2)}, u32[]{:S(2)}) collective-permute-start(bf16[208,1024]{1,0:T(8,128)(2,1)} %normalize_pack.1.refs_0_.refs_4_), channel_id=1, source_target_pairs={{0,16},{16,32},{32,48},{48,64},{64,80},{80,96},{96,112},{112,128},... | collective-permute-start | bytes 1277960 | tf_op jit(solution)/shard_map/ppermute | solution.py:228
  5.6 2.4 %collective-permute-start.2 = (bf16[208,1024]{1,0:T(8,128)(2,1)}, bf16[208,1024]{1,0:T(8,128)(2,1)S(1)}, u32[]{:S(2)}, u32[]{:S(2)}) collective-permute-start(bf16[208,1024]{1,0:T(8,128)(2,1)} %normalize_pack.1.refs_0_.refs_4_), channel_id=1, source_target_pairs={{16,0},{32,16},{48,32},{64,48},{80,64},{96,80},{112,96},{128,112},... | collective-permute-start | bytes 1277960 | tf_op jit(solution)/shard_map/ppermute | solution.py:228
  8.0 3.4 %collective-permute-start.10 = (bf16[208,1024]{1,0:T(8,128)(2,1)}, bf16[208,1024]{1,0:T(8,128)(2,1)S(1)}, u32[]{:S(2)}, u32[]{:S(2)}) collective-permute-start(bf16[208,1024]{1,0:T(8,128)(2,1)} %normalize_pack.1.refs_0_.refs_4_), channel_id=1, source_target_pairs={{0,2},{2,4},{4,6},{6,0},{1,7},{3,1},{5,3},{7,5},{8,10},{10,12},{12... | collective-permute-start | bytes 1277960 | tf_op jit(solution)/shard_map/ppermute | solution.py:250
  11.4 6.1 %collective-permute-start.8 = (bf16[208,1024]{1,0:T(8,128)(2,1)}, bf16[208,1024]{1,0:T(8,128)(2,1)S(1)}, u32[]{:S(2)}, u32[]{:S(2)}) collective-permute-start(bf16[208,1024]{1,0:T(8,128)(2,1)} %normalize_pack.1.refs_0_.refs_4_), channel_id=1, source_target_pairs={{0,256},{1,265},{8,264},{9,257},{16,272},{17,281},{24,280},{25,273... | collective-permute-start | bytes 1277960 | tf_op jit(solution)/shard_map/ppermute | solution.py:244
  17.5 4.5 %collective-permute-start.7 = (bf16[208,1024]{1,0:T(8,128)(2,1)}, bf16[208,1024]{1,0:T(8,128)(2,1)S(1)}, u32[]{:S(2)}, u32[]{:S(2)}) collective-permute-start(bf16[208,1024]{1,0:T(8,128)(2,1)} %normalize_pack.1.refs_0_.refs_4_), channel_id=1, source_target_pairs={{0,1},{1,0},{2,3},{3,2},{4,5},{5,4},{6,7},{7,6},{8,9},{9,8},{10,11... | collective-permute-start | bytes 1277960 | tf_op jit(solution)/shard_map/ppermute | solution.py:232
  22.0 0.0 collective-permute-done.refs_1_
  22.0 4.7 %collective-permute-start.12 = (bf16[208,1024]{1,0:T(8,128)(2,1)}, bf16[208,1024]{1,0:T(8,128)(2,1)S(1)}, u32[]{:S(2)}, u32[]{:S(2)}) collective-permute-start(bf16[208,1024]{1,0:T(8,128)(2,1)} %normalize_pack.1.refs_0_.refs_4_), channel_id=1, source_target_pairs={{0,6},{2,0},{4,2},{6,4},{1,3},{3,5},{5,7},{7,1},{8,14},{10,8},{12,... | collective-permute-start | bytes 1277960 | tf_op jit(solution)/shard_map/ppermute | solution.py:250
  26.7 0.0 collective-permute-done.2
  26.7 1.9 %collective-permute-start.1 = (bf16[208,1024]{1,0:T(8,128)(2,1)S(1)}, bf16[208,1024]{1,0:T(8,128)(2,1)S(1)}, u32[]{:S(2)}, u32[]{:S(2)}) collective-permute-start(bf16[208,1024]{1,0:T(8,128)(2,1)S(1)} %collective-permute-done.refs_1_), channel_id=1, source_target_pairs={{0,1},{1,0},{2,3},{3,2},{4,5},{5,4},{6,7},{7,6},{8,9},{9,8},{10,11... | collective-permute-start | bytes 1277960 | tf_op jit(solution)/shard_map/ppermute | solution.py:232
  28.6 0.0 collective-permute-done.10.refs_5_
  28.6 1.9 %collective-permute-start.11 = (bf16[208,1024]{1,0:T(8,128)(2,1)S(1)}, bf16[208,1024]{1,0:T(8,128)(2,1)S(1)}, u32[]{:S(2)}, u32[]{:S(2)}) collective-permute-start(bf16[208,1024]{1,0:T(8,128)(2,1)S(1)} %collective-permute-done.10.refs_5_), channel_id=1, source_target_pairs={{0,2},{2,4},{4,6},{6,0},{1,7},{3,1},{5,3},{7,5},{8,10},{10,12},{12... | collective-permute-start | bytes 1277960 | tf_op jit(solution)/shard_map/ppermute | solution.py:250
  30.6 0.8 copy-done.2
  31.3 0.0 collective-permute-done.8
  31.4 4.0 %collective-permute-start.9 = (bf16[208,1024]{1,0:T(8,128)(2,1)S(1)}, bf16[208,1024]{1,0:T(8,128)(2,1)S(1)}, u32[]{:S(2)}, u32[]{:S(2)}) collective-permute-start(bf16[208,1024]{1,0:T(8,128)(2,1)S(1)} %collective-permute-done.8), channel_id=1, source_target_pairs={{0,256},{1,265},{8,264},{9,257},{16,272},{17,281},{24,280},{25,273... | collective-permute-start | bytes 1277960 | tf_op jit(solution)/shard_map/ppermute | solution.py:244
  35.3 0.0 collective-permute-done.7.refs_7_.refs_3_
  35.3 3.5 %collective-permute-start.5 = (bf16[208,1024]{1,0:T(8,128)(2,1)S(1)}, bf16[208,1024]{1,0:T(8,128)(2,1)S(1)}, u32[]{:S(2)}, u32[]{:S(2)}) collective-permute-start(bf16[208,1024]{1,0:T(8,128)(2,1)S(1)} %collective-permute-done.refs_1_), channel_id=1, source_target_pairs={{0,16},{16,32},{32,48},{48,64},{64,80},{80,96},{96,112},{112,128},... | collective-permute-start | bytes 1277960 | tf_op jit(solution)/shard_map/ppermute | solution.py:228
  38.8 0.0 collective-permute-done.12.refs_4_.refs_6_
  38.8 1.3 %collective-permute-start.3 = (bf16[208,1024]{1,0:T(8,128)(2,1)S(1)}, bf16[208,1024]{1,0:T(8,128)(2,1)}, u32[]{:S(2)}, u32[]{:S(2)}) collective-permute-start(bf16[208,1024]{1,0:T(8,128)(2,1)S(1)} %collective-permute-done.2), channel_id=1, source_target_pairs={{32,0},{48,16},{64,32},{80,48},{96,64},{112,80},{128,96},{144,112}... | collective-permute-start | bytes 1277960 | tf_op jit(solution)/shard_map/ppermute | solution.py:228
  40.1 0.0 collective-permute-done.1.refs_2_
  40.1 0.0 collective-permute-done.11.refs_1_.refs_7_
  40.1 8.5 %collective-permute-done.9.refs_0_ = bf16[208,1024]{1,0:T(8,128)(2,1)S(1)} collective-permute-done((bf16[208,1024]{1,0:T(8,128)(2,1)S(1)}, bf16[208,1024]{1,0:T(8,128)(2,1)S(1)}, u32[]{:S(2)}, u32[]{:S(2)}) %collective-permute-start.9) | collective-permute-done | bytes 426016 | tf_op jit(solution)/shard_map/ppermute | solution.py:244
  48.7 3.7 %collective-permute-start.13 = (bf16[208,1024]{1,0:T(8,128)(2,1)S(1)}, bf16[208,1024]{1,0:T(8,128)(2,1)}, u32[]{:S(2)}, u32[]{:S(2)}) collective-permute-start(bf16[208,1024]{1,0:T(8,128)(2,1)S(1)} %gate.1.refs_4_), channel_id=1, source_target_pairs={{0,2},{2,4},{4,6},{6,0},{1,7},{3,1},{5,3},{7,5},{8,10},{10,12},{12... | collective-permute-start | bytes 1277960 | tf_op jit(solution)/shard_map/ppermute | solution.py:250
  52.4 1.9 %collective-permute-start.6 = (bf16[208,1024]{1,0:T(8,128)(2,1)S(1)}, bf16[208,1024]{1,0:T(8,128)(2,1)}, u32[]{:S(2)}, u32[]{:S(2)}) collective-permute-start(bf16[208,1024]{1,0:T(8,128)(2,1)S(1)} %collective-permute-done.5.refs_5_), channel_id=1, source_target_pairs={{0,1},{1,0},{2,3},{3,2},{4,5},{5,4},{6,7},{7,6},{8,9},{9,8},{10,11... | collective-permute-start | bytes 1277960 | tf_op jit(solution)/shard_map/ppermute | solution.py:232
  54.3 11.1 %collective-permute-done.3.refs_3_ = bf16[208,1024]{1,0:T(8,128)(2,1)} collective-permute-done((bf16[208,1024]{1,0:T(8,128)(2,1)S(1)}, bf16[208,1024]{1,0:T(8,128)(2,1)}, u32[]{:S(2)}, u32[]{:S(2)}) %collective-permute-start.3) | collective-permute-done | bytes 426016 | tf_op jit(solution)/shard_map/ppermute | solution.py:228
  65.5 2.0 %collective-permute-start.4 = (bf16[208,1024]{1,0:T(8,128)(2,1)}, bf16[208,1024]{1,0:T(8,128)(2,1)}, u32[]{:S(2)}, u32[]{:S(2)}) collective-permute-start(bf16[208,1024]{1,0:T(8,128)(2,1)} %collective-permute-done.3.refs_3_), channel_id=1, source_target_pairs={{0,1},{1,0},{2,3},{3,2},{4,5},{5,4},{6,7},{7,6},{8,9},{9,8},{10,11... | collective-permute-start | bytes 1277960 | tf_op jit(solution)/shard_map/ppermute | solution.py:232
  67.5 3.2 %collective-permute-start.15 = (bf16[208,1024]{1,0:T(8,128)(2,1)S(1)}, bf16[208,1024]{1,0:T(8,128)(2,1)}, u32[]{:S(2)}, u32[]{:S(2)}) collective-permute-start(bf16[208,1024]{1,0:T(8,128)(2,1)S(1)} %gate.1.refs_4_), channel_id=1, source_target_pairs={{0,6},{2,0},{4,2},{6,4},{1,3},{3,5},{5,7},{7,1},{8,14},{10,8},{12,... | collective-permute-start | bytes 1277960 | tf_op jit(solution)/shard_map/ppermute | solution.py:250
  70.7 0.0 collective-permute-done.13.refs_5_
  70.7 2.6 %collective-permute-start.14 = (bf16[208,1024]{1,0:T(8,128)(2,1)}, bf16[208,1024]{1,0:T(8,128)(2,1)}, u32[]{:S(2)}, u32[]{:S(2)}) collective-permute-start(bf16[208,1024]{1,0:T(8,128)(2,1)} %collective-permute-done.13.refs_5_), channel_id=1, source_target_pairs={{0,2},{2,4},{4,6},{6,0},{1,7},{3,1},{5,3},{7,5},{8,10},{10,12},{12... | collective-permute-start | bytes 1277960 | tf_op jit(solution)/shard_map/ppermute | solution.py:250
  73.4 0.1 stack.35.refs_0_
  73.5 0.0 collective-permute-done.6.refs_6_
  73.5 0.0 collective-permute-done.4.refs_4_
  73.5 1.0 copy-done
  74.5 1.8 %near_prep.1 = (bf16[1536,1024]{1,0:T(8,128)(2,1)S(1)}, f32[1536,128]{1,0:T(8,128)S(1)}, f32[6,1,192]{2,1,0:T(1,128)S(1)}) custom-call(bf16[208,1024]{1,0:T(8,128)(2,1)S(1)} %copy-done, bf16[208,1024]{1,0:T(8,128)(2,1)S(1)} %collective-permute-done.refs_1_, bf16[208,1024]{1,0:T(8,128)(2,1)S(1)} %collective-permute-done.1.refs_2_, ...), custom_call_target="tpu_custom_call" | custom-call | bytes 6291456 | tf_op jit(solution)/shard_map/near_prep/pallas_call | solution.py:137
  76.4 3.5 %panel_maxima.3 = (f32[8,1,192]{2,1,0:T(1,128)S(1)}, f32[1152,128]{1,0:T(8,128)S(1)}) custom-call(s32[8]{0:T(128)S(1)} %stack.35.refs_0_, bf16[1536,1024]{1,0:T(8,128)(2,1)S(1)} %get-tuple-element.15.refs_1_, f32[1536,128]{1,0:T(8,128)S(1)} %get-tuple-element.16.refs_2_, f32[6,1,192]{2,1,0:T(1,128)S(1)} %get-tuple-element.17.refs_3_, ...), custom_call_target="tpu_custom_call" | custom-call | flops 2415919104 | bytes 5111808 | tf_op jit(solution)/shard_map/panel_maxima/pallas_call | solution.py:212
  79.8 4.0 %panel_maxima.4 = (f32[8,1,192]{2,1,0:T(1,128)S(1)}, f32[1152,128]{1,0:T(8,128)S(1)}) custom-call(s32[8]{0:T(128)S(1)} %stack.35.refs_0_, bf16[1536,1024]{1,0:T(8,128)(2,1)S(1)} %get-tuple-element.15.refs_1_, f32[1536,128]{1,0:T(8,128)S(1)} %get-tuple-element.16.refs_2_, f32[6,1,192]{2,1,0:T(1,128)S(1)} %get-tuple-element.17.refs_3_, ...), custom_call_target="tpu_custom_call" | custom-call | flops 1811939328 | bytes 4685824 | tf_op jit(solution)/shard_map/panel_maxima/pallas_call | solution.py:212
  83.9 0.0 collective-permute-done.14.refs_4_
  83.9 2.7 %panel_maxima.5 = (f32[8,1,192]{2,1,0:T(1,128)}, f32[3,1,192]{2,1,0:T(1,128)S(1)}, f32[3,1,192]{2,1,0:T(1,128)S(1)}) custom-call(s32[8]{0:T(128)S(1)} %stack.35.refs_0_, bf16[1536,1024]{1,0:T(8,128)(2,1)S(1)} %get-tuple-element.15.refs_1_, f32[1536,128]{1,0:T(8,128)S(1)} %get-tuple-element.16.refs_2_, f32[6,1,192]{2,1,0:T(1,128)S(1)} %get-tuple-element.17.refs_3_, ...), custom_call_target="tpu_custom_call" | custom-call | flops 603979776 | bytes 3833856 | tf_op jit(solution)/shard_map/panel_maxima/pallas_call | solution.py:212
  86.5 1.9 %collective-permute-start.16 = (f32[3,1,192]{2,1,0:T(1,128)S(1)}, f32[3,1,192]{2,1,0:T(1,128)S(1)}, u32[]{:S(2)}, u32[]{:S(2)}) collective-permute-start(f32[3,1,192]{2,1,0:T(1,128)S(1)} %get-tuple-element.24), channel_id=1, source_target_pairs={{0,1},{1,0},{2,3},{3,2},{4,5},{5,4},{6,7},{7,6},{8,9},{9,8},{10,11... | collective-permute-start | bytes 6920 | tf_op jit(solution)/shard_map/ppermute | solution.py:232
  88.4 7.2 %all-to-all-start = ((f32[8,1,192]{2,1,0:T(1,128)}), f32[8,1,192]{2,1,0:T(1,128)S(1)}, u32[]{:S(2)}, u32[]{:S(2)}) async-start(f32[8,1,192]{2,1,0:T(1,128)} %get-tuple-element.22), calls=%async_computation | async-start | bytes 16384 | tf_op jit(solution)/shard_map/all_to_all | solution.py:283
  95.7 0.0 collective-permute-done.16
  95.7 4.4 %collective-permute-start.17 = (f32[1,192]{1,0:T(1,128)S(1)}, f32[1,192]{1,0:T(1,128)S(1)}, u32[]{:S(2)}, u32[]{:S(2)}) collective-permute-start(f32[1,192]{1,0:T(1,128)S(1)} %get-tuple-element.27), channel_id=1, source_target_pairs={{16,0},{32,16},{48,32},{64,48},{80,64},{96,80},{112,96},{128,112},... | collective-permute-start | bytes 2312 | tf_op jit(solution)/shard_map/ppermute | solution.py:228
  100.1 5.8 %collective-permute-start.18 = (f32[1,192]{1,0:T(1,128)S(1)}, f32[1,192]{1,0:T(1,128)S(1)}, u32[]{:S(2)}, u32[]{:S(2)}) collective-permute-start(f32[1,192]{1,0:T(1,128)S(1)} %get-tuple-element.26), channel_id=1, source_target_pairs={{0,48},{16,64},{32,80},{48,96},{64,112},{80,128},{96,144},{112,160... | collective-permute-start | bytes 2312 | tf_op jit(solution)/shard_map/ppermute | solution.py:228
  105.9 1.3 %collective-permute-start.19 = (f32[1,192]{1,0:T(1,128)S(1)}, f32[1,192]{1,0:T(1,128)S(1)}, u32[]{:S(2)}, u32[]{:S(2)}) collective-permute-start(f32[1,192]{1,0:T(1,128)S(1)} %get-tuple-element.25), channel_id=1, source_target_pairs={{32,0},{48,16},{64,32},{80,48},{96,64},{112,80},{128,96},{144,112}... | collective-permute-start | bytes 2312 | tf_op jit(solution)/shard_map/ppermute | solution.py:228
  107.3 0.0 all-to-all-done
  107.3 0.0 collective-permute-done.18
  107.3 5.0 %collective-permute-done.19 = f32[1,192]{1,0:T(1,128)S(1)} collective-permute-done((f32[1,192]{1,0:T(1,128)S(1)}, f32[1,192]{1,0:T(1,128)S(1)}, u32[]{:S(2)}, u32[]{:S(2)}) %collective-permute-start.19) | collective-permute-done | bytes 800 | tf_op jit(solution)/shard_map/ppermute | solution.py:228
  112.3 0.6 fusion.2
  (13 shorter events, 0.1 us)
Async XLA Ops:
  2.0 74.4 %copy-start.1 = (bf16[208,1024]{1,0:T(8,128)(2,1)S(1)}, bf16[208,1024]{1,0:T(8,128)(2,1)}, u32[]{:S(2)}) copy-start(bf16[208,1024]{1,0:T(8,128)(2,1)} %normalize_pack.1.refs_0_.refs_4_) | copy-start | bytes 1277956
  2.0 20.0 %collective-permute-start = (bf16[208,1024]{1,0:T(8,128)(2,1)}, bf16[208,1024]{1,0:T(8,128)(2,1)S(1)}, u32[]{:S(2)}, u32[]{:S(2)}) collective-permute-start(bf16[208,1024]{1,0:T(8,128)(2,1)} %normalize_pack.1.refs_0_.refs_4_), channel_id=1, source_target_pairs={{0,16},{16,32},{32,48},{48,64},{64,80},{80,96},{96,112},{112,128},... | collective-permute-start | bytes 1277960 | tf_op jit(solution)/shard_map/ppermute | solution.py:228
  5.6 21.1 %collective-permute-start.2 = (bf16[208,1024]{1,0:T(8,128)(2,1)}, bf16[208,1024]{1,0:T(8,128)(2,1)S(1)}, u32[]{:S(2)}, u32[]{:S(2)}) collective-permute-start(bf16[208,1024]{1,0:T(8,128)(2,1)} %normalize_pack.1.refs_0_.refs_4_), channel_id=1, source_target_pairs={{16,0},{32,16},{48,32},{64,48},{80,64},{96,80},{112,96},{128,112},... | collective-permute-start | bytes 1277960 | tf_op jit(solution)/shard_map/ppermute | solution.py:228
  8.0 20.6 %collective-permute-start.10 = (bf16[208,1024]{1,0:T(8,128)(2,1)}, bf16[208,1024]{1,0:T(8,128)(2,1)S(1)}, u32[]{:S(2)}, u32[]{:S(2)}) collective-permute-start(bf16[208,1024]{1,0:T(8,128)(2,1)} %normalize_pack.1.refs_0_.refs_4_), channel_id=1, source_target_pairs={{0,2},{2,4},{4,6},{6,0},{1,7},{3,1},{5,3},{7,5},{8,10},{10,12},{12... | collective-permute-start | bytes 1277960 | tf_op jit(solution)/shard_map/ppermute | solution.py:250
  11.4 20.0 %collective-permute-start.8 = (bf16[208,1024]{1,0:T(8,128)(2,1)}, bf16[208,1024]{1,0:T(8,128)(2,1)S(1)}, u32[]{:S(2)}, u32[]{:S(2)}) collective-permute-start(bf16[208,1024]{1,0:T(8,128)(2,1)} %normalize_pack.1.refs_0_.refs_4_), channel_id=1, source_target_pairs={{0,256},{1,265},{8,264},{9,257},{16,272},{17,281},{24,280},{25,273... | collective-permute-start | bytes 1277960 | tf_op jit(solution)/shard_map/ppermute | solution.py:244
  17.5 17.9 %collective-permute-start.7 = (bf16[208,1024]{1,0:T(8,128)(2,1)}, bf16[208,1024]{1,0:T(8,128)(2,1)S(1)}, u32[]{:S(2)}, u32[]{:S(2)}) collective-permute-start(bf16[208,1024]{1,0:T(8,128)(2,1)} %normalize_pack.1.refs_0_.refs_4_), channel_id=1, source_target_pairs={{0,1},{1,0},{2,3},{3,2},{4,5},{5,4},{6,7},{7,6},{8,9},{9,8},{10,11... | collective-permute-start | bytes 1277960 | tf_op jit(solution)/shard_map/ppermute | solution.py:232
  22.0 16.8 %collective-permute-start.12 = (bf16[208,1024]{1,0:T(8,128)(2,1)}, bf16[208,1024]{1,0:T(8,128)(2,1)S(1)}, u32[]{:S(2)}, u32[]{:S(2)}) collective-permute-start(bf16[208,1024]{1,0:T(8,128)(2,1)} %normalize_pack.1.refs_0_.refs_4_), channel_id=1, source_target_pairs={{0,6},{2,0},{4,2},{6,4},{1,3},{3,5},{5,7},{7,1},{8,14},{10,8},{12,... | collective-permute-start | bytes 1277960 | tf_op jit(solution)/shard_map/ppermute | solution.py:250
  26.7 13.4 %collective-permute-start.1 = (bf16[208,1024]{1,0:T(8,128)(2,1)S(1)}, bf16[208,1024]{1,0:T(8,128)(2,1)S(1)}, u32[]{:S(2)}, u32[]{:S(2)}) collective-permute-start(bf16[208,1024]{1,0:T(8,128)(2,1)S(1)} %collective-permute-done.refs_1_), channel_id=1, source_target_pairs={{0,1},{1,0},{2,3},{3,2},{4,5},{5,4},{6,7},{7,6},{8,9},{9,8},{10,11... | collective-permute-start | bytes 1277960 | tf_op jit(solution)/shard_map/ppermute | solution.py:232
  28.6 11.5 %collective-permute-start.11 = (bf16[208,1024]{1,0:T(8,128)(2,1)S(1)}, bf16[208,1024]{1,0:T(8,128)(2,1)S(1)}, u32[]{:S(2)}, u32[]{:S(2)}) collective-permute-start(bf16[208,1024]{1,0:T(8,128)(2,1)S(1)} %collective-permute-done.10.refs_5_), channel_id=1, source_target_pairs={{0,2},{2,4},{4,6},{6,0},{1,7},{3,1},{5,3},{7,5},{8,10},{10,12},{12... | collective-permute-start | bytes 1277960 | tf_op jit(solution)/shard_map/ppermute | solution.py:250
  30.6 0.8 copy-start.2
  31.4 17.3 %collective-permute-start.9 = (bf16[208,1024]{1,0:T(8,128)(2,1)S(1)}, bf16[208,1024]{1,0:T(8,128)(2,1)S(1)}, u32[]{:S(2)}, u32[]{:S(2)}) collective-permute-start(bf16[208,1024]{1,0:T(8,128)(2,1)S(1)} %collective-permute-done.8), channel_id=1, source_target_pairs={{0,256},{1,265},{8,264},{9,257},{16,272},{17,281},{24,280},{25,273... | collective-permute-start | bytes 1277960 | tf_op jit(solution)/shard_map/ppermute | solution.py:244
  35.3 17.0 %collective-permute-start.5 = (bf16[208,1024]{1,0:T(8,128)(2,1)S(1)}, bf16[208,1024]{1,0:T(8,128)(2,1)S(1)}, u32[]{:S(2)}, u32[]{:S(2)}) collective-permute-start(bf16[208,1024]{1,0:T(8,128)(2,1)S(1)} %collective-permute-done.refs_1_), channel_id=1, source_target_pairs={{0,16},{16,32},{32,48},{48,64},{64,80},{80,96},{96,112},{112,128},... | collective-permute-start | bytes 1277960 | tf_op jit(solution)/shard_map/ppermute | solution.py:228
  38.8 26.6 %collective-permute-start.3 = (bf16[208,1024]{1,0:T(8,128)(2,1)S(1)}, bf16[208,1024]{1,0:T(8,128)(2,1)}, u32[]{:S(2)}, u32[]{:S(2)}) collective-permute-start(bf16[208,1024]{1,0:T(8,128)(2,1)S(1)} %collective-permute-done.2), channel_id=1, source_target_pairs={{32,0},{48,16},{64,32},{80,48},{96,64},{112,80},{128,96},{144,112}... | collective-permute-start | bytes 1277960 | tf_op jit(solution)/shard_map/ppermute | solution.py:228
  48.7 22.0 %collective-permute-start.13 = (bf16[208,1024]{1,0:T(8,128)(2,1)S(1)}, bf16[208,1024]{1,0:T(8,128)(2,1)}, u32[]{:S(2)}, u32[]{:S(2)}) collective-permute-start(bf16[208,1024]{1,0:T(8,128)(2,1)S(1)} %gate.1.refs_4_), channel_id=1, source_target_pairs={{0,2},{2,4},{4,6},{6,0},{1,7},{3,1},{5,3},{7,5},{8,10},{10,12},{12... | collective-permute-start | bytes 1277960 | tf_op jit(solution)/shard_map/ppermute | solution.py:250
  52.4 21.1 %collective-permute-start.6 = (bf16[208,1024]{1,0:T(8,128)(2,1)S(1)}, bf16[208,1024]{1,0:T(8,128)(2,1)}, u32[]{:S(2)}, u32[]{:S(2)}) collective-permute-start(bf16[208,1024]{1,0:T(8,128)(2,1)S(1)} %collective-permute-done.5.refs_5_), channel_id=1, source_target_pairs={{0,1},{1,0},{2,3},{3,2},{4,5},{5,4},{6,7},{7,6},{8,9},{9,8},{10,11... | collective-permute-start | bytes 1277960 | tf_op jit(solution)/shard_map/ppermute | solution.py:232
  65.5 8.0 %collective-permute-start.4 = (bf16[208,1024]{1,0:T(8,128)(2,1)}, bf16[208,1024]{1,0:T(8,128)(2,1)}, u32[]{:S(2)}, u32[]{:S(2)}) collective-permute-start(bf16[208,1024]{1,0:T(8,128)(2,1)} %collective-permute-done.3.refs_3_), channel_id=1, source_target_pairs={{0,1},{1,0},{2,3},{3,2},{4,5},{5,4},{6,7},{7,6},{8,9},{9,8},{10,11... | collective-permute-start | bytes 1277960 | tf_op jit(solution)/shard_map/ppermute | solution.py:232
  67.5 12.4 %collective-permute-start.15 = (bf16[208,1024]{1,0:T(8,128)(2,1)S(1)}, bf16[208,1024]{1,0:T(8,128)(2,1)}, u32[]{:S(2)}, u32[]{:S(2)}) collective-permute-start(bf16[208,1024]{1,0:T(8,128)(2,1)S(1)} %gate.1.refs_4_), channel_id=1, source_target_pairs={{0,6},{2,0},{4,2},{6,4},{1,3},{3,5},{5,7},{7,1},{8,14},{10,8},{12,... | collective-permute-start | bytes 1277960 | tf_op jit(solution)/shard_map/ppermute | solution.py:250
  70.7 13.1 %collective-permute-start.14 = (bf16[208,1024]{1,0:T(8,128)(2,1)}, bf16[208,1024]{1,0:T(8,128)(2,1)}, u32[]{:S(2)}, u32[]{:S(2)}) collective-permute-start(bf16[208,1024]{1,0:T(8,128)(2,1)} %collective-permute-done.13.refs_5_), channel_id=1, source_target_pairs={{0,2},{2,4},{4,6},{6,0},{1,7},{3,1},{5,3},{7,5},{8,10},{10,12},{12... | collective-permute-start | bytes 1277960 | tf_op jit(solution)/shard_map/ppermute | solution.py:250
  73.5 1.0 copy-start
  74.5 1.8 %copy-start.3 = (bf16[208,1024]{1,0:T(8,128)(2,1)S(1)}, bf16[208,1024]{1,0:T(8,128)(2,1)}, u32[]{:S(2)}) copy-start(bf16[208,1024]{1,0:T(8,128)(2,1)} %copy-done.2) | copy-start | bytes 1277956
  86.5 9.1 %collective-permute-start.16 = (f32[3,1,192]{2,1,0:T(1,128)S(1)}, f32[3,1,192]{2,1,0:T(1,128)S(1)}, u32[]{:S(2)}, u32[]{:S(2)}) collective-permute-start(f32[3,1,192]{2,1,0:T(1,128)S(1)} %get-tuple-element.24), channel_id=1, source_target_pairs={{0,1},{1,0},{2,3},{3,2},{4,5},{5,4},{6,7},{7,6},{8,9},{9,8},{10,11... | collective-permute-start | bytes 6920 | tf_op jit(solution)/shard_map/ppermute | solution.py:232
  88.4 18.8 %all-to-all-start = ((f32[8,1,192]{2,1,0:T(1,128)}), f32[8,1,192]{2,1,0:T(1,128)S(1)}, u32[]{:S(2)}, u32[]{:S(2)}) async-start(f32[8,1,192]{2,1,0:T(1,128)} %get-tuple-element.22), calls=%async_computation | async-start | bytes 16384 | tf_op jit(solution)/shard_map/all_to_all | solution.py:283
  95.7 11.6 %collective-permute-start.17 = (f32[1,192]{1,0:T(1,128)S(1)}, f32[1,192]{1,0:T(1,128)S(1)}, u32[]{:S(2)}, u32[]{:S(2)}) collective-permute-start(f32[1,192]{1,0:T(1,128)S(1)} %get-tuple-element.27), channel_id=1, source_target_pairs={{16,0},{32,16},{48,32},{64,48},{80,64},{96,80},{112,96},{128,112},... | collective-permute-start | bytes 2312 | tf_op jit(solution)/shard_map/ppermute | solution.py:228
  100.1 7.2 %collective-permute-start.18 = (f32[1,192]{1,0:T(1,128)S(1)}, f32[1,192]{1,0:T(1,128)S(1)}, u32[]{:S(2)}, u32[]{:S(2)}) collective-permute-start(f32[1,192]{1,0:T(1,128)S(1)} %get-tuple-element.26), channel_id=1, source_target_pairs={{0,48},{16,64},{32,80},{48,96},{64,112},{80,128},{96,144},{112,160... | collective-permute-start | bytes 2312 | tf_op jit(solution)/shard_map/ppermute | solution.py:228
  105.9 6.4 %collective-permute-start.19 = (f32[1,192]{1,0:T(1,128)S(1)}, f32[1,192]{1,0:T(1,128)S(1)}, u32[]{:S(2)}, u32[]{:S(2)}) collective-permute-start(f32[1,192]{1,0:T(1,128)S(1)} %get-tuple-element.25), channel_id=1, source_target_pairs={{32,0},{48,16},{64,32},{80,48},{96,64},{112,80},{128,96},{144,112}... | collective-permute-start | bytes 2312 | tf_op jit(solution)/shard_map/ppermute | solution.py:228

commit v6 on v5

v6 whole, which is shorter than its diff:
```python
import jax
import jax.numpy as jnp
from jax import lax
from jax.experimental import pallas as pl
from jax.experimental.pallas import tpu as pltpu
from jax.sharding import Mesh, PartitionSpec as P

ROWS = 192
EXTRA = 16
PACK = ROWS + EXTRA
D = 1024
X = 4
Z_LO = 4
MOVES = (1, -2, 3)
NEAR = 1 + len(MOVES)
LEFT = 2 * NEAR * ROWS
TILE = 256
FAR = 1.0e9


def pack_kernel(emb_any, lab_any, ord_any, out_ref, emb_ref, lab_ref, ord_ref, sems):
    copies = [
        pltpu.make_async_copy(source, target, sems.at[k])
        for k, (source, target) in enumerate(((emb_any, emb_ref), (lab_any, lab_ref), (ord_any, ord_ref)))
    ]
    for copy in copies:
        copy.start()
    for copy in copies:
        copy.wait()
    values = emb_ref[...].astype(jnp.float32)
    scale = lax.rsqrt(jnp.sum(values * values, axis=1, keepdims=True) + 1e-06)
    out_ref[0:ROWS, :] = (values * scale).astype(jnp.bfloat16)
    rank = jnp.broadcast_to(ord_ref[...], (EXTRA, ROWS))
    label = jnp.broadcast_to(lab_ref[...], (EXTRA, ROWS))
    line = lax.broadcasted_iota(jnp.int32, (EXTRA, ROWS), 0)
    digits = jnp.where(
        line == 0,
        rank >> 12,
        jnp.where(line == 1, (rank >> 6) & 63, jnp.where(line == 2, rank & 63, label + 1)),
    )
    digits = jnp.where(line < 4, digits, 0).astype(jnp.float32)
    digits = jnp.concatenate([digits, jnp.zeros((EXTRA, D - ROWS), jnp.float32)], axis=1)
    out_ref[ROWS:PACK, :] = digits.astype(jnp.bfloat16)


def pack(embeddings, labels, order):
    anywhere = pl.BlockSpec(memory_space=pl.ANY)
    return pl.pallas_call(
        pack_kernel,
        out_shape=jax.ShapeDtypeStruct((PACK, D), jnp.bfloat16),
        in_specs=[anywhere] * 3,
        out_specs=pl.BlockSpec(memory_space=pltpu.VMEM),
        scratch_shapes=[
            pltpu.VMEM((ROWS, D), jnp.bfloat16),
            pltpu.VMEM((1, ROWS), jnp.int32),
            pltpu.VMEM((1, ROWS), jnp.int32),
            pltpu.SemaphoreType.DMA((3,)),
        ],
        name="normalize_pack",
        cost_estimate=pl.CostEstimate(flops=4 * ROWS * D, bytes_accessed=4 * ROWS * D, transcendentals=ROWS),
    )(embeddings, labels.reshape(1, ROWS), order.reshape(1, ROWS))


def ranks(extra):
    return extra[0:1] * 4096.0 + extra[1:2] * 64.0 + extra[2:3]


def stack_kernel(*refs):
    out_ref = refs[-1]
    for k in range(out_ref.shape[0]):
        out_ref[k] = refs[k][...]


def stack(blocks, after=()):
    inside = pl.BlockSpec(memory_space=pltpu.VMEM)
    n = len(blocks)
    return pl.pallas_call(
        stack_kernel,
        out_shape=jax.ShapeDtypeStruct((n, PACK, D), jnp.bfloat16),
        in_specs=[inside] * (n + len(after)),
        out_specs=inside,
        compiler_params=pltpu.CompilerParams(vmem_limit_bytes=8 * 1024 * 1024),
        name="stack_blocks",
        cost_estimate=pl.CostEstimate(flops=0, bytes_accessed=4 * n * PACK * D, transcendentals=0),
    )(*blocks, *after)


def extra_of(ref):
    return ref[ROWS:PACK, 0:256].astype(jnp.float32)[:, :ROWS]


def gate_kernel(*refs):
    refs[-1][...] = refs[0][...]


def gate(value, *others):
    inside = pl.BlockSpec(memory_space=pltpu.VMEM)
    return pl.pallas_call(
        gate_kernel,
        out_shape=jax.ShapeDtypeStruct(value.shape, value.dtype),
        in_specs=[inside] * (1 + len(others)),
        out_specs=inside,
        compiler_params=pltpu.CompilerParams(vmem_limit_bytes=8 * 1024 * 1024),
        name="gate",
        cost_estimate=pl.CostEstimate(flops=0, bytes_accessed=4 * PACK * D, transcendentals=0),
    )(value, *others)


def lay_out(near, left_ref, rank_ref, valid_ref):
    for s in range(2 * NEAR):
        left_ref[s * ROWS:(s + 1) * ROWS, :] = near[s][0:ROWS, :]
    extras = [extra_of(ref) for ref in near]
    same = [extra[3:4] == extras[0][3:4] for extra in extras]
    near_rank = jnp.concatenate([jnp.where(same[s], ranks(extras[s]), FAR) for s in range(2 * NEAR)], axis=1)
    rank_ref[...] = jnp.transpose(jnp.broadcast_to(near_rank, (128, LEFT)), (1, 0))
    for s in range(2, 2 * NEAR):
        valid_ref[s - 2] = same[s].astype(jnp.float32)


def panel_maxima(panel, right, left_ref, rank_ref):
    blocks = len(panel)
    width = blocks * ROWS
    for k in range(blocks):
        right[k * ROWS:(k + 1) * ROWS, :] = panel[k][0:ROWS, :]
    panel_rank = jnp.concatenate([ranks(extra_of(ref)) for ref in panel], axis=1)
    split = 2 * ROWS
    cols = []
    rows = None
    for start in range(0, width, TILE):
        tile = min(TILE, width - start)
        sims = lax.dot_general(
            left_ref[...], right[start:start + tile, :], (((1,), (1,)), ((), ())),
            preferred_element_type=jnp.float32,
        )
        for lane in range(0, tile, 128):
            part = sims[:, lane:lane + 128]
            rank_row = panel_rank[:, start + lane:start + lane + 128]
            here = part[:split]
            best = jnp.max(jnp.where(rank_ref[:split] < rank_row, here, -1.0), axis=0, keepdims=True)
            there = part[split:]
            earlier = rank_row < rank_ref[split:]
            best = jnp.maximum(best, jnp.max(jnp.where(earlier, -1.0, there), axis=0, keepdims=True))
            cols.append(best)
            found = jnp.where(earlier, there, -1.0)
            rows = found if rows is None else jnp.maximum(rows, found)
    return jnp.concatenate(cols, axis=1), rows


def first_kernel(place_ref, mine_a_ref, mine_b_ref, theirs_a_ref, theirs_b_ref, *refs):
    pairs = ((mine_a_ref, theirs_a_ref), (mine_b_ref, theirs_b_ref))
    near = [ref.at[k] for pair in pairs for k in range(2) for ref in pair]
    *panel, cols_ref, rows_ref, left_ref, rank_ref, valid_ref, right = refs
    lay_out(near, left_ref, rank_ref, valid_ref)
    best, rows = panel_maxima(panel, right, left_ref, rank_ref)
    cols_ref[...] = jnp.full(cols_ref.shape, -1.0, jnp.float32)
    for k in range(len(panel)):
        cols_ref[place_ref[k]] = best[:, k * ROWS:(k + 1) * ROWS]
    rows_ref[...] = rows


def last_kernel(place_ref, cols_in_ref, rows_in_ref, left_ref, rank_ref, valid_ref, pair_ref, cols_ref, mine_ref, theirs_ref, right):
    panel = [pair_ref.at[k] for k in range(2)]
    best, rows = panel_maxima(panel, right, left_ref, rank_ref)
    cols_ref[...] = cols_in_ref[...]
    for k in range(2):
        cols_ref[place_ref[2 * X - 2 + k]] = best[:, k * ROWS:(k + 1) * ROWS]
    rows = jnp.maximum(rows, rows_in_ref[...])
    line = jnp.max(jnp.transpose(rows, (1, 0)), axis=0, keepdims=True)
    for s in range(NEAR - 1):
        for k, ref in enumerate((mine_ref, theirs_ref)):
            at = 2 * s + k
            ref[s] = jnp.where(valid_ref[at] > 0.5, line[:, at * ROWS:(at + 1) * ROWS], -1.0)


def cost(blocks):
    return pl.CostEstimate(
        flops=2 * LEFT * blocks * ROWS * D, bytes_accessed=2 * (2 * NEAR + blocks) * PACK * D, transcendentals=0
    )


def first_maxima(place, near, panel):
    inside = pl.BlockSpec(memory_space=pltpu.VMEM)
    blocks = len(panel)
    return pl.pallas_call(
        first_kernel,
        out_shape=(
            jax.ShapeDtypeStruct((2 * X, 1, ROWS), jnp.float32),
            jax.ShapeDtypeStruct((LEFT - 2 * ROWS, 128), jnp.float32),
            jax.ShapeDtypeStruct((LEFT, D), jnp.bfloat16),
            jax.ShapeDtypeStruct((LEFT, 128), jnp.float32),
            jax.ShapeDtypeStruct((2 * (NEAR - 1), 1, ROWS), jnp.float32),
        ),
        in_specs=[pl.BlockSpec(memory_space=pltpu.SMEM)] + [inside] * (4 + blocks),
        out_specs=(inside,) * 5,
        scratch_shapes=[pltpu.VMEM((blocks * ROWS, D), jnp.bfloat16)],
        compiler_params=pltpu.CompilerParams(vmem_limit_bytes=20 * 1024 * 1024),
        name="first_maxima",
        cost_estimate=cost(blocks),
    )(place, *near, *panel)


def last_maxima(place, carried, pair):
    inside = pl.BlockSpec(memory_space=pltpu.VMEM)
    lines = jax.ShapeDtypeStruct((NEAR - 1, 1, ROWS), jnp.float32)
    return pl.pallas_call(
        last_kernel,
        out_shape=(jax.ShapeDtypeStruct((2 * X, 1, ROWS), jnp.float32), lines, lines),
        in_specs=[pl.BlockSpec(memory_space=pltpu.SMEM)] + [inside] * (1 + len(carried)),
        out_specs=(inside,) * 3,
        scratch_shapes=[pltpu.VMEM((2 * ROWS, D), jnp.bfloat16)],
        compiler_params=pltpu.CompilerParams(vmem_limit_bytes=20 * 1024 * 1024),
        name="last_maxima",
        cost_estimate=cost(2),
    )(place, *carried, pair)


def half_flip(value, count):
    pairs = []
    for g in range(count):
        low, y = divmod(g, count // Z_LO)
        for h in range(2):
            for c in range(2):
                z = (h * Z_LO + low + (2 if c == 0 else 2 * Z_LO - 2)) % (2 * Z_LO)
                target = z % Z_LO * (count // Z_LO) + y
                pairs.append(((g * 2 + h) * 2 + c, (target * 2 + z // Z_LO) * 2 + c))
    return lax.ppermute(value, ("grp", "zh", "core"), pairs)


def shift(value, steps, count):
    pairs = [(i, i + steps) for i in range(count) if 0 <= i + steps < count]
    return lax.ppermute(value, "grp", pairs)


def swap(value, axis):
    return lax.ppermute(value, axis, [(0, 1), (1, 0)])


def turn_x(value, even):
    pairs = [(2 * i, 2 * ((i + even) % X)) for i in range(X)]
    pairs += [(2 * i + 1, 2 * ((i + X - even) % X) + 1) for i in range(X)]
    return lax.ppermute(value, ("x", "core"), pairs)


def per_device(embeddings, labels, order):
    count = lax.axis_size("grp")
    grp, zh, x, core = (lax.axis_index(axis) for axis in ("grp", "zh", "x", "core"))
    block = pack(embeddings, labels, order)
    one = shift(block, MOVES[0], count)
    two = shift(block, MOVES[1], count)
    three = shift(one, MOVES[2] - MOVES[0], count)
    ahead, behind = turn_x(block, 1), turn_x(block, -1)
    flipped = gate(half_flip(half_flip(block, count), count), ahead)
    flip_ahead, flip_behind = turn_x(flipped, 1), turn_x(flipped, -1)
    across = turn_x(stack((ahead, flip_ahead), (flip_behind, behind)), 1)
    mine = (stack((block, one)), stack((two, three)))
    theirs = [swap(value, "core") for value in mine]
    turn = jnp.where(core == 0, 1, X - 1)
    slots = [(zh + h) % 2 * X + (x + (X - k) * turn) % X for k in (0, 1, X - 1, 2) for h in range(2)]
    place = jnp.stack(slots).astype(jnp.int32)
    carried = first_maxima(place, (*mine, *theirs), [block, flipped, ahead, flip_ahead, behind, flip_behind])
    cols, rows, rows_sib = last_maxima(place, carried, across)
    best = jnp.max(lax.all_to_all(cols, ("zh", "x"), 0, 0, tiled=True), axis=0)
    mine = jnp.maximum(rows, swap(rows_sib, "core"))
    for i, steps in enumerate(MOVES):
        back = shift(mine[i], -steps, count)
        source = grp + steps
        best = jnp.maximum(best, jnp.where((source >= 0) & (source < count), back, -1.0))
    return best.reshape(ROWS)


def solution(mesh):
    axes = ("grp", "zh", "x", "core")
    fine = Mesh(mesh.devices.reshape(mesh.shape["grp"], 2, X, 2), axes)
    return jax.shard_map(
        per_device,
        mesh=fine,
        in_specs=(P(axes, None), P(axes), P(axes)),
        out_specs=P(axes),
        check_vma=False,
    )
```

time: 114 us -> 110 us (0.965)
  waiting for transfers between devices: 24.7 us -> 17.2 us
  local copies, waits for them, and re-layouts: 1.88 us -> 5.13 us
  starting transfers between devices: 71.3 us -> 73.8 us
  Pallas kernels: 13.9 us -> 11.8 us
    ppermute x7 -> x6, waiting for transfers between devices: 16.1 us -> 10.8 us  [shift(): return lax.ppermute(value, 'grp', pairs)]
    all_to_all x1, starting transfers between devices: 7.22 us -> 12.2 us  [per_device(): best = jnp.max(lax.all_to_all(cols, ('zh', 'x'), 0, 0, tiled=True), axis=0)]
    ppermute x6 -> x5, starting transfers between devices: 19.5 us -> 15.2 us  [turn_x(): return lax.ppermute(value, ('x', 'core'), pairs)]
    ppermute x5 -> x3, starting transfers between devices: 12.3 us -> 8.08 us  [swap(): return lax.ppermute(value, axis, [(0, 1), (1, 0)])]
    ppermute x7 -> x6, starting transfers between devices: 22.3 us -> 25.7 us  [shift(): return lax.ppermute(value, 'grp', pairs)]
    unnamed x8 -> x20, local copies, waits for them, and re-layouts: 1.79 us -> 5.04 us
    ppermute x2, waiting for transfers between devices: 8.53 us -> 5.28 us  [half_flip(): return lax.ppermute(value, ('grp', 'zh', 'core'), pairs)]
    ppermute x2, starting transfers between devices: 10 us -> 12.6 us  [half_flip(): return lax.ppermute(value, ('grp', 'zh', 'core'), pairs)]
  transfers between devices with their start and end apart: 21 -> 17, of which waited for: 3 -> 5; matrix products, arithmetic and copies ran while one was open for 0% -> 0% of each run, Pallas kernels for 8% -> 6%
where the time goes in v6:
time: 110 us; the launch traced here: 109 us
  starting transfers between devices  73.8 us (67%)
  waiting for transfers between devices  17.2 us (16%)
  Pallas kernels  11.8 us (11%)
  local copies, waits for them, and re-layouts  5.13 us (5%)
    ppermute x6, starting transfers between devices, shift(): return lax.ppermute(value, 'grp', pairs)  25.7 us
    ppermute x5, starting transfers between devices, turn_x(): return lax.ppermute(value, ('x', 'core'), pairs)  15.2 us
    ppermute x2, starting transfers between devices, half_flip(): return lax.ppermute(value, ('grp', 'zh', 'core'), pairs)  12.6 us
    all_to_all x1, starting transfers between devices, per_device(): best = jnp.max(lax.all_to_all(cols, ('zh', 'x'), 0, 0, tiled=True), axis=0)  12.2 us
    ppermute x6, waiting for transfers between devices, shift(): return lax.ppermute(value, 'grp', pairs)  10.8 us
    ppermute x3, starting transfers between devices, swap(): return lax.ppermute(value, axis, [(0, 1), (1, 0)])  8.08 us
    pallas_call x1, Pallas kernels, first_maxima(): pl.pallas_call(first_kernel, out_shape=(jax.ShapeDtypeStruct((2 * X, 1, R...  5.93 us
    ppermute x2, waiting for transfers between devices, half_flip(): return lax.ppermute(value, ('grp', 'zh', 'core'), pairs)  5.28 us
  transfers between devices with their start and end apart: 17, of which 5 were waited for; matrix products, arithmetic and copies ran while one was open for 0% of the time, Pallas kernels for 6%

profile of v6, /device:TPU:10, one launch (start us, length us, event | category | flops | bytes accessed | tf_op | source)
XLA Modules:
  0.0 108.9 jit_solution(12598837202253208219)
XLA Ops:
  0.0 2.0 %normalize_pack.1.refs_0_ = bf16[208,1024]{1,0:T(8,128)(2,1)} custom-call(bf16[192,1024]{1,0:T(8,128)(2,1)} %emb_any.1, s32[1,192]{1,0:T(1,128)} %bitcast.19, s32[1,192]{1,0:T(1,128)} %bitcast.20), custom_call_target="tpu_custom_call" | custom-call | flops 786432 | bytes 786432 | tf_op jit(solution)/shard_map/normalize_pack/pallas_call | solution.py:48
  2.0 6.1 %collective-permute-start.5 = (bf16[208,1024]{1,0:T(8,128)(2,1)}, bf16[208,1024]{1,0:T(8,128)(2,1)S(1)}, u32[]{:S(2)}, u32[]{:S(2)}) collective-permute-start(bf16[208,1024]{1,0:T(8,128)(2,1)} %normalize_pack.1.refs_0_), channel_id=1, source_target_pairs={{0,256},{1,265},{8,264},{9,257},{16,272},{17,281},{24,280},{25,273... | collective-permute-start | bytes 1277960 | tf_op jit(solution)/shard_map/ppermute | solution.py:226
  8.1 3.5 %collective-permute-start = (bf16[208,1024]{1,0:T(8,128)(2,1)}, bf16[208,1024]{1,0:T(8,128)(2,1)S(1)}, u32[]{:S(2)}, u32[]{:S(2)}) collective-permute-start(bf16[208,1024]{1,0:T(8,128)(2,1)} %normalize_pack.1.refs_0_), channel_id=1, source_target_pairs={{0,16},{16,32},{32,48},{48,64},{64,80},{80,96},{96,112},{112,128},... | collective-permute-start | bytes 1277960 | tf_op jit(solution)/shard_map/ppermute | solution.py:231
  11.6 3.4 %collective-permute-start.7 = (bf16[208,1024]{1,0:T(8,128)(2,1)}, bf16[208,1024]{1,0:T(8,128)(2,1)S(1)}, u32[]{:S(2)}, u32[]{:S(2)}) collective-permute-start(bf16[208,1024]{1,0:T(8,128)(2,1)} %normalize_pack.1.refs_0_), channel_id=1, source_target_pairs={{0,2},{2,4},{4,6},{6,0},{1,7},{3,1},{5,3},{7,5},{8,10},{10,12},{12... | collective-permute-start | bytes 1277960 | tf_op jit(solution)/shard_map/ppermute | solution.py:241
  15.0 4.4 %collective-permute-done.5 = bf16[208,1024]{1,0:T(8,128)(2,1)S(1)} collective-permute-done((bf16[208,1024]{1,0:T(8,128)(2,1)}, bf16[208,1024]{1,0:T(8,128)(2,1)S(1)}, u32[]{:S(2)}, u32[]{:S(2)}) %collective-permute-start.5) | collective-permute-done | bytes 426016 | tf_op jit(solution)/shard_map/ppermute | solution.py:226
  19.4 6.5 %collective-permute-start.6 = (bf16[208,1024]{1,0:T(8,128)(2,1)S(1)}, bf16[208,1024]{1,0:T(8,128)(2,1)S(1)}, u32[]{:S(2)}, u32[]{:S(2)}) collective-permute-start(bf16[208,1024]{1,0:T(8,128)(2,1)S(1)} %collective-permute-done.5), channel_id=1, source_target_pairs={{0,256},{1,265},{8,264},{9,257},{16,272},{17,281},{24,280},{25,273... | collective-permute-start | bytes 1277960 | tf_op jit(solution)/shard_map/ppermute | solution.py:226
  25.8 1.3 %collective-permute-start.1 = (bf16[208,1024]{1,0:T(8,128)(2,1)}, bf16[208,1024]{1,0:T(8,128)(2,1)S(1)}, u32[]{:S(2)}, u32[]{:S(2)}) collective-permute-start(bf16[208,1024]{1,0:T(8,128)(2,1)} %normalize_pack.1.refs_0_), channel_id=1, source_target_pairs={{32,0},{48,16},{64,32},{80,48},{96,64},{112,80},{128,96},{144,112}... | collective-permute-start | bytes 1277960 | tf_op jit(solution)/shard_map/ppermute | solution.py:231
  27.1 0.0 collective-permute-done.refs_1_
  27.1 5.5 %collective-permute-start.2 = (bf16[208,1024]{1,0:T(8,128)(2,1)S(1)}, bf16[208,1024]{1,0:T(8,128)(2,1)S(1)}, u32[]{:S(2)}, u32[]{:S(2)}) collective-permute-start(bf16[208,1024]{1,0:T(8,128)(2,1)S(1)} %collective-permute-done.refs_1_), channel_id=1, source_target_pairs={{0,32},{16,48},{32,64},{48,80},{64,96},{80,112},{96,128},{112,144}... | collective-permute-start | bytes 1277960 | tf_op jit(solution)/shard_map/ppermute | solution.py:231
  32.6 2.4 %collective-permute-start.9 = (bf16[208,1024]{1,0:T(8,128)(2,1)}, bf16[208,1024]{1,0:T(8,128)(2,1)S(1)}, u32[]{:S(2)}, u32[]{:S(2)}) collective-permute-start(bf16[208,1024]{1,0:T(8,128)(2,1)} %normalize_pack.1.refs_0_), channel_id=1, source_target_pairs={{0,6},{2,0},{4,2},{6,4},{1,3},{3,5},{5,7},{7,1},{8,14},{10,8},{12,... | collective-permute-start | bytes 1277960 | tf_op jit(solution)/shard_map/ppermute | solution.py:241
  35.1 0.0 collective-permute-done.7.refs_1_.refs_2_.refs_0_
  35.1 0.9 collective-permute-done.6.refs_0_
  36.0 3.9 %collective-permute-start.10 = (bf16[208,1024]{1,0:T(8,128)(2,1)S(1)}, bf16[208,1024]{1,0:T(8,128)(2,1)S(1)}, u32[]{:S(2)}, u32[]{:S(2)}) collective-permute-start(bf16[208,1024]{1,0:T(8,128)(2,1)S(1)} %gate.1.refs_1_), channel_id=1, source_target_pairs={{0,6},{2,0},{4,2},{6,4},{1,3},{3,5},{5,7},{7,1},{8,14},{10,8},{12,... | collective-permute-start | bytes 1277960 | tf_op jit(solution)/shard_map/ppermute | solution.py:241
  40.0 2.0 %collective-permute-start.8 = (bf16[208,1024]{1,0:T(8,128)(2,1)S(1)}, bf16[208,1024]{1,0:T(8,128)(2,1)S(1)}, u32[]{:S(2)}, u32[]{:S(2)}) collective-permute-start(bf16[208,1024]{1,0:T(8,128)(2,1)S(1)} %gate.1.refs_1_), channel_id=1, source_target_pairs={{0,2},{2,4},{4,6},{6,0},{1,7},{3,1},{5,3},{7,5},{8,10},{10,12},{12... | collective-permute-start | bytes 1277960 | tf_op jit(solution)/shard_map/ppermute | solution.py:241
  42.0 1.0 copy-done
  43.0 0.1 stack_blocks.3.mine_a_ref
  43.1 0.0 collective-permute-done.1.refs_0_
  43.1 3.0 %collective-permute-start.3 = (bf16[2,208,1024]{2,1,0:T(8,128)(2,1)S(1)}, bf16[2,208,1024]{2,1,0:T(8,128)(2,1)}, u32[]{:S(2)}, u32[]{:S(2)}) collective-permute-start(bf16[2,208,1024]{2,1,0:T(8,128)(2,1)S(1)} %stack_blocks.3.mine_a_ref), channel_id=1, source_target_pairs={{0,1},{1,0},{2,3},{3,2},{4,5},{5,4},{6,7},{7,6},{8,9},{9,8},{10,11... | collective-permute-start | bytes 2555912 | tf_op jit(solution)/shard_map/ppermute | solution.py:235
  46.1 3.6 %collective-permute-done.2.refs_1_ = bf16[208,1024]{1,0:T(8,128)(2,1)S(1)} collective-permute-done((bf16[208,1024]{1,0:T(8,128)(2,1)S(1)}, bf16[208,1024]{1,0:T(8,128)(2,1)S(1)}, u32[]{:S(2)}, u32[]{:S(2)}) %collective-permute-start.2) | collective-permute-done | bytes 426016 | tf_op jit(solution)/shard_map/ppermute | solution.py:231
  49.7 0.1 stack_blocks.4.mine_b_ref
  49.8 3.2 %collective-permute-start.4 = (bf16[2,208,1024]{2,1,0:T(8,128)(2,1)S(1)}, bf16[2,208,1024]{2,1,0:T(8,128)(2,1)}, u32[]{:S(2)}, u32[]{:S(2)}) collective-permute-start(bf16[2,208,1024]{2,1,0:T(8,128)(2,1)S(1)} %stack_blocks.4.mine_b_ref), channel_id=1, source_target_pairs={{0,1},{1,0},{2,3},{3,2},{4,5},{5,4},{6,7},{7,6},{8,9},{9,8},{10,11... | collective-permute-start | bytes 2555912 | tf_op jit(solution)/shard_map/ppermute | solution.py:235
  53.0 0.0 collective-permute-done.9.refs_4_.refs_3_
  53.0 0.0 collective-permute-done.10.refs_5_.refs_2_
  53.0 0.0 collective-permute-done.8.refs_3_.refs_1_
  53.0 0.1 stack_blocks.5
  53.1 3.4 %collective-permute-start.11 = (bf16[2,208,1024]{2,1,0:T(8,128)(2,1)S(1)}, bf16[2,208,1024]{2,1,0:T(8,128)(2,1)}, u32[]{:S(2)}, u32[]{:S(2)}) collective-permute-start(bf16[2,208,1024]{2,1,0:T(8,128)(2,1)S(1)} %stack_blocks.5), channel_id=1, source_target_pairs={{0,2},{2,4},{4,6},{6,0},{1,7},{3,1},{5,3},{7,5},{8,10},{10,12},{12... | collective-permute-start | bytes 2555912 | tf_op jit(solution)/shard_map/ppermute | solution.py:241
  56.5 0.0 copy-done.8
  56.6 0.1 stack.35.place_ref
  56.7 0.0 collective-permute-done.3.theirs_a_ref
  56.7 0.0 collective-permute-done.4.theirs_b_ref
  56.7 1.0 copy-done.3
  57.7 1.0 copy-done.5
  58.7 1.0 copy-done.7
  59.8 1.0 copy-done.9
  60.8 5.9 %first_maxima.1 = (f32[8,1,192]{2,1,0:T(1,128)S(1)}, f32[1152,128]{1,0:T(8,128)S(1)}, bf16[1536,1024]{1,0:T(8,128)(2,1)S(1)}, f32[1536,128]{1,0:T(8,128)S(1)}, f32[6,1,192]{2,1,0:T(1,128)S(1)}) custom-call(s32[8]{0:T(128)S(1)} %stack.35.place_ref, bf16[2,208,1024]{2,1,0:T(8,128)(2,1)S(1)} %stack_blocks.3.mine_a_ref, ...), custom_call_target="tpu_custom_call" | custom-call | flops 3623878656 | bytes 5963776 | tf_op jit(solution)/shard_map/first_maxima/pallas_call | solution.py:184
  66.7 1.1 %collective-permute-done.11.pair_ref = bf16[2,208,1024]{2,1,0:T(8,128)(2,1)} collective-permute-done((bf16[2,208,1024]{2,1,0:T(8,128)(2,1)S(1)}, bf16[2,208,1024]{2,1,0:T(8,128)(2,1)}, u32[]{:S(2)}, u32[]{:S(2)}) %collective-permute-start.11) | collective-permute-done | bytes 852000 | tf_op jit(solution)/shard_map/ppermute | solution.py:241
  67.8 3.7 %last_maxima.1 = (f32[8,1,192]{2,1,0:T(1,128)}, f32[3,1,192]{2,1,0:T(1,128)S(1)}, f32[3,1,192]{2,1,0:T(1,128)S(1)}) custom-call(s32[8]{0:T(128)S(1)} %stack.35.place_ref, f32[8,1,192]{2,1,0:T(1,128)S(1)} %get-tuple-element.13.cols_in_ref, f32[1152,128]{1,0:T(8,128)S(1)} %get-tuple-element.14.rows_in_ref, bf16[1536,1024]{1,0:T(8,128)(2,1)S(1)} %get-tuple-element.15.left_ref, ...), custom_call_target="tpu_custom_call" | custom-call | flops 1207959552 | bytes 4259840 | tf_op jit(solution)/shard_map/last_maxima/pallas_call | solution.py:205
  71.5 1.9 %collective-permute-start.12 = (f32[3,1,192]{2,1,0:T(1,128)S(1)}, f32[3,1,192]{2,1,0:T(1,128)S(1)}, u32[]{:S(2)}, u32[]{:S(2)}) collective-permute-start(f32[3,1,192]{2,1,0:T(1,128)S(1)} %get-tuple-element.20), channel_id=1, source_target_pairs={{0,1},{1,0},{2,3},{3,2},{4,5},{5,4},{6,7},{7,6},{8,9},{9,8},{10,11... | collective-permute-start | bytes 6920 | tf_op jit(solution)/shard_map/ppermute | solution.py:235
  73.5 12.2 %all-to-all-start = ((f32[8,1,192]{2,1,0:T(1,128)}), f32[8,1,192]{2,1,0:T(1,128)S(1)}, u32[]{:S(2)}, u32[]{:S(2)}) async-start(f32[8,1,192]{2,1,0:T(1,128)} %get-tuple-element.18), calls=%async_computation | async-start | bytes 16384 | tf_op jit(solution)/shard_map/all_to_all | solution.py:262
  85.6 0.0 collective-permute-done.12
  85.7 12.9 %collective-permute-start.13 = (f32[1,192]{1,0:T(1,128)S(1)}, f32[1,192]{1,0:T(1,128)S(1)}, u32[]{:S(2)}, u32[]{:S(2)}) collective-permute-start(f32[1,192]{1,0:T(1,128)S(1)} %get-tuple-element.23), channel_id=1, source_target_pairs={{16,0},{32,16},{48,32},{64,48},{80,64},{96,80},{112,96},{128,112},... | collective-permute-start | bytes 2312 | tf_op jit(solution)/shard_map/ppermute | solution.py:231
  98.6 1.3 %collective-permute-start.14 = (f32[1,192]{1,0:T(1,128)S(1)}, f32[1,192]{1,0:T(1,128)S(1)}, u32[]{:S(2)}, u32[]{:S(2)}) collective-permute-start(f32[1,192]{1,0:T(1,128)S(1)} %get-tuple-element.22), channel_id=1, source_target_pairs={{0,32},{16,48},{32,64},{48,80},{64,96},{80,112},{96,128},{112,144}... | collective-permute-start | bytes 2312 | tf_op jit(solution)/shard_map/ppermute | solution.py:231
  99.9 1.3 %collective-permute-start.15 = (f32[1,192]{1,0:T(1,128)S(1)}, f32[1,192]{1,0:T(1,128)S(1)}, u32[]{:S(2)}, u32[]{:S(2)}) collective-permute-start(f32[1,192]{1,0:T(1,128)S(1)} %get-tuple-element.21), channel_id=1, source_target_pairs={{48,0},{64,16},{80,32},{96,48},{112,64},{128,80},{144,96},{160,112... | collective-permute-start | bytes 2312 | tf_op jit(solution)/shard_map/ppermute | solution.py:231
  101.2 0.0 all-to-all-done
  101.2 0.0 collective-permute-done.13
  101.2 0.0 collective-permute-done.14
  101.2 7.1 %collective-permute-done.15 = f32[1,192]{1,0:T(1,128)S(1)} collective-permute-done((f32[1,192]{1,0:T(1,128)S(1)}, f32[1,192]{1,0:T(1,128)S(1)}, u32[]{:S(2)}, u32[]{:S(2)}) %collective-permute-start.15) | collective-permute-done | bytes 800 | tf_op jit(solution)/shard_map/ppermute | solution.py:231
  108.3 0.6 fusion.2
  (18 shorter events, 0.1 us)
Async XLA Ops:
  2.0 17.4 %collective-permute-start.5 = (bf16[208,1024]{1,0:T(8,128)(2,1)}, bf16[208,1024]{1,0:T(8,128)(2,1)S(1)}, u32[]{:S(2)}, u32[]{:S(2)}) collective-permute-start(bf16[208,1024]{1,0:T(8,128)(2,1)} %normalize_pack.1.refs_0_), channel_id=1, source_target_pairs={{0,256},{1,265},{8,264},{9,257},{16,272},{17,281},{24,280},{25,273... | collective-permute-start | bytes 1277960 | tf_op jit(solution)/shard_map/ppermute | solution.py:226
  8.1 19.1 %collective-permute-start = (bf16[208,1024]{1,0:T(8,128)(2,1)}, bf16[208,1024]{1,0:T(8,128)(2,1)S(1)}, u32[]{:S(2)}, u32[]{:S(2)}) collective-permute-start(bf16[208,1024]{1,0:T(8,128)(2,1)} %normalize_pack.1.refs_0_), channel_id=1, source_target_pairs={{0,16},{16,32},{32,48},{48,64},{64,80},{80,96},{96,112},{112,128},... | collective-permute-start | bytes 1277960 | tf_op jit(solution)/shard_map/ppermute | solution.py:231
  11.6 23.5 %collective-permute-start.7 = (bf16[208,1024]{1,0:T(8,128)(2,1)}, bf16[208,1024]{1,0:T(8,128)(2,1)S(1)}, u32[]{:S(2)}, u32[]{:S(2)}) collective-permute-start(bf16[208,1024]{1,0:T(8,128)(2,1)} %normalize_pack.1.refs_0_), channel_id=1, source_target_pairs={{0,2},{2,4},{4,6},{6,0},{1,7},{3,1},{5,3},{7,5},{8,10},{10,12},{12... | collective-permute-start | bytes 1277960 | tf_op jit(solution)/shard_map/ppermute | solution.py:241
  19.4 16.6 %collective-permute-start.6 = (bf16[208,1024]{1,0:T(8,128)(2,1)S(1)}, bf16[208,1024]{1,0:T(8,128)(2,1)S(1)}, u32[]{:S(2)}, u32[]{:S(2)}) collective-permute-start(bf16[208,1024]{1,0:T(8,128)(2,1)S(1)} %collective-permute-done.5), channel_id=1, source_target_pairs={{0,256},{1,265},{8,264},{9,257},{16,272},{17,281},{24,280},{25,273... | collective-permute-start | bytes 1277960 | tf_op jit(solution)/shard_map/ppermute | solution.py:226
  25.8 17.2 %collective-permute-start.1 = (bf16[208,1024]{1,0:T(8,128)(2,1)}, bf16[208,1024]{1,0:T(8,128)(2,1)S(1)}, u32[]{:S(2)}, u32[]{:S(2)}) collective-permute-start(bf16[208,1024]{1,0:T(8,128)(2,1)} %normalize_pack.1.refs_0_), channel_id=1, source_target_pairs={{32,0},{48,16},{64,32},{80,48},{96,64},{112,80},{128,96},{144,112}... | collective-permute-start | bytes 1277960 | tf_op jit(solution)/shard_map/ppermute | solution.py:231
  27.1 22.6 %collective-permute-start.2 = (bf16[208,1024]{1,0:T(8,128)(2,1)S(1)}, bf16[208,1024]{1,0:T(8,128)(2,1)S(1)}, u32[]{:S(2)}, u32[]{:S(2)}) collective-permute-start(bf16[208,1024]{1,0:T(8,128)(2,1)S(1)} %collective-permute-done.refs_1_), channel_id=1, source_target_pairs={{0,32},{16,48},{32,64},{48,80},{64,96},{80,112},{96,128},{112,144}... | collective-permute-start | bytes 1277960 | tf_op jit(solution)/shard_map/ppermute | solution.py:231
  32.6 20.4 %collective-permute-start.9 = (bf16[208,1024]{1,0:T(8,128)(2,1)}, bf16[208,1024]{1,0:T(8,128)(2,1)S(1)}, u32[]{:S(2)}, u32[]{:S(2)}) collective-permute-start(bf16[208,1024]{1,0:T(8,128)(2,1)} %normalize_pack.1.refs_0_), channel_id=1, source_target_pairs={{0,6},{2,0},{4,2},{6,4},{1,3},{3,5},{5,7},{7,1},{8,14},{10,8},{12,... | collective-permute-start | bytes 1277960 | tf_op jit(solution)/shard_map/ppermute | solution.py:241
  36.0 20.8 %copy-start.1 = (bf16[208,1024]{1,0:T(8,128)(2,1)S(1)}, bf16[208,1024]{1,0:T(8,128)(2,1)}, u32[]{:S(2)}) copy-start(bf16[208,1024]{1,0:T(8,128)(2,1)} %normalize_pack.1.refs_0_) | copy-start | bytes 1277956
  36.0 20.5 %copy-start.8 = (bf16[208,1024]{1,0:T(8,128)(2,1)}, bf16[208,1024]{1,0:T(8,128)(2,1)S(1)}, u32[]{:S(2)}) copy-start(bf16[208,1024]{1,0:T(8,128)(2,1)S(1)} %gate.1.refs_1_) | copy-start | bytes 1277956
  36.0 17.0 %collective-permute-start.10 = (bf16[208,1024]{1,0:T(8,128)(2,1)S(1)}, bf16[208,1024]{1,0:T(8,128)(2,1)S(1)}, u32[]{:S(2)}, u32[]{:S(2)}) collective-permute-start(bf16[208,1024]{1,0:T(8,128)(2,1)S(1)} %gate.1.refs_1_), channel_id=1, source_target_pairs={{0,6},{2,0},{4,2},{6,4},{1,3},{3,5},{5,7},{7,1},{8,14},{10,8},{12,... | collective-permute-start | bytes 1277960 | tf_op jit(solution)/shard_map/ppermute | solution.py:241
  40.0 13.1 %collective-permute-start.8 = (bf16[208,1024]{1,0:T(8,128)(2,1)S(1)}, bf16[208,1024]{1,0:T(8,128)(2,1)S(1)}, u32[]{:S(2)}, u32[]{:S(2)}) collective-permute-start(bf16[208,1024]{1,0:T(8,128)(2,1)S(1)} %gate.1.refs_1_), channel_id=1, source_target_pairs={{0,2},{2,4},{4,6},{6,0},{1,7},{3,1},{5,3},{7,5},{8,10},{10,12},{12... | collective-permute-start | bytes 1277960 | tf_op jit(solution)/shard_map/ppermute | solution.py:241
  42.0 1.0 copy-start
  43.1 13.6 %collective-permute-start.3 = (bf16[2,208,1024]{2,1,0:T(8,128)(2,1)S(1)}, bf16[2,208,1024]{2,1,0:T(8,128)(2,1)}, u32[]{:S(2)}, u32[]{:S(2)}) collective-permute-start(bf16[2,208,1024]{2,1,0:T(8,128)(2,1)S(1)} %stack_blocks.3.mine_a_ref), channel_id=1, source_target_pairs={{0,1},{1,0},{2,3},{3,2},{4,5},{5,4},{6,7},{7,6},{8,9},{9,8},{10,11... | collective-permute-start | bytes 2555912 | tf_op jit(solution)/shard_map/ppermute | solution.py:235
  49.8 6.9 %collective-permute-start.4 = (bf16[2,208,1024]{2,1,0:T(8,128)(2,1)S(1)}, bf16[2,208,1024]{2,1,0:T(8,128)(2,1)}, u32[]{:S(2)}, u32[]{:S(2)}) collective-permute-start(bf16[2,208,1024]{2,1,0:T(8,128)(2,1)S(1)} %stack_blocks.4.mine_b_ref), channel_id=1, source_target_pairs={{0,1},{1,0},{2,3},{3,2},{4,5},{5,4},{6,7},{7,6},{8,9},{9,8},{10,11... | collective-permute-start | bytes 2555912 | tf_op jit(solution)/shard_map/ppermute | solution.py:235
  53.0 3.5 %copy-start.2 = (bf16[208,1024]{1,0:T(8,128)(2,1)}, bf16[208,1024]{1,0:T(8,128)(2,1)S(1)}, u32[]{:S(2)}) copy-start(bf16[208,1024]{1,0:T(8,128)(2,1)S(1)} %collective-permute-done.9.refs_4_.refs_3_) | copy-start | bytes 1277956
  53.0 3.5 %copy-start.4 = (bf16[208,1024]{1,0:T(8,128)(2,1)}, bf16[208,1024]{1,0:T(8,128)(2,1)S(1)}, u32[]{:S(2)}) copy-start(bf16[208,1024]{1,0:T(8,128)(2,1)S(1)} %collective-permute-done.10.refs_5_.refs_2_) | copy-start | bytes 1277956
  53.0 3.5 %copy-start.6 = (bf16[208,1024]{1,0:T(8,128)(2,1)}, bf16[208,1024]{1,0:T(8,128)(2,1)S(1)}, u32[]{:S(2)}) copy-start(bf16[208,1024]{1,0:T(8,128)(2,1)S(1)} %collective-permute-done.8.refs_3_.refs_1_) | copy-start | bytes 1277956
  53.1 14.7 %collective-permute-start.11 = (bf16[2,208,1024]{2,1,0:T(8,128)(2,1)S(1)}, bf16[2,208,1024]{2,1,0:T(8,128)(2,1)}, u32[]{:S(2)}, u32[]{:S(2)}) collective-permute-start(bf16[2,208,1024]{2,1,0:T(8,128)(2,1)S(1)} %stack_blocks.5), channel_id=1, source_target_pairs={{0,2},{2,4},{4,6},{6,0},{1,7},{3,1},{5,3},{7,5},{8,10},{10,12},{12... | collective-permute-start | bytes 2555912 | tf_op jit(solution)/shard_map/ppermute | solution.py:241
  56.7 1.0 copy-start.3
  57.7 1.0 copy-start.5
  58.7 1.0 copy-start.7
  59.8 1.0 copy-start.9
  71.5 14.1 %collective-permute-start.12 = (f32[3,1,192]{2,1,0:T(1,128)S(1)}, f32[3,1,192]{2,1,0:T(1,128)S(1)}, u32[]{:S(2)}, u32[]{:S(2)}) collective-permute-start(f32[3,1,192]{2,1,0:T(1,128)S(1)} %get-tuple-element.20), channel_id=1, source_target_pairs={{0,1},{1,0},{2,3},{3,2},{4,5},{5,4},{6,7},{7,6},{8,9},{9,8},{10,11... | collective-permute-start | bytes 6920 | tf_op jit(solution)/shard_map/ppermute | solution.py:235
  73.5 27.7 %all-to-all-start = ((f32[8,1,192]{2,1,0:T(1,128)}), f32[8,1,192]{2,1,0:T(1,128)S(1)}, u32[]{:S(2)}, u32[]{:S(2)}) async-start(f32[8,1,192]{2,1,0:T(1,128)} %get-tuple-element.18), calls=%async_computation | async-start | bytes 16384 | tf_op jit(solution)/shard_map/all_to_all | solution.py:262
  85.7 15.6 %collective-permute-start.13 = (f32[1,192]{1,0:T(1,128)S(1)}, f32[1,192]{1,0:T(1,128)S(1)}, u32[]{:S(2)}, u32[]{:S(2)}) collective-permute-start(f32[1,192]{1,0:T(1,128)S(1)} %get-tuple-element.23), channel_id=1, source_target_pairs={{16,0},{32,16},{48,32},{64,48},{80,64},{96,80},{112,96},{128,112},... | collective-permute-start | bytes 2312 | tf_op jit(solution)/shard_map/ppermute | solution.py:231
  98.6 2.7 %collective-permute-start.14 = (f32[1,192]{1,0:T(1,128)S(1)}, f32[1,192]{1,0:T(1,128)S(1)}, u32[]{:S(2)}, u32[]{:S(2)}) collective-permute-start(f32[1,192]{1,0:T(1,128)S(1)} %get-tuple-element.22), channel_id=1, source_target_pairs={{0,32},{16,48},{32,64},{48,80},{64,96},{80,112},{96,128},{112,144}... | collective-permute-start | bytes 2312 | tf_op jit(solution)/shard_map/ppermute | solution.py:231
  99.9 8.5 %collective-permute-start.15 = (f32[1,192]{1,0:T(1,128)S(1)}, f32[1,192]{1,0:T(1,128)S(1)}, u32[]{:S(2)}, u32[]{:S(2)}) collective-permute-start(f32[1,192]{1,0:T(1,128)S(1)} %get-tuple-element.21), channel_id=1, source_target_pairs={{48,0},{64,16},{80,32},{96,48},{112,64},{128,80},{144,96},{160,112... | collective-permute-start | bytes 2312 | tf_op jit(solution)/shard_map/ppermute | solution.py:231

commit v7 on v6

--- a/solution.py
+++ b/solution.py
@@ -11,11 +11,12 @@
 D = 1024
 X = 4
 Z_LO = 4
-MOVES = (1, -2, 3)
+MOVES = (1, 2, -3)
 NEAR = 1 + len(MOVES)
 LEFT = 2 * NEAR * ROWS
 TILE = 256
 FAR = 1.0e9
+FIRST = 6
 
 
 def pack_kernel(emb_any, lab_any, ord_any, out_ref, emb_ref, lab_ref, ord_ref, sems):
@@ -146,24 +147,31 @@
     return jnp.concatenate(cols, axis=1), rows
 
 
-def first_kernel(place_ref, mine_a_ref, mine_b_ref, theirs_a_ref, theirs_b_ref, *refs):
-    pairs = ((mine_a_ref, theirs_a_ref), (mine_b_ref, theirs_b_ref))
-    near = [ref.at[k] for pair in pairs for k in range(2) for ref in pair]
-    *panel, cols_ref, rows_ref, left_ref, rank_ref, valid_ref, right = refs
+def first_kernel(place_ref, *refs):
+    *given, cols_ref, rows_ref, left_ref, rank_ref, valid_ref, right = refs
+    panel, given = given[:FIRST], given[FIRST:]
+    mine, theirs = given[:len(given) // 2], given[len(given) // 2:]
+    near = []
+    for pair in zip(mine, theirs):
+        if len(pair[0].shape) == 2:
+            near += pair
+        else:
+            near += [ref.at[k] for k in range(pair[0].shape[0]) for ref in pair]
     lay_out(near, left_ref, rank_ref, valid_ref)
     best, rows = panel_maxima(panel, right, left_ref, rank_ref)
     cols_ref[...] = jnp.full(cols_ref.shape, -1.0, jnp.float32)
-    for k in range(len(panel)):
+    for k in range(FIRST):
         cols_ref[place_ref[k]] = best[:, k * ROWS:(k + 1) * ROWS]
     rows_ref[...] = rows
 
 
-def last_kernel(place_ref, cols_in_ref, rows_in_ref, left_ref, rank_ref, valid_ref, pair_ref, cols_ref, mine_ref, theirs_ref, right):
-    panel = [pair_ref.at[k] for k in range(2)]
+def last_kernel(place_ref, *refs):
+    *given, cols_in_ref, rows_in_ref, left_ref, rank_ref, valid_ref, cols_ref, mine_ref, theirs_ref, right = refs
+    panel = [ref.at[k] for ref in given for k in range(2)] if len(given) == 1 else given
     best, rows = panel_maxima(panel, right, left_ref, rank_ref)
     cols_ref[...] = cols_in_ref[...]
-    for k in range(2):
-        cols_ref[place_ref[2 * X - 2 + k]] = best[:, k * ROWS:(k + 1) * ROWS]
+    for k in range(2 * X - FIRST):
+        cols_ref[place_ref[FIRST + k]] = best[:, k * ROWS:(k + 1) * ROWS]
     rows = jnp.maximum(rows, rows_in_ref[...])
     line = jnp.max(jnp.transpose(rows, (1, 0)), axis=0, keepdims=True)
     for s in range(NEAR - 1):
@@ -190,28 +198,29 @@
             jax.ShapeDtypeStruct((LEFT, 128), jnp.float32),
             jax.ShapeDtypeStruct((2 * (NEAR - 1), 1, ROWS), jnp.float32),
         ),
-        in_specs=[pl.BlockSpec(memory_space=pltpu.SMEM)] + [inside] * (4 + blocks),
+        in_specs=[pl.BlockSpec(memory_space=pltpu.SMEM)] + [inside] * (len(near) + blocks),
         out_specs=(inside,) * 5,
         scratch_shapes=[pltpu.VMEM((blocks * ROWS, D), jnp.bfloat16)],
         compiler_params=pltpu.CompilerParams(vmem_limit_bytes=20 * 1024 * 1024),
         name="first_maxima",
         cost_estimate=cost(blocks),
-    )(place, *near, *panel)
-
-
-def last_maxima(place, carried, pair):
+    )(place, *panel, *near)
+
+
+def last_maxima(place, panel, carried):
     inside = pl.BlockSpec(memory_space=pltpu.VMEM)
     lines = jax.ShapeDtypeStruct((NEAR - 1, 1, ROWS), jnp.float32)
+    blocks = 2 * X - FIRST
     return pl.pallas_call(
         last_kernel,
         out_shape=(jax.ShapeDtypeStruct((2 * X, 1, ROWS), jnp.float32), lines, lines),
-        in_specs=[pl.BlockSpec(memory_space=pltpu.SMEM)] + [inside] * (1 + len(carried)),
+        in_specs=[pl.BlockSpec(memory_space=pltpu.SMEM)] + [inside] * (len(panel) + len(carried)),
         out_specs=(inside,) * 3,
-        scratch_shapes=[pltpu.VMEM((2 * ROWS, D), jnp.bfloat16)],
+        scratch_shapes=[pltpu.VMEM((blocks * ROWS, D), jnp.bfloat16)],
         compiler_params=pltpu.CompilerParams(vmem_limit_bytes=20 * 1024 * 1024),
         name="last_maxima",
-        cost_estimate=cost(2),
-    )(place, *carried, pair)
+        cost_estimate=cost(blocks),
+    )(place, *panel, *carried)
 
 
 def half_flip(value, count):
@@ -247,18 +256,21 @@
     block = pack(embeddings, labels, order)
     one = shift(block, MOVES[0], count)
     two = shift(block, MOVES[1], count)
-    three = shift(one, MOVES[2] - MOVES[0], count)
+    three = shift(block, MOVES[2], count)
     ahead, behind = turn_x(block, 1), turn_x(block, -1)
-    flipped = gate(half_flip(half_flip(block, count), count), ahead)
+    across = turn_x(ahead, 1)
+    sib = swap(block, "core")
+    flipped = gate(swap(block, "zh"), ahead, behind, across)
     flip_ahead, flip_behind = turn_x(flipped, 1), turn_x(flipped, -1)
-    across = turn_x(stack((ahead, flip_ahead), (flip_behind, behind)), 1)
-    mine = (stack((block, one)), stack((two, three)))
-    theirs = [swap(value, "core") for value in mine]
+    flip_across = turn_x(flip_ahead, 1)
+    mine = (block, one, stack((two, three)))
+    theirs = [sib] + [swap(value, "core") for value in mine[1:]]
     turn = jnp.where(core == 0, 1, X - 1)
-    slots = [(zh + h) % 2 * X + (x + (X - k) * turn) % X for k in (0, 1, X - 1, 2) for h in range(2)]
+    order_held = ((0, 0), (1, 0), (0, 1), (1, 1), (0, X - 1), (0, 2), (1, X - 1), (1, 2))
+    slots = [(zh + h) % 2 * X + (x + (X - k) * turn) % X for h, k in order_held]
     place = jnp.stack(slots).astype(jnp.int32)
-    carried = first_maxima(place, (*mine, *theirs), [block, flipped, ahead, flip_ahead, behind, flip_behind])
-    cols, rows, rows_sib = last_maxima(place, carried, across)
+    carried = first_maxima(place, (*mine, *theirs), [block, flipped, ahead, flip_ahead, behind, across])
+    cols, rows, rows_sib = last_maxima(place, [flip_behind, flip_across], carried)
     best = jnp.max(lax.all_to_all(cols, ("zh", "x"), 0, 0, tiled=True), axis=0)
     mine = jnp.maximum(rows, swap(rows_sib, "core"))
     for i, steps in enumerate(MOVES):

time: 110 us -> 108 us (0.982)
  the two profiles are of different devices: /device:TPU:10 before, /device:TPU:138 now
where the time goes in v7:
time: 108 us; the launch traced here: 107 us
  starting transfers between devices  69.1 us (64%)
  waiting for transfers between devices  25 us (23%)
  Pallas kernels  12.3 us (11%)
    ppermute x6, starting transfers between devices, shift(): return lax.ppermute(value, 'grp', pairs)  23.2 us
    ppermute x6, starting transfers between devices, turn_x(): return lax.ppermute(value, ('x', 'core'), pairs)  18.8 us
    ppermute x5, starting transfers between devices, swap(): return lax.ppermute(value, axis, [(0, 1), (1, 0)])  17.5 us
    ppermute x6, waiting for transfers between devices, shift(): return lax.ppermute(value, 'grp', pairs)  17.3 us
    all_to_all x1, starting transfers between devices, per_device(): best = jnp.max(lax.all_to_all(cols, ('zh', 'x'), 0, 0, tiled=True), axis=0)  9.63 us
    pallas_call x1, Pallas kernels, first_maxima(): pl.pallas_call(first_kernel, out_shape=(jax.ShapeDtypeStruct((2 * X, 1, R...  6.34 us
    ppermute x5, waiting for transfers between devices, swap(): return lax.ppermute(value, axis, [(0, 1), (1, 0)])  5.59 us
    pallas_call x1, Pallas kernels, last_maxima(): pl.pallas_call(last_kernel, out_shape=(jax.ShapeDtypeStruct((2 * X, 1, RO...  3.11 us
  transfers between devices with their start and end apart: 18, of which 7 were waited for; matrix products, arithmetic and copies ran while one was open for 0% of the time, Pallas kernels for 7%

profile of v7, /device:TPU:138, one launch (start us, length us, event | category | flops | bytes accessed | tf_op | source)
XLA Modules:
  0.0 107.4 jit_solution(11080405417117486451)
XLA Ops:
  0.0 2.0 %normalize_pack.1.refs_0_.refs_6_ = bf16[208,1024]{1,0:T(8,128)(2,1)} custom-call(bf16[192,1024]{1,0:T(8,128)(2,1)} %emb_any.1, s32[1,192]{1,0:T(1,128)} %bitcast.19, s32[1,192]{1,0:T(1,128)} %bitcast.20), custom_call_target="tpu_custom_call" | custom-call | flops 786432 | bytes 786432 | tf_op jit(solution)/shard_map/normalize_pack/pallas_call | solution.py:49
  2.0 0.0 copy-start
  2.0 3.5 %collective-permute-start.1 = (bf16[208,1024]{1,0:T(8,128)(2,1)}, bf16[208,1024]{1,0:T(8,128)(2,1)S(1)}, u32[]{:S(2)}, u32[]{:S(2)}) collective-permute-start(bf16[208,1024]{1,0:T(8,128)(2,1)} %normalize_pack.1.refs_0_.refs_6_), channel_id=1, source_target_pairs={{0,2},{2,4},{4,6},{6,0},{1,7},{3,1},{5,3},{7,5},{8,10},{10,12},{12... | collective-permute-start | bytes 1277960 | tf_op jit(solution)/shard_map/ppermute | solution.py:250
  5.5 4.5 %collective-permute-start.8 = (bf16[208,1024]{1,0:T(8,128)(2,1)}, bf16[208,1024]{1,0:T(8,128)(2,1)S(1)}, u32[]{:S(2)}, u32[]{:S(2)}) collective-permute-start(bf16[208,1024]{1,0:T(8,128)(2,1)} %normalize_pack.1.refs_0_.refs_6_), channel_id=1, source_target_pairs={{0,32},{16,48},{32,64},{48,80},{64,96},{80,112},{96,128},{112,144}... | collective-permute-start | bytes 1277960 | tf_op jit(solution)/shard_map/ppermute | solution.py:240
  10.0 4.2 %collective-permute-start.9 = (bf16[208,1024]{1,0:T(8,128)(2,1)}, bf16[208,1024]{1,0:T(8,128)(2,1)S(1)}, u32[]{:S(2)}, u32[]{:S(2)}) collective-permute-start(bf16[208,1024]{1,0:T(8,128)(2,1)} %normalize_pack.1.refs_0_.refs_6_), channel_id=1, source_target_pairs={{48,0},{64,16},{80,32},{96,48},{112,64},{128,80},{144,96},{160,112... | collective-permute-start | bytes 1277960 | tf_op jit(solution)/shard_map/ppermute | solution.py:240
  14.3 2.4 %collective-permute-start.2 = (bf16[208,1024]{1,0:T(8,128)(2,1)}, bf16[208,1024]{1,0:T(8,128)(2,1)S(1)}, u32[]{:S(2)}, u32[]{:S(2)}) collective-permute-start(bf16[208,1024]{1,0:T(8,128)(2,1)} %normalize_pack.1.refs_0_.refs_6_), channel_id=1, source_target_pairs={{0,6},{2,0},{4,2},{6,4},{1,3},{3,5},{5,7},{7,1},{8,14},{10,8},{12,... | collective-permute-start | bytes 1277960 | tf_op jit(solution)/shard_map/ppermute | solution.py:250
  16.7 9.1 %collective-permute-start = (bf16[208,1024]{1,0:T(8,128)(2,1)}, bf16[208,1024]{1,0:T(8,128)(2,1)S(1)}, u32[]{:S(2)}, u32[]{:S(2)}) collective-permute-start(bf16[208,1024]{1,0:T(8,128)(2,1)} %normalize_pack.1.refs_0_.refs_6_), channel_id=1, source_target_pairs={{0,8},{8,0},{1,9},{9,1},{2,10},{10,2},{3,11},{11,3},{4,12},{12,4},... | collective-permute-start | bytes 1277960 | tf_op jit(solution)/shard_map/ppermute | solution.py:244
  25.8 0.0 collective-permute-done.1.refs_1_.refs_2_
  25.8 3.4 %collective-permute-start.3 = (bf16[208,1024]{1,0:T(8,128)(2,1)S(1)}, bf16[208,1024]{1,0:T(8,128)(2,1)S(1)}, u32[]{:S(2)}, u32[]{:S(2)}) collective-permute-start(bf16[208,1024]{1,0:T(8,128)(2,1)S(1)} %collective-permute-done.1.refs_1_.refs_2_), channel_id=1, source_target_pairs={{0,2},{2,4},{4,6},{6,0},{1,7},{3,1},{5,3},{7,5},{8,10},{10,12},{12... | collective-permute-start | bytes 1277960 | tf_op jit(solution)/shard_map/ppermute | solution.py:250
  29.3 1.7 %collective-permute-done.8.refs_0_ = bf16[208,1024]{1,0:T(8,128)(2,1)S(1)} collective-permute-done((bf16[208,1024]{1,0:T(8,128)(2,1)}, bf16[208,1024]{1,0:T(8,128)(2,1)S(1)}, u32[]{:S(2)}, u32[]{:S(2)}) %collective-permute-start.8) | collective-permute-done | bytes 426016 | tf_op jit(solution)/shard_map/ppermute | solution.py:240
  31.0 1.9 %collective-permute-start.7 = (bf16[208,1024]{1,0:T(8,128)(2,1)}, bf16[208,1024]{1,0:T(8,128)(2,1)}, u32[]{:S(2)}, u32[]{:S(2)}) collective-permute-start(bf16[208,1024]{1,0:T(8,128)(2,1)} %normalize_pack.1.refs_0_.refs_6_), channel_id=1, source_target_pairs={{0,16},{16,32},{32,48},{48,64},{64,80},{80,96},{96,112},{112,128},... | collective-permute-start | bytes 1277960 | tf_op jit(solution)/shard_map/ppermute | solution.py:240
  32.9 8.2 %collective-permute-done.9.refs_1_ = bf16[208,1024]{1,0:T(8,128)(2,1)S(1)} collective-permute-done((bf16[208,1024]{1,0:T(8,128)(2,1)}, bf16[208,1024]{1,0:T(8,128)(2,1)S(1)}, u32[]{:S(2)}, u32[]{:S(2)}) %collective-permute-start.9) | collective-permute-done | bytes 426016 | tf_op jit(solution)/shard_map/ppermute | solution.py:240
  41.1 0.1 stack_blocks.1.refs_8_
  41.2 1.9 %collective-permute-start.12 = (bf16[2,208,1024]{2,1,0:T(8,128)(2,1)S(1)}, bf16[2,208,1024]{2,1,0:T(8,128)(2,1)}, u32[]{:S(2)}, u32[]{:S(2)}) collective-permute-start(bf16[2,208,1024]{2,1,0:T(8,128)(2,1)S(1)} %stack_blocks.1.refs_8_), channel_id=1, source_target_pairs={{0,1},{1,0},{2,3},{3,2},{4,5},{5,4},{6,7},{7,6},{8,9},{9,8},{10,11... | collective-permute-start | bytes 2555912 | tf_op jit(solution)/shard_map/ppermute | solution.py:244
  43.1 0.0 collective-permute-done.2.refs_2_.refs_4_
  43.1 5.6 %collective-permute-done.refs_0_ = bf16[208,1024]{1,0:T(8,128)(2,1)S(1)} collective-permute-done((bf16[208,1024]{1,0:T(8,128)(2,1)}, bf16[208,1024]{1,0:T(8,128)(2,1)S(1)}, u32[]{:S(2)}, u32[]{:S(2)}) %collective-permute-start) | collective-permute-done | bytes 426016 | tf_op jit(solution)/shard_map/ppermute | solution.py:244
  48.7 0.0 collective-permute-done.3.refs_3_.refs_5_
  48.7 0.8 gate.1.refs_1_
  49.5 3.4 %collective-permute-start.5 = (bf16[208,1024]{1,0:T(8,128)(2,1)}, bf16[208,1024]{1,0:T(8,128)(2,1)}, u32[]{:S(2)}, u32[]{:S(2)}) collective-permute-start(bf16[208,1024]{1,0:T(8,128)(2,1)} %gate.1.refs_1_), channel_id=1, source_target_pairs={{0,2},{2,4},{4,6},{6,0},{1,7},{3,1},{5,3},{7,5},{8,10},{10,12},{12... | collective-permute-start | bytes 1277960 | tf_op jit(solution)/shard_map/ppermute | solution.py:250
  52.9 0.0 copy-done
  52.9 2.5 %collective-permute-start.10 = (bf16[208,1024]{1,0:T(8,128)(2,1)S(1)}, bf16[208,1024]{1,0:T(8,128)(2,1)}, u32[]{:S(2)}, u32[]{:S(2)}) collective-permute-start(bf16[208,1024]{1,0:T(8,128)(2,1)S(1)} %copy-done), channel_id=1, source_target_pairs={{0,1},{1,0},{2,3},{3,2},{4,5},{5,4},{6,7},{7,6},{8,9},{9,8},{10,11... | collective-permute-start | bytes 1277960 | tf_op jit(solution)/shard_map/ppermute | solution.py:244
  55.4 0.0 collective-permute-done.7.refs_7_
  55.4 1.9 %collective-permute-start.11 = (bf16[208,1024]{1,0:T(8,128)(2,1)}, bf16[208,1024]{1,0:T(8,128)(2,1)}, u32[]{:S(2)}, u32[]{:S(2)}) collective-permute-start(bf16[208,1024]{1,0:T(8,128)(2,1)} %collective-permute-done.7.refs_7_), channel_id=1, source_target_pairs={{0,1},{1,0},{2,3},{3,2},{4,5},{5,4},{6,7},{7,6},{8,9},{9,8},{10,11... | collective-permute-start | bytes 1277960 | tf_op jit(solution)/shard_map/ppermute | solution.py:244
  57.3 3.9 %collective-permute-start.4 = (bf16[208,1024]{1,0:T(8,128)(2,1)}, bf16[208,1024]{1,0:T(8,128)(2,1)S(1)}, u32[]{:S(2)}, u32[]{:S(2)}) collective-permute-start(bf16[208,1024]{1,0:T(8,128)(2,1)} %gate.1.refs_1_), channel_id=1, source_target_pairs={{0,6},{2,0},{4,2},{6,4},{1,3},{3,5},{5,7},{7,1},{8,14},{10,8},{12,... | collective-permute-start | bytes 1277960 | tf_op jit(solution)/shard_map/ppermute | solution.py:250
  61.3 0.0 collective-permute-done.5.refs_3_
  61.3 2.0 %collective-permute-start.6 = (bf16[208,1024]{1,0:T(8,128)(2,1)}, bf16[208,1024]{1,0:T(8,128)(2,1)S(1)}, u32[]{:S(2)}, u32[]{:S(2)}) collective-permute-start(bf16[208,1024]{1,0:T(8,128)(2,1)} %collective-permute-done.5.refs_3_), channel_id=1, source_target_pairs={{0,2},{2,4},{4,6},{6,0},{1,7},{3,1},{5,3},{7,5},{8,10},{10,12},{12... | collective-permute-start | bytes 1277960 | tf_op jit(solution)/shard_map/ppermute | solution.py:250
  63.4 0.1 stack.35.place_ref
  63.5 0.0 collective-permute-done.10.refs_9_
  63.5 0.0 collective-permute-done.11.refs_10_
  63.5 0.0 collective-permute-done.12.refs_11_
  63.5 6.3 %first_maxima.1 = (f32[8,1,192]{2,1,0:T(1,128)S(1)}, f32[1152,128]{1,0:T(8,128)S(1)}, bf16[1536,1024]{1,0:T(8,128)(2,1)S(1)}, f32[1536,128]{1,0:T(8,128)S(1)}, f32[6,1,192]{2,1,0:T(1,128)S(1)}) custom-call(s32[8]{0:T(128)S(1)} %stack.35.place_ref, bf16[208,1024]{1,0:T(8,128)(2,1)S(1)} %copy-done, bf16[208,1024]{1,0:T(8,128)(2,1)} %gate.1.refs_1_, ...), custom_call_target="tpu_custom_call" | custom-call | flops 3623878656 | bytes 5963776 | tf_op jit(solution)/shard_map/first_maxima/pallas_call | solution.py:192
  69.9 0.4 collective-permute-done.4.refs_0_
  70.2 1.7 %collective-permute-done.6.refs_1_ = bf16[208,1024]{1,0:T(8,128)(2,1)S(1)} collective-permute-done((bf16[208,1024]{1,0:T(8,128)(2,1)}, bf16[208,1024]{1,0:T(8,128)(2,1)S(1)}, u32[]{:S(2)}, u32[]{:S(2)}) %collective-permute-start.6) | collective-permute-done | bytes 426016 | tf_op jit(solution)/shard_map/ppermute | solution.py:250
  71.9 3.1 %last_maxima.1 = (f32[8,1,192]{2,1,0:T(1,128)}, f32[3,1,192]{2,1,0:T(1,128)S(1)}, f32[3,1,192]{2,1,0:T(1,128)S(1)}) custom-call(s32[8]{0:T(128)S(1)} %stack.35.place_ref, bf16[208,1024]{1,0:T(8,128)(2,1)S(1)} %collective-permute-done.4.refs_0_, bf16[208,1024]{1,0:T(8,128)(2,1)S(1)} %collective-permute-done.6.refs_1_, ...), custom_call_target="tpu_custom_call" | custom-call | flops 1207959552 | bytes 4259840 | tf_op jit(solution)/shard_map/last_maxima/pallas_call | solution.py:214
  75.1 2.0 %collective-permute-start.13 = (f32[3,1,192]{2,1,0:T(1,128)S(1)}, f32[3,1,192]{2,1,0:T(1,128)S(1)}, u32[]{:S(2)}, u32[]{:S(2)}) collective-permute-start(f32[3,1,192]{2,1,0:T(1,128)S(1)} %get-tuple-element.20), channel_id=1, source_target_pairs={{0,1},{1,0},{2,3},{3,2},{4,5},{5,4},{6,7},{7,6},{8,9},{9,8},{10,11... | collective-permute-start | bytes 6920 | tf_op jit(solution)/shard_map/ppermute | solution.py:244
  77.1 9.6 %all-to-all-start = ((f32[8,1,192]{2,1,0:T(1,128)}), f32[8,1,192]{2,1,0:T(1,128)S(1)}, u32[]{:S(2)}, u32[]{:S(2)}) async-start(f32[8,1,192]{2,1,0:T(1,128)} %get-tuple-element.18), calls=%async_computation | async-start | bytes 16384 | tf_op jit(solution)/shard_map/all_to_all | solution.py:274
  86.7 0.0 collective-permute-done.13
  86.8 8.7 %collective-permute-start.14 = (f32[1,192]{1,0:T(1,128)S(1)}, f32[1,192]{1,0:T(1,128)S(1)}, u32[]{:S(2)}, u32[]{:S(2)}) collective-permute-start(f32[1,192]{1,0:T(1,128)S(1)} %get-tuple-element.23), channel_id=1, source_target_pairs={{16,0},{32,16},{48,32},{64,48},{80,64},{96,80},{112,96},{128,112},... | collective-permute-start | bytes 2312 | tf_op jit(solution)/shard_map/ppermute | solution.py:240
  95.5 1.9 %collective-permute-start.15 = (f32[1,192]{1,0:T(1,128)S(1)}, f32[1,192]{1,0:T(1,128)S(1)}, u32[]{:S(2)}, u32[]{:S(2)}) collective-permute-start(f32[1,192]{1,0:T(1,128)S(1)} %get-tuple-element.22), channel_id=1, source_target_pairs={{32,0},{48,16},{64,32},{80,48},{96,64},{112,80},{128,96},{144,112}... | collective-permute-start | bytes 2312 | tf_op jit(solution)/shard_map/ppermute | solution.py:240
  97.4 1.9 %collective-permute-start.16 = (f32[1,192]{1,0:T(1,128)S(1)}, f32[1,192]{1,0:T(1,128)S(1)}, u32[]{:S(2)}, u32[]{:S(2)}) collective-permute-start(f32[1,192]{1,0:T(1,128)S(1)} %get-tuple-element.21), channel_id=1, source_target_pairs={{0,48},{16,64},{32,80},{48,96},{64,112},{80,128},{96,144},{112,160... | collective-permute-start | bytes 2312 | tf_op jit(solution)/shard_map/ppermute | solution.py:240
  99.4 0.0 all-to-all-done
  99.4 0.0 collective-permute-done.14
  99.4 2.4 %collective-permute-done.15 = f32[1,192]{1,0:T(1,128)S(1)} collective-permute-done((f32[1,192]{1,0:T(1,128)S(1)}, f32[1,192]{1,0:T(1,128)S(1)}, u32[]{:S(2)}, u32[]{:S(2)}) %collective-permute-start.15) | collective-permute-done | bytes 800 | tf_op jit(solution)/shard_map/ppermute | solution.py:240
  101.9 4.9 %collective-permute-done.16 = f32[1,192]{1,0:T(1,128)S(1)} collective-permute-done((f32[1,192]{1,0:T(1,128)S(1)}, f32[1,192]{1,0:T(1,128)S(1)}, u32[]{:S(2)}, u32[]{:S(2)}) %collective-permute-start.16) | collective-permute-done | bytes 800 | tf_op jit(solution)/shard_map/ppermute | solution.py:240
  106.8 0.6 fusion.2
  (3 shorter events, 0.0 us)
Async XLA Ops:
  2.0 50.9 %copy-start = (bf16[208,1024]{1,0:T(8,128)(2,1)S(1)}, bf16[208,1024]{1,0:T(8,128)(2,1)}, u32[]{:S(2)}) copy-start(bf16[208,1024]{1,0:T(8,128)(2,1)} %normalize_pack.1.refs_0_.refs_6_) | copy-start | bytes 1277956
  2.0 23.9 %collective-permute-start.1 = (bf16[208,1024]{1,0:T(8,128)(2,1)}, bf16[208,1024]{1,0:T(8,128)(2,1)S(1)}, u32[]{:S(2)}, u32[]{:S(2)}) collective-permute-start(bf16[208,1024]{1,0:T(8,128)(2,1)} %normalize_pack.1.refs_0_.refs_6_), channel_id=1, source_target_pairs={{0,2},{2,4},{4,6},{6,0},{1,7},{3,1},{5,3},{7,5},{8,10},{10,12},{12... | collective-permute-start | bytes 1277960 | tf_op jit(solution)/shard_map/ppermute | solution.py:250
  5.5 25.5 %collective-permute-start.8 = (bf16[208,1024]{1,0:T(8,128)(2,1)}, bf16[208,1024]{1,0:T(8,128)(2,1)S(1)}, u32[]{:S(2)}, u32[]{:S(2)}) collective-permute-start(bf16[208,1024]{1,0:T(8,128)(2,1)} %normalize_pack.1.refs_0_.refs_6_), channel_id=1, source_target_pairs={{0,32},{16,48},{32,64},{48,80},{64,96},{80,112},{96,128},{112,144}... | collective-permute-start | bytes 1277960 | tf_op jit(solution)/shard_map/ppermute | solution.py:240
  10.0 31.1 %collective-permute-start.9 = (bf16[208,1024]{1,0:T(8,128)(2,1)}, bf16[208,1024]{1,0:T(8,128)(2,1)S(1)}, u32[]{:S(2)}, u32[]{:S(2)}) collective-permute-start(bf16[208,1024]{1,0:T(8,128)(2,1)} %normalize_pack.1.refs_0_.refs_6_), channel_id=1, source_target_pairs={{48,0},{64,16},{80,32},{96,48},{112,64},{128,80},{144,96},{160,112... | collective-permute-start | bytes 1277960 | tf_op jit(solution)/shard_map/ppermute | solution.py:240
  14.3 28.8 %collective-permute-start.2 = (bf16[208,1024]{1,0:T(8,128)(2,1)}, bf16[208,1024]{1,0:T(8,128)(2,1)S(1)}, u32[]{:S(2)}, u32[]{:S(2)}) collective-permute-start(bf16[208,1024]{1,0:T(8,128)(2,1)} %normalize_pack.1.refs_0_.refs_6_), channel_id=1, source_target_pairs={{0,6},{2,0},{4,2},{6,4},{1,3},{3,5},{5,7},{7,1},{8,14},{10,8},{12,... | collective-permute-start | bytes 1277960 | tf_op jit(solution)/shard_map/ppermute | solution.py:250
  16.7 32.0 %collective-permute-start = (bf16[208,1024]{1,0:T(8,128)(2,1)}, bf16[208,1024]{1,0:T(8,128)(2,1)S(1)}, u32[]{:S(2)}, u32[]{:S(2)}) collective-permute-start(bf16[208,1024]{1,0:T(8,128)(2,1)} %normalize_pack.1.refs_0_.refs_6_), channel_id=1, source_target_pairs={{0,8},{8,0},{1,9},{9,1},{2,10},{10,2},{3,11},{11,3},{4,12},{12,4},... | collective-permute-start | bytes 1277960 | tf_op jit(solution)/shard_map/ppermute | solution.py:244
  25.8 22.8 %collective-permute-start.3 = (bf16[208,1024]{1,0:T(8,128)(2,1)S(1)}, bf16[208,1024]{1,0:T(8,128)(2,1)S(1)}, u32[]{:S(2)}, u32[]{:S(2)}) collective-permute-start(bf16[208,1024]{1,0:T(8,128)(2,1)S(1)} %collective-permute-done.1.refs_1_.refs_2_), channel_id=1, source_target_pairs={{0,2},{2,4},{4,6},{6,0},{1,7},{3,1},{5,3},{7,5},{8,10},{10,12},{12... | collective-permute-start | bytes 1277960 | tf_op jit(solution)/shard_map/ppermute | solution.py:250
  31.0 24.4 %collective-permute-start.7 = (bf16[208,1024]{1,0:T(8,128)(2,1)}, bf16[208,1024]{1,0:T(8,128)(2,1)}, u32[]{:S(2)}, u32[]{:S(2)}) collective-permute-start(bf16[208,1024]{1,0:T(8,128)(2,1)} %normalize_pack.1.refs_0_.refs_6_), channel_id=1, source_target_pairs={{0,16},{16,32},{32,48},{48,64},{64,80},{80,96},{96,112},{112,128},... | collective-permute-start | bytes 1277960 | tf_op jit(solution)/shard_map/ppermute | solution.py:240
  41.2 22.3 %collective-permute-start.12 = (bf16[2,208,1024]{2,1,0:T(8,128)(2,1)S(1)}, bf16[2,208,1024]{2,1,0:T(8,128)(2,1)}, u32[]{:S(2)}, u32[]{:S(2)}) collective-permute-start(bf16[2,208,1024]{2,1,0:T(8,128)(2,1)S(1)} %stack_blocks.1.refs_8_), channel_id=1, source_target_pairs={{0,1},{1,0},{2,3},{3,2},{4,5},{5,4},{6,7},{7,6},{8,9},{9,8},{10,11... | collective-permute-start | bytes 2555912 | tf_op jit(solution)/shard_map/ppermute | solution.py:244
  49.5 11.8 %collective-permute-start.5 = (bf16[208,1024]{1,0:T(8,128)(2,1)}, bf16[208,1024]{1,0:T(8,128)(2,1)}, u32[]{:S(2)}, u32[]{:S(2)}) collective-permute-start(bf16[208,1024]{1,0:T(8,128)(2,1)} %gate.1.refs_1_), channel_id=1, source_target_pairs={{0,2},{2,4},{4,6},{6,0},{1,7},{3,1},{5,3},{7,5},{8,10},{10,12},{12... | collective-permute-start | bytes 1277960 | tf_op jit(solution)/shard_map/ppermute | solution.py:250
  52.9 10.6 %collective-permute-start.10 = (bf16[208,1024]{1,0:T(8,128)(2,1)S(1)}, bf16[208,1024]{1,0:T(8,128)(2,1)}, u32[]{:S(2)}, u32[]{:S(2)}) collective-permute-start(bf16[208,1024]{1,0:T(8,128)(2,1)S(1)} %copy-done), channel_id=1, source_target_pairs={{0,1},{1,0},{2,3},{3,2},{4,5},{5,4},{6,7},{7,6},{8,9},{9,8},{10,11... | collective-permute-start | bytes 1277960 | tf_op jit(solution)/shard_map/ppermute | solution.py:244
  55.4 8.1 %collective-permute-start.11 = (bf16[208,1024]{1,0:T(8,128)(2,1)}, bf16[208,1024]{1,0:T(8,128)(2,1)}, u32[]{:S(2)}, u32[]{:S(2)}) collective-permute-start(bf16[208,1024]{1,0:T(8,128)(2,1)} %collective-permute-done.7.refs_7_), channel_id=1, source_target_pairs={{0,1},{1,0},{2,3},{3,2},{4,5},{5,4},{6,7},{7,6},{8,9},{9,8},{10,11... | collective-permute-start | bytes 1277960 | tf_op jit(solution)/shard_map/ppermute | solution.py:244
  57.3 12.9 %collective-permute-start.4 = (bf16[208,1024]{1,0:T(8,128)(2,1)}, bf16[208,1024]{1,0:T(8,128)(2,1)S(1)}, u32[]{:S(2)}, u32[]{:S(2)}) collective-permute-start(bf16[208,1024]{1,0:T(8,128)(2,1)} %gate.1.refs_1_), channel_id=1, source_target_pairs={{0,6},{2,0},{4,2},{6,4},{1,3},{3,5},{5,7},{7,1},{8,14},{10,8},{12,... | collective-permute-start | bytes 1277960 | tf_op jit(solution)/shard_map/ppermute | solution.py:250
  61.3 10.7 %collective-permute-start.6 = (bf16[208,1024]{1,0:T(8,128)(2,1)}, bf16[208,1024]{1,0:T(8,128)(2,1)S(1)}, u32[]{:S(2)}, u32[]{:S(2)}) collective-permute-start(bf16[208,1024]{1,0:T(8,128)(2,1)} %collective-permute-done.5.refs_3_), channel_id=1, source_target_pairs={{0,2},{2,4},{4,6},{6,0},{1,7},{3,1},{5,3},{7,5},{8,10},{10,12},{12... | collective-permute-start | bytes 1277960 | tf_op jit(solution)/shard_map/ppermute | solution.py:250
  75.1 11.7 %collective-permute-start.13 = (f32[3,1,192]{2,1,0:T(1,128)S(1)}, f32[3,1,192]{2,1,0:T(1,128)S(1)}, u32[]{:S(2)}, u32[]{:S(2)}) collective-permute-start(f32[3,1,192]{2,1,0:T(1,128)S(1)} %get-tuple-element.20), channel_id=1, source_target_pairs={{0,1},{1,0},{2,3},{3,2},{4,5},{5,4},{6,7},{7,6},{8,9},{9,8},{10,11... | collective-permute-start | bytes 6920 | tf_op jit(solution)/shard_map/ppermute | solution.py:244
  77.1 22.3 %all-to-all-start = ((f32[8,1,192]{2,1,0:T(1,128)}), f32[8,1,192]{2,1,0:T(1,128)S(1)}, u32[]{:S(2)}, u32[]{:S(2)}) async-start(f32[8,1,192]{2,1,0:T(1,128)} %get-tuple-element.18), calls=%async_computation | async-start | bytes 16384 | tf_op jit(solution)/shard_map/all_to_all | solution.py:274
  86.8 12.7 %collective-permute-start.14 = (f32[1,192]{1,0:T(1,128)S(1)}, f32[1,192]{1,0:T(1,128)S(1)}, u32[]{:S(2)}, u32[]{:S(2)}) collective-permute-start(f32[1,192]{1,0:T(1,128)S(1)} %get-tuple-element.23), channel_id=1, source_target_pairs={{16,0},{32,16},{48,32},{64,48},{80,64},{96,80},{112,96},{128,112},... | collective-permute-start | bytes 2312 | tf_op jit(solution)/shard_map/ppermute | solution.py:240
  95.5 6.4 %collective-permute-start.15 = (f32[1,192]{1,0:T(1,128)S(1)}, f32[1,192]{1,0:T(1,128)S(1)}, u32[]{:S(2)}, u32[]{:S(2)}) collective-permute-start(f32[1,192]{1,0:T(1,128)S(1)} %get-tuple-element.22), channel_id=1, source_target_pairs={{32,0},{48,16},{64,32},{80,48},{96,64},{112,80},{128,96},{144,112}... | collective-permute-start | bytes 2312 | tf_op jit(solution)/shard_map/ppermute | solution.py:240
  97.4 9.4 %collective-permute-start.16 = (f32[1,192]{1,0:T(1,128)S(1)}, f32[1,192]{1,0:T(1,128)S(1)}, u32[]{:S(2)}, u32[]{:S(2)}) collective-permute-start(f32[1,192]{1,0:T(1,128)S(1)} %get-tuple-element.21), channel_id=1, source_target_pairs={{0,48},{16,64},{32,80},{48,96},{64,112},{80,128},{96,144},{112,160... | collective-permute-start | bytes 2312 | tf_op jit(solution)/shard_map/ppermute | solution.py:240

commit v8 on v7

--- a/solution.py
+++ b/solution.py
@@ -6,7 +6,7 @@
 from jax.sharding import Mesh, PartitionSpec as P
 
 ROWS = 192
-EXTRA = 16
+EXTRA = 8
 PACK = ROWS + EXTRA
 D = 1024
 X = 4
@@ -260,8 +260,9 @@
     ahead, behind = turn_x(block, 1), turn_x(block, -1)
     across = turn_x(ahead, 1)
     sib = swap(block, "core")
-    flipped = gate(swap(block, "zh"), ahead, behind, across)
-    flip_ahead, flip_behind = turn_x(flipped, 1), turn_x(flipped, -1)
+    flipped = half_flip(half_flip(block, count), count)
+    flip_ahead = turn_x(flipped, 1)
+    flip_behind = turn_x(gate(flipped, ahead, behind), -1)
     flip_across = turn_x(flip_ahead, 1)
     mine = (block, one, stack((two, three)))
     theirs = [sib] + [swap(value, "core") for value in mine[1:]]

time: 108 us -> 109 us (level)
  the two profiles are of different devices: /device:TPU:138 before, /device:TPU:66 now
where the time goes in v8:
time: 109 us; the launch traced here: 108 us
  starting transfers between devices  75.2 us (69%)
  waiting for transfers between devices  17.9 us (16%)
  Pallas kernels  12.1 us (11%)
  local copies, waits for them, and re-layouts  1.83 us (2%)
    ppermute x6, starting transfers between devices, shift(): return lax.ppermute(value, 'grp', pairs)  23.1 us
    ppermute x6, starting transfers between devices, turn_x(): return lax.ppermute(value, ('x', 'core'), pairs)  17.6 us
    ppermute x4, starting transfers between devices, swap(): return lax.ppermute(value, axis, [(0, 1), (1, 0)])  15 us
    ppermute x6, waiting for transfers between devices, shift(): return lax.ppermute(value, 'grp', pairs)  13.6 us
    ppermute x2, starting transfers between devices, half_flip(): return lax.ppermute(value, ('grp', 'zh', 'core'), pairs)  11.2 us
    all_to_all x1, starting transfers between devices, per_device(): best = jnp.max(lax.all_to_all(cols, ('zh', 'x'), 0, 0, tiled=True), axis=0)  8.3 us
    pallas_call x1, Pallas kernels, first_maxima(): pl.pallas_call(first_kernel, out_shape=(jax.ShapeDtypeStruct((2 * X, 1, R...  6.17 us
    ppermute x2, waiting for transfers between devices, half_flip(): return lax.ppermute(value, ('grp', 'zh', 'core'), pairs)  3.6 us
  transfers between devices with their start and end apart: 19, of which 5 were waited for; matrix products, arithmetic and copies ran while one was open for 0% of the time, Pallas kernels for 6%

profile of v8, /device:TPU:66, one launch (start us, length us, event | category | flops | bytes accessed | tf_op | source)
XLA Modules:
  0.0 108.0 jit_solution(7481252507204327836)
XLA Ops:
  0.0 2.0 %normalize_pack.1.refs_0_.refs_6_ = bf16[200,1024]{1,0:T(8,128)(2,1)} custom-call(bf16[192,1024]{1,0:T(8,128)(2,1)} %emb_any.1, s32[1,192]{1,0:T(1,128)} %bitcast.19, s32[1,192]{1,0:T(1,128)} %bitcast.20), custom_call_target="tpu_custom_call" | custom-call | flops 786432 | bytes 786432 | tf_op jit(solution)/shard_map/normalize_pack/pallas_call | solution.py:49
  2.0 0.0 copy-start
  2.0 6.2 %collective-permute-start = (bf16[200,1024]{1,0:T(8,128)(2,1)}, bf16[200,1024]{1,0:T(8,128)(2,1)S(1)}, u32[]{:S(2)}, u32[]{:S(2)}) collective-permute-start(bf16[200,1024]{1,0:T(8,128)(2,1)} %normalize_pack.1.refs_0_.refs_6_), channel_id=1, source_target_pairs={{0,256},{1,265},{8,264},{9,257},{16,272},{17,281},{24,280},{25,273... | collective-permute-start | bytes 1228808 | tf_op jit(solution)/shard_map/ppermute | solution.py:235
  8.2 6.0 %collective-permute-start.10 = (bf16[200,1024]{1,0:T(8,128)(2,1)}, bf16[200,1024]{1,0:T(8,128)(2,1)S(1)}, u32[]{:S(2)}, u32[]{:S(2)}) collective-permute-start(bf16[200,1024]{1,0:T(8,128)(2,1)} %normalize_pack.1.refs_0_.refs_6_), channel_id=1, source_target_pairs={{48,0},{64,16},{80,32},{96,48},{112,64},{128,80},{144,96},{160,112... | collective-permute-start | bytes 1228808 | tf_op jit(solution)/shard_map/ppermute | solution.py:240
  14.3 2.7 %collective-permute-start.9 = (bf16[200,1024]{1,0:T(8,128)(2,1)}, bf16[200,1024]{1,0:T(8,128)(2,1)S(1)}, u32[]{:S(2)}, u32[]{:S(2)}) collective-permute-start(bf16[200,1024]{1,0:T(8,128)(2,1)} %normalize_pack.1.refs_0_.refs_6_), channel_id=1, source_target_pairs={{0,32},{16,48},{32,64},{48,80},{64,96},{80,112},{96,128},{112,144}... | collective-permute-start | bytes 1228808 | tf_op jit(solution)/shard_map/ppermute | solution.py:240
  17.0 3.4 %collective-permute-start.2 = (bf16[200,1024]{1,0:T(8,128)(2,1)}, bf16[200,1024]{1,0:T(8,128)(2,1)S(1)}, u32[]{:S(2)}, u32[]{:S(2)}) collective-permute-start(bf16[200,1024]{1,0:T(8,128)(2,1)} %normalize_pack.1.refs_0_.refs_6_), channel_id=1, source_target_pairs={{0,2},{2,4},{4,6},{6,0},{1,7},{3,1},{5,3},{7,5},{8,10},{10,12},{12... | collective-permute-start | bytes 1228808 | tf_op jit(solution)/shard_map/ppermute | solution.py:250
  20.4 2.3 %collective-permute-done = bf16[200,1024]{1,0:T(8,128)(2,1)S(1)} collective-permute-done((bf16[200,1024]{1,0:T(8,128)(2,1)}, bf16[200,1024]{1,0:T(8,128)(2,1)S(1)}, u32[]{:S(2)}, u32[]{:S(2)}) %collective-permute-start) | collective-permute-done | bytes 409632 | tf_op jit(solution)/shard_map/ppermute | solution.py:235
  22.7 5.0 %collective-permute-start.1 = (bf16[200,1024]{1,0:T(8,128)(2,1)S(1)}, bf16[200,1024]{1,0:T(8,128)(2,1)S(1)}, u32[]{:S(2)}, u32[]{:S(2)}) collective-permute-start(bf16[200,1024]{1,0:T(8,128)(2,1)S(1)} %collective-permute-done), channel_id=1, source_target_pairs={{0,256},{1,265},{8,264},{9,257},{16,272},{17,281},{24,280},{25,273... | collective-permute-start | bytes 1228808 | tf_op jit(solution)/shard_map/ppermute | solution.py:235
  27.7 1.9 %collective-permute-start.8 = (bf16[200,1024]{1,0:T(8,128)(2,1)}, bf16[200,1024]{1,0:T(8,128)(2,1)}, u32[]{:S(2)}, u32[]{:S(2)}) collective-permute-start(bf16[200,1024]{1,0:T(8,128)(2,1)} %normalize_pack.1.refs_0_.refs_6_), channel_id=1, source_target_pairs={{0,16},{16,32},{32,48},{48,64},{64,80},{80,96},{96,112},{112,128},... | collective-permute-start | bytes 1228808 | tf_op jit(solution)/shard_map/ppermute | solution.py:240
  29.6 6.2 %collective-permute-done.10.refs_1_ = bf16[200,1024]{1,0:T(8,128)(2,1)S(1)} collective-permute-done((bf16[200,1024]{1,0:T(8,128)(2,1)}, bf16[200,1024]{1,0:T(8,128)(2,1)S(1)}, u32[]{:S(2)}, u32[]{:S(2)}) %collective-permute-start.10) | collective-permute-done | bytes 409632 | tf_op jit(solution)/shard_map/ppermute | solution.py:240
  35.8 2.4 %collective-permute-start.3 = (bf16[200,1024]{1,0:T(8,128)(2,1)}, bf16[200,1024]{1,0:T(8,128)(2,1)S(1)}, u32[]{:S(2)}, u32[]{:S(2)}) collective-permute-start(bf16[200,1024]{1,0:T(8,128)(2,1)} %normalize_pack.1.refs_0_.refs_6_), channel_id=1, source_target_pairs={{0,6},{2,0},{4,2},{6,4},{1,3},{3,5},{5,7},{7,1},{8,14},{10,8},{12,... | collective-permute-start | bytes 1228808 | tf_op jit(solution)/shard_map/ppermute | solution.py:250
  38.3 0.0 collective-permute-done.9.refs_0_
  38.3 0.1 stack_blocks.1.refs_8_
  38.3 9.0 %collective-permute-start.13 = (bf16[2,200,1024]{2,1,0:T(8,128)(2,1)S(1)}, bf16[2,200,1024]{2,1,0:T(8,128)(2,1)}, u32[]{:S(2)}, u32[]{:S(2)}) collective-permute-start(bf16[2,200,1024]{2,1,0:T(8,128)(2,1)S(1)} %stack_blocks.1.refs_8_), channel_id=1, source_target_pairs={{0,1},{1,0},{2,3},{3,2},{4,5},{5,4},{6,7},{7,6},{8,9},{9,8},{10,11... | collective-permute-start | bytes 2457608 | tf_op jit(solution)/shard_map/ppermute | solution.py:244
  47.3 0.0 collective-permute-done.2.refs_1_.refs_2_
  47.3 1.9 %collective-permute-start.11 = (bf16[200,1024]{1,0:T(8,128)(2,1)}, bf16[200,1024]{1,0:T(8,128)(2,1)S(1)}, u32[]{:S(2)}, u32[]{:S(2)}) collective-permute-start(bf16[200,1024]{1,0:T(8,128)(2,1)} %normalize_pack.1.refs_0_.refs_6_), channel_id=1, source_target_pairs={{0,1},{1,0},{2,3},{3,2},{4,5},{5,4},{6,7},{7,6},{8,9},{9,8},{10,11... | collective-permute-start | bytes 1228808 | tf_op jit(solution)/shard_map/ppermute | solution.py:244
  49.3 1.3 %collective-permute-done.1.refs_0_.refs_1_ = bf16[200,1024]{1,0:T(8,128)(2,1)S(1)} collective-permute-done((bf16[200,1024]{1,0:T(8,128)(2,1)S(1)}, bf16[200,1024]{1,0:T(8,128)(2,1)S(1)}, u32[]{:S(2)}, u32[]{:S(2)}) %collective-permute-start.1) | collective-permute-done | bytes 409632 | tf_op jit(solution)/shard_map/ppermute | solution.py:235
  50.6 2.9 %collective-permute-start.5 = (bf16[200,1024]{1,0:T(8,128)(2,1)S(1)}, bf16[200,1024]{1,0:T(8,128)(2,1)}, u32[]{:S(2)}, u32[]{:S(2)}) collective-permute-start(bf16[200,1024]{1,0:T(8,128)(2,1)S(1)} %collective-permute-done.1.refs_0_.refs_1_), channel_id=1, source_target_pairs={{0,2},{2,4},{4,6},{6,0},{1,7},{3,1},{5,3},{7,5},{8,10},{10,12},{12... | collective-permute-start | bytes 1228808 | tf_op jit(solution)/shard_map/ppermute | solution.py:250
  53.4 0.0 collective-permute-done.8.refs_7_
  53.5 3.0 %collective-permute-start.7 = (bf16[200,1024]{1,0:T(8,128)(2,1)S(1)}, bf16[200,1024]{1,0:T(8,128)(2,1)}, u32[]{:S(2)}, u32[]{:S(2)}) collective-permute-start(bf16[200,1024]{1,0:T(8,128)(2,1)S(1)} %collective-permute-done.2.refs_1_.refs_2_), channel_id=1, source_target_pairs={{0,2},{2,4},{4,6},{6,0},{1,7},{3,1},{5,3},{7,5},{8,10},{10,12},{12... | collective-permute-start | bytes 1228808 | tf_op jit(solution)/shard_map/ppermute | solution.py:250
  56.5 0.0 collective-permute-done.3.refs_2_.refs_4_
  56.5 1.9 %collective-permute-start.12 = (bf16[200,1024]{1,0:T(8,128)(2,1)}, bf16[200,1024]{1,0:T(8,128)(2,1)}, u32[]{:S(2)}, u32[]{:S(2)}) collective-permute-start(bf16[200,1024]{1,0:T(8,128)(2,1)} %collective-permute-done.8.refs_7_), channel_id=1, source_target_pairs={{0,1},{1,0},{2,3},{3,2},{4,5},{5,4},{6,7},{7,6},{8,9},{9,8},{10,11... | collective-permute-start | bytes 1228808 | tf_op jit(solution)/shard_map/ppermute | solution.py:244
  58.4 0.8 gate.1
  59.2 0.0 collective-permute-done.11.refs_9_
  59.2 0.7 copy-done.1
  60.0 2.8 %collective-permute-start.4 = (bf16[200,1024]{1,0:T(8,128)(2,1)}, bf16[200,1024]{1,0:T(8,128)(2,1)S(1)}, u32[]{:S(2)}, u32[]{:S(2)}) collective-permute-start(bf16[200,1024]{1,0:T(8,128)(2,1)} %gate.1), channel_id=1, source_target_pairs={{0,6},{2,0},{4,2},{6,4},{1,3},{3,5},{5,7},{7,1},{8,14},{10,8},{12,... | collective-permute-start | bytes 1228808 | tf_op jit(solution)/shard_map/ppermute | solution.py:250
  62.8 0.0 collective-permute-done.5.refs_3_
  62.8 3.0 %collective-permute-start.6 = (bf16[200,1024]{1,0:T(8,128)(2,1)}, bf16[200,1024]{1,0:T(8,128)(2,1)S(1)}, u32[]{:S(2)}, u32[]{:S(2)}) collective-permute-start(bf16[200,1024]{1,0:T(8,128)(2,1)} %collective-permute-done.5.refs_3_), channel_id=1, source_target_pairs={{0,2},{2,4},{4,6},{6,0},{1,7},{3,1},{5,3},{7,5},{8,10},{10,12},{12... | collective-permute-start | bytes 1228808 | tf_op jit(solution)/shard_map/ppermute | solution.py:250
  65.9 0.1 stack.35.place_ref
  66.0 0.0 collective-permute-done.7.refs_5_
  66.0 0.0 collective-permute-done.12.refs_10_
  66.0 0.0 collective-permute-done.13.refs_11_
  66.0 1.0 copy-done.2
  67.0 6.2 %first_maxima.1 = (f32[8,1,192]{2,1,0:T(1,128)S(1)}, f32[1152,128]{1,0:T(8,128)S(1)}, bf16[1536,1024]{1,0:T(8,128)(2,1)S(1)}, f32[1536,128]{1,0:T(8,128)S(1)}, f32[6,1,192]{2,1,0:T(1,128)S(1)}) custom-call(s32[8]{0:T(128)S(1)} %stack.35.place_ref, bf16[200,1024]{1,0:T(8,128)(2,1)S(1)} %copy-done, ...), custom_call_target="tpu_custom_call" | custom-call | flops 3623878656 | bytes 5734400 | tf_op jit(solution)/shard_map/first_maxima/pallas_call | solution.py:192
  73.2 0.0 collective-permute-done.4.refs_0_
  73.2 0.7 collective-permute-done.6.refs_1_
  73.9 3.1 %last_maxima.1 = (f32[8,1,192]{2,1,0:T(1,128)}, f32[3,1,192]{2,1,0:T(1,128)S(1)}, f32[3,1,192]{2,1,0:T(1,128)S(1)}) custom-call(s32[8]{0:T(128)S(1)} %stack.35.place_ref, bf16[200,1024]{1,0:T(8,128)(2,1)S(1)} %collective-permute-done.4.refs_0_, bf16[200,1024]{1,0:T(8,128)(2,1)S(1)} %collective-permute-done.6.refs_1_, ...), custom_call_target="tpu_custom_call" | custom-call | flops 1207959552 | bytes 4096000 | tf_op jit(solution)/shard_map/last_maxima/pallas_call | solution.py:214
  77.1 2.2 %collective-permute-start.14 = (f32[3,1,192]{2,1,0:T(1,128)S(1)}, f32[3,1,192]{2,1,0:T(1,128)S(1)}, u32[]{:S(2)}, u32[]{:S(2)}) collective-permute-start(f32[3,1,192]{2,1,0:T(1,128)S(1)} %get-tuple-element.20), channel_id=1, source_target_pairs={{0,1},{1,0},{2,3},{3,2},{4,5},{5,4},{6,7},{7,6},{8,9},{9,8},{10,11... | collective-permute-start | bytes 6920 | tf_op jit(solution)/shard_map/ppermute | solution.py:244
  79.3 8.3 %all-to-all-start = ((f32[8,1,192]{2,1,0:T(1,128)}), f32[8,1,192]{2,1,0:T(1,128)S(1)}, u32[]{:S(2)}, u32[]{:S(2)}) async-start(f32[8,1,192]{2,1,0:T(1,128)} %get-tuple-element.18), calls=%async_computation | async-start | bytes 16384 | tf_op jit(solution)/shard_map/all_to_all | solution.py:275
  87.6 0.0 collective-permute-done.14
  87.6 5.0 %collective-permute-start.15 = (f32[1,192]{1,0:T(1,128)S(1)}, f32[1,192]{1,0:T(1,128)S(1)}, u32[]{:S(2)}, u32[]{:S(2)}) collective-permute-start(f32[1,192]{1,0:T(1,128)S(1)} %get-tuple-element.23), channel_id=1, source_target_pairs={{16,0},{32,16},{48,32},{64,48},{80,64},{96,80},{112,96},{128,112},... | collective-permute-start | bytes 2312 | tf_op jit(solution)/shard_map/ppermute | solution.py:240
  92.6 5.5 %collective-permute-start.16 = (f32[1,192]{1,0:T(1,128)S(1)}, f32[1,192]{1,0:T(1,128)S(1)}, u32[]{:S(2)}, u32[]{:S(2)}) collective-permute-start(f32[1,192]{1,0:T(1,128)S(1)} %get-tuple-element.22), channel_id=1, source_target_pairs={{32,0},{48,16},{64,32},{80,48},{96,64},{112,80},{128,96},{144,112}... | collective-permute-start | bytes 2312 | tf_op jit(solution)/shard_map/ppermute | solution.py:240
  98.1 1.9 %collective-permute-start.17 = (f32[1,192]{1,0:T(1,128)S(1)}, f32[1,192]{1,0:T(1,128)S(1)}, u32[]{:S(2)}, u32[]{:S(2)}) collective-permute-start(f32[1,192]{1,0:T(1,128)S(1)} %get-tuple-element.21), channel_id=1, source_target_pairs={{0,48},{16,64},{32,80},{48,96},{64,112},{80,128},{96,144},{112,160... | collective-permute-start | bytes 2312 | tf_op jit(solution)/shard_map/ppermute | solution.py:240
  100.0 0.0 all-to-all-done
  100.1 0.0 collective-permute-done.15
  100.1 0.0 collective-permute-done.16
  100.1 7.4 %collective-permute-done.17 = f32[1,192]{1,0:T(1,128)S(1)} collective-permute-done((f32[1,192]{1,0:T(1,128)S(1)}, f32[1,192]{1,0:T(1,128)S(1)}, u32[]{:S(2)}, u32[]{:S(2)}) %collective-permute-start.17) | collective-permute-done | bytes 800 | tf_op jit(solution)/shard_map/ppermute | solution.py:240
  107.4 0.6 fusion.2
  (6 shorter events, 0.0 us)
Async XLA Ops:
  2.0 64.0 %copy-start = (bf16[200,1024]{1,0:T(8,128)(2,1)S(1)}, bf16[200,1024]{1,0:T(8,128)(2,1)}, u32[]{:S(2)}) copy-start(bf16[200,1024]{1,0:T(8,128)(2,1)} %normalize_pack.1.refs_0_.refs_6_) | copy-start | bytes 1228804
  2.0 20.7 %collective-permute-start = (bf16[200,1024]{1,0:T(8,128)(2,1)}, bf16[200,1024]{1,0:T(8,128)(2,1)S(1)}, u32[]{:S(2)}, u32[]{:S(2)}) collective-permute-start(bf16[200,1024]{1,0:T(8,128)(2,1)} %normalize_pack.1.refs_0_.refs_6_), channel_id=1, source_target_pairs={{0,256},{1,265},{8,264},{9,257},{16,272},{17,281},{24,280},{25,273... | collective-permute-start | bytes 1228808 | tf_op jit(solution)/shard_map/ppermute | solution.py:235
  8.2 27.6 %collective-permute-start.10 = (bf16[200,1024]{1,0:T(8,128)(2,1)}, bf16[200,1024]{1,0:T(8,128)(2,1)S(1)}, u32[]{:S(2)}, u32[]{:S(2)}) collective-permute-start(bf16[200,1024]{1,0:T(8,128)(2,1)} %normalize_pack.1.refs_0_.refs_6_), channel_id=1, source_target_pairs={{48,0},{64,16},{80,32},{96,48},{112,64},{128,80},{144,96},{160,112... | collective-permute-start | bytes 1228808 | tf_op jit(solution)/shard_map/ppermute | solution.py:240
  14.3 24.0 %collective-permute-start.9 = (bf16[200,1024]{1,0:T(8,128)(2,1)}, bf16[200,1024]{1,0:T(8,128)(2,1)S(1)}, u32[]{:S(2)}, u32[]{:S(2)}) collective-permute-start(bf16[200,1024]{1,0:T(8,128)(2,1)} %normalize_pack.1.refs_0_.refs_6_), channel_id=1, source_target_pairs={{0,32},{16,48},{32,64},{48,80},{64,96},{80,112},{96,128},{112,144}... | collective-permute-start | bytes 1228808 | tf_op jit(solution)/shard_map/ppermute | solution.py:240
  17.0 30.3 %collective-permute-start.2 = (bf16[200,1024]{1,0:T(8,128)(2,1)}, bf16[200,1024]{1,0:T(8,128)(2,1)S(1)}, u32[]{:S(2)}, u32[]{:S(2)}) collective-permute-start(bf16[200,1024]{1,0:T(8,128)(2,1)} %normalize_pack.1.refs_0_.refs_6_), channel_id=1, source_target_pairs={{0,2},{2,4},{4,6},{6,0},{1,7},{3,1},{5,3},{7,5},{8,10},{10,12},{12... | collective-permute-start | bytes 1228808 | tf_op jit(solution)/shard_map/ppermute | solution.py:250
  22.7 27.9 %collective-permute-start.1 = (bf16[200,1024]{1,0:T(8,128)(2,1)S(1)}, bf16[200,1024]{1,0:T(8,128)(2,1)S(1)}, u32[]{:S(2)}, u32[]{:S(2)}) collective-permute-start(bf16[200,1024]{1,0:T(8,128)(2,1)S(1)} %collective-permute-done), channel_id=1, source_target_pairs={{0,256},{1,265},{8,264},{9,257},{16,272},{17,281},{24,280},{25,273... | collective-permute-start | bytes 1228808 | tf_op jit(solution)/shard_map/ppermute | solution.py:235
  27.7 25.7 %collective-permute-start.8 = (bf16[200,1024]{1,0:T(8,128)(2,1)}, bf16[200,1024]{1,0:T(8,128)(2,1)}, u32[]{:S(2)}, u32[]{:S(2)}) collective-permute-start(bf16[200,1024]{1,0:T(8,128)(2,1)} %normalize_pack.1.refs_0_.refs_6_), channel_id=1, source_target_pairs={{0,16},{16,32},{32,48},{48,64},{64,80},{80,96},{96,112},{112,128},... | collective-permute-start | bytes 1228808 | tf_op jit(solution)/shard_map/ppermute | solution.py:240
  35.8 20.7 %collective-permute-start.3 = (bf16[200,1024]{1,0:T(8,128)(2,1)}, bf16[200,1024]{1,0:T(8,128)(2,1)S(1)}, u32[]{:S(2)}, u32[]{:S(2)}) collective-permute-start(bf16[200,1024]{1,0:T(8,128)(2,1)} %normalize_pack.1.refs_0_.refs_6_), channel_id=1, source_target_pairs={{0,6},{2,0},{4,2},{6,4},{1,3},{3,5},{5,7},{7,1},{8,14},{10,8},{12,... | collective-permute-start | bytes 1228808 | tf_op jit(solution)/shard_map/ppermute | solution.py:250
  38.3 27.7 %collective-permute-start.13 = (bf16[2,200,1024]{2,1,0:T(8,128)(2,1)S(1)}, bf16[2,200,1024]{2,1,0:T(8,128)(2,1)}, u32[]{:S(2)}, u32[]{:S(2)}) collective-permute-start(bf16[2,200,1024]{2,1,0:T(8,128)(2,1)S(1)} %stack_blocks.1.refs_8_), channel_id=1, source_target_pairs={{0,1},{1,0},{2,3},{3,2},{4,5},{5,4},{6,7},{7,6},{8,9},{9,8},{10,11... | collective-permute-start | bytes 2457608 | tf_op jit(solution)/shard_map/ppermute | solution.py:244
  47.3 11.9 %collective-permute-start.11 = (bf16[200,1024]{1,0:T(8,128)(2,1)}, bf16[200,1024]{1,0:T(8,128)(2,1)S(1)}, u32[]{:S(2)}, u32[]{:S(2)}) collective-permute-start(bf16[200,1024]{1,0:T(8,128)(2,1)} %normalize_pack.1.refs_0_.refs_6_), channel_id=1, source_target_pairs={{0,1},{1,0},{2,3},{3,2},{4,5},{5,4},{6,7},{7,6},{8,9},{9,8},{10,11... | collective-permute-start | bytes 1228808 | tf_op jit(solution)/shard_map/ppermute | solution.py:244
  50.6 12.2 %collective-permute-start.5 = (bf16[200,1024]{1,0:T(8,128)(2,1)S(1)}, bf16[200,1024]{1,0:T(8,128)(2,1)}, u32[]{:S(2)}, u32[]{:S(2)}) collective-permute-start(bf16[200,1024]{1,0:T(8,128)(2,1)S(1)} %collective-permute-done.1.refs_0_.refs_1_), channel_id=1, source_target_pairs={{0,2},{2,4},{4,6},{6,0},{1,7},{3,1},{5,3},{7,5},{8,10},{10,12},{12... | collective-permute-start | bytes 1228808 | tf_op jit(solution)/shard_map/ppermute | solution.py:250
  53.5 12.5 %collective-permute-start.7 = (bf16[200,1024]{1,0:T(8,128)(2,1)S(1)}, bf16[200,1024]{1,0:T(8,128)(2,1)}, u32[]{:S(2)}, u32[]{:S(2)}) collective-permute-start(bf16[200,1024]{1,0:T(8,128)(2,1)S(1)} %collective-permute-done.2.refs_1_.refs_2_), channel_id=1, source_target_pairs={{0,2},{2,4},{4,6},{6,0},{1,7},{3,1},{5,3},{7,5},{8,10},{10,12},{12... | collective-permute-start | bytes 1228808 | tf_op jit(solution)/shard_map/ppermute | solution.py:250
  56.5 9.5 %collective-permute-start.12 = (bf16[200,1024]{1,0:T(8,128)(2,1)}, bf16[200,1024]{1,0:T(8,128)(2,1)}, u32[]{:S(2)}, u32[]{:S(2)}) collective-permute-start(bf16[200,1024]{1,0:T(8,128)(2,1)} %collective-permute-done.8.refs_7_), channel_id=1, source_target_pairs={{0,1},{1,0},{2,3},{3,2},{4,5},{5,4},{6,7},{7,6},{8,9},{9,8},{10,11... | collective-permute-start | bytes 1228808 | tf_op jit(solution)/shard_map/ppermute | solution.py:244
  59.2 0.7 copy-start.1
  60.0 13.2 %collective-permute-start.4 = (bf16[200,1024]{1,0:T(8,128)(2,1)}, bf16[200,1024]{1,0:T(8,128)(2,1)S(1)}, u32[]{:S(2)}, u32[]{:S(2)}) collective-permute-start(bf16[200,1024]{1,0:T(8,128)(2,1)} %gate.1), channel_id=1, source_target_pairs={{0,6},{2,0},{4,2},{6,4},{1,3},{3,5},{5,7},{7,1},{8,14},{10,8},{12,... | collective-permute-start | bytes 1228808 | tf_op jit(solution)/shard_map/ppermute | solution.py:250
  62.8 11.2 %collective-permute-start.6 = (bf16[200,1024]{1,0:T(8,128)(2,1)}, bf16[200,1024]{1,0:T(8,128)(2,1)S(1)}, u32[]{:S(2)}, u32[]{:S(2)}) collective-permute-start(bf16[200,1024]{1,0:T(8,128)(2,1)} %collective-permute-done.5.refs_3_), channel_id=1, source_target_pairs={{0,2},{2,4},{4,6},{6,0},{1,7},{3,1},{5,3},{7,5},{8,10},{10,12},{12... | collective-permute-start | bytes 1228808 | tf_op jit(solution)/shard_map/ppermute | solution.py:250
  66.0 1.0 copy-start.2
  77.1 10.5 %collective-permute-start.14 = (f32[3,1,192]{2,1,0:T(1,128)S(1)}, f32[3,1,192]{2,1,0:T(1,128)S(1)}, u32[]{:S(2)}, u32[]{:S(2)}) collective-permute-start(f32[3,1,192]{2,1,0:T(1,128)S(1)} %get-tuple-element.20), channel_id=1, source_target_pairs={{0,1},{1,0},{2,3},{3,2},{4,5},{5,4},{6,7},{7,6},{8,9},{9,8},{10,11... | collective-permute-start | bytes 6920 | tf_op jit(solution)/shard_map/ppermute | solution.py:244
  79.3 20.8 %all-to-all-start = ((f32[8,1,192]{2,1,0:T(1,128)}), f32[8,1,192]{2,1,0:T(1,128)S(1)}, u32[]{:S(2)}, u32[]{:S(2)}) async-start(f32[8,1,192]{2,1,0:T(1,128)} %get-tuple-element.18), calls=%async_computation | async-start | bytes 16384 | tf_op jit(solution)/shard_map/all_to_all | solution.py:275
  87.6 12.5 %collective-permute-start.15 = (f32[1,192]{1,0:T(1,128)S(1)}, f32[1,192]{1,0:T(1,128)S(1)}, u32[]{:S(2)}, u32[]{:S(2)}) collective-permute-start(f32[1,192]{1,0:T(1,128)S(1)} %get-tuple-element.23), channel_id=1, source_target_pairs={{16,0},{32,16},{48,32},{64,48},{80,64},{96,80},{112,96},{128,112},... | collective-permute-start | bytes 2312 | tf_op jit(solution)/shard_map/ppermute | solution.py:240
  92.6 7.5 %collective-permute-start.16 = (f32[1,192]{1,0:T(1,128)S(1)}, f32[1,192]{1,0:T(1,128)S(1)}, u32[]{:S(2)}, u32[]{:S(2)}) collective-permute-start(f32[1,192]{1,0:T(1,128)S(1)} %get-tuple-element.22), channel_id=1, source_target_pairs={{32,0},{48,16},{64,32},{80,48},{96,64},{112,80},{128,96},{144,112}... | collective-permute-start | bytes 2312 | tf_op jit(solution)/shard_map/ppermute | solution.py:240
  98.1 9.4 %collective-permute-start.17 = (f32[1,192]{1,0:T(1,128)S(1)}, f32[1,192]{1,0:T(1,128)S(1)}, u32[]{:S(2)}, u32[]{:S(2)}) collective-permute-start(f32[1,192]{1,0:T(1,128)S(1)} %get-tuple-element.21), channel_id=1, source_target_pairs={{0,48},{16,64},{32,80},{48,96},{64,112},{80,128},{96,144},{112,160... | collective-permute-start | bytes 2312 | tf_op jit(solution)/shard_map/ppermute | solution.py:240

commit v9 on v8

--- a/solution.py
+++ b/solution.py
@@ -260,9 +260,9 @@
     ahead, behind = turn_x(block, 1), turn_x(block, -1)
     across = turn_x(ahead, 1)
     sib = swap(block, "core")
-    flipped = half_flip(half_flip(block, count), count)
+    flipped = gate(swap(block, "zh"), ahead)
     flip_ahead = turn_x(flipped, 1)
-    flip_behind = turn_x(gate(flipped, ahead, behind), -1)
+    flip_behind = turn_x(gate(flipped, across, behind), -1)
     flip_across = turn_x(flip_ahead, 1)
     mine = (block, one, stack((two, three)))
     theirs = [sib] + [swap(value, "core") for value in mine[1:]]

time: 109 us -> 105 us (0.963)
  the two profiles are of different devices: /device:TPU:66 before, /device:TPU:74 now
where the time goes in v9:
time: 105 us; the launch traced here: 104 us
  starting transfers between devices  74.2 us (71%)
  waiting for transfers between devices  15.6 us (15%)
  Pallas kernels  12.2 us (12%)
  local copies, waits for them, and re-layouts  1.09 us (1%)
    ppermute x6, starting transfers between devices, shift(): return lax.ppermute(value, 'grp', pairs)  24 us
    ppermute x5, starting transfers between devices, swap(): return lax.ppermute(value, axis, [(0, 1), (1, 0)])  18.5 us
    ppermute x6, starting transfers between devices, turn_x(): return lax.ppermute(value, ('x', 'core'), pairs)  18.2 us
    ppermute x6, waiting for transfers between devices, shift(): return lax.ppermute(value, 'grp', pairs)  14.9 us
    all_to_all x1, starting transfers between devices, per_device(): best = jnp.max(lax.all_to_all(cols, ('zh', 'x'), 0, 0, tiled=True), axis=0)  13.4 us
    pallas_call x1, Pallas kernels, first_maxima(): pl.pallas_call(first_kernel, out_shape=(jax.ShapeDtypeStruct((2 * X, 1, R...  6.17 us
    pallas_call x1, Pallas kernels, last_maxima(): pl.pallas_call(last_kernel, out_shape=(jax.ShapeDtypeStruct((2 * X, 1, RO...  3.12 us
  transfers between devices with their start and end apart: 18, of which 3 were waited for; matrix products, arithmetic and copies ran while one was open for 0% of the time, Pallas kernels for 7%

profile of v9, /device:TPU:74, one launch (start us, length us, event | category | flops | bytes accessed | tf_op | source)
XLA Modules:
  0.0 104.0 jit_solution(13731837204664971020)
XLA Ops:
  0.0 2.0 %normalize_pack.1.refs_0_.refs_6_ = bf16[200,1024]{1,0:T(8,128)(2,1)} custom-call(bf16[192,1024]{1,0:T(8,128)(2,1)} %emb_any.1, s32[1,192]{1,0:T(1,128)} %bitcast.19, s32[1,192]{1,0:T(1,128)} %bitcast.20), custom_call_target="tpu_custom_call" | custom-call | flops 786432 | bytes 786432 | tf_op jit(solution)/shard_map/normalize_pack/pallas_call | solution.py:49
  2.0 0.0 copy-start
  2.0 4.6 %collective-permute-start.8 = (bf16[200,1024]{1,0:T(8,128)(2,1)}, bf16[200,1024]{1,0:T(8,128)(2,1)S(1)}, u32[]{:S(2)}, u32[]{:S(2)}) collective-permute-start(bf16[200,1024]{1,0:T(8,128)(2,1)} %normalize_pack.1.refs_0_.refs_6_), channel_id=1, source_target_pairs={{0,32},{16,48},{32,64},{48,80},{64,96},{80,112},{96,128},{112,144}... | collective-permute-start | bytes 1228808 | tf_op jit(solution)/shard_map/ppermute | solution.py:240
  6.6 4.2 %collective-permute-start.9 = (bf16[200,1024]{1,0:T(8,128)(2,1)}, bf16[200,1024]{1,0:T(8,128)(2,1)S(1)}, u32[]{:S(2)}, u32[]{:S(2)}) collective-permute-start(bf16[200,1024]{1,0:T(8,128)(2,1)} %normalize_pack.1.refs_0_.refs_6_), channel_id=1, source_target_pairs={{48,0},{64,16},{80,32},{96,48},{112,64},{128,80},{144,96},{160,112... | collective-permute-start | bytes 1228808 | tf_op jit(solution)/shard_map/ppermute | solution.py:240
  10.9 3.4 %collective-permute-start.1 = (bf16[200,1024]{1,0:T(8,128)(2,1)}, bf16[200,1024]{1,0:T(8,128)(2,1)S(1)}, u32[]{:S(2)}, u32[]{:S(2)}) collective-permute-start(bf16[200,1024]{1,0:T(8,128)(2,1)} %normalize_pack.1.refs_0_.refs_6_), channel_id=1, source_target_pairs={{0,2},{2,4},{4,6},{6,0},{1,7},{3,1},{5,3},{7,5},{8,10},{10,12},{12... | collective-permute-start | bytes 1228808 | tf_op jit(solution)/shard_map/ppermute | solution.py:250
  14.3 10.0 %collective-permute-start = (bf16[200,1024]{1,0:T(8,128)(2,1)}, bf16[200,1024]{1,0:T(8,128)(2,1)S(1)}, u32[]{:S(2)}, u32[]{:S(2)}) collective-permute-start(bf16[200,1024]{1,0:T(8,128)(2,1)} %normalize_pack.1.refs_0_.refs_6_), channel_id=1, source_target_pairs={{0,8},{8,0},{1,9},{9,1},{2,10},{10,2},{3,11},{11,3},{4,12},{12,4},... | collective-permute-start | bytes 1228808 | tf_op jit(solution)/shard_map/ppermute | solution.py:244
  24.3 3.5 %collective-permute-start.7 = (bf16[200,1024]{1,0:T(8,128)(2,1)}, bf16[200,1024]{1,0:T(8,128)(2,1)}, u32[]{:S(2)}, u32[]{:S(2)}) collective-permute-start(bf16[200,1024]{1,0:T(8,128)(2,1)} %normalize_pack.1.refs_0_.refs_6_), channel_id=1, source_target_pairs={{0,16},{16,32},{32,48},{48,64},{64,80},{80,96},{96,112},{112,128},... | collective-permute-start | bytes 1228808 | tf_op jit(solution)/shard_map/ppermute | solution.py:240
  27.8 0.0 collective-permute-done.8.refs_0_
  27.8 2.4 %collective-permute-start.3 = (bf16[200,1024]{1,0:T(8,128)(2,1)}, bf16[200,1024]{1,0:T(8,128)(2,1)S(1)}, u32[]{:S(2)}, u32[]{:S(2)}) collective-permute-start(bf16[200,1024]{1,0:T(8,128)(2,1)} %normalize_pack.1.refs_0_.refs_6_), channel_id=1, source_target_pairs={{0,6},{2,0},{4,2},{6,4},{1,3},{3,5},{5,7},{7,1},{8,14},{10,8},{12,... | collective-permute-start | bytes 1228808 | tf_op jit(solution)/shard_map/ppermute | solution.py:250
  30.3 7.7 %collective-permute-done.9.refs_1_ = bf16[200,1024]{1,0:T(8,128)(2,1)S(1)} collective-permute-done((bf16[200,1024]{1,0:T(8,128)(2,1)}, bf16[200,1024]{1,0:T(8,128)(2,1)S(1)}, u32[]{:S(2)}, u32[]{:S(2)}) %collective-permute-start.9) | collective-permute-done | bytes 409632 | tf_op jit(solution)/shard_map/ppermute | solution.py:240
  38.0 0.1 stack_blocks.1.refs_8_
  38.0 1.9 %collective-permute-start.12 = (bf16[2,200,1024]{2,1,0:T(8,128)(2,1)S(1)}, bf16[2,200,1024]{2,1,0:T(8,128)(2,1)}, u32[]{:S(2)}, u32[]{:S(2)}) collective-permute-start(bf16[2,200,1024]{2,1,0:T(8,128)(2,1)S(1)} %stack_blocks.1.refs_8_), channel_id=1, source_target_pairs={{0,1},{1,0},{2,3},{3,2},{4,5},{5,4},{6,7},{7,6},{8,9},{9,8},{10,11... | collective-permute-start | bytes 2457608 | tf_op jit(solution)/shard_map/ppermute | solution.py:244
  40.0 0.0 collective-permute-done.1.refs_1_.refs_2_
  40.0 3.4 %collective-permute-start.2 = (bf16[200,1024]{1,0:T(8,128)(2,1)S(1)}, bf16[200,1024]{1,0:T(8,128)(2,1)S(1)}, u32[]{:S(2)}, u32[]{:S(2)}) collective-permute-start(bf16[200,1024]{1,0:T(8,128)(2,1)S(1)} %collective-permute-done.1.refs_1_.refs_2_), channel_id=1, source_target_pairs={{0,2},{2,4},{4,6},{6,0},{1,7},{3,1},{5,3},{7,5},{8,10},{10,12},{12... | collective-permute-start | bytes 1228808 | tf_op jit(solution)/shard_map/ppermute | solution.py:250
  43.4 0.0 collective-permute-done.refs_0_
  43.4 3.1 %collective-permute-start.5 = (bf16[200,1024]{1,0:T(8,128)(2,1)S(1)}, bf16[200,1024]{1,0:T(8,128)(2,1)}, u32[]{:S(2)}, u32[]{:S(2)}) collective-permute-start(bf16[200,1024]{1,0:T(8,128)(2,1)S(1)} %gate.2.refs_0_.refs_1_), channel_id=1, source_target_pairs={{0,2},{2,4},{4,6},{6,0},{1,7},{3,1},{5,3},{7,5},{8,10},{10,12},{12... | collective-permute-start | bytes 1228808 | tf_op jit(solution)/shard_map/ppermute | solution.py:250
  46.5 0.0 collective-permute-done.7.refs_7_
  46.5 2.5 %collective-permute-start.10 = (bf16[200,1024]{1,0:T(8,128)(2,1)}, bf16[200,1024]{1,0:T(8,128)(2,1)}, u32[]{:S(2)}, u32[]{:S(2)}) collective-permute-start(bf16[200,1024]{1,0:T(8,128)(2,1)} %normalize_pack.1.refs_0_.refs_6_), channel_id=1, source_target_pairs={{0,1},{1,0},{2,3},{3,2},{4,5},{5,4},{6,7},{7,6},{8,9},{9,8},{10,11... | collective-permute-start | bytes 1228808 | tf_op jit(solution)/shard_map/ppermute | solution.py:244
  49.0 0.0 collective-permute-done.3.refs_2_.refs_4_
  49.0 1.9 %collective-permute-start.11 = (bf16[200,1024]{1,0:T(8,128)(2,1)}, bf16[200,1024]{1,0:T(8,128)(2,1)}, u32[]{:S(2)}, u32[]{:S(2)}) collective-permute-start(bf16[200,1024]{1,0:T(8,128)(2,1)} %collective-permute-done.7.refs_7_), channel_id=1, source_target_pairs={{0,1},{1,0},{2,3},{3,2},{4,5},{5,4},{6,7},{7,6},{8,9},{9,8},{10,11... | collective-permute-start | bytes 1228808 | tf_op jit(solution)/shard_map/ppermute | solution.py:244
  50.9 0.0 collective-permute-done.2.refs_1_.refs_5_
  51.0 0.0 copy-start.1
  51.0 0.8 gate.3
  51.8 2.7 %collective-permute-start.4 = (bf16[200,1024]{1,0:T(8,128)(2,1)}, bf16[200,1024]{1,0:T(8,128)(2,1)S(1)}, u32[]{:S(2)}, u32[]{:S(2)}) collective-permute-start(bf16[200,1024]{1,0:T(8,128)(2,1)} %gate.3), channel_id=1, source_target_pairs={{0,6},{2,0},{4,2},{6,4},{1,3},{3,5},{5,7},{7,1},{8,14},{10,8},{12,... | collective-permute-start | bytes 1228808 | tf_op jit(solution)/shard_map/ppermute | solution.py:250
  54.5 0.0 copy-done.1
  54.5 0.0 collective-permute-done.5.refs_3_
  54.6 3.1 %collective-permute-start.6 = (bf16[200,1024]{1,0:T(8,128)(2,1)}, bf16[200,1024]{1,0:T(8,128)(2,1)S(1)}, u32[]{:S(2)}, u32[]{:S(2)}) collective-permute-start(bf16[200,1024]{1,0:T(8,128)(2,1)} %collective-permute-done.5.refs_3_), channel_id=1, source_target_pairs={{0,2},{2,4},{4,6},{6,0},{1,7},{3,1},{5,3},{7,5},{8,10},{10,12},{12... | collective-permute-start | bytes 1228808 | tf_op jit(solution)/shard_map/ppermute | solution.py:250
  57.8 0.1 stack.35.place_ref
  57.9 0.0 collective-permute-done.10.refs_9_
  57.9 0.0 collective-permute-done.11.refs_10_
  57.9 0.0 collective-permute-done.12.refs_11_
  57.9 0.0 copy-done
  57.9 1.0 copy-done.2
  58.9 6.2 %first_maxima.1 = (f32[8,1,192]{2,1,0:T(1,128)S(1)}, f32[1152,128]{1,0:T(8,128)S(1)}, bf16[1536,1024]{1,0:T(8,128)(2,1)S(1)}, f32[1536,128]{1,0:T(8,128)S(1)}, f32[6,1,192]{2,1,0:T(1,128)S(1)}) custom-call(s32[8]{0:T(128)S(1)} %stack.35.place_ref, bf16[200,1024]{1,0:T(8,128)(2,1)S(1)} %copy-done, bf16[200,1024]{1,0:T(8,128)(2,1)S(1)} %gate.2.refs_0_.refs_1_, ...), custom_call_target="tpu_custom_call" | custom-call | flops 3623878656 | bytes 5734400 | tf_op jit(solution)/shard_map/first_maxima/pallas_call | solution.py:192
  65.1 0.0 collective-permute-done.4.refs_0_
  65.1 0.7 collective-permute-done.6.refs_1_
  65.8 3.1 %last_maxima.1 = (f32[8,1,192]{2,1,0:T(1,128)}, f32[3,1,192]{2,1,0:T(1,128)S(1)}, f32[3,1,192]{2,1,0:T(1,128)S(1)}) custom-call(s32[8]{0:T(128)S(1)} %stack.35.place_ref, bf16[200,1024]{1,0:T(8,128)(2,1)S(1)} %collective-permute-done.4.refs_0_, bf16[200,1024]{1,0:T(8,128)(2,1)S(1)} %collective-permute-done.6.refs_1_, ...), custom_call_target="tpu_custom_call" | custom-call | flops 1207959552 | bytes 4096000 | tf_op jit(solution)/shard_map/last_maxima/pallas_call | solution.py:214
  68.9 2.2 %collective-permute-start.13 = (f32[3,1,192]{2,1,0:T(1,128)S(1)}, f32[3,1,192]{2,1,0:T(1,128)S(1)}, u32[]{:S(2)}, u32[]{:S(2)}) collective-permute-start(f32[3,1,192]{2,1,0:T(1,128)S(1)} %get-tuple-element.20), channel_id=1, source_target_pairs={{0,1},{1,0},{2,3},{3,2},{4,5},{5,4},{6,7},{7,6},{8,9},{9,8},{10,11... | collective-permute-start | bytes 6920 | tf_op jit(solution)/shard_map/ppermute | solution.py:244
  71.1 13.4 %all-to-all-start = ((f32[8,1,192]{2,1,0:T(1,128)}), f32[8,1,192]{2,1,0:T(1,128)S(1)}, u32[]{:S(2)}, u32[]{:S(2)}) async-start(f32[8,1,192]{2,1,0:T(1,128)} %get-tuple-element.18), calls=%async_computation | async-start | bytes 16384 | tf_op jit(solution)/shard_map/all_to_all | solution.py:275
  84.5 0.0 collective-permute-done.13
  84.5 1.9 %collective-permute-start.14 = (f32[1,192]{1,0:T(1,128)S(1)}, f32[1,192]{1,0:T(1,128)S(1)}, u32[]{:S(2)}, u32[]{:S(2)}) collective-permute-start(f32[1,192]{1,0:T(1,128)S(1)} %get-tuple-element.23), channel_id=1, source_target_pairs={{16,0},{32,16},{48,32},{64,48},{80,64},{96,80},{112,96},{128,112},... | collective-permute-start | bytes 2312 | tf_op jit(solution)/shard_map/ppermute | solution.py:240
  86.5 7.6 %collective-permute-start.15 = (f32[1,192]{1,0:T(1,128)S(1)}, f32[1,192]{1,0:T(1,128)S(1)}, u32[]{:S(2)}, u32[]{:S(2)}) collective-permute-start(f32[1,192]{1,0:T(1,128)S(1)} %get-tuple-element.22), channel_id=1, source_target_pairs={{32,0},{48,16},{64,32},{80,48},{96,64},{112,80},{128,96},{144,112}... | collective-permute-start | bytes 2312 | tf_op jit(solution)/shard_map/ppermute | solution.py:240
  94.1 2.1 %collective-permute-start.16 = (f32[1,192]{1,0:T(1,128)S(1)}, f32[1,192]{1,0:T(1,128)S(1)}, u32[]{:S(2)}, u32[]{:S(2)}) collective-permute-start(f32[1,192]{1,0:T(1,128)S(1)} %get-tuple-element.21), channel_id=1, source_target_pairs={{0,48},{16,64},{32,80},{48,96},{64,112},{80,128},{96,144},{112,160... | collective-permute-start | bytes 2312 | tf_op jit(solution)/shard_map/ppermute | solution.py:240
  96.3 0.0 all-to-all-done
  96.3 0.0 collective-permute-done.14
  96.3 0.0 collective-permute-done.15
  96.3 7.1 %collective-permute-done.16 = f32[1,192]{1,0:T(1,128)S(1)} collective-permute-done((f32[1,192]{1,0:T(1,128)S(1)}, f32[1,192]{1,0:T(1,128)S(1)}, u32[]{:S(2)}, u32[]{:S(2)}) %collective-permute-start.16) | collective-permute-done | bytes 800 | tf_op jit(solution)/shard_map/ppermute | solution.py:240
  103.5 0.6 fusion.2
  (5 shorter events, 0.1 us)
Async XLA Ops:
  2.0 55.9 %copy-start = (bf16[200,1024]{1,0:T(8,128)(2,1)S(1)}, bf16[200,1024]{1,0:T(8,128)(2,1)}, u32[]{:S(2)}) copy-start(bf16[200,1024]{1,0:T(8,128)(2,1)} %normalize_pack.1.refs_0_.refs_6_) | copy-start | bytes 1228804
  2.0 25.8 %collective-permute-start.8 = (bf16[200,1024]{1,0:T(8,128)(2,1)}, bf16[200,1024]{1,0:T(8,128)(2,1)S(1)}, u32[]{:S(2)}, u32[]{:S(2)}) collective-permute-start(bf16[200,1024]{1,0:T(8,128)(2,1)} %normalize_pack.1.refs_0_.refs_6_), channel_id=1, source_target_pairs={{0,32},{16,48},{32,64},{48,80},{64,96},{80,112},{96,128},{112,144}... | collective-permute-start | bytes 1228808 | tf_op jit(solution)/shard_map/ppermute | solution.py:240
  6.6 31.3 %collective-permute-start.9 = (bf16[200,1024]{1,0:T(8,128)(2,1)}, bf16[200,1024]{1,0:T(8,128)(2,1)S(1)}, u32[]{:S(2)}, u32[]{:S(2)}) collective-permute-start(bf16[200,1024]{1,0:T(8,128)(2,1)} %normalize_pack.1.refs_0_.refs_6_), channel_id=1, source_target_pairs={{48,0},{64,16},{80,32},{96,48},{112,64},{128,80},{144,96},{160,112... | collective-permute-start | bytes 1228808 | tf_op jit(solution)/shard_map/ppermute | solution.py:240
  10.9 29.1 %collective-permute-start.1 = (bf16[200,1024]{1,0:T(8,128)(2,1)}, bf16[200,1024]{1,0:T(8,128)(2,1)S(1)}, u32[]{:S(2)}, u32[]{:S(2)}) collective-permute-start(bf16[200,1024]{1,0:T(8,128)(2,1)} %normalize_pack.1.refs_0_.refs_6_), channel_id=1, source_target_pairs={{0,2},{2,4},{4,6},{6,0},{1,7},{3,1},{5,3},{7,5},{8,10},{10,12},{12... | collective-permute-start | bytes 1228808 | tf_op jit(solution)/shard_map/ppermute | solution.py:250
  14.3 29.1 %collective-permute-start = (bf16[200,1024]{1,0:T(8,128)(2,1)}, bf16[200,1024]{1,0:T(8,128)(2,1)S(1)}, u32[]{:S(2)}, u32[]{:S(2)}) collective-permute-start(bf16[200,1024]{1,0:T(8,128)(2,1)} %normalize_pack.1.refs_0_.refs_6_), channel_id=1, source_target_pairs={{0,8},{8,0},{1,9},{9,1},{2,10},{10,2},{3,11},{11,3},{4,12},{12,4},... | collective-permute-start | bytes 1228808 | tf_op jit(solution)/shard_map/ppermute | solution.py:244
  24.3 22.2 %collective-permute-start.7 = (bf16[200,1024]{1,0:T(8,128)(2,1)}, bf16[200,1024]{1,0:T(8,128)(2,1)}, u32[]{:S(2)}, u32[]{:S(2)}) collective-permute-start(bf16[200,1024]{1,0:T(8,128)(2,1)} %normalize_pack.1.refs_0_.refs_6_), channel_id=1, source_target_pairs={{0,16},{16,32},{32,48},{48,64},{64,80},{80,96},{96,112},{112,128},... | collective-permute-start | bytes 1228808 | tf_op jit(solution)/shard_map/ppermute | solution.py:240
  27.8 21.2 %collective-permute-start.3 = (bf16[200,1024]{1,0:T(8,128)(2,1)}, bf16[200,1024]{1,0:T(8,128)(2,1)S(1)}, u32[]{:S(2)}, u32[]{:S(2)}) collective-permute-start(bf16[200,1024]{1,0:T(8,128)(2,1)} %normalize_pack.1.refs_0_.refs_6_), channel_id=1, source_target_pairs={{0,6},{2,0},{4,2},{6,4},{1,3},{3,5},{5,7},{7,1},{8,14},{10,8},{12,... | collective-permute-start | bytes 1228808 | tf_op jit(solution)/shard_map/ppermute | solution.py:250
  38.0 19.8 %collective-permute-start.12 = (bf16[2,200,1024]{2,1,0:T(8,128)(2,1)S(1)}, bf16[2,200,1024]{2,1,0:T(8,128)(2,1)}, u32[]{:S(2)}, u32[]{:S(2)}) collective-permute-start(bf16[2,200,1024]{2,1,0:T(8,128)(2,1)S(1)} %stack_blocks.1.refs_8_), channel_id=1, source_target_pairs={{0,1},{1,0},{2,3},{3,2},{4,5},{5,4},{6,7},{7,6},{8,9},{9,8},{10,11... | collective-permute-start | bytes 2457608 | tf_op jit(solution)/shard_map/ppermute | solution.py:244
  40.0 11.0 %collective-permute-start.2 = (bf16[200,1024]{1,0:T(8,128)(2,1)S(1)}, bf16[200,1024]{1,0:T(8,128)(2,1)S(1)}, u32[]{:S(2)}, u32[]{:S(2)}) collective-permute-start(bf16[200,1024]{1,0:T(8,128)(2,1)S(1)} %collective-permute-done.1.refs_1_.refs_2_), channel_id=1, source_target_pairs={{0,2},{2,4},{4,6},{6,0},{1,7},{3,1},{5,3},{7,5},{8,10},{10,12},{12... | collective-permute-start | bytes 1228808 | tf_op jit(solution)/shard_map/ppermute | solution.py:250
  43.4 11.1 %collective-permute-start.5 = (bf16[200,1024]{1,0:T(8,128)(2,1)S(1)}, bf16[200,1024]{1,0:T(8,128)(2,1)}, u32[]{:S(2)}, u32[]{:S(2)}) collective-permute-start(bf16[200,1024]{1,0:T(8,128)(2,1)S(1)} %gate.2.refs_0_.refs_1_), channel_id=1, source_target_pairs={{0,2},{2,4},{4,6},{6,0},{1,7},{3,1},{5,3},{7,5},{8,10},{10,12},{12... | collective-permute-start | bytes 1228808 | tf_op jit(solution)/shard_map/ppermute | solution.py:250
  46.5 11.3 %collective-permute-start.10 = (bf16[200,1024]{1,0:T(8,128)(2,1)}, bf16[200,1024]{1,0:T(8,128)(2,1)}, u32[]{:S(2)}, u32[]{:S(2)}) collective-permute-start(bf16[200,1024]{1,0:T(8,128)(2,1)} %normalize_pack.1.refs_0_.refs_6_), channel_id=1, source_target_pairs={{0,1},{1,0},{2,3},{3,2},{4,5},{5,4},{6,7},{7,6},{8,9},{9,8},{10,11... | collective-permute-start | bytes 1228808 | tf_op jit(solution)/shard_map/ppermute | solution.py:244
  49.0 8.8 %collective-permute-start.11 = (bf16[200,1024]{1,0:T(8,128)(2,1)}, bf16[200,1024]{1,0:T(8,128)(2,1)}, u32[]{:S(2)}, u32[]{:S(2)}) collective-permute-start(bf16[200,1024]{1,0:T(8,128)(2,1)} %collective-permute-done.7.refs_7_), channel_id=1, source_target_pairs={{0,1},{1,0},{2,3},{3,2},{4,5},{5,4},{6,7},{7,6},{8,9},{9,8},{10,11... | collective-permute-start | bytes 1228808 | tf_op jit(solution)/shard_map/ppermute | solution.py:244
  51.0 3.6 %copy-start.1 = (bf16[200,1024]{1,0:T(8,128)(2,1)}, bf16[200,1024]{1,0:T(8,128)(2,1)S(1)}, u32[]{:S(2)}) copy-start(bf16[200,1024]{1,0:T(8,128)(2,1)S(1)} %collective-permute-done.2.refs_1_.refs_5_) | copy-start | bytes 1228804
  51.8 13.3 %collective-permute-start.4 = (bf16[200,1024]{1,0:T(8,128)(2,1)}, bf16[200,1024]{1,0:T(8,128)(2,1)S(1)}, u32[]{:S(2)}, u32[]{:S(2)}) collective-permute-start(bf16[200,1024]{1,0:T(8,128)(2,1)} %gate.3), channel_id=1, source_target_pairs={{0,6},{2,0},{4,2},{6,4},{1,3},{3,5},{5,7},{7,1},{8,14},{10,8},{12,... | collective-permute-start | bytes 1228808 | tf_op jit(solution)/shard_map/ppermute | solution.py:250
  54.6 11.2 %collective-permute-start.6 = (bf16[200,1024]{1,0:T(8,128)(2,1)}, bf16[200,1024]{1,0:T(8,128)(2,1)S(1)}, u32[]{:S(2)}, u32[]{:S(2)}) collective-permute-start(bf16[200,1024]{1,0:T(8,128)(2,1)} %collective-permute-done.5.refs_3_), channel_id=1, source_target_pairs={{0,2},{2,4},{4,6},{6,0},{1,7},{3,1},{5,3},{7,5},{8,10},{10,12},{12... | collective-permute-start | bytes 1228808 | tf_op jit(solution)/shard_map/ppermute | solution.py:250
  57.9 1.0 copy-start.2
  68.9 15.6 %collective-permute-start.13 = (f32[3,1,192]{2,1,0:T(1,128)S(1)}, f32[3,1,192]{2,1,0:T(1,128)S(1)}, u32[]{:S(2)}, u32[]{:S(2)}) collective-permute-start(f32[3,1,192]{2,1,0:T(1,128)S(1)} %get-tuple-element.20), channel_id=1, source_target_pairs={{0,1},{1,0},{2,3},{3,2},{4,5},{5,4},{6,7},{7,6},{8,9},{9,8},{10,11... | collective-permute-start | bytes 6920 | tf_op jit(solution)/shard_map/ppermute | solution.py:244
  71.1 25.2 %all-to-all-start = ((f32[8,1,192]{2,1,0:T(1,128)}), f32[8,1,192]{2,1,0:T(1,128)S(1)}, u32[]{:S(2)}, u32[]{:S(2)}) async-start(f32[8,1,192]{2,1,0:T(1,128)} %get-tuple-element.18), calls=%async_computation | async-start | bytes 16384 | tf_op jit(solution)/shard_map/all_to_all | solution.py:275
  84.5 11.8 %collective-permute-start.14 = (f32[1,192]{1,0:T(1,128)S(1)}, f32[1,192]{1,0:T(1,128)S(1)}, u32[]{:S(2)}, u32[]{:S(2)}) collective-permute-start(f32[1,192]{1,0:T(1,128)S(1)} %get-tuple-element.23), channel_id=1, source_target_pairs={{16,0},{32,16},{48,32},{64,48},{80,64},{96,80},{112,96},{128,112},... | collective-permute-start | bytes 2312 | tf_op jit(solution)/shard_map/ppermute | solution.py:240
  86.5 9.8 %collective-permute-start.15 = (f32[1,192]{1,0:T(1,128)S(1)}, f32[1,192]{1,0:T(1,128)S(1)}, u32[]{:S(2)}, u32[]{:S(2)}) collective-permute-start(f32[1,192]{1,0:T(1,128)S(1)} %get-tuple-element.22), channel_id=1, source_target_pairs={{32,0},{48,16},{64,32},{80,48},{96,64},{112,80},{128,96},{144,112}... | collective-permute-start | bytes 2312 | tf_op jit(solution)/shard_map/ppermute | solution.py:240
  94.1 9.4 %collective-permute-start.16 = (f32[1,192]{1,0:T(1,128)S(1)}, f32[1,192]{1,0:T(1,128)S(1)}, u32[]{:S(2)}, u32[]{:S(2)}) collective-permute-start(f32[1,192]{1,0:T(1,128)S(1)} %get-tuple-element.21), channel_id=1, source_target_pairs={{0,48},{16,64},{32,80},{48,96},{64,112},{80,128},{96,144},{112,160... | collective-permute-start | bytes 2312 | tf_op jit(solution)/shard_map/ppermute | solution.py:240

commit v10 on v9

--- a/solution.py
+++ b/solution.py
@@ -10,13 +10,13 @@
 PACK = ROWS + EXTRA
 D = 1024
 X = 4
-Z_LO = 4
-MOVES = (1, 2, -3)
+MOVES = (1, -3, 2)
 NEAR = 1 + len(MOVES)
 LEFT = 2 * NEAR * ROWS
 TILE = 256
 FAR = 1.0e9
 FIRST = 6
+HELD = ((0, 0), (1, 0), (0, 1), (1, 1), (0, 3), (0, 2), (1, 3), (1, 2))
 
 
 def pack_kernel(emb_any, lab_any, ord_any, out_ref, emb_ref, lab_ref, ord_ref, sems):
@@ -147,7 +147,14 @@
     return jnp.concatenate(cols, axis=1), rows
 
 
-def first_kernel(place_ref, *refs):
+def slot(number):
+    zh, x, core = (lax.axis_index(axis) for axis in ("zh", "x", "core"))
+    half, step = HELD[number]
+    turn = jnp.where(core == 0, X - step, step)
+    return lax.rem(zh + half, 2) * X + lax.rem(x + turn, X)
+
+
+def first_kernel(*refs):
     *given, cols_ref, rows_ref, left_ref, rank_ref, valid_ref, right = refs
     panel, given = given[:FIRST], given[FIRST:]
     mine, theirs = given[:len(given) // 2], given[len(given) // 2:]
@@ -161,17 +168,17 @@
     best, rows = panel_maxima(panel, right, left_ref, rank_ref)
     cols_ref[...] = jnp.full(cols_ref.shape, -1.0, jnp.float32)
     for k in range(FIRST):
-        cols_ref[place_ref[k]] = best[:, k * ROWS:(k + 1) * ROWS]
+        cols_ref[slot(k)] = best[:, k * ROWS:(k + 1) * ROWS]
     rows_ref[...] = rows
 
 
-def last_kernel(place_ref, *refs):
+def last_kernel(*refs):
     *given, cols_in_ref, rows_in_ref, left_ref, rank_ref, valid_ref, cols_ref, mine_ref, theirs_ref, right = refs
     panel = [ref.at[k] for ref in given for k in range(2)] if len(given) == 1 else given
     best, rows = panel_maxima(panel, right, left_ref, rank_ref)
     cols_ref[...] = cols_in_ref[...]
     for k in range(2 * X - FIRST):
-        cols_ref[place_ref[FIRST + k]] = best[:, k * ROWS:(k + 1) * ROWS]
+        cols_ref[slot(FIRST + k)] = best[:, k * ROWS:(k + 1) * ROWS]
     rows = jnp.maximum(rows, rows_in_ref[...])
     line = jnp.max(jnp.transpose(rows, (1, 0)), axis=0, keepdims=True)
     for s in range(NEAR - 1):
@@ -186,7 +193,7 @@
     )
 
 
-def first_maxima(place, near, panel):
+def first_maxima(near, panel):
     inside = pl.BlockSpec(memory_space=pltpu.VMEM)
     blocks = len(panel)
     return pl.pallas_call(
@@ -198,41 +205,29 @@
             jax.ShapeDtypeStruct((LEFT, 128), jnp.float32),
             jax.ShapeDtypeStruct((2 * (NEAR - 1), 1, ROWS), jnp.float32),
         ),
-        in_specs=[pl.BlockSpec(memory_space=pltpu.SMEM)] + [inside] * (len(near) + blocks),
+        in_specs=[inside] * (len(near) + blocks),
         out_specs=(inside,) * 5,
         scratch_shapes=[pltpu.VMEM((blocks * ROWS, D), jnp.bfloat16)],
         compiler_params=pltpu.CompilerParams(vmem_limit_bytes=20 * 1024 * 1024),
         name="first_maxima",
         cost_estimate=cost(blocks),
-    )(place, *panel, *near)
-
-
-def last_maxima(place, panel, carried):
+    )(*panel, *near)
+
+
+def last_maxima(panel, carried):
     inside = pl.BlockSpec(memory_space=pltpu.VMEM)
     lines = jax.ShapeDtypeStruct((NEAR - 1, 1, ROWS), jnp.float32)
     blocks = 2 * X - FIRST
     return pl.pallas_call(
         last_kernel,
         out_shape=(jax.ShapeDtypeStruct((2 * X, 1, ROWS), jnp.float32), lines, lines),
-        in_specs=[pl.BlockSpec(memory_space=pltpu.SMEM)] + [inside] * (len(panel) + len(carried)),
+        in_specs=[inside] * (len(panel) + len(carried)),
         out_specs=(inside,) * 3,
         scratch_shapes=[pltpu.VMEM((blocks * ROWS, D), jnp.bfloat16)],
         compiler_params=pltpu.CompilerParams(vmem_limit_bytes=20 * 1024 * 1024),
         name="last_maxima",
         cost_estimate=cost(blocks),
-    )(place, *panel, *carried)
-
-
-def half_flip(value, count):
-    pairs = []
-    for g in range(count):
-        low, y = divmod(g, count // Z_LO)
-        for h in range(2):
-            for c in range(2):
-                z = (h * Z_LO + low + (2 if c == 0 else 2 * Z_LO - 2)) % (2 * Z_LO)
-                target = z % Z_LO * (count // Z_LO) + y
-                pairs.append(((g * 2 + h) * 2 + c, (target * 2 + z // Z_LO) * 2 + c))
-    return lax.ppermute(value, ("grp", "zh", "core"), pairs)
+    )(*panel, *carried)
 
 
 def shift(value, steps, count):
@@ -252,11 +247,9 @@
 
 def per_device(embeddings, labels, order):
     count = lax.axis_size("grp")
-    grp, zh, x, core = (lax.axis_index(axis) for axis in ("grp", "zh", "x", "core"))
+    grp = lax.axis_index("grp")
     block = pack(embeddings, labels, order)
-    one = shift(block, MOVES[0], count)
-    two = shift(block, MOVES[1], count)
-    three = shift(block, MOVES[2], count)
+    one, far, two = (shift(block, steps, count) for steps in MOVES)
     ahead, behind = turn_x(block, 1), turn_x(block, -1)
     across = turn_x(ahead, 1)
     sib = swap(block, "core")
@@ -264,14 +257,10 @@
     flip_ahead = turn_x(flipped, 1)
     flip_behind = turn_x(gate(flipped, across, behind), -1)
     flip_across = turn_x(flip_ahead, 1)
-    mine = (block, one, stack((two, three)))
-    theirs = [sib] + [swap(value, "core") for value in mine[1:]]
-    turn = jnp.where(core == 0, 1, X - 1)
-    order_held = ((0, 0), (1, 0), (0, 1), (1, 1), (0, X - 1), (0, 2), (1, X - 1), (1, 2))
-    slots = [(zh + h) % 2 * X + (x + (X - k) * turn) % X for h, k in order_held]
-    place = jnp.stack(slots).astype(jnp.int32)
-    carried = first_maxima(place, (*mine, *theirs), [block, flipped, ahead, flip_ahead, behind, across])
-    cols, rows, rows_sib = last_maxima(place, [flip_behind, flip_across], carried)
+    mine = (block, stack((one, far)), two)
+    theirs = [swap(value, "core") for value in mine]
+    carried = first_maxima((*mine, *theirs), [block, flipped, ahead, flip_ahead, behind, across])
+    cols, rows, rows_sib = last_maxima([flip_behind, flip_across], carried)
     best = jnp.max(lax.all_to_all(cols, ("zh", "x"), 0, 0, tiled=True), axis=0)
     mine = jnp.maximum(rows, swap(rows_sib, "core"))
     for i, steps in enumerate(MOVES):

time: 105 us -> 102 us (0.971)
  the two profiles are of different devices: /device:TPU:74 before, /device:TPU:90 now
where the time goes in v10:
time: 102 us; the launch traced here: 101 us
  starting transfers between devices  71.9 us (70%)
  waiting for transfers between devices  19.1 us (19%)
  Pallas kernels  9.15 us (9%)
    ppermute x6, starting transfers between devices, shift(): return lax.ppermute(value, 'grp', pairs)  25.2 us
    ppermute x5, starting transfers between devices, swap(): return lax.ppermute(value, axis, [(0, 1), (1, 0)])  18.5 us
    ppermute x6, starting transfers between devices, turn_x(): return lax.ppermute(value, ('x', 'core'), pairs)  18.5 us
    ppermute x6, waiting for transfers between devices, shift(): return lax.ppermute(value, 'grp', pairs)  16 us
    all_to_all x1, starting transfers between devices, per_device(): best = jnp.max(lax.all_to_all(cols, ('zh', 'x'), 0, 0, tiled=True), axis=0)  9.74 us
    pallas_call x1, Pallas kernels, first_maxima(): pl.pallas_call(first_kernel, out_shape=(jax.ShapeDtypeStruct((2 * X, 1, R...  4.52 us
    ppermute x6, waiting for transfers between devices, turn_x(): return lax.ppermute(value, ('x', 'core'), pairs)  3.07 us
    pallas_call x1, Pallas kernels, last_maxima(): pl.pallas_call(last_kernel, out_shape=(jax.ShapeDtypeStruct((2 * X, 1, RO...  2.58 us
  transfers between devices with their start and end apart: 18, of which 5 were waited for; matrix products, arithmetic and copies ran while one was open for 0% of the time, Pallas kernels for 5%

profile of v10, /device:TPU:90, one launch (start us, length us, event | category | flops | bytes accessed | tf_op | source)
XLA Modules:
  0.0 101.1 jit_solution(12031636748771162354)
XLA Ops:
  0.0 1.9 %normalize_pack.1.refs_0_.refs_6_ = bf16[200,1024]{1,0:T(8,128)(2,1)} custom-call(bf16[192,1024]{1,0:T(8,128)(2,1)} %emb_any.1, s32[1,192]{1,0:T(1,128)} %bitcast.11, s32[1,192]{1,0:T(1,128)} %bitcast.12), custom_call_target="tpu_custom_call" | custom-call | flops 786432 | bytes 786432 | tf_op jit(solution)/shard_map/normalize_pack/pallas_call | solution.py:49
  1.9 0.0 copy-start
  2.0 4.8 %collective-permute-start.7 = (bf16[200,1024]{1,0:T(8,128)(2,1)}, bf16[200,1024]{1,0:T(8,128)(2,1)S(1)}, u32[]{:S(2)}, u32[]{:S(2)}) collective-permute-start(bf16[200,1024]{1,0:T(8,128)(2,1)} %normalize_pack.1.refs_0_.refs_6_), channel_id=1, source_target_pairs={{0,16},{16,32},{32,48},{48,64},{64,80},{80,96},{96,112},{112,128},... | collective-permute-start | bytes 1228808 | tf_op jit(solution)/shard_map/ppermute | solution.py:235
  6.8 1.9 %collective-permute-start.8 = (bf16[200,1024]{1,0:T(8,128)(2,1)}, bf16[200,1024]{1,0:T(8,128)(2,1)S(1)}, u32[]{:S(2)}, u32[]{:S(2)}) collective-permute-start(bf16[200,1024]{1,0:T(8,128)(2,1)} %normalize_pack.1.refs_0_.refs_6_), channel_id=1, source_target_pairs={{48,0},{64,16},{80,32},{96,48},{112,64},{128,80},{144,96},{160,112... | collective-permute-start | bytes 1228808 | tf_op jit(solution)/shard_map/ppermute | solution.py:235
  8.7 3.4 %collective-permute-start.1 = (bf16[200,1024]{1,0:T(8,128)(2,1)}, bf16[200,1024]{1,0:T(8,128)(2,1)S(1)}, u32[]{:S(2)}, u32[]{:S(2)}) collective-permute-start(bf16[200,1024]{1,0:T(8,128)(2,1)} %normalize_pack.1.refs_0_.refs_6_), channel_id=1, source_target_pairs={{0,2},{2,4},{4,6},{6,0},{1,7},{3,1},{5,3},{7,5},{8,10},{10,12},{12... | collective-permute-start | bytes 1228808 | tf_op jit(solution)/shard_map/ppermute | solution.py:245
  12.1 10.0 %collective-permute-start = (bf16[200,1024]{1,0:T(8,128)(2,1)}, bf16[200,1024]{1,0:T(8,128)(2,1)S(1)}, u32[]{:S(2)}, u32[]{:S(2)}) collective-permute-start(bf16[200,1024]{1,0:T(8,128)(2,1)} %normalize_pack.1.refs_0_.refs_6_), channel_id=1, source_target_pairs={{0,8},{8,0},{1,9},{9,1},{2,10},{10,2},{3,11},{11,3},{4,12},{12,4},... | collective-permute-start | bytes 1228808 | tf_op jit(solution)/shard_map/ppermute | solution.py:239
  22.2 4.7 %collective-permute-start.9 = (bf16[200,1024]{1,0:T(8,128)(2,1)}, bf16[200,1024]{1,0:T(8,128)(2,1)S(1)}, u32[]{:S(2)}, u32[]{:S(2)}) collective-permute-start(bf16[200,1024]{1,0:T(8,128)(2,1)} %normalize_pack.1.refs_0_.refs_6_), channel_id=1, source_target_pairs={{0,32},{16,48},{32,64},{48,80},{64,96},{80,112},{96,128},{112,144}... | collective-permute-start | bytes 1228808 | tf_op jit(solution)/shard_map/ppermute | solution.py:235
  26.9 0.0 collective-permute-done.7.refs_0_
  26.9 2.4 %collective-permute-start.3 = (bf16[200,1024]{1,0:T(8,128)(2,1)}, bf16[200,1024]{1,0:T(8,128)(2,1)S(1)}, u32[]{:S(2)}, u32[]{:S(2)}) collective-permute-start(bf16[200,1024]{1,0:T(8,128)(2,1)} %normalize_pack.1.refs_0_.refs_6_), channel_id=1, source_target_pairs={{0,6},{2,0},{4,2},{6,4},{1,3},{3,5},{5,7},{7,1},{8,14},{10,8},{12,... | collective-permute-start | bytes 1228808 | tf_op jit(solution)/shard_map/ppermute | solution.py:245
  29.3 10.5 %collective-permute-done.8.refs_1_ = bf16[200,1024]{1,0:T(8,128)(2,1)S(1)} collective-permute-done((bf16[200,1024]{1,0:T(8,128)(2,1)}, bf16[200,1024]{1,0:T(8,128)(2,1)S(1)}, u32[]{:S(2)}, u32[]{:S(2)}) %collective-permute-start.8) | collective-permute-done | bytes 409632 | tf_op jit(solution)/shard_map/ppermute | solution.py:235
  39.8 0.1 stack_blocks.1.refs_7_
  39.8 1.9 %collective-permute-start.11 = (bf16[2,200,1024]{2,1,0:T(8,128)(2,1)S(1)}, bf16[2,200,1024]{2,1,0:T(8,128)(2,1)S(1)}, u32[]{:S(2)}, u32[]{:S(2)}) collective-permute-start(bf16[2,200,1024]{2,1,0:T(8,128)(2,1)S(1)} %stack_blocks.1.refs_7_), channel_id=1, source_target_pairs={{0,1},{1,0},{2,3},{3,2},{4,5},{5,4},{6,7},{7,6},{8,9},{9,8},{10,11... | collective-permute-start | bytes 2457608 | tf_op jit(solution)/shard_map/ppermute | solution.py:239
  41.8 0.0 collective-permute-done.1.refs_1_.refs_2_
  41.8 3.4 %collective-permute-start.2 = (bf16[200,1024]{1,0:T(8,128)(2,1)S(1)}, bf16[200,1024]{1,0:T(8,128)(2,1)S(1)}, u32[]{:S(2)}, u32[]{:S(2)}) collective-permute-start(bf16[200,1024]{1,0:T(8,128)(2,1)S(1)} %collective-permute-done.1.refs_1_.refs_2_), channel_id=1, source_target_pairs={{0,2},{2,4},{4,6},{6,0},{1,7},{3,1},{5,3},{7,5},{8,10},{10,12},{12... | collective-permute-start | bytes 1228808 | tf_op jit(solution)/shard_map/ppermute | solution.py:245
  45.2 0.0 collective-permute-done.refs_0_
  45.2 3.1 %collective-permute-start.5 = (bf16[200,1024]{1,0:T(8,128)(2,1)S(1)}, bf16[200,1024]{1,0:T(8,128)(2,1)S(1)}, u32[]{:S(2)}, u32[]{:S(2)}) collective-permute-start(bf16[200,1024]{1,0:T(8,128)(2,1)S(1)} %gate.2.refs_0_.refs_1_), channel_id=1, source_target_pairs={{0,2},{2,4},{4,6},{6,0},{1,7},{3,1},{5,3},{7,5},{8,10},{10,12},{12... | collective-permute-start | bytes 1228808 | tf_op jit(solution)/shard_map/ppermute | solution.py:245
  48.4 0.0 collective-permute-done.9.refs_8_
  48.4 2.5 %collective-permute-start.10 = (bf16[200,1024]{1,0:T(8,128)(2,1)}, bf16[200,1024]{1,0:T(8,128)(2,1)S(1)}, u32[]{:S(2)}, u32[]{:S(2)}) collective-permute-start(bf16[200,1024]{1,0:T(8,128)(2,1)} %normalize_pack.1.refs_0_.refs_6_), channel_id=1, source_target_pairs={{0,1},{1,0},{2,3},{3,2},{4,5},{5,4},{6,7},{7,6},{8,9},{9,8},{10,11... | collective-permute-start | bytes 1228808 | tf_op jit(solution)/shard_map/ppermute | solution.py:239
  50.8 0.0 collective-permute-done.3.refs_2_.refs_4_
  50.8 1.9 %collective-permute-start.12 = (bf16[200,1024]{1,0:T(8,128)(2,1)S(1)}, bf16[200,1024]{1,0:T(8,128)(2,1)S(1)}, u32[]{:S(2)}, u32[]{:S(2)}) collective-permute-start(bf16[200,1024]{1,0:T(8,128)(2,1)S(1)} %collective-permute-done.9.refs_8_), channel_id=1, source_target_pairs={{0,1},{1,0},{2,3},{3,2},{4,5},{5,4},{6,7},{7,6},{8,9},{9,8},{10,11... | collective-permute-start | bytes 1228808 | tf_op jit(solution)/shard_map/ppermute | solution.py:239
  52.8 0.0 collective-permute-done.2.refs_1_.refs_5_
  52.8 2.7 %collective-permute-start.4 = (bf16[200,1024]{1,0:T(8,128)(2,1)S(1)}, bf16[200,1024]{1,0:T(8,128)(2,1)S(1)}, u32[]{:S(2)}, u32[]{:S(2)}) collective-permute-start(bf16[200,1024]{1,0:T(8,128)(2,1)S(1)} %gate.3), channel_id=1, source_target_pairs={{0,6},{2,0},{4,2},{6,4},{1,3},{3,5},{5,7},{7,1},{8,14},{10,8},{12,... | collective-permute-start | bytes 1228808 | tf_op jit(solution)/shard_map/ppermute | solution.py:245
  55.6 0.5 collective-permute-done.5.refs_3_
  56.0 3.4 %collective-permute-start.6 = (bf16[200,1024]{1,0:T(8,128)(2,1)S(1)}, bf16[200,1024]{1,0:T(8,128)(2,1)S(1)}, u32[]{:S(2)}, u32[]{:S(2)}) collective-permute-start(bf16[200,1024]{1,0:T(8,128)(2,1)S(1)} %collective-permute-done.5.refs_3_), channel_id=1, source_target_pairs={{0,2},{2,4},{4,6},{6,0},{1,7},{3,1},{5,3},{7,5},{8,10},{10,12},{12... | collective-permute-start | bytes 1228808 | tf_op jit(solution)/shard_map/ppermute | solution.py:245
  59.4 0.0 collective-permute-done.10.refs_9_
  59.4 0.0 collective-permute-done.12.refs_11_
  59.4 0.0 collective-permute-done.11.refs_10_
  59.4 0.0 copy-done
  59.5 4.5 %first_maxima.1 = (f32[8,1,192]{2,1,0:T(1,128)S(1)}, f32[1152,128]{1,0:T(8,128)S(1)}, bf16[1536,1024]{1,0:T(8,128)(2,1)S(1)}, f32[1536,128]{1,0:T(8,128)S(1)}, f32[6,1,192]{2,1,0:T(1,128)S(1)}) custom-call(bf16[200,1024]{1,0:T(8,128)(2,1)S(1)} %copy-done, bf16[200,1024]{1,0:T(8,128)(2,1)S(1)} %gate.2.refs_0_.refs_1_, ...), custom_call_target="tpu_custom_call" | custom-call | flops 3623878656 | bytes 5734400 | tf_op jit(solution)/shard_map/first_maxima/pallas_call | solution.py:199
  64.0 1.1 %collective-permute-done.4.refs_0_ = bf16[200,1024]{1,0:T(8,128)(2,1)S(1)} collective-permute-done((bf16[200,1024]{1,0:T(8,128)(2,1)S(1)}, bf16[200,1024]{1,0:T(8,128)(2,1)S(1)}, u32[]{:S(2)}, u32[]{:S(2)}) %collective-permute-start.4) | collective-permute-done | bytes 409632 | tf_op jit(solution)/shard_map/ppermute | solution.py:245
  65.1 1.5 %collective-permute-done.6.refs_1_ = bf16[200,1024]{1,0:T(8,128)(2,1)S(1)} collective-permute-done((bf16[200,1024]{1,0:T(8,128)(2,1)S(1)}, bf16[200,1024]{1,0:T(8,128)(2,1)S(1)}, u32[]{:S(2)}, u32[]{:S(2)}) %collective-permute-start.6) | collective-permute-done | bytes 409632 | tf_op jit(solution)/shard_map/ppermute | solution.py:245
  66.6 2.6 %last_maxima.1 = (f32[8,1,192]{2,1,0:T(1,128)}, f32[3,1,192]{2,1,0:T(1,128)S(1)}, f32[3,1,192]{2,1,0:T(1,128)S(1)}) custom-call(bf16[200,1024]{1,0:T(8,128)(2,1)S(1)} %collective-permute-done.4.refs_0_, bf16[200,1024]{1,0:T(8,128)(2,1)S(1)} %collective-permute-done.6.refs_1_, f32[8,1,192]{2,1,0:T(1,128)S(1)} %get-tuple-element.13.refs_2_, ...), custom_call_target="tpu_custom_call" | custom-call | flops 1207959552 | bytes 4096000 | tf_op jit(solution)/shard_map/last_maxima/pallas_call | solution.py:221
  69.1 2.2 %collective-permute-start.13 = (f32[3,1,192]{2,1,0:T(1,128)S(1)}, f32[3,1,192]{2,1,0:T(1,128)S(1)}, u32[]{:S(2)}, u32[]{:S(2)}) collective-permute-start(f32[3,1,192]{2,1,0:T(1,128)S(1)} %get-tuple-element.20), channel_id=1, source_target_pairs={{0,1},{1,0},{2,3},{3,2},{4,5},{5,4},{6,7},{7,6},{8,9},{9,8},{10,11... | collective-permute-start | bytes 6920 | tf_op jit(solution)/shard_map/ppermute | solution.py:239
  71.4 9.7 %all-to-all-start = ((f32[8,1,192]{2,1,0:T(1,128)}), f32[8,1,192]{2,1,0:T(1,128)S(1)}, u32[]{:S(2)}, u32[]{:S(2)}) async-start(f32[8,1,192]{2,1,0:T(1,128)} %get-tuple-element.18), calls=%async_computation | async-start | bytes 16384 | tf_op jit(solution)/shard_map/all_to_all | solution.py:264
  81.1 0.0 collective-permute-done.13
  81.1 4.7 %collective-permute-start.14 = (f32[1,192]{1,0:T(1,128)S(1)}, f32[1,192]{1,0:T(1,128)S(1)}, u32[]{:S(2)}, u32[]{:S(2)}) collective-permute-start(f32[1,192]{1,0:T(1,128)S(1)} %get-tuple-element.23), channel_id=1, source_target_pairs={{16,0},{32,16},{48,32},{64,48},{80,64},{96,80},{112,96},{128,112},... | collective-permute-start | bytes 2312 | tf_op jit(solution)/shard_map/ppermute | solution.py:235
  85.8 7.1 %collective-permute-start.15 = (f32[1,192]{1,0:T(1,128)S(1)}, f32[1,192]{1,0:T(1,128)S(1)}, u32[]{:S(2)}, u32[]{:S(2)}) collective-permute-start(f32[1,192]{1,0:T(1,128)S(1)} %get-tuple-element.22), channel_id=1, source_target_pairs={{0,48},{16,64},{32,80},{48,96},{64,112},{80,128},{96,144},{112,160... | collective-permute-start | bytes 2312 | tf_op jit(solution)/shard_map/ppermute | solution.py:235
  92.9 1.9 %collective-permute-start.16 = (f32[1,192]{1,0:T(1,128)S(1)}, f32[1,192]{1,0:T(1,128)S(1)}, u32[]{:S(2)}, u32[]{:S(2)}) collective-permute-start(f32[1,192]{1,0:T(1,128)S(1)} %get-tuple-element.21), channel_id=1, source_target_pairs={{32,0},{48,16},{64,32},{80,48},{96,64},{112,80},{128,96},{144,112}... | collective-permute-start | bytes 2312 | tf_op jit(solution)/shard_map/ppermute | solution.py:235
  94.9 0.0 all-to-all-done
  94.9 0.0 collective-permute-done.14
  94.9 0.0 collective-permute-done.15
  94.9 5.6 %collective-permute-done.16 = f32[1,192]{1,0:T(1,128)S(1)} collective-permute-done((f32[1,192]{1,0:T(1,128)S(1)}, f32[1,192]{1,0:T(1,128)S(1)}, u32[]{:S(2)}, u32[]{:S(2)}) %collective-permute-start.16) | collective-permute-done | bytes 800 | tf_op jit(solution)/shard_map/ppermute | solution.py:235
  100.5 0.6 fusion.2
  (5 shorter events, 0.1 us)
Async XLA Ops:
  1.9 57.5 %copy-start = (bf16[200,1024]{1,0:T(8,128)(2,1)S(1)}, bf16[200,1024]{1,0:T(8,128)(2,1)}, u32[]{:S(2)}) copy-start(bf16[200,1024]{1,0:T(8,128)(2,1)} %normalize_pack.1.refs_0_.refs_6_) | copy-start | bytes 1228804
  2.0 24.9 %collective-permute-start.7 = (bf16[200,1024]{1,0:T(8,128)(2,1)}, bf16[200,1024]{1,0:T(8,128)(2,1)S(1)}, u32[]{:S(2)}, u32[]{:S(2)}) collective-permute-start(bf16[200,1024]{1,0:T(8,128)(2,1)} %normalize_pack.1.refs_0_.refs_6_), channel_id=1, source_target_pairs={{0,16},{16,32},{32,48},{48,64},{64,80},{80,96},{96,112},{112,128},... | collective-permute-start | bytes 1228808 | tf_op jit(solution)/shard_map/ppermute | solution.py:235
  6.8 33.0 %collective-permute-start.8 = (bf16[200,1024]{1,0:T(8,128)(2,1)}, bf16[200,1024]{1,0:T(8,128)(2,1)S(1)}, u32[]{:S(2)}, u32[]{:S(2)}) collective-permute-start(bf16[200,1024]{1,0:T(8,128)(2,1)} %normalize_pack.1.refs_0_.refs_6_), channel_id=1, source_target_pairs={{48,0},{64,16},{80,32},{96,48},{112,64},{128,80},{144,96},{160,112... | collective-permute-start | bytes 1228808 | tf_op jit(solution)/shard_map/ppermute | solution.py:235
  8.7 33.1 %collective-permute-start.1 = (bf16[200,1024]{1,0:T(8,128)(2,1)}, bf16[200,1024]{1,0:T(8,128)(2,1)S(1)}, u32[]{:S(2)}, u32[]{:S(2)}) collective-permute-start(bf16[200,1024]{1,0:T(8,128)(2,1)} %normalize_pack.1.refs_0_.refs_6_), channel_id=1, source_target_pairs={{0,2},{2,4},{4,6},{6,0},{1,7},{3,1},{5,3},{7,5},{8,10},{10,12},{12... | collective-permute-start | bytes 1228808 | tf_op jit(solution)/shard_map/ppermute | solution.py:245
  12.1 33.1 %collective-permute-start = (bf16[200,1024]{1,0:T(8,128)(2,1)}, bf16[200,1024]{1,0:T(8,128)(2,1)S(1)}, u32[]{:S(2)}, u32[]{:S(2)}) collective-permute-start(bf16[200,1024]{1,0:T(8,128)(2,1)} %normalize_pack.1.refs_0_.refs_6_), channel_id=1, source_target_pairs={{0,8},{8,0},{1,9},{9,1},{2,10},{10,2},{3,11},{11,3},{4,12},{12,4},... | collective-permute-start | bytes 1228808 | tf_op jit(solution)/shard_map/ppermute | solution.py:239
  22.2 26.2 %collective-permute-start.9 = (bf16[200,1024]{1,0:T(8,128)(2,1)}, bf16[200,1024]{1,0:T(8,128)(2,1)S(1)}, u32[]{:S(2)}, u32[]{:S(2)}) collective-permute-start(bf16[200,1024]{1,0:T(8,128)(2,1)} %normalize_pack.1.refs_0_.refs_6_), channel_id=1, source_target_pairs={{0,32},{16,48},{32,64},{48,80},{64,96},{80,112},{96,128},{112,144}... | collective-permute-start | bytes 1228808 | tf_op jit(solution)/shard_map/ppermute | solution.py:235
  26.9 23.9 %collective-permute-start.3 = (bf16[200,1024]{1,0:T(8,128)(2,1)}, bf16[200,1024]{1,0:T(8,128)(2,1)S(1)}, u32[]{:S(2)}, u32[]{:S(2)}) collective-permute-start(bf16[200,1024]{1,0:T(8,128)(2,1)} %normalize_pack.1.refs_0_.refs_6_), channel_id=1, source_target_pairs={{0,6},{2,0},{4,2},{6,4},{1,3},{3,5},{5,7},{7,1},{8,14},{10,8},{12,... | collective-permute-start | bytes 1228808 | tf_op jit(solution)/shard_map/ppermute | solution.py:245
  39.8 19.6 %collective-permute-start.11 = (bf16[2,200,1024]{2,1,0:T(8,128)(2,1)S(1)}, bf16[2,200,1024]{2,1,0:T(8,128)(2,1)S(1)}, u32[]{:S(2)}, u32[]{:S(2)}) collective-permute-start(bf16[2,200,1024]{2,1,0:T(8,128)(2,1)S(1)} %stack_blocks.1.refs_7_), channel_id=1, source_target_pairs={{0,1},{1,0},{2,3},{3,2},{4,5},{5,4},{6,7},{7,6},{8,9},{9,8},{10,11... | collective-permute-start | bytes 2457608 | tf_op jit(solution)/shard_map/ppermute | solution.py:239
  41.8 11.0 %collective-permute-start.2 = (bf16[200,1024]{1,0:T(8,128)(2,1)S(1)}, bf16[200,1024]{1,0:T(8,128)(2,1)S(1)}, u32[]{:S(2)}, u32[]{:S(2)}) collective-permute-start(bf16[200,1024]{1,0:T(8,128)(2,1)S(1)} %collective-permute-done.1.refs_1_.refs_2_), channel_id=1, source_target_pairs={{0,2},{2,4},{4,6},{6,0},{1,7},{3,1},{5,3},{7,5},{8,10},{10,12},{12... | collective-permute-start | bytes 1228808 | tf_op jit(solution)/shard_map/ppermute | solution.py:245
  45.2 10.8 %collective-permute-start.5 = (bf16[200,1024]{1,0:T(8,128)(2,1)S(1)}, bf16[200,1024]{1,0:T(8,128)(2,1)S(1)}, u32[]{:S(2)}, u32[]{:S(2)}) collective-permute-start(bf16[200,1024]{1,0:T(8,128)(2,1)S(1)} %gate.2.refs_0_.refs_1_), channel_id=1, source_target_pairs={{0,2},{2,4},{4,6},{6,0},{1,7},{3,1},{5,3},{7,5},{8,10},{10,12},{12... | collective-permute-start | bytes 1228808 | tf_op jit(solution)/shard_map/ppermute | solution.py:245
  48.4 11.1 %collective-permute-start.10 = (bf16[200,1024]{1,0:T(8,128)(2,1)}, bf16[200,1024]{1,0:T(8,128)(2,1)S(1)}, u32[]{:S(2)}, u32[]{:S(2)}) collective-permute-start(bf16[200,1024]{1,0:T(8,128)(2,1)} %normalize_pack.1.refs_0_.refs_6_), channel_id=1, source_target_pairs={{0,1},{1,0},{2,3},{3,2},{4,5},{5,4},{6,7},{7,6},{8,9},{9,8},{10,11... | collective-permute-start | bytes 1228808 | tf_op jit(solution)/shard_map/ppermute | solution.py:239
  50.8 8.6 %collective-permute-start.12 = (bf16[200,1024]{1,0:T(8,128)(2,1)S(1)}, bf16[200,1024]{1,0:T(8,128)(2,1)S(1)}, u32[]{:S(2)}, u32[]{:S(2)}) collective-permute-start(bf16[200,1024]{1,0:T(8,128)(2,1)S(1)} %collective-permute-done.9.refs_8_), channel_id=1, source_target_pairs={{0,1},{1,0},{2,3},{3,2},{4,5},{5,4},{6,7},{7,6},{8,9},{9,8},{10,11... | collective-permute-start | bytes 1228808 | tf_op jit(solution)/shard_map/ppermute | solution.py:239
  52.8 12.3 %collective-permute-start.4 = (bf16[200,1024]{1,0:T(8,128)(2,1)S(1)}, bf16[200,1024]{1,0:T(8,128)(2,1)S(1)}, u32[]{:S(2)}, u32[]{:S(2)}) collective-permute-start(bf16[200,1024]{1,0:T(8,128)(2,1)S(1)} %gate.3), channel_id=1, source_target_pairs={{0,6},{2,0},{4,2},{6,4},{1,3},{3,5},{5,7},{7,1},{8,14},{10,8},{12,... | collective-permute-start | bytes 1228808 | tf_op jit(solution)/shard_map/ppermute | solution.py:245
  56.0 10.6 %collective-permute-start.6 = (bf16[200,1024]{1,0:T(8,128)(2,1)S(1)}, bf16[200,1024]{1,0:T(8,128)(2,1)S(1)}, u32[]{:S(2)}, u32[]{:S(2)}) collective-permute-start(bf16[200,1024]{1,0:T(8,128)(2,1)S(1)} %collective-permute-done.5.refs_3_), channel_id=1, source_target_pairs={{0,2},{2,4},{4,6},{6,0},{1,7},{3,1},{5,3},{7,5},{8,10},{10,12},{12... | collective-permute-start | bytes 1228808 | tf_op jit(solution)/shard_map/ppermute | solution.py:245
  69.1 12.0 %collective-permute-start.13 = (f32[3,1,192]{2,1,0:T(1,128)S(1)}, f32[3,1,192]{2,1,0:T(1,128)S(1)}, u32[]{:S(2)}, u32[]{:S(2)}) collective-permute-start(f32[3,1,192]{2,1,0:T(1,128)S(1)} %get-tuple-element.20), channel_id=1, source_target_pairs={{0,1},{1,0},{2,3},{3,2},{4,5},{5,4},{6,7},{7,6},{8,9},{9,8},{10,11... | collective-permute-start | bytes 6920 | tf_op jit(solution)/shard_map/ppermute | solution.py:239
  71.4 23.5 %all-to-all-start = ((f32[8,1,192]{2,1,0:T(1,128)}), f32[8,1,192]{2,1,0:T(1,128)S(1)}, u32[]{:S(2)}, u32[]{:S(2)}) async-start(f32[8,1,192]{2,1,0:T(1,128)} %get-tuple-element.18), calls=%async_computation | async-start | bytes 16384 | tf_op jit(solution)/shard_map/all_to_all | solution.py:264
  81.1 13.8 %collective-permute-start.14 = (f32[1,192]{1,0:T(1,128)S(1)}, f32[1,192]{1,0:T(1,128)S(1)}, u32[]{:S(2)}, u32[]{:S(2)}) collective-permute-start(f32[1,192]{1,0:T(1,128)S(1)} %get-tuple-element.23), channel_id=1, source_target_pairs={{16,0},{32,16},{48,32},{64,48},{80,64},{96,80},{112,96},{128,112},... | collective-permute-start | bytes 2312 | tf_op jit(solution)/shard_map/ppermute | solution.py:235
  85.8 9.1 %collective-permute-start.15 = (f32[1,192]{1,0:T(1,128)S(1)}, f32[1,192]{1,0:T(1,128)S(1)}, u32[]{:S(2)}, u32[]{:S(2)}) collective-permute-start(f32[1,192]{1,0:T(1,128)S(1)} %get-tuple-element.22), channel_id=1, source_target_pairs={{0,48},{16,64},{32,80},{48,96},{64,112},{80,128},{96,144},{112,160... | collective-permute-start | bytes 2312 | tf_op jit(solution)/shard_map/ppermute | solution.py:235
  92.9 7.6 %collective-permute-start.16 = (f32[1,192]{1,0:T(1,128)S(1)}, f32[1,192]{1,0:T(1,128)S(1)}, u32[]{:S(2)}, u32[]{:S(2)}) collective-permute-start(f32[1,192]{1,0:T(1,128)S(1)} %get-tuple-element.21), channel_id=1, source_target_pairs={{32,0},{48,16},{64,32},{80,48},{96,64},{112,80},{128,96},{144,112}... | collective-permute-start | bytes 2312 | tf_op jit(solution)/shard_map/ppermute | solution.py:235

commit v11 on v10

--- a/solution.py
+++ b/solution.py
@@ -7,6 +7,7 @@
 
 ROWS = 192
 EXTRA = 8
+PAD = 8
 PACK = ROWS + EXTRA
 D = 1024
 X = 4
@@ -19,7 +20,7 @@
 HELD = ((0, 0), (1, 0), (0, 1), (1, 1), (0, 3), (0, 2), (1, 3), (1, 2))
 
 
-def pack_kernel(emb_any, lab_any, ord_any, out_ref, emb_ref, lab_ref, ord_ref, sems):
+def pack_kernel(emb_any, lab_any, ord_any, out_ref, tall_ref, emb_ref, lab_ref, ord_ref, sems):
     copies = [
         pltpu.make_async_copy(source, target, sems.at[k])
         for k, (source, target) in enumerate(((emb_any, emb_ref), (lab_any, lab_ref), (ord_any, ord_ref)))
@@ -42,15 +43,20 @@
     digits = jnp.where(line < 4, digits, 0).astype(jnp.float32)
     digits = jnp.concatenate([digits, jnp.zeros((EXTRA, D - ROWS), jnp.float32)], axis=1)
     out_ref[ROWS:PACK, :] = digits.astype(jnp.bfloat16)
+    tall_ref[0:PACK, :] = out_ref[...]
+    tall_ref[PACK:PACK + PAD, :] = jnp.zeros((PAD, D), jnp.bfloat16)
 
 
 def pack(embeddings, labels, order):
     anywhere = pl.BlockSpec(memory_space=pl.ANY)
     return pl.pallas_call(
         pack_kernel,
-        out_shape=jax.ShapeDtypeStruct((PACK, D), jnp.bfloat16),
+        out_shape=(
+            jax.ShapeDtypeStruct((PACK, D), jnp.bfloat16),
+            jax.ShapeDtypeStruct((PACK + PAD, D), jnp.bfloat16),
+        ),
         in_specs=[anywhere] * 3,
-        out_specs=pl.BlockSpec(memory_space=pltpu.VMEM),
+        out_specs=(pl.BlockSpec(memory_space=pltpu.VMEM),) * 2,
         scratch_shapes=[
             pltpu.VMEM((ROWS, D), jnp.bfloat16),
             pltpu.VMEM((1, ROWS), jnp.int32),
@@ -91,14 +97,14 @@
 
 
 def gate_kernel(*refs):
-    refs[-1][...] = refs[0][...]
+    refs[-1][...] = refs[0][0:PACK, :]
 
 
 def gate(value, *others):
     inside = pl.BlockSpec(memory_space=pltpu.VMEM)
     return pl.pallas_call(
         gate_kernel,
-        out_shape=jax.ShapeDtypeStruct(value.shape, value.dtype),
+        out_shape=jax.ShapeDtypeStruct((PACK, D), value.dtype),
         in_specs=[inside] * (1 + len(others)),
         out_specs=inside,
         compiler_params=pltpu.CompilerParams(vmem_limit_bytes=8 * 1024 * 1024),
@@ -248,12 +254,12 @@
 def per_device(embeddings, labels, order):
     count = lax.axis_size("grp")
     grp = lax.axis_index("grp")
-    block = pack(embeddings, labels, order)
+    block, tall = pack(embeddings, labels, order)
     one, far, two = (shift(block, steps, count) for steps in MOVES)
     ahead, behind = turn_x(block, 1), turn_x(block, -1)
     across = turn_x(ahead, 1)
     sib = swap(block, "core")
-    flipped = gate(swap(block, "zh"), ahead)
+    flipped = gate(swap(tall, "zh"), ahead)
     flip_ahead = turn_x(flipped, 1)
     flip_behind = turn_x(gate(flipped, across, behind), -1)
     flip_across = turn_x(flip_ahead, 1)

time: 102 us -> 102 us (level)
    all_to_all x1, starting transfers between devices: 9.74 us -> 11 us  [per_device(): best = jnp.max(lax.all_to_all(cols, ('zh', 'x'), 0, 0, tiled=True), axis=0)]
    ppermute x6, starting transfers between devices: 25.2 us -> 23.9 us  [shift(): return lax.ppermute(value, 'grp', pairs)]
where the time goes in v11:
time: 102 us; the launch traced here: 101 us
  starting transfers between devices  71.9 us (70%)
  waiting for transfers between devices  19 us (19%)
  Pallas kernels  9.42 us (9%)
    ppermute x6, starting transfers between devices, shift(): return lax.ppermute(value, 'grp', pairs)  23.9 us
    ppermute x5, starting transfers between devices, swap(): return lax.ppermute(value, axis, [(0, 1), (1, 0)])  18.5 us
    ppermute x6, starting transfers between devices, turn_x(): return lax.ppermute(value, ('x', 'core'), pairs)  18.5 us
    ppermute x6, waiting for transfers between devices, shift(): return lax.ppermute(value, 'grp', pairs)  16 us
    all_to_all x1, starting transfers between devices, per_device(): best = jnp.max(lax.all_to_all(cols, ('zh', 'x'), 0, 0, tiled=True), axis=0)  11 us
    pallas_call x1, Pallas kernels, first_maxima(): pl.pallas_call(first_kernel, out_shape=(jax.ShapeDtypeStruct((2 * X, 1, R...  4.61 us
    ppermute x6, waiting for transfers between devices, turn_x(): return lax.ppermute(value, ('x', 'core'), pairs)  2.98 us
    pallas_call x1, Pallas kernels, last_maxima(): pl.pallas_call(last_kernel, out_shape=(jax.ShapeDtypeStruct((2 * X, 1, RO...  2.62 us
  transfers between devices with their start and end apart: 18, of which 5 were waited for; matrix products, arithmetic and copies ran while one was open for 0% of the time, Pallas kernels for 5%

profile of v11, /device:TPU:90, one launch (start us, length us, event | category | flops | bytes accessed | tf_op | source)
XLA Modules:
  0.0 101.2 jit_solution(15976620615840681585)
XLA Ops:
  0.0 2.1 %normalize_pack.1 = (bf16[200,1024]{1,0:T(8,128)(2,1)}, bf16[208,1024]{1,0:T(8,128)(2,1)}) custom-call(bf16[192,1024]{1,0:T(8,128)(2,1)} %emb_any.1, s32[1,192]{1,0:T(1,128)} %bitcast.11, s32[1,192]{1,0:T(1,128)} %bitcast.12), custom_call_target="tpu_custom_call" | custom-call | flops 786432 | bytes 786432 | tf_op jit(solution)/shard_map/normalize_pack/pallas_call | solution.py:52
  2.1 0.0 copy-start
  2.1 4.8 %collective-permute-start.7 = (bf16[200,1024]{1,0:T(8,128)(2,1)}, bf16[200,1024]{1,0:T(8,128)(2,1)S(1)}, u32[]{:S(2)}, u32[]{:S(2)}) collective-permute-start(bf16[200,1024]{1,0:T(8,128)(2,1)} %get-tuple-element.16.refs_0_.refs_6_), channel_id=1, source_target_pairs={{0,16},{16,32},{32,48},{48,64},{64,80},{80,96},{96,112},{112,128},... | collective-permute-start | bytes 1228808 | tf_op jit(solution)/shard_map/ppermute | solution.py:241
  6.9 1.9 %collective-permute-start.8 = (bf16[200,1024]{1,0:T(8,128)(2,1)}, bf16[200,1024]{1,0:T(8,128)(2,1)S(1)}, u32[]{:S(2)}, u32[]{:S(2)}) collective-permute-start(bf16[200,1024]{1,0:T(8,128)(2,1)} %get-tuple-element.16.refs_0_.refs_6_), channel_id=1, source_target_pairs={{48,0},{64,16},{80,32},{96,48},{112,64},{128,80},{144,96},{160,112... | collective-permute-start | bytes 1228808 | tf_op jit(solution)/shard_map/ppermute | solution.py:241
  8.9 10.0 %collective-permute-start = (bf16[208,1024]{1,0:T(8,128)(2,1)}, bf16[208,1024]{1,0:T(8,128)(2,1)S(1)}, u32[]{:S(2)}, u32[]{:S(2)}) collective-permute-start(bf16[208,1024]{1,0:T(8,128)(2,1)} %get-tuple-element.15), channel_id=1, source_target_pairs={{0,8},{8,0},{1,9},{9,1},{2,10},{10,2},{3,11},{11,3},{4,12},{12,4},... | collective-permute-start | bytes 1277960 | tf_op jit(solution)/shard_map/ppermute | solution.py:245
  18.9 3.4 %collective-permute-start.1 = (bf16[200,1024]{1,0:T(8,128)(2,1)}, bf16[200,1024]{1,0:T(8,128)(2,1)S(1)}, u32[]{:S(2)}, u32[]{:S(2)}) collective-permute-start(bf16[200,1024]{1,0:T(8,128)(2,1)} %get-tuple-element.16.refs_0_.refs_6_), channel_id=1, source_target_pairs={{0,2},{2,4},{4,6},{6,0},{1,7},{3,1},{5,3},{7,5},{8,10},{10,12},{12... | collective-permute-start | bytes 1228808 | tf_op jit(solution)/shard_map/ppermute | solution.py:251
  22.3 4.7 %collective-permute-start.9 = (bf16[200,1024]{1,0:T(8,128)(2,1)}, bf16[200,1024]{1,0:T(8,128)(2,1)S(1)}, u32[]{:S(2)}, u32[]{:S(2)}) collective-permute-start(bf16[200,1024]{1,0:T(8,128)(2,1)} %get-tuple-element.16.refs_0_.refs_6_), channel_id=1, source_target_pairs={{0,32},{16,48},{32,64},{48,80},{64,96},{80,112},{96,128},{112,144}... | collective-permute-start | bytes 1228808 | tf_op jit(solution)/shard_map/ppermute | solution.py:241
  27.0 0.0 collective-permute-done.7.refs_0_
  27.0 2.4 %collective-permute-start.3 = (bf16[200,1024]{1,0:T(8,128)(2,1)}, bf16[200,1024]{1,0:T(8,128)(2,1)S(1)}, u32[]{:S(2)}, u32[]{:S(2)}) collective-permute-start(bf16[200,1024]{1,0:T(8,128)(2,1)} %get-tuple-element.16.refs_0_.refs_6_), channel_id=1, source_target_pairs={{0,6},{2,0},{4,2},{6,4},{1,3},{3,5},{5,7},{7,1},{8,14},{10,8},{12,... | collective-permute-start | bytes 1228808 | tf_op jit(solution)/shard_map/ppermute | solution.py:251
  29.5 10.4 %collective-permute-done.8.refs_1_ = bf16[200,1024]{1,0:T(8,128)(2,1)S(1)} collective-permute-done((bf16[200,1024]{1,0:T(8,128)(2,1)}, bf16[200,1024]{1,0:T(8,128)(2,1)S(1)}, u32[]{:S(2)}, u32[]{:S(2)}) %collective-permute-start.8) | collective-permute-done | bytes 409632 | tf_op jit(solution)/shard_map/ppermute | solution.py:241
  39.9 0.1 stack_blocks.1.refs_7_
  39.9 1.9 %collective-permute-start.11 = (bf16[2,200,1024]{2,1,0:T(8,128)(2,1)S(1)}, bf16[2,200,1024]{2,1,0:T(8,128)(2,1)S(1)}, u32[]{:S(2)}, u32[]{:S(2)}) collective-permute-start(bf16[2,200,1024]{2,1,0:T(8,128)(2,1)S(1)} %stack_blocks.1.refs_7_), channel_id=1, source_target_pairs={{0,1},{1,0},{2,3},{3,2},{4,5},{5,4},{6,7},{7,6},{8,9},{9,8},{10,11... | collective-permute-start | bytes 2457608 | tf_op jit(solution)/shard_map/ppermute | solution.py:245
  41.9 0.0 collective-permute-done.1.refs_1_.refs_2_
  41.9 3.4 %collective-permute-start.2 = (bf16[200,1024]{1,0:T(8,128)(2,1)S(1)}, bf16[200,1024]{1,0:T(8,128)(2,1)S(1)}, u32[]{:S(2)}, u32[]{:S(2)}) collective-permute-start(bf16[200,1024]{1,0:T(8,128)(2,1)S(1)} %collective-permute-done.1.refs_1_.refs_2_), channel_id=1, source_target_pairs={{0,2},{2,4},{4,6},{6,0},{1,7},{3,1},{5,3},{7,5},{8,10},{10,12},{12... | collective-permute-start | bytes 1228808 | tf_op jit(solution)/shard_map/ppermute | solution.py:251
  45.3 0.0 collective-permute-done.refs_0_
  45.3 3.1 %collective-permute-start.5 = (bf16[200,1024]{1,0:T(8,128)(2,1)S(1)}, bf16[200,1024]{1,0:T(8,128)(2,1)S(1)}, u32[]{:S(2)}, u32[]{:S(2)}) collective-permute-start(bf16[200,1024]{1,0:T(8,128)(2,1)S(1)} %gate.2.refs_0_.refs_1_), channel_id=1, source_target_pairs={{0,2},{2,4},{4,6},{6,0},{1,7},{3,1},{5,3},{7,5},{8,10},{10,12},{12... | collective-permute-start | bytes 1228808 | tf_op jit(solution)/shard_map/ppermute | solution.py:251
  48.5 0.0 collective-permute-done.9.refs_8_
  48.5 2.5 %collective-permute-start.10 = (bf16[200,1024]{1,0:T(8,128)(2,1)}, bf16[200,1024]{1,0:T(8,128)(2,1)S(1)}, u32[]{:S(2)}, u32[]{:S(2)}) collective-permute-start(bf16[200,1024]{1,0:T(8,128)(2,1)} %get-tuple-element.16.refs_0_.refs_6_), channel_id=1, source_target_pairs={{0,1},{1,0},{2,3},{3,2},{4,5},{5,4},{6,7},{7,6},{8,9},{9,8},{10,11... | collective-permute-start | bytes 1228808 | tf_op jit(solution)/shard_map/ppermute | solution.py:245
  50.9 0.0 collective-permute-done.3.refs_2_.refs_4_
  50.9 1.9 %collective-permute-start.12 = (bf16[200,1024]{1,0:T(8,128)(2,1)S(1)}, bf16[200,1024]{1,0:T(8,128)(2,1)S(1)}, u32[]{:S(2)}, u32[]{:S(2)}) collective-permute-start(bf16[200,1024]{1,0:T(8,128)(2,1)S(1)} %collective-permute-done.9.refs_8_), channel_id=1, source_target_pairs={{0,1},{1,0},{2,3},{3,2},{4,5},{5,4},{6,7},{7,6},{8,9},{9,8},{10,11... | collective-permute-start | bytes 1228808 | tf_op jit(solution)/shard_map/ppermute | solution.py:245
  52.9 0.0 collective-permute-done.2.refs_1_.refs_5_
  52.9 2.7 %collective-permute-start.4 = (bf16[200,1024]{1,0:T(8,128)(2,1)S(1)}, bf16[200,1024]{1,0:T(8,128)(2,1)S(1)}, u32[]{:S(2)}, u32[]{:S(2)}) collective-permute-start(bf16[200,1024]{1,0:T(8,128)(2,1)S(1)} %gate.3), channel_id=1, source_target_pairs={{0,6},{2,0},{4,2},{6,4},{1,3},{3,5},{5,7},{7,1},{8,14},{10,8},{12,... | collective-permute-start | bytes 1228808 | tf_op jit(solution)/shard_map/ppermute | solution.py:251
  55.6 0.5 collective-permute-done.5.refs_3_
  56.1 3.4 %collective-permute-start.6 = (bf16[200,1024]{1,0:T(8,128)(2,1)S(1)}, bf16[200,1024]{1,0:T(8,128)(2,1)S(1)}, u32[]{:S(2)}, u32[]{:S(2)}) collective-permute-start(bf16[200,1024]{1,0:T(8,128)(2,1)S(1)} %collective-permute-done.5.refs_3_), channel_id=1, source_target_pairs={{0,2},{2,4},{4,6},{6,0},{1,7},{3,1},{5,3},{7,5},{8,10},{10,12},{12... | collective-permute-start | bytes 1228808 | tf_op jit(solution)/shard_map/ppermute | solution.py:251
  59.5 0.0 collective-permute-done.10.refs_9_
  59.5 0.0 collective-permute-done.12.refs_11_
  59.5 0.0 collective-permute-done.11.refs_10_
  59.5 0.0 copy-done
  59.6 4.6 %first_maxima.1 = (f32[8,1,192]{2,1,0:T(1,128)S(1)}, f32[1152,128]{1,0:T(8,128)S(1)}, bf16[1536,1024]{1,0:T(8,128)(2,1)S(1)}, f32[1536,128]{1,0:T(8,128)S(1)}, f32[6,1,192]{2,1,0:T(1,128)S(1)}) custom-call(bf16[200,1024]{1,0:T(8,128)(2,1)S(1)} %copy-done, bf16[200,1024]{1,0:T(8,128)(2,1)S(1)} %gate.2.refs_0_.refs_1_, ...), custom_call_target="tpu_custom_call" | custom-call | flops 3623878656 | bytes 5734400 | tf_op jit(solution)/shard_map/first_maxima/pallas_call | solution.py:205
  64.2 1.0 %collective-permute-done.4.refs_0_ = bf16[200,1024]{1,0:T(8,128)(2,1)S(1)} collective-permute-done((bf16[200,1024]{1,0:T(8,128)(2,1)S(1)}, bf16[200,1024]{1,0:T(8,128)(2,1)S(1)}, u32[]{:S(2)}, u32[]{:S(2)}) %collective-permute-start.4) | collective-permute-done | bytes 409632 | tf_op jit(solution)/shard_map/ppermute | solution.py:251
  65.2 1.5 %collective-permute-done.6.refs_1_ = bf16[200,1024]{1,0:T(8,128)(2,1)S(1)} collective-permute-done((bf16[200,1024]{1,0:T(8,128)(2,1)S(1)}, bf16[200,1024]{1,0:T(8,128)(2,1)S(1)}, u32[]{:S(2)}, u32[]{:S(2)}) %collective-permute-start.6) | collective-permute-done | bytes 409632 | tf_op jit(solution)/shard_map/ppermute | solution.py:251
  66.7 2.6 %last_maxima.1 = (f32[8,1,192]{2,1,0:T(1,128)}, f32[3,1,192]{2,1,0:T(1,128)S(1)}, f32[3,1,192]{2,1,0:T(1,128)S(1)}) custom-call(bf16[200,1024]{1,0:T(8,128)(2,1)S(1)} %collective-permute-done.4.refs_0_, bf16[200,1024]{1,0:T(8,128)(2,1)S(1)} %collective-permute-done.6.refs_1_, f32[8,1,192]{2,1,0:T(1,128)S(1)} %get-tuple-element.17.refs_2_, ...), custom_call_target="tpu_custom_call" | custom-call | flops 1207959552 | bytes 4096000 | tf_op jit(solution)/shard_map/last_maxima/pallas_call | solution.py:227
  69.3 2.2 %collective-permute-start.13 = (f32[3,1,192]{2,1,0:T(1,128)S(1)}, f32[3,1,192]{2,1,0:T(1,128)S(1)}, u32[]{:S(2)}, u32[]{:S(2)}) collective-permute-start(f32[3,1,192]{2,1,0:T(1,128)S(1)} %get-tuple-element.24), channel_id=1, source_target_pairs={{0,1},{1,0},{2,3},{3,2},{4,5},{5,4},{6,7},{7,6},{8,9},{9,8},{10,11... | collective-permute-start | bytes 6920 | tf_op jit(solution)/shard_map/ppermute | solution.py:245
  71.5 11.0 %all-to-all-start = ((f32[8,1,192]{2,1,0:T(1,128)}), f32[8,1,192]{2,1,0:T(1,128)S(1)}, u32[]{:S(2)}, u32[]{:S(2)}) async-start(f32[8,1,192]{2,1,0:T(1,128)} %get-tuple-element.22), calls=%async_computation | async-start | bytes 16384 | tf_op jit(solution)/shard_map/all_to_all | solution.py:270
  82.5 0.0 collective-permute-done.13
  82.6 3.3 %collective-permute-start.14 = (f32[1,192]{1,0:T(1,128)S(1)}, f32[1,192]{1,0:T(1,128)S(1)}, u32[]{:S(2)}, u32[]{:S(2)}) collective-permute-start(f32[1,192]{1,0:T(1,128)S(1)} %get-tuple-element.27), channel_id=1, source_target_pairs={{16,0},{32,16},{48,32},{64,48},{80,64},{96,80},{112,96},{128,112},... | collective-permute-start | bytes 2312 | tf_op jit(solution)/shard_map/ppermute | solution.py:241
  85.8 7.3 %collective-permute-start.15 = (f32[1,192]{1,0:T(1,128)S(1)}, f32[1,192]{1,0:T(1,128)S(1)}, u32[]{:S(2)}, u32[]{:S(2)}) collective-permute-start(f32[1,192]{1,0:T(1,128)S(1)} %get-tuple-element.26), channel_id=1, source_target_pairs={{0,48},{16,64},{32,80},{48,96},{64,112},{80,128},{96,144},{112,160... | collective-permute-start | bytes 2312 | tf_op jit(solution)/shard_map/ppermute | solution.py:241
  93.1 1.9 %collective-permute-start.16 = (f32[1,192]{1,0:T(1,128)S(1)}, f32[1,192]{1,0:T(1,128)S(1)}, u32[]{:S(2)}, u32[]{:S(2)}) collective-permute-start(f32[1,192]{1,0:T(1,128)S(1)} %get-tuple-element.25), channel_id=1, source_target_pairs={{32,0},{48,16},{64,32},{80,48},{96,64},{112,80},{128,96},{144,112}... | collective-permute-start | bytes 2312 | tf_op jit(solution)/shard_map/ppermute | solution.py:241
  95.0 0.0 all-to-all-done
  95.1 0.0 collective-permute-done.14
  95.1 0.0 collective-permute-done.15
  95.1 5.6 %collective-permute-done.16 = f32[1,192]{1,0:T(1,128)S(1)} collective-permute-done((f32[1,192]{1,0:T(1,128)S(1)}, f32[1,192]{1,0:T(1,128)S(1)}, u32[]{:S(2)}, u32[]{:S(2)}) %collective-permute-start.16) | collective-permute-done | bytes 800 | tf_op jit(solution)/shard_map/ppermute | solution.py:241
  100.7 0.6 fusion.2
  (5 shorter events, 0.1 us)
Async XLA Ops:
  2.1 57.5 %copy-start = (bf16[200,1024]{1,0:T(8,128)(2,1)S(1)}, bf16[200,1024]{1,0:T(8,128)(2,1)}, u32[]{:S(2)}) copy-start(bf16[200,1024]{1,0:T(8,128)(2,1)} %get-tuple-element.16.refs_0_.refs_6_) | copy-start | bytes 1228804
  2.1 24.9 %collective-permute-start.7 = (bf16[200,1024]{1,0:T(8,128)(2,1)}, bf16[200,1024]{1,0:T(8,128)(2,1)S(1)}, u32[]{:S(2)}, u32[]{:S(2)}) collective-permute-start(bf16[200,1024]{1,0:T(8,128)(2,1)} %get-tuple-element.16.refs_0_.refs_6_), channel_id=1, source_target_pairs={{0,16},{16,32},{32,48},{48,64},{64,80},{80,96},{96,112},{112,128},... | collective-permute-start | bytes 1228808 | tf_op jit(solution)/shard_map/ppermute | solution.py:241
  6.9 33.0 %collective-permute-start.8 = (bf16[200,1024]{1,0:T(8,128)(2,1)}, bf16[200,1024]{1,0:T(8,128)(2,1)S(1)}, u32[]{:S(2)}, u32[]{:S(2)}) collective-permute-start(bf16[200,1024]{1,0:T(8,128)(2,1)} %get-tuple-element.16.refs_0_.refs_6_), channel_id=1, source_target_pairs={{48,0},{64,16},{80,32},{96,48},{112,64},{128,80},{144,96},{160,112... | collective-permute-start | bytes 1228808 | tf_op jit(solution)/shard_map/ppermute | solution.py:241
  8.9 36.4 %collective-permute-start = (bf16[208,1024]{1,0:T(8,128)(2,1)}, bf16[208,1024]{1,0:T(8,128)(2,1)S(1)}, u32[]{:S(2)}, u32[]{:S(2)}) collective-permute-start(bf16[208,1024]{1,0:T(8,128)(2,1)} %get-tuple-element.15), channel_id=1, source_target_pairs={{0,8},{8,0},{1,9},{9,1},{2,10},{10,2},{3,11},{11,3},{4,12},{12,4},... | collective-permute-start | bytes 1277960 | tf_op jit(solution)/shard_map/ppermute | solution.py:245
  18.9 23.0 %collective-permute-start.1 = (bf16[200,1024]{1,0:T(8,128)(2,1)}, bf16[200,1024]{1,0:T(8,128)(2,1)S(1)}, u32[]{:S(2)}, u32[]{:S(2)}) collective-permute-start(bf16[200,1024]{1,0:T(8,128)(2,1)} %get-tuple-element.16.refs_0_.refs_6_), channel_id=1, source_target_pairs={{0,2},{2,4},{4,6},{6,0},{1,7},{3,1},{5,3},{7,5},{8,10},{10,12},{12... | collective-permute-start | bytes 1228808 | tf_op jit(solution)/shard_map/ppermute | solution.py:251
  22.3 26.2 %collective-permute-start.9 = (bf16[200,1024]{1,0:T(8,128)(2,1)}, bf16[200,1024]{1,0:T(8,128)(2,1)S(1)}, u32[]{:S(2)}, u32[]{:S(2)}) collective-permute-start(bf16[200,1024]{1,0:T(8,128)(2,1)} %get-tuple-element.16.refs_0_.refs_6_), channel_id=1, source_target_pairs={{0,32},{16,48},{32,64},{48,80},{64,96},{80,112},{96,128},{112,144}... | collective-permute-start | bytes 1228808 | tf_op jit(solution)/shard_map/ppermute | solution.py:241
  27.0 23.9 %collective-permute-start.3 = (bf16[200,1024]{1,0:T(8,128)(2,1)}, bf16[200,1024]{1,0:T(8,128)(2,1)S(1)}, u32[]{:S(2)}, u32[]{:S(2)}) collective-permute-start(bf16[200,1024]{1,0:T(8,128)(2,1)} %get-tuple-element.16.refs_0_.refs_6_), channel_id=1, source_target_pairs={{0,6},{2,0},{4,2},{6,4},{1,3},{3,5},{5,7},{7,1},{8,14},{10,8},{12,... | collective-permute-start | bytes 1228808 | tf_op jit(solution)/shard_map/ppermute | solution.py:251
  39.9 19.6 %collective-permute-start.11 = (bf16[2,200,1024]{2,1,0:T(8,128)(2,1)S(1)}, bf16[2,200,1024]{2,1,0:T(8,128)(2,1)S(1)}, u32[]{:S(2)}, u32[]{:S(2)}) collective-permute-start(bf16[2,200,1024]{2,1,0:T(8,128)(2,1)S(1)} %stack_blocks.1.refs_7_), channel_id=1, source_target_pairs={{0,1},{1,0},{2,3},{3,2},{4,5},{5,4},{6,7},{7,6},{8,9},{9,8},{10,11... | collective-permute-start | bytes 2457608 | tf_op jit(solution)/shard_map/ppermute | solution.py:245
  41.9 11.0 %collective-permute-start.2 = (bf16[200,1024]{1,0:T(8,128)(2,1)S(1)}, bf16[200,1024]{1,0:T(8,128)(2,1)S(1)}, u32[]{:S(2)}, u32[]{:S(2)}) collective-permute-start(bf16[200,1024]{1,0:T(8,128)(2,1)S(1)} %collective-permute-done.1.refs_1_.refs_2_), channel_id=1, source_target_pairs={{0,2},{2,4},{4,6},{6,0},{1,7},{3,1},{5,3},{7,5},{8,10},{10,12},{12... | collective-permute-start | bytes 1228808 | tf_op jit(solution)/shard_map/ppermute | solution.py:251
  45.3 10.8 %collective-permute-start.5 = (bf16[200,1024]{1,0:T(8,128)(2,1)S(1)}, bf16[200,1024]{1,0:T(8,128)(2,1)S(1)}, u32[]{:S(2)}, u32[]{:S(2)}) collective-permute-start(bf16[200,1024]{1,0:T(8,128)(2,1)S(1)} %gate.2.refs_0_.refs_1_), channel_id=1, source_target_pairs={{0,2},{2,4},{4,6},{6,0},{1,7},{3,1},{5,3},{7,5},{8,10},{10,12},{12... | collective-permute-start | bytes 1228808 | tf_op jit(solution)/shard_map/ppermute | solution.py:251
  48.5 11.1 %collective-permute-start.10 = (bf16[200,1024]{1,0:T(8,128)(2,1)}, bf16[200,1024]{1,0:T(8,128)(2,1)S(1)}, u32[]{:S(2)}, u32[]{:S(2)}) collective-permute-start(bf16[200,1024]{1,0:T(8,128)(2,1)} %get-tuple-element.16.refs_0_.refs_6_), channel_id=1, source_target_pairs={{0,1},{1,0},{2,3},{3,2},{4,5},{5,4},{6,7},{7,6},{8,9},{9,8},{10,11... | collective-permute-start | bytes 1228808 | tf_op jit(solution)/shard_map/ppermute | solution.py:245
  50.9 8.6 %collective-permute-start.12 = (bf16[200,1024]{1,0:T(8,128)(2,1)S(1)}, bf16[200,1024]{1,0:T(8,128)(2,1)S(1)}, u32[]{:S(2)}, u32[]{:S(2)}) collective-permute-start(bf16[200,1024]{1,0:T(8,128)(2,1)S(1)} %collective-permute-done.9.refs_8_), channel_id=1, source_target_pairs={{0,1},{1,0},{2,3},{3,2},{4,5},{5,4},{6,7},{7,6},{8,9},{9,8},{10,11... | collective-permute-start | bytes 1228808 | tf_op jit(solution)/shard_map/ppermute | solution.py:245
  52.9 12.3 %collective-permute-start.4 = (bf16[200,1024]{1,0:T(8,128)(2,1)S(1)}, bf16[200,1024]{1,0:T(8,128)(2,1)S(1)}, u32[]{:S(2)}, u32[]{:S(2)}) collective-permute-start(bf16[200,1024]{1,0:T(8,128)(2,1)S(1)} %gate.3), channel_id=1, source_target_pairs={{0,6},{2,0},{4,2},{6,4},{1,3},{3,5},{5,7},{7,1},{8,14},{10,8},{12,... | collective-permute-start | bytes 1228808 | tf_op jit(solution)/shard_map/ppermute | solution.py:251
  56.1 10.6 %collective-permute-start.6 = (bf16[200,1024]{1,0:T(8,128)(2,1)S(1)}, bf16[200,1024]{1,0:T(8,128)(2,1)S(1)}, u32[]{:S(2)}, u32[]{:S(2)}) collective-permute-start(bf16[200,1024]{1,0:T(8,128)(2,1)S(1)} %collective-permute-done.5.refs_3_), channel_id=1, source_target_pairs={{0,2},{2,4},{4,6},{6,0},{1,7},{3,1},{5,3},{7,5},{8,10},{10,12},{12... | collective-permute-start | bytes 1228808 | tf_op jit(solution)/shard_map/ppermute | solution.py:251
  69.3 13.2 %collective-permute-start.13 = (f32[3,1,192]{2,1,0:T(1,128)S(1)}, f32[3,1,192]{2,1,0:T(1,128)S(1)}, u32[]{:S(2)}, u32[]{:S(2)}) collective-permute-start(f32[3,1,192]{2,1,0:T(1,128)S(1)} %get-tuple-element.24), channel_id=1, source_target_pairs={{0,1},{1,0},{2,3},{3,2},{4,5},{5,4},{6,7},{7,6},{8,9},{9,8},{10,11... | collective-permute-start | bytes 6920 | tf_op jit(solution)/shard_map/ppermute | solution.py:245
  71.5 23.5 %all-to-all-start = ((f32[8,1,192]{2,1,0:T(1,128)}), f32[8,1,192]{2,1,0:T(1,128)S(1)}, u32[]{:S(2)}, u32[]{:S(2)}) async-start(f32[8,1,192]{2,1,0:T(1,128)} %get-tuple-element.22), calls=%async_computation | async-start | bytes 16384 | tf_op jit(solution)/shard_map/all_to_all | solution.py:270
  82.6 12.5 %collective-permute-start.14 = (f32[1,192]{1,0:T(1,128)S(1)}, f32[1,192]{1,0:T(1,128)S(1)}, u32[]{:S(2)}, u32[]{:S(2)}) collective-permute-start(f32[1,192]{1,0:T(1,128)S(1)} %get-tuple-element.27), channel_id=1, source_target_pairs={{16,0},{32,16},{48,32},{64,48},{80,64},{96,80},{112,96},{128,112},... | collective-permute-start | bytes 2312 | tf_op jit(solution)/shard_map/ppermute | solution.py:241
  85.8 9.3 %collective-permute-start.15 = (f32[1,192]{1,0:T(1,128)S(1)}, f32[1,192]{1,0:T(1,128)S(1)}, u32[]{:S(2)}, u32[]{:S(2)}) collective-permute-start(f32[1,192]{1,0:T(1,128)S(1)} %get-tuple-element.26), channel_id=1, source_target_pairs={{0,48},{16,64},{32,80},{48,96},{64,112},{80,128},{96,144},{112,160... | collective-permute-start | bytes 2312 | tf_op jit(solution)/shard_map/ppermute | solution.py:241
  93.1 7.6 %collective-permute-start.16 = (f32[1,192]{1,0:T(1,128)S(1)}, f32[1,192]{1,0:T(1,128)S(1)}, u32[]{:S(2)}, u32[]{:S(2)}) collective-permute-start(f32[1,192]{1,0:T(1,128)S(1)} %get-tuple-element.25), channel_id=1, source_target_pairs={{32,0},{48,16},{64,32},{80,48},{96,64},{112,80},{128,96},{144,112}... | collective-permute-start | bytes 2312 | tf_op jit(solution)/shard_map/ppermute | solution.py:241

commit v12 on v11

--- a/solution.py
+++ b/solution.py
@@ -17,7 +17,7 @@
 TILE = 256
 FAR = 1.0e9
 FIRST = 6
-HELD = ((0, 0), (1, 0), (0, 1), (1, 1), (0, 3), (0, 2), (1, 3), (1, 2))
+HELD = ((0, 0), (1, 0), (0, 1), (1, 1), (0, 3), (1, 3), (0, 2), (1, 2))
 
 
 def pack_kernel(emb_any, lab_any, ord_any, out_ref, tall_ref, emb_ref, lab_ref, ord_ref, sems):
@@ -261,12 +261,12 @@
     sib = swap(block, "core")
     flipped = gate(swap(tall, "zh"), ahead)
     flip_ahead = turn_x(flipped, 1)
-    flip_behind = turn_x(gate(flipped, across, behind), -1)
+    flip_behind = turn_x(gate(flipped, behind), -1)
     flip_across = turn_x(flip_ahead, 1)
     mine = (block, stack((one, far)), two)
     theirs = [swap(value, "core") for value in mine]
-    carried = first_maxima((*mine, *theirs), [block, flipped, ahead, flip_ahead, behind, across])
-    cols, rows, rows_sib = last_maxima([flip_behind, flip_across], carried)
+    carried = first_maxima((*mine, *theirs), [block, flipped, ahead, flip_ahead, behind, flip_behind])
+    cols, rows, rows_sib = last_maxima([across, flip_across], carried)
     best = jnp.max(lax.all_to_all(cols, ("zh", "x"), 0, 0, tiled=True), axis=0)
     mine = jnp.maximum(rows, swap(rows_sib, "core"))
     for i, steps in enumerate(MOVES):

time: 102 us -> 103 us (level)
  waiting for transfers between devices: 19 us -> 20.6 us
    ppermute x6, waiting for transfers between devices: 2.98 us -> 4.55 us  [turn_x(): return lax.ppermute(value, ('x', 'core'), pairs)]
  transfers between devices with their start and end apart: 18 -> 18, of which waited for: 5 -> 4; matrix products, arithmetic and copies ran while one was open for 0% -> 0% of each run, Pallas kernels for 5% -> 5%
where the time goes in v12:
time: 103 us; the launch traced here: 102 us
  starting transfers between devices  71.4 us (69%)
  waiting for transfers between devices  20.6 us (20%)
  Pallas kernels  9.41 us (9%)
    ppermute x6, starting transfers between devices, shift(): return lax.ppermute(value, 'grp', pairs)  23.9 us
    ppermute x5, starting transfers between devices, swap(): return lax.ppermute(value, axis, [(0, 1), (1, 0)])  18.5 us
    ppermute x6, starting transfers between devices, turn_x(): return lax.ppermute(value, ('x', 'core'), pairs)  18.2 us
    ppermute x6, waiting for transfers between devices, shift(): return lax.ppermute(value, 'grp', pairs)  16 us
    all_to_all x1, starting transfers between devices, per_device(): best = jnp.max(lax.all_to_all(cols, ('zh', 'x'), 0, 0, tiled=True), axis=0)  10.9 us
    pallas_call x1, Pallas kernels, first_maxima(): pl.pallas_call(first_kernel, out_shape=(jax.ShapeDtypeStruct((2 * X, 1, R...  4.6 us
    ppermute x6, waiting for transfers between devices, turn_x(): return lax.ppermute(value, ('x', 'core'), pairs)  4.55 us
    pallas_call x1, Pallas kernels, last_maxima(): pl.pallas_call(last_kernel, out_shape=(jax.ShapeDtypeStruct((2 * X, 1, RO...  2.62 us
  transfers between devices with their start and end apart: 18, of which 4 were waited for; matrix products, arithmetic and copies ran while one was open for 0% of the time, Pallas kernels for 5%

profile of v12, /device:TPU:90, one launch (start us, length us, event | category | flops | bytes accessed | tf_op | source)
XLA Modules:
  0.0 102.3 jit_solution(10741877674897526408)
XLA Ops:
  0.0 2.1 %normalize_pack.1 = (bf16[200,1024]{1,0:T(8,128)(2,1)}, bf16[208,1024]{1,0:T(8,128)(2,1)}) custom-call(bf16[192,1024]{1,0:T(8,128)(2,1)} %emb_any.1, s32[1,192]{1,0:T(1,128)} %bitcast.11, s32[1,192]{1,0:T(1,128)} %bitcast.12), custom_call_target="tpu_custom_call" | custom-call | flops 786432 | bytes 786432 | tf_op jit(solution)/shard_map/normalize_pack/pallas_call | solution.py:52
  2.1 0.0 copy-start
  2.1 4.8 %collective-permute-start.7 = (bf16[200,1024]{1,0:T(8,128)(2,1)}, bf16[200,1024]{1,0:T(8,128)(2,1)S(1)}, u32[]{:S(2)}, u32[]{:S(2)}) collective-permute-start(bf16[200,1024]{1,0:T(8,128)(2,1)} %get-tuple-element.15.refs_0_.refs_6_), channel_id=1, source_target_pairs={{0,16},{16,32},{32,48},{48,64},{64,80},{80,96},{96,112},{112,128},... | collective-permute-start | bytes 1228808 | tf_op jit(solution)/shard_map/ppermute | solution.py:241
  6.9 1.9 %collective-permute-start.8 = (bf16[200,1024]{1,0:T(8,128)(2,1)}, bf16[200,1024]{1,0:T(8,128)(2,1)S(1)}, u32[]{:S(2)}, u32[]{:S(2)}) collective-permute-start(bf16[200,1024]{1,0:T(8,128)(2,1)} %get-tuple-element.15.refs_0_.refs_6_), channel_id=1, source_target_pairs={{48,0},{64,16},{80,32},{96,48},{112,64},{128,80},{144,96},{160,112... | collective-permute-start | bytes 1228808 | tf_op jit(solution)/shard_map/ppermute | solution.py:241
  8.9 10.0 %collective-permute-start.2 = (bf16[208,1024]{1,0:T(8,128)(2,1)}, bf16[208,1024]{1,0:T(8,128)(2,1)S(1)}, u32[]{:S(2)}, u32[]{:S(2)}) collective-permute-start(bf16[208,1024]{1,0:T(8,128)(2,1)} %get-tuple-element.16), channel_id=1, source_target_pairs={{0,8},{8,0},{1,9},{9,1},{2,10},{10,2},{3,11},{11,3},{4,12},{12,4},... | collective-permute-start | bytes 1277960 | tf_op jit(solution)/shard_map/ppermute | solution.py:245
  18.9 3.4 %collective-permute-start = (bf16[200,1024]{1,0:T(8,128)(2,1)}, bf16[200,1024]{1,0:T(8,128)(2,1)S(1)}, u32[]{:S(2)}, u32[]{:S(2)}) collective-permute-start(bf16[200,1024]{1,0:T(8,128)(2,1)} %get-tuple-element.15.refs_0_.refs_6_), channel_id=1, source_target_pairs={{0,2},{2,4},{4,6},{6,0},{1,7},{3,1},{5,3},{7,5},{8,10},{10,12},{12... | collective-permute-start | bytes 1228808 | tf_op jit(solution)/shard_map/ppermute | solution.py:251
  22.3 4.7 %collective-permute-start.9 = (bf16[200,1024]{1,0:T(8,128)(2,1)}, bf16[200,1024]{1,0:T(8,128)(2,1)S(1)}, u32[]{:S(2)}, u32[]{:S(2)}) collective-permute-start(bf16[200,1024]{1,0:T(8,128)(2,1)} %get-tuple-element.15.refs_0_.refs_6_), channel_id=1, source_target_pairs={{0,32},{16,48},{32,64},{48,80},{64,96},{80,112},{96,128},{112,144}... | collective-permute-start | bytes 1228808 | tf_op jit(solution)/shard_map/ppermute | solution.py:241
  27.0 0.0 collective-permute-done.7.refs_0_
  27.0 2.4 %collective-permute-start.5 = (bf16[200,1024]{1,0:T(8,128)(2,1)}, bf16[200,1024]{1,0:T(8,128)(2,1)S(1)}, u32[]{:S(2)}, u32[]{:S(2)}) collective-permute-start(bf16[200,1024]{1,0:T(8,128)(2,1)} %get-tuple-element.15.refs_0_.refs_6_), channel_id=1, source_target_pairs={{0,6},{2,0},{4,2},{6,4},{1,3},{3,5},{5,7},{7,1},{8,14},{10,8},{12,... | collective-permute-start | bytes 1228808 | tf_op jit(solution)/shard_map/ppermute | solution.py:251
  29.5 10.4 %collective-permute-done.8.refs_1_ = bf16[200,1024]{1,0:T(8,128)(2,1)S(1)} collective-permute-done((bf16[200,1024]{1,0:T(8,128)(2,1)}, bf16[200,1024]{1,0:T(8,128)(2,1)S(1)}, u32[]{:S(2)}, u32[]{:S(2)}) %collective-permute-start.8) | collective-permute-done | bytes 409632 | tf_op jit(solution)/shard_map/ppermute | solution.py:241
  39.9 0.1 stack_blocks.1.refs_7_
  39.9 1.9 %collective-permute-start.11 = (bf16[2,200,1024]{2,1,0:T(8,128)(2,1)S(1)}, bf16[2,200,1024]{2,1,0:T(8,128)(2,1)S(1)}, u32[]{:S(2)}, u32[]{:S(2)}) collective-permute-start(bf16[2,200,1024]{2,1,0:T(8,128)(2,1)S(1)} %stack_blocks.1.refs_7_), channel_id=1, source_target_pairs={{0,1},{1,0},{2,3},{3,2},{4,5},{5,4},{6,7},{7,6},{8,9},{9,8},{10,11... | collective-permute-start | bytes 2457608 | tf_op jit(solution)/shard_map/ppermute | solution.py:245
  41.9 0.0 collective-permute-done.refs_1_.refs_2_
  41.9 2.4 %collective-permute-start.10 = (bf16[200,1024]{1,0:T(8,128)(2,1)}, bf16[200,1024]{1,0:T(8,128)(2,1)S(1)}, u32[]{:S(2)}, u32[]{:S(2)}) collective-permute-start(bf16[200,1024]{1,0:T(8,128)(2,1)} %get-tuple-element.15.refs_0_.refs_6_), channel_id=1, source_target_pairs={{0,1},{1,0},{2,3},{3,2},{4,5},{5,4},{6,7},{7,6},{8,9},{9,8},{10,11... | collective-permute-start | bytes 1228808 | tf_op jit(solution)/shard_map/ppermute | solution.py:245
  44.3 0.0 collective-permute-done.2.refs_0_
  44.3 3.4 %collective-permute-start.3 = (bf16[200,1024]{1,0:T(8,128)(2,1)S(1)}, bf16[200,1024]{1,0:T(8,128)(2,1)S(1)}, u32[]{:S(2)}, u32[]{:S(2)}) collective-permute-start(bf16[200,1024]{1,0:T(8,128)(2,1)S(1)} %gate.2.refs_0_.refs_1_), channel_id=1, source_target_pairs={{0,2},{2,4},{4,6},{6,0},{1,7},{3,1},{5,3},{7,5},{8,10},{10,12},{12... | collective-permute-start | bytes 1228808 | tf_op jit(solution)/shard_map/ppermute | solution.py:251
  47.8 0.0 collective-permute-done.9.refs_8_
  47.8 1.9 %collective-permute-start.12 = (bf16[200,1024]{1,0:T(8,128)(2,1)S(1)}, bf16[200,1024]{1,0:T(8,128)(2,1)S(1)}, u32[]{:S(2)}, u32[]{:S(2)}) collective-permute-start(bf16[200,1024]{1,0:T(8,128)(2,1)S(1)} %collective-permute-done.9.refs_8_), channel_id=1, source_target_pairs={{0,1},{1,0},{2,3},{3,2},{4,5},{5,4},{6,7},{7,6},{8,9},{9,8},{10,11... | collective-permute-start | bytes 1228808 | tf_op jit(solution)/shard_map/ppermute | solution.py:245
  49.7 0.0 collective-permute-done.5.refs_1_.refs_4_
  49.7 3.4 %collective-permute-start.6 = (bf16[200,1024]{1,0:T(8,128)(2,1)S(1)}, bf16[200,1024]{1,0:T(8,128)(2,1)S(1)}, u32[]{:S(2)}, u32[]{:S(2)}) collective-permute-start(bf16[200,1024]{1,0:T(8,128)(2,1)S(1)} %gate.3), channel_id=1, source_target_pairs={{0,6},{2,0},{4,2},{6,4},{1,3},{3,5},{5,7},{7,1},{8,14},{10,8},{12,... | collective-permute-start | bytes 1228808 | tf_op jit(solution)/shard_map/ppermute | solution.py:251
  53.2 0.0 collective-permute-done.10.refs_9_
  53.2 2.4 %collective-permute-start.1 = (bf16[200,1024]{1,0:T(8,128)(2,1)S(1)}, bf16[200,1024]{1,0:T(8,128)(2,1)S(1)}, u32[]{:S(2)}, u32[]{:S(2)}) collective-permute-start(bf16[200,1024]{1,0:T(8,128)(2,1)S(1)} %collective-permute-done.refs_1_.refs_2_), channel_id=1, source_target_pairs={{0,2},{2,4},{4,6},{6,0},{1,7},{3,1},{5,3},{7,5},{8,10},{10,12},{12... | collective-permute-start | bytes 1228808 | tf_op jit(solution)/shard_map/ppermute | solution.py:251
  55.6 0.0 collective-permute-done.3.refs_3_
  55.6 3.1 %collective-permute-start.4 = (bf16[200,1024]{1,0:T(8,128)(2,1)S(1)}, bf16[200,1024]{1,0:T(8,128)(2,1)S(1)}, u32[]{:S(2)}, u32[]{:S(2)}) collective-permute-start(bf16[200,1024]{1,0:T(8,128)(2,1)S(1)} %collective-permute-done.3.refs_3_), channel_id=1, source_target_pairs={{0,2},{2,4},{4,6},{6,0},{1,7},{3,1},{5,3},{7,5},{8,10},{10,12},{12... | collective-permute-start | bytes 1228808 | tf_op jit(solution)/shard_map/ppermute | solution.py:251
  58.7 0.0 collective-permute-done.12.refs_11_
  58.7 2.8 %collective-permute-done.6.refs_5_ = bf16[200,1024]{1,0:T(8,128)(2,1)S(1)} collective-permute-done((bf16[200,1024]{1,0:T(8,128)(2,1)S(1)}, bf16[200,1024]{1,0:T(8,128)(2,1)S(1)}, u32[]{:S(2)}, u32[]{:S(2)}) %collective-permute-start.6) | collective-permute-done | bytes 409632 | tf_op jit(solution)/shard_map/ppermute | solution.py:251
  61.5 0.0 collective-permute-done.11.refs_10_
  61.5 0.0 copy-done
  61.5 4.6 %first_maxima.1 = (f32[8,1,192]{2,1,0:T(1,128)S(1)}, f32[1152,128]{1,0:T(8,128)S(1)}, bf16[1536,1024]{1,0:T(8,128)(2,1)S(1)}, f32[1536,128]{1,0:T(8,128)S(1)}, f32[6,1,192]{2,1,0:T(1,128)S(1)}) custom-call(bf16[200,1024]{1,0:T(8,128)(2,1)S(1)} %copy-done, bf16[200,1024]{1,0:T(8,128)(2,1)S(1)} %gate.2.refs_0_.refs_1_, ...), custom_call_target="tpu_custom_call" | custom-call | flops 3623878656 | bytes 5734400 | tf_op jit(solution)/shard_map/first_maxima/pallas_call | solution.py:205
  66.1 0.0 collective-permute-done.1.refs_0_
  66.1 1.7 %collective-permute-done.4.refs_1_ = bf16[200,1024]{1,0:T(8,128)(2,1)S(1)} collective-permute-done((bf16[200,1024]{1,0:T(8,128)(2,1)S(1)}, bf16[200,1024]{1,0:T(8,128)(2,1)S(1)}, u32[]{:S(2)}, u32[]{:S(2)}) %collective-permute-start.4) | collective-permute-done | bytes 409632 | tf_op jit(solution)/shard_map/ppermute | solution.py:251
  67.9 2.6 %last_maxima.1 = (f32[8,1,192]{2,1,0:T(1,128)}, f32[3,1,192]{2,1,0:T(1,128)S(1)}, f32[3,1,192]{2,1,0:T(1,128)S(1)}) custom-call(bf16[200,1024]{1,0:T(8,128)(2,1)S(1)} %collective-permute-done.1.refs_0_, bf16[200,1024]{1,0:T(8,128)(2,1)S(1)} %collective-permute-done.4.refs_1_, f32[8,1,192]{2,1,0:T(1,128)S(1)} %get-tuple-element.17.refs_2_, ...), custom_call_target="tpu_custom_call" | custom-call | flops 1207959552 | bytes 4096000 | tf_op jit(solution)/shard_map/last_maxima/pallas_call | solution.py:227
  70.5 2.2 %collective-permute-start.13 = (f32[3,1,192]{2,1,0:T(1,128)S(1)}, f32[3,1,192]{2,1,0:T(1,128)S(1)}, u32[]{:S(2)}, u32[]{:S(2)}) collective-permute-start(f32[3,1,192]{2,1,0:T(1,128)S(1)} %get-tuple-element.24), channel_id=1, source_target_pairs={{0,1},{1,0},{2,3},{3,2},{4,5},{5,4},{6,7},{7,6},{8,9},{9,8},{10,11... | collective-permute-start | bytes 6920 | tf_op jit(solution)/shard_map/ppermute | solution.py:245
  72.7 10.9 %all-to-all-start = ((f32[8,1,192]{2,1,0:T(1,128)}), f32[8,1,192]{2,1,0:T(1,128)S(1)}, u32[]{:S(2)}, u32[]{:S(2)}) async-start(f32[8,1,192]{2,1,0:T(1,128)} %get-tuple-element.22), calls=%async_computation | async-start | bytes 16384 | tf_op jit(solution)/shard_map/all_to_all | solution.py:270
  83.6 0.0 collective-permute-done.13
  83.6 3.3 %collective-permute-start.14 = (f32[1,192]{1,0:T(1,128)S(1)}, f32[1,192]{1,0:T(1,128)S(1)}, u32[]{:S(2)}, u32[]{:S(2)}) collective-permute-start(f32[1,192]{1,0:T(1,128)S(1)} %get-tuple-element.27), channel_id=1, source_target_pairs={{16,0},{32,16},{48,32},{64,48},{80,64},{96,80},{112,96},{128,112},... | collective-permute-start | bytes 2312 | tf_op jit(solution)/shard_map/ppermute | solution.py:241
  86.9 7.3 %collective-permute-start.15 = (f32[1,192]{1,0:T(1,128)S(1)}, f32[1,192]{1,0:T(1,128)S(1)}, u32[]{:S(2)}, u32[]{:S(2)}) collective-permute-start(f32[1,192]{1,0:T(1,128)S(1)} %get-tuple-element.26), channel_id=1, source_target_pairs={{0,48},{16,64},{32,80},{48,96},{64,112},{80,128},{96,144},{112,160... | collective-permute-start | bytes 2312 | tf_op jit(solution)/shard_map/ppermute | solution.py:241
  94.1 1.9 %collective-permute-start.16 = (f32[1,192]{1,0:T(1,128)S(1)}, f32[1,192]{1,0:T(1,128)S(1)}, u32[]{:S(2)}, u32[]{:S(2)}) collective-permute-start(f32[1,192]{1,0:T(1,128)S(1)} %get-tuple-element.25), channel_id=1, source_target_pairs={{32,0},{48,16},{64,32},{80,48},{96,64},{112,80},{128,96},{144,112}... | collective-permute-start | bytes 2312 | tf_op jit(solution)/shard_map/ppermute | solution.py:241
  96.1 0.0 all-to-all-done
  96.1 0.0 collective-permute-done.14
  96.1 0.0 collective-permute-done.15
  96.1 5.6 %collective-permute-done.16 = f32[1,192]{1,0:T(1,128)S(1)} collective-permute-done((f32[1,192]{1,0:T(1,128)S(1)}, f32[1,192]{1,0:T(1,128)S(1)}, u32[]{:S(2)}, u32[]{:S(2)}) %collective-permute-start.16) | collective-permute-done | bytes 800 | tf_op jit(solution)/shard_map/ppermute | solution.py:241
  101.7 0.6 fusion.2
  (5 shorter events, 0.1 us)
Async XLA Ops:
  2.1 59.4 %copy-start = (bf16[200,1024]{1,0:T(8,128)(2,1)S(1)}, bf16[200,1024]{1,0:T(8,128)(2,1)}, u32[]{:S(2)}) copy-start(bf16[200,1024]{1,0:T(8,128)(2,1)} %get-tuple-element.15.refs_0_.refs_6_) | copy-start | bytes 1228804
  2.1 24.9 %collective-permute-start.7 = (bf16[200,1024]{1,0:T(8,128)(2,1)}, bf16[200,1024]{1,0:T(8,128)(2,1)S(1)}, u32[]{:S(2)}, u32[]{:S(2)}) collective-permute-start(bf16[200,1024]{1,0:T(8,128)(2,1)} %get-tuple-element.15.refs_0_.refs_6_), channel_id=1, source_target_pairs={{0,16},{16,32},{32,48},{48,64},{64,80},{80,96},{96,112},{112,128},... | collective-permute-start | bytes 1228808 | tf_op jit(solution)/shard_map/ppermute | solution.py:241
  6.9 33.0 %collective-permute-start.8 = (bf16[200,1024]{1,0:T(8,128)(2,1)}, bf16[200,1024]{1,0:T(8,128)(2,1)S(1)}, u32[]{:S(2)}, u32[]{:S(2)}) collective-permute-start(bf16[200,1024]{1,0:T(8,128)(2,1)} %get-tuple-element.15.refs_0_.refs_6_), channel_id=1, source_target_pairs={{48,0},{64,16},{80,32},{96,48},{112,64},{128,80},{144,96},{160,112... | collective-permute-start | bytes 1228808 | tf_op jit(solution)/shard_map/ppermute | solution.py:241
  8.9 35.4 %collective-permute-start.2 = (bf16[208,1024]{1,0:T(8,128)(2,1)}, bf16[208,1024]{1,0:T(8,128)(2,1)S(1)}, u32[]{:S(2)}, u32[]{:S(2)}) collective-permute-start(bf16[208,1024]{1,0:T(8,128)(2,1)} %get-tuple-element.16), channel_id=1, source_target_pairs={{0,8},{8,0},{1,9},{9,1},{2,10},{10,2},{3,11},{11,3},{4,12},{12,4},... | collective-permute-start | bytes 1277960 | tf_op jit(solution)/shard_map/ppermute | solution.py:245
  18.9 23.0 %collective-permute-start = (bf16[200,1024]{1,0:T(8,128)(2,1)}, bf16[200,1024]{1,0:T(8,128)(2,1)S(1)}, u32[]{:S(2)}, u32[]{:S(2)}) collective-permute-start(bf16[200,1024]{1,0:T(8,128)(2,1)} %get-tuple-element.15.refs_0_.refs_6_), channel_id=1, source_target_pairs={{0,2},{2,4},{4,6},{6,0},{1,7},{3,1},{5,3},{7,5},{8,10},{10,12},{12... | collective-permute-start | bytes 1228808 | tf_op jit(solution)/shard_map/ppermute | solution.py:251
  22.3 25.5 %collective-permute-start.9 = (bf16[200,1024]{1,0:T(8,128)(2,1)}, bf16[200,1024]{1,0:T(8,128)(2,1)S(1)}, u32[]{:S(2)}, u32[]{:S(2)}) collective-permute-start(bf16[200,1024]{1,0:T(8,128)(2,1)} %get-tuple-element.15.refs_0_.refs_6_), channel_id=1, source_target_pairs={{0,32},{16,48},{32,64},{48,80},{64,96},{80,112},{96,128},{112,144}... | collective-permute-start | bytes 1228808 | tf_op jit(solution)/shard_map/ppermute | solution.py:241
  27.0 22.7 %collective-permute-start.5 = (bf16[200,1024]{1,0:T(8,128)(2,1)}, bf16[200,1024]{1,0:T(8,128)(2,1)S(1)}, u32[]{:S(2)}, u32[]{:S(2)}) collective-permute-start(bf16[200,1024]{1,0:T(8,128)(2,1)} %get-tuple-element.15.refs_0_.refs_6_), channel_id=1, source_target_pairs={{0,6},{2,0},{4,2},{6,4},{1,3},{3,5},{5,7},{7,1},{8,14},{10,8},{12,... | collective-permute-start | bytes 1228808 | tf_op jit(solution)/shard_map/ppermute | solution.py:251
  39.9 21.6 %collective-permute-start.11 = (bf16[2,200,1024]{2,1,0:T(8,128)(2,1)S(1)}, bf16[2,200,1024]{2,1,0:T(8,128)(2,1)S(1)}, u32[]{:S(2)}, u32[]{:S(2)}) collective-permute-start(bf16[2,200,1024]{2,1,0:T(8,128)(2,1)S(1)} %stack_blocks.1.refs_7_), channel_id=1, source_target_pairs={{0,1},{1,0},{2,3},{3,2},{4,5},{5,4},{6,7},{7,6},{8,9},{9,8},{10,11... | collective-permute-start | bytes 2457608 | tf_op jit(solution)/shard_map/ppermute | solution.py:245
  41.9 11.3 %collective-permute-start.10 = (bf16[200,1024]{1,0:T(8,128)(2,1)}, bf16[200,1024]{1,0:T(8,128)(2,1)S(1)}, u32[]{:S(2)}, u32[]{:S(2)}) collective-permute-start(bf16[200,1024]{1,0:T(8,128)(2,1)} %get-tuple-element.15.refs_0_.refs_6_), channel_id=1, source_target_pairs={{0,1},{1,0},{2,3},{3,2},{4,5},{5,4},{6,7},{7,6},{8,9},{9,8},{10,11... | collective-permute-start | bytes 1228808 | tf_op jit(solution)/shard_map/ppermute | solution.py:245
  44.3 11.3 %collective-permute-start.3 = (bf16[200,1024]{1,0:T(8,128)(2,1)S(1)}, bf16[200,1024]{1,0:T(8,128)(2,1)S(1)}, u32[]{:S(2)}, u32[]{:S(2)}) collective-permute-start(bf16[200,1024]{1,0:T(8,128)(2,1)S(1)} %gate.2.refs_0_.refs_1_), channel_id=1, source_target_pairs={{0,2},{2,4},{4,6},{6,0},{1,7},{3,1},{5,3},{7,5},{8,10},{10,12},{12... | collective-permute-start | bytes 1228808 | tf_op jit(solution)/shard_map/ppermute | solution.py:251
  47.8 11.0 %collective-permute-start.12 = (bf16[200,1024]{1,0:T(8,128)(2,1)S(1)}, bf16[200,1024]{1,0:T(8,128)(2,1)S(1)}, u32[]{:S(2)}, u32[]{:S(2)}) collective-permute-start(bf16[200,1024]{1,0:T(8,128)(2,1)S(1)} %collective-permute-done.9.refs_8_), channel_id=1, source_target_pairs={{0,1},{1,0},{2,3},{3,2},{4,5},{5,4},{6,7},{7,6},{8,9},{9,8},{10,11... | collective-permute-start | bytes 1228808 | tf_op jit(solution)/shard_map/ppermute | solution.py:245
  49.7 11.8 %collective-permute-start.6 = (bf16[200,1024]{1,0:T(8,128)(2,1)S(1)}, bf16[200,1024]{1,0:T(8,128)(2,1)S(1)}, u32[]{:S(2)}, u32[]{:S(2)}) collective-permute-start(bf16[200,1024]{1,0:T(8,128)(2,1)S(1)} %gate.3), channel_id=1, source_target_pairs={{0,6},{2,0},{4,2},{6,4},{1,3},{3,5},{5,7},{7,1},{8,14},{10,8},{12,... | collective-permute-start | bytes 1228808 | tf_op jit(solution)/shard_map/ppermute | solution.py:251
  53.2 13.0 %collective-permute-start.1 = (bf16[200,1024]{1,0:T(8,128)(2,1)S(1)}, bf16[200,1024]{1,0:T(8,128)(2,1)S(1)}, u32[]{:S(2)}, u32[]{:S(2)}) collective-permute-start(bf16[200,1024]{1,0:T(8,128)(2,1)S(1)} %collective-permute-done.refs_1_.refs_2_), channel_id=1, source_target_pairs={{0,2},{2,4},{4,6},{6,0},{1,7},{3,1},{5,3},{7,5},{8,10},{10,12},{12... | collective-permute-start | bytes 1228808 | tf_op jit(solution)/shard_map/ppermute | solution.py:251
  55.6 12.3 %collective-permute-start.4 = (bf16[200,1024]{1,0:T(8,128)(2,1)S(1)}, bf16[200,1024]{1,0:T(8,128)(2,1)S(1)}, u32[]{:S(2)}, u32[]{:S(2)}) collective-permute-start(bf16[200,1024]{1,0:T(8,128)(2,1)S(1)} %collective-permute-done.3.refs_3_), channel_id=1, source_target_pairs={{0,2},{2,4},{4,6},{6,0},{1,7},{3,1},{5,3},{7,5},{8,10},{10,12},{12... | collective-permute-start | bytes 1228808 | tf_op jit(solution)/shard_map/ppermute | solution.py:251
  70.5 13.1 %collective-permute-start.13 = (f32[3,1,192]{2,1,0:T(1,128)S(1)}, f32[3,1,192]{2,1,0:T(1,128)S(1)}, u32[]{:S(2)}, u32[]{:S(2)}) collective-permute-start(f32[3,1,192]{2,1,0:T(1,128)S(1)} %get-tuple-element.24), channel_id=1, source_target_pairs={{0,1},{1,0},{2,3},{3,2},{4,5},{5,4},{6,7},{7,6},{8,9},{9,8},{10,11... | collective-permute-start | bytes 6920 | tf_op jit(solution)/shard_map/ppermute | solution.py:245
  72.7 23.4 %all-to-all-start = ((f32[8,1,192]{2,1,0:T(1,128)}), f32[8,1,192]{2,1,0:T(1,128)S(1)}, u32[]{:S(2)}, u32[]{:S(2)}) async-start(f32[8,1,192]{2,1,0:T(1,128)} %get-tuple-element.22), calls=%async_computation | async-start | bytes 16384 | tf_op jit(solution)/shard_map/all_to_all | solution.py:270
  83.6 12.5 %collective-permute-start.14 = (f32[1,192]{1,0:T(1,128)S(1)}, f32[1,192]{1,0:T(1,128)S(1)}, u32[]{:S(2)}, u32[]{:S(2)}) collective-permute-start(f32[1,192]{1,0:T(1,128)S(1)} %get-tuple-element.27), channel_id=1, source_target_pairs={{16,0},{32,16},{48,32},{64,48},{80,64},{96,80},{112,96},{128,112},... | collective-permute-start | bytes 2312 | tf_op jit(solution)/shard_map/ppermute | solution.py:241
  86.9 9.3 %collective-permute-start.15 = (f32[1,192]{1,0:T(1,128)S(1)}, f32[1,192]{1,0:T(1,128)S(1)}, u32[]{:S(2)}, u32[]{:S(2)}) collective-permute-start(f32[1,192]{1,0:T(1,128)S(1)} %get-tuple-element.26), channel_id=1, source_target_pairs={{0,48},{16,64},{32,80},{48,96},{64,112},{80,128},{96,144},{112,160... | collective-permute-start | bytes 2312 | tf_op jit(solution)/shard_map/ppermute | solution.py:241
  94.1 7.6 %collective-permute-start.16 = (f32[1,192]{1,0:T(1,128)S(1)}, f32[1,192]{1,0:T(1,128)S(1)}, u32[]{:S(2)}, u32[]{:S(2)}) collective-permute-start(f32[1,192]{1,0:T(1,128)S(1)} %get-tuple-element.25), channel_id=1, source_target_pairs={{32,0},{48,16},{64,32},{80,48},{96,64},{112,80},{128,96},{144,112}... | collective-permute-start | bytes 2312 | tf_op jit(solution)/shard_map/ppermute | solution.py:241
